TPU v7x, 32 devices: a whole 2x2x4 slice. The times are simulated.
32 devices in a mesh: row: 8 (over z, x), col: 4 (over y, core).
Axes of the slice: x: 2, y: 2, z: 4, core: 2. Of those that a mesh axis runs over, the one named last changes fastest.
Arguments:
- layer_input: bfloat16 [16384, 896], P(('row', 'col')), may hold values from -40 to 40
- gain_attn: bfloat16 [896], replicated, may hold values from 0.099609375 to 1.8984375
- qkv_weight: bfloat16 [896, 1152], P('row', 'col'), may hold values from -0.1875 to 0.1875
- qkv_bias: bfloat16 [1152], P('col'), may hold values from -3 to 3
- out_weight: bfloat16 [896, 896], P('col', 'row'), may hold values from -1 to 1
- gain_mlp: bfloat16 [896], replicated, may hold values from 0.099609375 to 1.8984375
- gate_weight: bfloat16 [896, 4864], P('row', 'col'), may hold values from -0.1875 to 0.1875
- up_weight: bfloat16 [896, 4864], P('row', 'col'), may hold values from -0.1875 to 0.1875
- down_weight: bfloat16 [4864, 896], P('col', 'row'), may hold values from -0.078125 to 0.078125
- cotangent: bfloat16 [16384, 896], P(('row', 'col')), may hold values from -6 to 6
Outputs:
- layer_output: bfloat16 [16384, 896], P(('row', 'col'))
- input_grad: bfloat16 [16384, 896], P(('row', 'col'))
- gain_attn_grad: float32 [896], replicated
- qkv_weight_grad: float32 [896, 1152], P('row', 'col')
- qkv_bias_grad: float32 [1152], P('col')
- out_weight_grad: float32 [896, 896], P('col', 'row')
- gain_mlp_grad: float32 [896], replicated
- gate_weight_grad: float32 [896, 4864], P('row', 'col')
- up_weight_grad: float32 [896, 4864], P('row', 'col')
- down_weight_grad: float32 [4864, 896], P('col', 'row')
All inputs are finite; a program needn't handle non-finite values.
Results may differ from a plain program's by a relative error of at most 0.02.
Values may be sent and summed in bfloat16 or wider, within the bound.
No kernel may reach another device: no remote copies, remote signals or barrier semaphores. Data moves between devices by JAX's collectives and lax.ppermute only.
A program may use at most 192 MiB of HBM per device.

v0:
```python
import jax
import jax.numpy as jnp
from jax import lax
from jax.sharding import PartitionSpec as P

HD = 64


eps = 1e-06
theta_base = 1000000.0


def swapped(block, axis, bit):
    count = lax.axis_size(axis)
    route = []
    for low in range(count):
        high = low | 1 << bit
        if high != low and high < count:
            route += [(low, high), (high, low)]
    return lax.ppermute(block, axis, route)


def tables(length):
    half_width = HD // 2
    inverse = theta_base ** (-(jnp.arange(half_width, dtype=jnp.float32) * 2.0 / HD))
    angles = jnp.arange(length, dtype=jnp.float32)[:, None] * inverse[None, :]
    return (jnp.cos(angles), jnp.sin(angles))


def rotate(value_in, cosine, sine_part):
    half_width = value_in.shape[-1] // 2
    first_half = value_in[..., :half_width]
    second = value_in[..., half_width:]
    return jnp.concatenate(
        [first_half * cosine - second * sine_part, second * cosine + first_half * sine_part],
        axis=-1,
    )


def causal(row_start, block_rows, row_stop):
    query_pos = row_start + jnp.arange(block_rows, dtype=jnp.int32)
    key_pos = jnp.arange(row_stop, dtype=jnp.int32)
    return key_pos[None, :] <= query_pos[:, None]


def widen(block_in):
    return lax.all_gather(block_in, "col", axis=0, tiled=True)


def narrow(partial_sum):
    return lax.psum_scatter(
        partial_sum.astype(jnp.bfloat16), "col", scatter_dimension=0, tiled=True
    ).astype(jnp.float32)


def to_heads(block_in, parity, length):
    outgoing = lax.dynamic_slice_in_dim(block_in, (1 - parity) * length, length, 0)
    staying = lax.dynamic_slice_in_dim(block_in, parity * length, length, 0)
    arrived = swapped(outgoing, "col", 0)
    return jnp.where(
        parity == 0, jnp.concatenate([staying, arrived], 1), jnp.concatenate([arrived, staying], 1)
    )


def to_blocks(group_in, parity):
    half_width = group_in.shape[1] // 2
    outgoing = lax.dynamic_slice_in_dim(group_in, (1 - parity) * half_width, half_width, 1)
    staying = lax.dynamic_slice_in_dim(group_in, parity * half_width, half_width, 1)
    arrived = swapped(outgoing, "col", 0)
    return jnp.where(
        parity == 0, jnp.concatenate([staying, arrived], 0), jnp.concatenate([arrived, staying], 0)
    )


def head_forward(query_rows, key_rows, value_rows, block_rows):
    length = query_rows.shape[0]
    score_scale = HD ** (-0.5)
    outputs = []
    log_parts = []
    for row_start in range(0, length, block_rows):
        row_stop = row_start + block_rows
        scores = (
            jnp.einsum(
                "qd,kd->qk",
                query_rows[row_start:row_stop],
                key_rows[:row_stop],
                preferred_element_type=jnp.float32,
            )
            * score_scale
        )
        scores = jnp.where(causal(row_start, block_rows, row_stop), scores, -1e30)
        largest = jnp.max(scores, axis=1, keepdims=True)
        exponent = jnp.exp(scores - largest)
        summed = jnp.sum(exponent, axis=1, keepdims=True)
        probability = (exponent / summed).astype(jnp.bfloat16)
        outputs.append(
            jnp.dot(probability, value_rows[:row_stop], preferred_element_type=jnp.float32)
        )
        log_parts.append((largest + jnp.log(summed))[:, 0])
    return (jnp.concatenate(outputs, 0), jnp.concatenate(log_parts, 0))


def shards(
    layer_input,
    gain_attn,
    qkv_weight,
    qkv_bias,
    out_weight,
    gain_mlp,
    gate_weight,
    up_weight,
    down_weight,
    cotangent,
):
    column = lax.axis_index("col")
    col_count = lax.axis_size("col")
    parity = column % 2
    tok_local, model_width = layer_input.shape
    tok_rows = tok_local * col_count
    length = tok_rows // 2
    ff_cols = gate_weight.shape[1]
    qkv_cols = qkv_weight.shape[1]
    group_width = 2 * qkv_cols
    query_width = group_width - 2 * HD
    head_count = query_width // HD
    block_rows = min(512, length)
    mlp_rows = min(tok_rows, 1024)
    score_scale = HD ** (-0.5)
    qkv_full, out_full, gate_full, up_full, down_full = (
        lax.all_gather(qkv_weight, "row", axis=0, tiled=True),
        lax.all_gather(out_weight.T, "row", axis=0, tiled=True),
        lax.all_gather(gate_weight, "row", axis=0, tiled=True),
        lax.all_gather(up_weight, "row", axis=0, tiled=True),
        lax.all_gather(down_weight.T, "row", axis=0, tiled=True),
    )
    input_rows = layer_input.astype(jnp.float32)
    gain_one = gain_attn.astype(jnp.float32)
    gain_two = gain_mlp.astype(jnp.float32)
    scale_one = lax.rsqrt(jnp.mean(input_rows * input_rows, axis=1) + eps)
    normed_one_blk = (input_rows * scale_one[:, None] * gain_one[None, :]).astype(jnp.bfloat16)
    normed_one = widen(normed_one_blk)
    mixed_blk = (
        jnp.dot(normed_one, qkv_full, preferred_element_type=jnp.float32)
        + qkv_bias.astype(jnp.float32)[None, :]
    ).astype(jnp.bfloat16)
    grouped = to_heads(mixed_blk, parity, length)
    cosine, sine_part = tables(length)
    query_heads = (
        grouped[:, :query_width]
        .astype(jnp.float32)
        .reshape(length, head_count, HD)
        .transpose(1, 0, 2)
    )
    query_heads = rotate(query_heads, cosine[None], sine_part[None]).astype(jnp.bfloat16)
    key_rows = rotate(
        grouped[:, query_width : query_width + HD].astype(jnp.float32), cosine, sine_part
    ).astype(jnp.bfloat16)
    value_rows = grouped[:, query_width + HD :]
    head_outputs, log_totals = lax.map(
        lambda query_one: head_forward(query_one, key_rows, value_rows, block_rows), query_heads
    )
    att_group = head_outputs.transpose(1, 0, 2).reshape(length, query_width).astype(jnp.bfloat16)
    att_blk = to_blocks(att_group, parity)
    attn_partial = jnp.einsum("ta,da->td", att_blk, out_full, preferred_element_type=jnp.float32)
    middle = input_rows + narrow(attn_partial)
    scale_two = lax.rsqrt(jnp.mean(middle * middle, axis=1) + eps)
    normed_two_blk = (middle * scale_two[:, None] * gain_two[None, :]).astype(jnp.bfloat16)
    normed_two = widen(normed_two_blk)
    gate_parts = []
    up_parts = []
    hidden_parts = []
    down_parts = []
    for row_start in range(0, tok_rows, mlp_rows):
        normed_piece = normed_two[row_start : row_start + mlp_rows]
        gate_lin = jnp.dot(normed_piece, gate_full, preferred_element_type=jnp.float32)
        up_lin = jnp.dot(normed_piece, up_full, preferred_element_type=jnp.float32)
        hidden = (jax.nn.silu(gate_lin) * up_lin).astype(jnp.bfloat16)
        down_parts.append(
            jnp.einsum("tf,df->td", hidden, down_full, preferred_element_type=jnp.float32)
        )
        gate_parts.append(gate_lin)
        up_parts.append(up_lin)
        hidden_parts.append(hidden)
    layer_output = (middle + narrow(jnp.concatenate(down_parts, 0))).astype(jnp.bfloat16)
    grad_out = cotangent.astype(jnp.float32)
    grad_full = widen(cotangent)
    down_grad = jnp.zeros((model_width, ff_cols), jnp.float32)
    gate_grad = jnp.zeros((model_width, ff_cols), jnp.float32)
    up_grad = jnp.zeros((model_width, ff_cols), jnp.float32)
    normed_grad_parts = []
    for part_index in range(len(gate_parts)):
        row_start = part_index * mlp_rows
        grad_piece = grad_full[row_start : row_start + mlp_rows]
        grad_hidden = jnp.dot(grad_piece, down_full, preferred_element_type=jnp.float32)
        down_grad = down_grad + jnp.einsum(
            "td,tf->df", grad_piece, hidden_parts[part_index], preferred_element_type=jnp.float32
        )
        gate_lin = gate_parts[part_index]
        sigmoid_gate = jax.nn.sigmoid(gate_lin)
        grad_gate = (
            grad_hidden
            * up_parts[part_index]
            * sigmoid_gate
            * (1.0 + gate_lin * (1.0 - sigmoid_gate))
        ).astype(jnp.bfloat16)
        grad_up = (grad_hidden * gate_lin * sigmoid_gate).astype(jnp.bfloat16)
        normed_piece = normed_two[row_start : row_start + mlp_rows]
        gate_grad = gate_grad + jnp.einsum(
            "td,tf->df", normed_piece, grad_gate, preferred_element_type=jnp.float32
        )
        up_grad = up_grad + jnp.einsum(
            "td,tf->df", normed_piece, grad_up, preferred_element_type=jnp.float32
        )
        normed_grad_parts.append(
            jnp.einsum("tf,df->td", grad_gate, gate_full, preferred_element_type=jnp.float32)
            + jnp.einsum("tf,df->td", grad_up, up_full, preferred_element_type=jnp.float32)
        )
    grad_normed_two = narrow(jnp.concatenate(normed_grad_parts, 0))
    scaled_two = gain_two[None, :] * grad_normed_two
    inner_two = jnp.sum(scaled_two * middle, axis=1)
    grad_middle = (
        grad_out
        + scale_two[:, None] * scaled_two
        - middle * (scale_two**3 * inner_two / model_width)[:, None]
    )
    gain_two_grad = jnp.sum(grad_normed_two * middle * scale_two[:, None], axis=0)
    grad_branch = widen(grad_middle.astype(jnp.bfloat16))
    grad_att_blk = jnp.dot(grad_branch, out_full, preferred_element_type=jnp.float32).astype(
        jnp.bfloat16
    )
    out_grad = jnp.einsum("td,ta->da", grad_branch, att_blk, preferred_element_type=jnp.float32)
    grad_att_group = to_heads(grad_att_blk, parity, length)
    grad_att_heads = grad_att_group.reshape(length, head_count, HD).transpose(1, 0, 2)

    def head_backward(carry, head_inputs):
        key_grad, value_grad = carry
        query_rows, head_grad, log_total = head_inputs
        query_parts = []
        for row_start in range(0, length, block_rows):
            row_stop = row_start + block_rows
            query_block = query_rows[row_start:row_stop]
            grad_block = head_grad[row_start:row_stop]
            scores = (
                jnp.einsum(
                    "qd,kd->qk",
                    query_block,
                    key_rows[:row_stop],
                    preferred_element_type=jnp.float32,
                )
                * score_scale
            )
            scores = jnp.where(causal(row_start, block_rows, row_stop), scores, -1e30)
            probability = jnp.exp(scores - log_total[row_start:row_stop, None])
            prob_grad = jnp.einsum(
                "qd,kd->qk", grad_block, value_rows[:row_stop], preferred_element_type=jnp.float32
            )
            row_inner = jnp.sum(probability * prob_grad, axis=1, keepdims=True)
            score_grad = (probability * (prob_grad - row_inner) * score_scale).astype(jnp.bfloat16)
            query_parts.append(
                jnp.dot(score_grad, key_rows[:row_stop], preferred_element_type=jnp.float32)
            )
            padding = ((0, length - row_stop), (0, 0))
            key_grad = key_grad + jnp.pad(
                jnp.einsum(
                    "qk,qd->kd", score_grad, query_block, preferred_element_type=jnp.float32
                ),
                padding,
            )
            value_grad = value_grad + jnp.pad(
                jnp.einsum(
                    "qk,qd->kd",
                    probability.astype(jnp.bfloat16),
                    grad_block,
                    preferred_element_type=jnp.float32,
                ),
                padding,
            )
        return ((key_grad, value_grad), jnp.concatenate(query_parts, 0))

    zero_rows = jnp.zeros((length, HD), jnp.float32)
    (key_grad, value_grad), query_grad = lax.scan(
        head_backward, (zero_rows, zero_rows), (query_heads, grad_att_heads, log_totals)
    )
    query_grad = rotate(query_grad, cosine[None], -sine_part[None])
    key_grad = rotate(key_grad, cosine, -sine_part)
    grad_group = jnp.concatenate(
        [query_grad.transpose(1, 0, 2).reshape(length, query_width), key_grad, value_grad], 1
    ).astype(jnp.bfloat16)
    grad_mixed = to_blocks(grad_group, parity)
    bias_grad = jnp.sum(grad_mixed, axis=0, dtype=jnp.float32)
    qkv_grad = jnp.einsum("td,tc->dc", normed_one, grad_mixed, preferred_element_type=jnp.float32)
    grad_normed_one = narrow(
        jnp.einsum("tc,dc->td", grad_mixed, qkv_full, preferred_element_type=jnp.float32)
    )
    scaled_one = gain_one[None, :] * grad_normed_one
    inner_one = jnp.sum(scaled_one * input_rows, axis=1)
    input_grad = (
        grad_middle
        + scale_one[:, None] * scaled_one
        - input_rows * (scale_one**3 * inner_one / model_width)[:, None]
    ).astype(jnp.bfloat16)
    gain_one_grad = jnp.sum(grad_normed_one * input_rows * scale_one[:, None], axis=0)
    bias_row = lax.dynamic_update_slice_in_dim(
        jnp.zeros((qkv_cols * col_count,), jnp.float32), bias_grad, column * qkv_cols, 0
    )
    qkv_total, out_total, gate_total, up_total, down_total = (
        lax.psum_scatter(qkv_grad, "row", scatter_dimension=0, tiled=True),
        lax.psum_scatter(out_grad, "row", scatter_dimension=0, tiled=True),
        lax.psum_scatter(gate_grad, "row", scatter_dimension=0, tiled=True),
        lax.psum_scatter(up_grad, "row", scatter_dimension=0, tiled=True),
        lax.psum_scatter(down_grad, "row", scatter_dimension=0, tiled=True),
    )
    gain_one_total, gain_two_total, bias_whole = lax.psum(
        (gain_one_grad, gain_two_grad, bias_row), ("row", "col")
    )
    bias_total = lax.dynamic_slice_in_dim(bias_whole, column * qkv_cols, qkv_cols, 0)
    return (
        layer_output,
        input_grad,
        gain_one_total,
        qkv_total,
        bias_total,
        out_total.T,
        gain_two_total,
        gate_total,
        up_total,
        down_total.T,
    )


def solution(mesh):
    in_specs = (
        P(("row", "col"), None),
        P(),
        P("row", "col"),
        P("col"),
        P("col", "row"),
        P(),
        P("row", "col"),
        P("row", "col"),
        P("col", "row"),
        P(("row", "col"), None),
    )
    out_specs = (
        P(("row", "col"), None),
        P(("row", "col"), None),
        P(),
        P("row", "col"),
        P("col"),
        P("col", "row"),
        P(),
        P("row", "col"),
        P("row", "col"),
        P("col", "row"),
    )
    return jax.shard_map(shards, mesh=mesh, in_specs=in_specs, out_specs=out_specs, check_vma=False)
```

profile of v0, /device:TPU:0, one launch (start us, length us, event | category | flops | bytes accessed | tf_op | source)
XLA Modules:
  0.0 1050.9 jit_solution(5089754904073125962)
XLA Ops:
  11.4 2.4 fusion.46
  13.8 33.3 %all-gather = bf16[8,112,288]{1,2,0:T(8,128)(2,1)S(1)} all-gather(bf16[1,112,288]{1,2,0:T(8,128)(2,1)S(1)} %bitcast.188), channel_id=1, replica_groups=mesh['row'=8,'col'=4] {'row'}, dimensions={0}, use_global_device_ids=true | all-gather | bytes 580608 | tf_op jit(solution)/shard_map/all_gather | solution.py:130
  48.1 3.5 fusion.32
  57.6 1.9 copy.40
  59.9 28.4 %while.31 = (s32[]{:T(128)}, bf16[7,1024,64]{1,2,0:T(8,128)(2,1)S(1)}, f32[7,1024]{1,0:T(8,128)}, bf16[7,1024,64]{2,1,0:T(8,128)(2,1)S(1)}, bf16[1024,64]{1,0:T(8,128)(2,1)S(1)}, /*index=5*/bf16[1024,64]{1,0:T(8,128)(2,1)S(1)}) while((s32[]{:T(128)}, bf16[7,1024,64]{1,2,0:T(8,128)(2,1)S(1)}, f32[7,1024]{1,0:T(8,128)}, ...), condition=%wide.region_6.7_spmd.clone, body=%wide.region_1.6_spmd.sunk.clone | while | flops 208667136 | bytes 10801261 | solution.py:159
  89.7 31.4 %all_gather.29 = bf16[896,224]{1,0:T(8,128)(2,1)S(1)} all-gather(bf16[112,224]{1,0:T(8,128)(2,1)S(1)} %bitcast.184), channel_id=1, replica_groups=mesh['row'=8,'col'=4] {'row'}, dimensions={0}, use_global_device_ids=true | all-gather | bytes 451584 | tf_op jit(solution)/shard_map/all_gather | solution.py:131
  121.9 4.3 convolution_convert_fusion.1
  126.9 41.4 %reduce-scatter.14.cloned.1.call-done = bf16[512,896]{1,0:T(8,128)(2,1)} async-done(((bf16[2048,896]{1,0:T(8,128)(2,1)}), bf16[512,896]{1,0:T(8,128)(2,1)}) %reduce-scatter.14.cloned.1.call-update) | async-done | bytes 917520 | tf_op jit(solution)/shard_map/reduce_scatter | solution.py:51
  173.6 7.1 all-gather.13.cloned.1.call-done
  180.7 32.0 %all-gather.11.cloned.1.call-done = bf16[2048,896]{1,0:T(8,128)(2,1)} async-done(((bf16[512,896]{1,0:T(8,128)(2,1)}), bf16[2048,896]{1,0:T(8,128)(2,1)}) %all-gather.11.cloned.1.call-update) | async-done | bytes 3670032 | tf_op jit(solution)/shard_map/all_gather | solution.py:47
  212.7 7.4 fusion.61
  220.1 4.5 fusion.69
  224.6 41.5 %all-gather.15.cloned.1.call-done = bf16[896,1216]{1,0:T(8,128)(2,1)} async-done(((bf16[112,1216]{1,0:T(8,128)(2,1)}), bf16[896,1216]{1,0:T(8,128)(2,1)}) %all-gather.15.cloned.1.call-update) | async-done | bytes 2179088 | tf_op jit(solution)/shard_map/all_gather | solution.py:133
  266.1 7.3 fusion.59
  273.4 4.5 fusion.67
  277.9 40.3 %all-gather.17.cloned.1.call-done = bf16[896,1216]{1,0:T(8,128)(2,1)} async-done(((bf16[112,1216]{1,0:T(8,128)(2,1)}), bf16[896,1216]{1,0:T(8,128)(2,1)}) %all-gather.17.cloned.1.call-update) | async-done | bytes 2179088 | tf_op jit(solution)/shard_map/all_gather | solution.py:134
  318.2 31.6 %all-gather.19.cloned.1.call-done = bf16[2048,896]{1,0:T(8,128)(2,1)} async-done(((bf16[512,896]{1,0:T(8,128)(2,1)}), bf16[2048,896]{1,0:T(8,128)(2,1)}) %all-gather.19.cloned.1.call-update) | async-done | bytes 3670032 | tf_op jit(solution)/shard_map/all_gather | solution.py:47
  349.8 10.4 multiply_convert_fusion.2
  360.2 2.9 fusion.88
  366.1 8.9 multiply_convert_fusion.4
  375.1 4.8 fusion.87
  379.9 3.0 add_convert_fusion
  382.9 3.0 add_convert_fusion.1
  385.9 2.1 pad_maximum_fusion.2
  388.2 41.2 %reduce-scatter.18.cloned.1.call-done = bf16[512,896]{1,0:T(8,128)(2,1)} async-done(((bf16[2048,896]{1,0:T(8,128)(2,1)}), bf16[512,896]{1,0:T(8,128)(2,1)}) %reduce-scatter.18.cloned.1.call-update) | async-done | bytes 917520 | tf_op jit(solution)/shard_map/reduce_scatter | solution.py:51
  429.4 2.1 fusion.43
  433.2 31.6 %all-gather.21.cloned.1.call-done = bf16[2048,896]{1,0:T(8,128)(2,1)} async-done(((bf16[512,896]{1,0:T(8,128)(2,1)}), bf16[2048,896]{1,0:T(8,128)(2,1)}) %all-gather.21.cloned.1.call-update) | async-done | bytes 3670032 | tf_op jit(solution)/shard_map/all_gather | solution.py:47
  464.8 3.5 convolution_convert_fusion.2
  468.7 4.3 fusion.71
  475.2 115.1 %while.32 = (s32[]{:T(128)}, f32[1024,64]{0,1:T(8,128)}, f32[1024,64]{0,1:T(8,128)}, f32[7,1024,64]{1,2,0:T(8,128)}, bf16[7,1024,64]{2,1,0:T(8,128)(2,1)}, /*ind...) while((s32[]{:T(128)}, f32[1024,64]{0,1:T(8,128)}, ...), condition=%wide.region_15.16_spmd.clone.clone, body=%wide.region_12.15_spmd.clone.sunk.clone | while | flops 512425472 | bytes 43540884 | solution.py:281
  485.5 2.1 convolution_add_fusion.9
  493.8 1.8 multiply_reduce_fusion.7
  501.9 2.2 convolution_add_fusion.9
  510.3 1.8 multiply_reduce_fusion.7
  518.3 2.2 convolution_add_fusion.9
  526.8 1.8 multiply_reduce_fusion.7
  534.8 2.2 convolution_add_fusion.9
  543.2 1.8 multiply_reduce_fusion.7
  551.2 2.2 convolution_add_fusion.9
  559.7 1.8 multiply_reduce_fusion.7
  567.7 2.2 convolution_add_fusion.9
  576.1 1.8 multiply_reduce_fusion.7
  584.2 2.2 convolution_add_fusion.9
  590.3 1.8 subtract_convert_fusion
  595.1 3.2 fusion.82
  598.7 4.2 convolution_convert_fusion
  604.5 4.9 convolution_convert_fusion.3
  609.4 2.9 convolution_convert_fusion.4
  612.4 2.1 pad_maximum_fusion.1
  615.0 5.1 fusion.65
  620.1 4.8 convolution_add_fusion.3
  625.1 5.0 fusion.63
  630.1 4.8 convolution_add_fusion.2
  635.2 5.2 fusion.53
  640.4 4.3 add_bitcast_fusion
  644.7 5.6 copy.52
  654.1 9.3 reduce-scatter.28.cloned.1.call-done
  665.1 40.9 %reduce-scatter.20.cloned.1.call-done = bf16[512,896]{1,0:T(8,128)(2,1)} async-done(((bf16[2048,896]{1,0:T(8,128)(2,1)}), bf16[512,896]{1,0:T(8,128)(2,1)}) %reduce-scatter.20.cloned.1.call-update) | async-done | bytes 917520 | tf_op jit(solution)/shard_map/reduce_scatter | solution.py:51
  706.0 2.0 fusion.49
  708.0 39.8 %all-reduce.2 = (f32[896]{0:T(1024)}, f32[1152]{0:T(1024)S(1)}, f32[896]{0:T(1024)}) all-reduce(f32[896]{0:T(1024)S(1)} %get-tuple-element.270, f32[1152]{0:T(1024)S(1)} %dynamic_update_slice.17, f32[896]{0:T(1024)S(1)} %get-tuple-element.268), channel_id=1, replica_groups=mesh['row'=8,'col'=4] {'row','col'}, use_global_device_ids=true, to_apply=%region_19.20 | all-reduce | flops 2944 | bytes 23552 | tf_op jit(solution)/shard_map/psum | solution.py:313
  750.2 4.2 fusion.38
  754.4 93.9 %reduce-scatter.24.cloned.1.call-done = f32[112,1216]{1,0:T(8,128)} async-done(((f32[896,1216]{1,0:T(8,128)}), f32[112,1216]{1,0:T(8,128)}) %reduce-scatter.24.cloned.1.call-update) | async-done | bytes 544784 | tf_op jit(solution)/shard_map/reduce_scatter | solution.py:309
  848.3 97.6 %reduce-scatter.26.cloned.1.call-done = f32[112,1216]{1,0:T(8,128)} async-done(((f32[896,1216]{1,0:T(8,128)}), f32[112,1216]{1,0:T(8,128)}) %reduce-scatter.26.cloned.1.call-update) | async-done | bytes 544784 | tf_op jit(solution)/shard_map/reduce_scatter | solution.py:310
  945.9 97.7 %reduce-scatter.30.cloned.1.call-done = f32[112,1216]{1,0:T(8,128)} async-done(((f32[896,1216]{1,0:T(8,128)}), f32[112,1216]{1,0:T(8,128)}) %reduce-scatter.30.cloned.1.call-update) | async-done | bytes 544784
  (470 shorter events, 156.0 us)
Async XLA Ops:
  8.0 5.8 copy-start.24
  8.0 40.1 %all-gather.9.cloned.1.call-start = ((), (), s32[]{:S(2)}) async-start(), calls=%async_computation.9 | async-start | bytes 4587520 | tf_op jit(solution)/shard_map/all_gather | solution.py:47
  13.7 34.1 %copy-start.35 = (bf16[288]{0:T(512)(128)(2,1)S(1)}, bf16[288]{0:T(512)(128)(2,1)}, u32[]{:S(2)}) copy-start(bf16[288]{0:T(512)(128)(2,1)} %param.17) | copy-start | bytes 1732
  13.8 154.5 %reduce-scatter.14.cloned.1.call-start = ((), (), s32[]{:S(2)}) async-start(), calls=%async_computation.10 | async-start | bytes 4587520 | tf_op jit(solution)/shard_map/reduce_scatter | solution.py:51
  47.9 3.7 copy-start.20
  51.7 2.1 collective-permute-start
  52.0 2.7 copy-start.33
  59.9 29.7 %copy-start.27 = (bf16[224,112]{1,0:T(8,128)(2,1)S(1)}, bf16[224,112]{1,0:T(8,128)(2,1)}, u32[]{:S(2)}) copy-start(bf16[224,112]{1,0:T(8,128)(2,1)} %param.18) | copy-start | bytes 150532
  88.3 32.9 %copy-start.10 = (bf16[7,1024,64]{2,1,0:T(8,128)(2,1)}, bf16[7,1024,64]{2,1,0:T(8,128)(2,1)S(1)}, u32[]{:S(2)}) copy-start(bf16[7,1024,64]{2,1,0:T(8,128)(2,1)S(1)} %get-tuple-element.584) | copy-start | bytes 2752516
  89.3 31.8 %collective-permute-start.1 = (bf16[1024,224]{0,1:T(8,128)(2,1)}, bf16[1024,224]{0,1:T(8,128)(2,1)S(1)}, u32[]{:S(2)}, u32[]{:S(2)}) collective-permute-start(bf16[1024,224]{0,1:T(8,128)(2,1)} %get-tuple-element.338), channel_id=1, source_target_pairs={{0,1},{1,0},{2,3},{3,2},{4,5},{5,4},{6,7},{7,6},{8,9},{9,8},{10,11... | collective-permute-start | bytes 1376264 | tf_op jit(solution)/shard_map/ppermute | solution.py:20
  121.1 5.1 copy-start.49
  126.2 42.1 %copy-start.4 = (bf16[512,896]{1,0:T(8,128)(2,1)S(1)}, bf16[512,896]{1,0:T(8,128)(2,1)}, u32[]{:S(2)}) copy-start(bf16[512,896]{1,0:T(8,128)(2,1)} %param.14) | copy-start | bytes 2752516
  126.2 54.4 %all-gather.13.cloned.1.call-start = ((), (), s32[]{:S(2)}) async-start(), calls=%async_computation.12 | async-start | bytes 2580480 | tf_op jit(solution)/shard_map/all_gather | solution.py:132
  126.8 85.8 %all-gather.11.cloned.1.call-start = ((), (), s32[]{:S(2)}) async-start(), calls=%async_computation.11 | async-start | bytes 4587520 | tf_op jit(solution)/shard_map/all_gather | solution.py:47
  171.3 94.8 %all-gather.15.cloned.1.call-start = ((), (), s32[]{:S(2)}) async-start(), calls=%async_computation.13 | async-start | bytes 2580480 | tf_op jit(solution)/shard_map/all_gather | solution.py:133
  171.8 146.4 %all-gather.17.cloned.1.call-start = ((), (), s32[]{:S(2)}) async-start(), calls=%async_computation.14 | async-start | bytes 2580480 | tf_op jit(solution)/shard_map/all_gather | solution.py:134
  172.6 177.2 %all-gather.19.cloned.1.call-start = ((), (), s32[]{:S(2)}) async-start(), calls=%async_computation.16 | async-start | bytes 4587520 | tf_op jit(solution)/shard_map/all_gather | solution.py:47
  173.3 256.1 %reduce-scatter.18.cloned.1.call-start = ((), (), s32[]{:S(2)}) async-start(), calls=%async_computation.17 | async-start | bytes 4587520 | tf_op jit(solution)/shard_map/reduce_scatter | solution.py:51
  212.7 7.4 copy-start.37
  212.7 7.4 copy-start.45
  266.1 7.3 copy-start.38
  266.1 7.3 copy-start.47
  349.8 10.4 copy-start.46
  360.2 3.0 copy-start.55
  360.2 19.7 %copy-start.53 = (bf16[1024,1216]{0,1:T(8,128)(2,1)}, bf16[1024,1216]{0,1:T(8,128)(2,1)S(1)}, u32[]{:S(2)}) copy-start(bf16[1024,1216]{0,1:T(8,128)(2,1)S(1)} %get-tuple-element.320) | copy-start | bytes 7471108
  360.2 3.8 copy-start.41
  360.2 4.5 copy-start.43
  360.2 6.0 copy-start.50
  375.1 4.8 copy-start.48
  379.9 3.0 copy-start.57
  388.0 43.5 %copy-start.15 = (bf16[512,896]{1,0:T(8,128)(2,1)S(1)}, bf16[512,896]{1,0:T(8,128)(2,1)}, u32[]{:S(2)}) copy-start(bf16[512,896]{1,0:T(8,128)(2,1)} %param.23) | copy-start | bytes 2752516
  388.0 76.8 %all-gather.21.cloned.1.call-start = ((), (), s32[]{:S(2)}) async-start(), calls=%async_computation.18 | async-start | bytes 4587520 | tf_op jit(solution)/shard_map/all_gather | solution.py:47
  433.1 35.6 %copy-start.22 = (bf16[1024,224]{0,1:T(8,128)(2,1)S(1)}, bf16[1024,224]{0,1:T(8,128)(2,1)}, u32[]{:S(2)}) copy-start(bf16[1024,224]{0,1:T(8,128)(2,1)} %get-tuple-element.337) | copy-start | bytes 1376260
  433.1 219.3 %reduce-scatter.22.cloned.1.call-start = ((), (), s32[]{:S(2)}) async-start(), calls=%async_computation.20 | async-start | bytes 1032192 | tf_op jit(solution)/shard_map/reduce_scatter | solution.py:308
  468.4 4.7 collective-permute-start.2
  473.1 190.3 %reduce-scatter.28.cloned.1.call-start = ((), (), s32[]{:S(2)}) async-start(), calls=%async_computation.23 | async-start | bytes 1548288
  485.5 3.3 copy-start.11
  501.8 3.4 copy-start.11
  518.3 3.4 copy-start.11
  534.8 3.4 copy-start.11
  551.2 3.4 copy-start.11
  567.7 3.4 copy-start.11
  584.1 3.4 copy-start.11
  593.1 2.1 collective-permute-start.3
  595.1 3.5 copy-start.19
  595.1 3.5 copy-start.21
  598.4 107.6 %reduce-scatter.20.cloned.1.call-start = ((), (), s32[]{:S(2)}) async-start(), calls=%async_computation.19 | async-start | bytes 4587520 | tf_op jit(solution)/shard_map/reduce_scatter | solution.py:51
  602.9 147.3 %reduce-scatter.16.cloned.1.call-start = ((), (), s32[]{:S(2)}) async-start(), calls=%async_computation.15 | async-start | bytes 4587520 | tf_op jit(solution)/shard_map/reduce_scatter | solution.py:51
  604.5 4.9 copy-start.52
  614.5 5.6 copy-start.56
  614.5 233.8 %reduce-scatter.24.cloned.1.call-start = ((), (), s32[]{:S(2)}) async-start(), calls=%async_computation.21 | async-start | bytes 5160960 | tf_op jit(solution)/shard_map/reduce_scatter | solution.py:309
  615.0 5.1 copy-start.39
  625.0 5.1 copy-start.54
  625.0 320.9 %reduce-scatter.26.cloned.1.call-start = ((), (), s32[]{:S(2)}) async-start(), calls=%async_computation.22 | async-start | bytes 5160960 | tf_op jit(solution)/shard_map/reduce_scatter | solution.py:310
  625.0 5.1 copy-start.40
  634.9 5.4 copy-start.51
  634.9 408.6 %reduce-scatter.30.cloned.1.call-start = ((), (), s32[]{:S(2)}) async-start(), calls=%async_computation.24 | async-start | bytes 5160960
  635.2 5.2 copy-start.42
  650.3 55.6 %copy-start.5 = (bf16[512,896]{1,0:T(8,128)(2,1)S(1)}, bf16[512,896]{1,0:T(8,128)(2,1)}, u32[]{:S(2)}) copy-start(bf16[512,896]{1,0:T(8,128)(2,1)} %param.14) | copy-start | bytes 2752516
  650.3 55.6 %copy-start.26 = (f32[896]{0:T(1024)S(1)}, f32[896]{0:T(1024)}, u32[]{:S(2)}) copy-start(f32[896]{0:T(1024)} %copy-done.25) | copy-start | bytes 10756
  650.3 55.6 %copy-start.29 = (f32[512]{0:T(512)S(1)}, f32[512]{0:T(512)}, u32[]{:S(2)}) copy-start(f32[512]{0:T(512)} %copy-done.28) | copy-start | bytes 6148
  650.4 98.1 %copy-start.31 = (f32[512]{0:T(512)S(1)}, f32[512]{0:T(512)}, u32[]{:S(2)}) copy-start(f32[512]{0:T(512)} %copy-done.30) | copy-start | bytes 6148
  650.4 99.9 %copy-start.7 = (bf16[512,896]{1,0:T(8,128)(2,1)S(1)}, bf16[512,896]{1,0:T(8,128)(2,1)}, u32[]{:S(2)}) copy-start(bf16[512,896]{1,0:T(8,128)(2,1)} %reduce-scatter.14.cloned.1.call-done) | copy-start | bytes 2752516
  650.4 99.9 %copy-start.16 = (bf16[512,896]{1,0:T(8,128)(2,1)S(1)}, bf16[512,896]{1,0:T(8,128)(2,1)}, u32[]{:S(2)}) copy-start(bf16[512,896]{1,0:T(8,128)(2,1)} %param.23) | copy-start | bytes 2752516
  (62 other events, 95.3 us)
Sparse Core Ops, SparseCore 0:
  13.9 34.1 all-gather.8
  126.4 41.8 reduce-scatter.13
  388.1 41.2 reduce-scatter.17
  433.2 31.4 all-gather.20
Sparse Core Ops, SparseCore 1:
  128.9 51.7 all-gather.12
  182.8 29.8 all-gather.10
  215.0 51.1 all-gather.14
  268.5 49.6 all-gather.16
  319.9 29.8 all-gather.18
  473.2 63.0 reduce-scatter.21
  598.5 64.8 reduce-scatter.27
  665.9 40.0 reduce-scatter.19
  708.4 41.8 reduce-scatter.15
  754.9 93.4 reduce-scatter.23
  852.8 93.0 reduce-scatter.25
  950.5 93.0 reduce-scatter.29
where the time goes:
time: 1060 us; the launch traced here: 1050 us
  waiting for transfers between devices  614 us (58%)
  matrix products  216 us (20%)
  blocking collectives  104 us (10%)
  local copies, waits for them, and re-layouts  51.2 us (5%)
  other arithmetic  44.5 us (4%)
  between operations  16.3 us (2%)
    reduce_scatter x4, waiting for transfers between devices, narrow(): lax.psum_scatter(partial_sum.astype(jnp.bfloat16), 'col', scatter_dimensi...  125 us
    unnamed x18, waiting for transfers between devices  110 us
    reduce_scatter x1, waiting for transfers between devices, shards(): lax.psum_scatter(up_grad, 'row', scatter_dimension=0, tiled=True)  97.6 us
    all_gather x4, waiting for transfers between devices, widen(): return lax.all_gather(block_in, 'col', axis=0, tiled=True)  95.4 us
    reduce_scatter x1, waiting for transfers between devices, shards(): lax.psum_scatter(gate_grad, 'row', scatter_dimension=0, tiled=True)  93.9 us
    all_gather x1, waiting for transfers between devices, shards(): lax.all_gather(up_weight, 'row', axis=0, tiled=True)  41.5 us
    all_gather x1, waiting for transfers between devices, shards(): lax.all_gather(down_weight.T, 'row', axis=0, tiled=True)  40.3 us
    psum x1, blocking collectives, shards(): lax.psum((gain_one_grad, gain_two_grad, bias_row), ('row', 'col'))  39.8 us
  transfers between devices with their start and end apart: 20, of which 17 were waited for; matrix products, arithmetic and copies ran while one was open for 19% of the time, Pallas kernels for 0%

commit v1 on v0

v1 whole, which is shorter than its diff:
```python
import jax
import jax.numpy as jnp
from jax import lax
from jax.sharding import PartitionSpec as P

HD = 64


eps = 1e-06
theta_base = 1000000.0
bf16 = jnp.bfloat16
f32 = jnp.float32


def flip(block, axis, bit):
    count = lax.axis_size(axis)
    return lax.ppermute(block, axis, [(i, i ^ 1 << bit) for i in range(count)])


def bit_reversed(value, bits):
    return sum((value >> b & 1) << (bits - 1 - b) for b in range(bits))


def tables(length):
    half_width = HD // 2
    inverse = theta_base ** (-(jnp.arange(half_width, dtype=jnp.float32) * 2.0 / HD))
    angles = jnp.arange(length, dtype=jnp.float32)[:, None] * inverse[None, :]
    return (jnp.cos(angles), jnp.sin(angles))


def rotate(value_in, cosine, sine_part):
    half_width = value_in.shape[-1] // 2
    first_half = value_in[..., :half_width]
    second = value_in[..., half_width:]
    return jnp.concatenate(
        [first_half * cosine - second * sine_part, second * cosine + first_half * sine_part],
        axis=-1,
    )


def causal(row_start, block_rows, row_stop):
    query_pos = row_start + jnp.arange(block_rows, dtype=jnp.int32)
    key_pos = jnp.arange(row_stop, dtype=jnp.int32)
    return key_pos[None, :] <= query_pos[:, None]


def gather_rows(block, bits):
    if bits > 3:
        for bit in reversed(range(bits)):
            block = jnp.concatenate([block, flip(block, "row", bit)], 0)
        return block
    held = [block]
    for bit in reversed(range(bits)):
        held = held + [flip(piece, "row", bit) for piece in held]
    return jnp.concatenate(held, 0)


def scatter_rows(total, bits):
    for bit in range(bits):
        half = total.shape[0] // 2
        got = flip(total[half:].astype(bf16), "row", bit)
        total = total[:half] + got.astype(f32)
    return total


def in_order(first, second, parity, axis=0):
    return jnp.where(
        parity == 0,
        jnp.concatenate([first, second], axis),
        jnp.concatenate([second, first], axis),
    )


def pair(block, parity):
    return in_order(block, flip(block, "col", 0), parity)


def keep_half(partial, parity):
    half = partial.shape[0] // 2
    outgoing = lax.dynamic_slice_in_dim(partial, (1 - parity) * half, half, 0).astype(bf16)
    staying = lax.dynamic_slice_in_dim(partial, parity * half, half, 0)
    return staying + flip(outgoing, "col", 0).astype(f32)


def to_pairs(block):
    first = lax.ppermute(block, "col", [(2 * a + b, 2 * b + a) for a in range(2) for b in range(2)])
    second = lax.ppermute(
        block, "col", [(2 * a + b, 2 * (1 - b) + a) for a in range(2) for b in range(2)]
    )
    return first, second


def from_pairs(same, other):
    first = lax.ppermute(same, "col", [(2 * a + b, 2 * b + a) for a in range(2) for b in range(2)])
    second = lax.ppermute(
        other, "col", [(2 * a + b, 2 * b + 1 - a) for a in range(2) for b in range(2)]
    )
    return first, second


def head_forward(query_rows, key_rows, value_rows, block_rows):
    length = query_rows.shape[0]
    score_scale = HD ** (-0.5)
    outputs = []
    log_parts = []
    for row_start in range(0, length, block_rows):
        row_stop = row_start + block_rows
        scores = (
            jnp.einsum(
                "qd,kd->qk",
                query_rows[row_start:row_stop],
                key_rows[:row_stop],
                preferred_element_type=jnp.float32,
            )
            * score_scale
        )
        scores = jnp.where(causal(row_start, block_rows, row_stop), scores, -1e30)
        largest = jnp.max(scores, axis=1, keepdims=True)
        exponent = jnp.exp(scores - largest)
        summed = jnp.sum(exponent, axis=1, keepdims=True)
        probability = (exponent / summed).astype(jnp.bfloat16)
        outputs.append(
            jnp.dot(probability, value_rows[:row_stop], preferred_element_type=jnp.float32)
        )
        log_parts.append((largest + jnp.log(summed))[:, 0])
    return (jnp.concatenate(outputs, 0), jnp.concatenate(log_parts, 0))


def attention_forward(query_heads, key_rows, value_rows, block_rows):
    return lax.map(
        lambda query_one: head_forward(query_one, key_rows, value_rows, block_rows), query_heads
    )


def attention_backward(query_heads, key_rows, value_rows, grad_heads, log_totals, block_rows):
    length = key_rows.shape[0]
    score_scale = HD ** (-0.5)

    def head_backward(carry, head_inputs):
        key_grad, value_grad = carry
        query_rows, head_grad, log_total = head_inputs
        query_parts = []
        for row_start in range(0, length, block_rows):
            row_stop = row_start + block_rows
            query_block = query_rows[row_start:row_stop]
            grad_block = head_grad[row_start:row_stop]
            scores = (
                jnp.einsum(
                    "qd,kd->qk",
                    query_block,
                    key_rows[:row_stop],
                    preferred_element_type=jnp.float32,
                )
                * score_scale
            )
            scores = jnp.where(causal(row_start, block_rows, row_stop), scores, -1e30)
            probability = jnp.exp(scores - log_total[row_start:row_stop, None])
            prob_grad = jnp.einsum(
                "qd,kd->qk", grad_block, value_rows[:row_stop], preferred_element_type=jnp.float32
            )
            row_inner = jnp.sum(probability * prob_grad, axis=1, keepdims=True)
            score_grad = (probability * (prob_grad - row_inner) * score_scale).astype(jnp.bfloat16)
            query_parts.append(
                jnp.dot(score_grad, key_rows[:row_stop], preferred_element_type=jnp.float32)
            )
            padding = ((0, length - row_stop), (0, 0))
            key_grad = key_grad + jnp.pad(
                jnp.einsum(
                    "qk,qd->kd", score_grad, query_block, preferred_element_type=jnp.float32
                ),
                padding,
            )
            value_grad = value_grad + jnp.pad(
                jnp.einsum(
                    "qk,qd->kd",
                    probability.astype(jnp.bfloat16),
                    grad_block,
                    preferred_element_type=jnp.float32,
                ),
                padding,
            )
        return ((key_grad, value_grad), jnp.concatenate(query_parts, 0))

    zero_rows = jnp.zeros((length, HD), jnp.float32)
    (key_grad, value_grad), query_grad = lax.scan(
        head_backward, (zero_rows, zero_rows), (query_heads, grad_heads, log_totals)
    )
    return query_grad, key_grad, value_grad


def cuts(width, count):
    step = -(-width // count // 128) * 128
    return [(start, min(start + step, width)) for start in range(0, width, step)]


def shards(
    layer_input,
    gain_attn,
    qkv_weight,
    qkv_bias,
    out_weight,
    gain_mlp,
    gate_weight,
    up_weight,
    down_weight,
    cotangent,
):
    row = lax.axis_index("row")
    column = lax.axis_index("col")
    row_count = lax.axis_size("row")
    bits = row_count.bit_length() - 1
    core = column % 2
    sequence = column // 2
    tok_local, model_width = layer_input.shape
    length = tok_local * 2
    deep = model_width // row_count
    ff_cols = gate_weight.shape[1]
    qkv_cols = qkv_weight.shape[1]
    out_cols = out_weight.shape[0]
    group_width = 2 * qkv_cols
    query_width = group_width - 2 * HD
    head_count = query_width // HD
    block_rows = min(512, length)
    score_scale = HD ** (-0.5)

    first, second = to_pairs(jnp.concatenate([qkv_weight, out_weight.T], 1))
    low = jnp.where(sequence == 0, first, second)
    high = jnp.where(sequence == 0, second, first)
    qkv_full = gather_rows(jnp.concatenate([low[:, :qkv_cols], high[:, :qkv_cols]], 1), bits)
    out_full = gather_rows(jnp.concatenate([low[:, qkv_cols:], high[:, qkv_cols:]], 1), bits)
    first, second = to_pairs(qkv_bias[None, :])
    bias_full = in_order(first, second, sequence, 1).astype(f32)

    place = jnp.arange(model_width, dtype=jnp.int32)
    masks = jnp.array([bit_reversed(p, bits) for p in range(row_count)], jnp.int32)
    source = jnp.repeat(masks ^ row, deep) * deep + place % deep
    to_stored = (place[:, None] == source[None, :]).astype(bf16)

    def stored(block):
        return jnp.dot(block, to_stored, preferred_element_type=f32)

    def unstored(block):
        return jnp.einsum("ts,fs->tf", block, to_stored, preferred_element_type=f32).astype(bf16)

    def unstored_row(vector):
        blocks = vector.reshape(row_count, deep)
        blocks = jnp.concatenate(
            [blocks[bit_reversed(m, bits)][None] for m in range(row_count)], 0
        )
        for bit in range(bits):
            wide = blocks.reshape(-1, 2, 1 << bit, deep)
            turned = jnp.concatenate([wide[:, 1:], wide[:, :1]], 1).reshape(row_count, deep)
            blocks = jnp.where((row >> bit) % 2 == 1, turned, blocks)
        return blocks.reshape(model_width)

    input_rows = stored(layer_input)
    grad_out = stored(cotangent)
    gain_one = stored(gain_attn[None, :])
    gain_two = stored(gain_mlp[None, :])

    scale_one = lax.rsqrt(jnp.mean(input_rows * input_rows, axis=1) + eps)
    normed_one_blk = (input_rows * scale_one[:, None] * gain_one).astype(bf16)
    normed_one = pair(normed_one_blk, core)
    grouped = (jnp.dot(normed_one, qkv_full, preferred_element_type=f32) + bias_full).astype(bf16)
    cosine, sine_part = tables(length)
    query_heads = (
        grouped[:, :query_width].astype(f32).reshape(length, head_count, HD).transpose(1, 0, 2)
    )
    query_heads = rotate(query_heads, cosine[None], sine_part[None]).astype(bf16)
    key_rows = rotate(
        grouped[:, query_width : query_width + HD].astype(f32), cosine, sine_part
    ).astype(bf16)
    value_rows = grouped[:, query_width + HD :]
    head_outputs, log_totals = attention_forward(query_heads, key_rows, value_rows, block_rows)
    att_group = head_outputs.transpose(1, 0, 2).reshape(length, query_width).astype(bf16)
    attn_partial = jnp.einsum("ta,da->td", att_group, out_full, preferred_element_type=f32)
    middle = input_rows + keep_half(attn_partial, core)
    scale_two = lax.rsqrt(jnp.mean(middle * middle, axis=1) + eps)
    normed_two_blk = (middle * scale_two[:, None] * gain_two).astype(bf16)

    def widen(block):
        beside = flip(block, "col", 0)
        across = flip(block, "col", 1)
        return jnp.concatenate([block, beside, across, flip(across, "col", 0)], 0)

    def narrow(partial):
        own, beside, across, far = jnp.split(partial, 4, 0)
        across = across + flip(far.astype(bf16), "col", 0).astype(f32)
        return (
            own
            + flip(beside.astype(bf16), "col", 0).astype(f32)
            + flip(across.astype(bf16), "col", 1).astype(f32)
        )

    normed_two = widen(normed_two_blk)
    grad_full = widen(grad_out.astype(bf16))
    down_flipped = down_weight.T
    down_sum = 0.0
    normed_sum = 0.0
    gate_total = []
    up_total = []
    down_total = []
    for start, stop in cuts(ff_cols, 2):
        width = stop - start
        joined = gather_rows(
            jnp.concatenate(
                [gate_weight[:, start:stop], up_weight[:, start:stop], down_flipped[:, start:stop]],
                1,
            ),
            bits,
        )
        gate_full = joined[:, :width]
        up_full = joined[:, width : 2 * width]
        down_full = joined[:, 2 * width :]
        gate_lin = jnp.dot(normed_two, gate_full, preferred_element_type=f32)
        up_lin = jnp.dot(normed_two, up_full, preferred_element_type=f32)
        grad_hidden = jnp.dot(grad_full, down_full, preferred_element_type=f32)
        sigmoid_gate = jax.nn.sigmoid(gate_lin)
        silu_gate = gate_lin * sigmoid_gate
        hidden = (silu_gate * up_lin).astype(bf16)
        grad_gate = (
            grad_hidden * up_lin * sigmoid_gate * (1.0 + gate_lin * (1.0 - sigmoid_gate))
        ).astype(bf16)
        grad_up = (grad_hidden * silu_gate).astype(bf16)
        down_sum = down_sum + jnp.einsum(
            "tf,df->td", hidden, down_full, preferred_element_type=f32
        )
        normed_sum = (
            normed_sum
            + jnp.einsum("tf,df->td", grad_gate, gate_full, preferred_element_type=f32)
            + jnp.einsum("tf,df->td", grad_up, up_full, preferred_element_type=f32)
        )
        gate_total.append(
            scatter_rows(
                jnp.einsum("td,tf->df", normed_two, grad_gate, preferred_element_type=f32), bits
            )
        )
        up_total.append(
            scatter_rows(
                jnp.einsum("td,tf->df", normed_two, grad_up, preferred_element_type=f32), bits
            )
        )
        down_total.append(
            scatter_rows(
                jnp.einsum("td,tf->df", grad_full, hidden, preferred_element_type=f32), bits
            )
        )
    grad_normed_two = narrow(normed_sum)
    layer_output = unstored((middle + narrow(down_sum)).astype(bf16))
    scaled_two = gain_two * grad_normed_two
    inner_two = jnp.sum(scaled_two * middle, axis=1)
    grad_middle = (
        grad_out
        + scale_two[:, None] * scaled_two
        - middle * (scale_two**3 * inner_two / model_width)[:, None]
    )
    gain_two_grad = jnp.sum(grad_normed_two * middle * scale_two[:, None], axis=0)
    grad_branch = pair(grad_middle.astype(bf16), core)
    grad_att = jnp.dot(grad_branch, out_full, preferred_element_type=f32).astype(bf16)
    out_grad = jnp.einsum("td,ta->da", grad_branch, att_group, preferred_element_type=f32)
    grad_att_heads = grad_att.reshape(length, head_count, HD).transpose(1, 0, 2)
    query_grad, key_grad, value_grad = attention_backward(
        query_heads, key_rows, value_rows, grad_att_heads, log_totals, block_rows
    )
    query_grad = rotate(query_grad, cosine[None], -sine_part[None])
    key_grad = rotate(key_grad, cosine, -sine_part)
    grad_mixed = jnp.concatenate(
        [query_grad.transpose(1, 0, 2).reshape(length, query_width), key_grad, value_grad], 1
    ).astype(bf16)
    bias_grad = jnp.sum(grad_mixed, axis=0, dtype=f32)
    qkv_grad = jnp.einsum("td,tc->dc", normed_one, grad_mixed, preferred_element_type=f32)
    grad_normed_one = keep_half(
        jnp.einsum("tc,dc->td", grad_mixed, qkv_full, preferred_element_type=f32), core
    )
    scaled_one = gain_one * grad_normed_one
    inner_one = jnp.sum(scaled_one * input_rows, axis=1)
    input_grad = unstored(
        (
            grad_middle
            + scale_one[:, None] * scaled_one
            - input_rows * (scale_one**3 * inner_one / model_width)[:, None]
        ).astype(bf16)
    )
    gain_one_grad = jnp.sum(grad_normed_one * input_rows * scale_one[:, None], axis=0)

    def to_columns(total):
        half = total.shape[1] // 2
        low, high = total[:, :half].astype(bf16), total[:, half:].astype(bf16)
        first, second = from_pairs(
            jnp.where(sequence == 0, low, high), jnp.where(sequence == 0, high, low)
        )
        return first.astype(f32) + second.astype(f32)

    out_total = to_columns(scatter_rows(out_grad, bits))
    qkv_total = to_columns(scatter_rows(qkv_grad, bits))
    bias_row = lax.dynamic_update_slice_in_dim(
        jnp.zeros((group_width * 2,), f32), bias_grad, core * group_width, 0
    )
    small = jnp.concatenate([unstored_row(gain_one_grad), unstored_row(gain_two_grad), bias_row])
    small = jnp.pad(small, (0, -small.shape[0] % 128)).reshape(-1, 128)
    for bit in range(2):
        small = small + flip(small, "col", bit)
    for bit in range(bits):
        small = small + flip(small, "row", bit)
    small = small.reshape(-1)
    gain_one_total = small[:model_width]
    gain_two_total = small[model_width : 2 * model_width]
    bias_total = lax.dynamic_slice_in_dim(small, 2 * model_width + column * qkv_cols, qkv_cols, 0)
    return (
        layer_output,
        input_grad,
        gain_one_total,
        qkv_total,
        bias_total,
        out_total.T,
        gain_two_total,
        jnp.concatenate(gate_total, 1),
        jnp.concatenate(up_total, 1),
        jnp.concatenate(down_total, 1).T,
    )


def solution(mesh):
    in_specs = (
        P(("row", "col"), None),
        P(),
        P("row", "col"),
        P("col"),
        P("col", "row"),
        P(),
        P("row", "col"),
        P("row", "col"),
        P("col", "row"),
        P(("row", "col"), None),
    )
    out_specs = (
        P(("row", "col"), None),
        P(("row", "col"), None),
        P(),
        P("row", "col"),
        P("col"),
        P("col", "row"),
        P(),
        P("row", "col"),
        P("row", "col"),
        P("col", "row"),
    )
    return jax.shard_map(shards, mesh=mesh, in_specs=in_specs, out_specs=out_specs, check_vma=False)
```

time: 1060 us -> 722 us (0.68)
  waiting for transfers between devices: 614 us -> 199 us
  blocking collectives: 104 us -> 0 us
  starting transfers between devices: 3.03 us -> 81.1 us
  matrix products: 216 us -> 293 us
  local copies, waits for them, and re-layouts: 51.2 us -> 84.7 us
  between operations: 16.3 us -> 2.86 us
    reduce_scatter x7 -> x0, waiting for transfers between devices: 317 us -> none  [the longest x4 125 us: narrow(): lax.psum_scatter(partial_sum.astype(jnp.bfloat16), 'col', scatter_dimensi...]
    ppermute x4 -> x81, waiting for transfers between devices: 3.37 us -> 199 us  [the longest x73 196 us: flip(): return lax.ppermute(block, axis, [(i, i ^ 1 << bit) for i in range(count)])]
    all_gather x7 -> x0, waiting for transfers between devices: 184 us -> none  [the longest x4 95.4 us: widen(): return lax.all_gather(block_in, 'col', axis=0, tiled=True)]
    unnamed x18 -> x0, waiting for transfers between devices: 110 us -> none
    ppermute x4 -> x81, starting transfers between devices: 1.21 us -> 81.1 us  [the longest x73 67.7 us: flip(): return lax.ppermute(block, axis, [(i, i ^ 1 << bit) for i in range(count)])]
    all_gather x2 -> x0, blocking collectives: 64.7 us -> none  [the longest x1 33.3 us: shards(): lax.all_gather(qkv_weight, 'row', axis=0, tiled=True)]
    dot_general x23 -> x30, matrix products: 114 us -> 161 us  [the longest x2 26.7 us: shards(): grad_hidden = jnp.dot(grad_full, down_full, preferred_element_type=f32)]
    psum x1 -> x0, blocking collectives: 39.8 us -> none  [shards(): lax.psum((gain_one_grad, gain_two_grad, bias_row), ('row', 'col'))]
  transfers between devices with their start and end apart: 20 -> 81, of which waited for: 17 -> 35; matrix products, arithmetic and copies ran while one was open for 19% -> 48% of each run, Pallas kernels for 0% -> 0%
where the time goes in v1:
time: 722 us; the launch traced here: 713 us
  matrix products  293 us (41%)
  waiting for transfers between devices  199 us (28%)
  local copies, waits for them, and re-layouts  84.7 us (12%)
  starting transfers between devices  81.1 us (11%)
  other arithmetic  52.4 us (7%)
    ppermute x73, waiting for transfers between devices, flip(): return lax.ppermute(block, axis, [(i, i ^ 1 << bit) for i in range(count)])  196 us
    ppermute x73, starting transfers between devices, flip(): return lax.ppermute(block, axis, [(i, i ^ 1 << bit) for i in range(count)])  67.7 us
    unnamed x196, local copies, waits for them, and re-layouts  29.6 us
    dot_general x2, matrix products, shards(): grad_hidden = jnp.dot(grad_full, down_full, preferred_element_type=f32)  26.7 us
    dot_general x2, matrix products, shards(): jnp.einsum('tf,df->td', grad_up, up_full, preferred_element_type=f32)  25.7 us
    dot_general x14, matrix products, head_backward(): jnp.einsum('qk,qd->kd', probability.astype(jnp.bfloat16), grad_block, pre...  25 us
    dot_general x14, matrix products, head_backward(): jnp.einsum('qk,qd->kd', score_grad, query_block, preferred_element_type=j...  22.7 us
    dot_general x14, matrix products, head_backward(): jnp.einsum('qd,kd->qk', query_block, key_rows[:row_stop], preferred_eleme...  21.8 us
  transfers between devices with their start and end apart: 81, of which 35 were waited for; matrix products, arithmetic and copies ran while one was open for 48% of the time, Pallas kernels for 0%

profile of v1, /device:TPU:0, one launch (start us, length us, event | category | flops | bytes accessed | tf_op | source)
XLA Modules:
  0.0 712.9 jit_solution(3336768972227082044)
XLA Ops:
  2.4 4.2 collective-permute-start.2
  8.0 3.0 collective-permute-start.11
  22.9 2.8 bitcast_convert_fusion
  30.9 2.7 collective-permute-start.3
  33.6 9.6 %collective-permute-done.12 = bf16[112,448]{0,1:T(8,128)(2,1)S(1)} collective-permute-done((bf16[112,448]{0,1:T(8,128)(2,1)S(1)}, bf16[112,448]{0,1:T(8,128)(2,1)S(1)}, u32[]{:S(2)}, u32[]{:S(2)}) %collective-permute-start.12) | collective-permute-done | bytes 100384 | tf_op jit(solution)/shard_map/ppermute | solution.py:17
  45.3 2.7 collective-permute-done.15
  51.9 8.2 %collective-permute-done.14 = bf16[112,448]{0,1:T(8,128)(2,1)S(1)} collective-permute-done((bf16[112,448]{0,1:T(8,128)(2,1)S(1)}, bf16[112,448]{0,1:T(8,128)(2,1)S(1)}, u32[]{:S(2)}, u32[]{:S(2)}) %collective-permute-start.14) | collective-permute-done | bytes 100384 | tf_op jit(solution)/shard_map/ppermute | solution.py:17
  72.9 3.1 collective-permute-start.23
  84.8 3.2 add_convert_fusion
  92.7 58.1 %while.31 = (s32[]{:T(128)}, bf16[7,1024,64]{1,2,0:T(8,128)(2,1)}, f32[7,1024]{1,0:T(8,128)}, bf16[7,1024,64]{2,1,0:T(8,128)(2,1)}, bf16[1024,64]{1,0:T(8,128)(2,1)S(1)}, /*index=5*/bf16[1024,64]{1,0:T(8,128)(2,1)}) while((s32[]{:T(128)}, bf16[7,1024,64]{1,2,0:T(8,128)(2,1)}, f32[7,1024]{1,0:T(8,128)}, ...), condition=%wide.region_6.7_spmd.clone, body=%wide.region_1.6_spmd.sunk.clone | while | flops 208667136 | bytes 10671705 | solution.py:130
  150.8 2.9 fusion.139
  164.5 6.1 collective-permute-done.34
  170.7 7.7 %collective-permute-done.35 = bf16[112,1728]{1,0:T(8,128)(2,1)S(1)} collective-permute-done((bf16[112,1728]{1,0:T(8,128)(2,1)S(1)}, bf16[112,1728]{1,0:T(8,128)(2,1)S(1)}, u32[]{:S(2)}, u32[]{:S(2)}) %collective-permute-start.35) | collective-permute-done | bytes 387104 | tf_op jit(solution)/shard_map/ppermute | solution.py:17
  182.0 9.4 %collective-permute-done.27 = bf16[112,1920]{1,0:T(8,128)(2,1)S(1)} collective-permute-done((bf16[112,1920]{1,0:T(8,128)(2,1)}, bf16[112,1920]{1,0:T(8,128)(2,1)S(1)}, u32[]{:S(2)}, u32[]{:S(2)}) %collective-permute-start.27) | collective-permute-done | bytes 430112 | tf_op jit(solution)/shard_map/ppermute | solution.py:17
  191.5 6.3 collective-permute-done.21
  197.8 2.9 collective-permute-done.28
  201.1 8.2 %collective-permute-done.36 = bf16[112,1728]{1,0:T(8,128)(2,1)S(1)} collective-permute-done((bf16[112,1728]{1,0:T(8,128)(2,1)}, bf16[112,1728]{1,0:T(8,128)(2,1)S(1)}, u32[]{:S(2)}, u32[]{:S(2)}) %collective-permute-start.36) | collective-permute-done | bytes 387104 | tf_op jit(solution)/shard_map/ppermute | solution.py:17
  209.3 7.4 %collective-permute-done.29 = bf16[112,1920]{1,0:T(8,128)(2,1)S(1)} collective-permute-done((bf16[112,1920]{1,0:T(8,128)(2,1)S(1)}, bf16[112,1920]{1,0:T(8,128)(2,1)S(1)}, u32[]{:S(2)}, u32[]{:S(2)}) %collective-permute-start.29) | collective-permute-done | bytes 430112 | tf_op jit(solution)/shard_map/ppermute | solution.py:17
  216.8 9.1 %fusion.71 = f32[2048,576]{0,1:T(8,128)} fusion(bf16[896,1728]{1,0:T(8,128)(2,1)S(1)} %constant_dynamic-update-slice_fusion.8, bf16[512,896]{1,0:T(8,128)(2,1)S(1)} %collective-permute-done.22, bf16[512,896]{1,0:T(8,128)(2,1)S(1)} %collective-permute-done.21, bf16[512,896]{1,0:T(8,128)(2,1)S(1)} %collective-permute-done.20, ...), kind=kOutput, calls=%fused_computation.158 | convolution fusion | flops 2128609280 | bytes 9535488 | tf_op jit(solution)/shard_map/dot_general | solution.py:316
  225.9 7.9 %fusion.77 = f32[2048,576]{0,1:T(8,128)} fusion(bf16[896,1728]{1,0:T(8,128)(2,1)S(1)} %constant_dynamic-update-slice_fusion.8, bf16[512,896]{1,0:T(8,128)(2,1)S(1)} %collective-permute-done.22, bf16[512,896]{1,0:T(8,128)(2,1)S(1)} %collective-permute-done.21, bf16[512,896]{1,0:T(8,128)(2,1)S(1)} %collective-permute-done.20, ...), kind=kOutput, calls=%fused_computation.162 | convolution fusion | flops 2128609280 | bytes 9535488 | tf_op jit(solution)/shard_map/dot_general | solution.py:315
  233.8 13.5 %multiply_convert_fusion.5 = (bf16[2048,576]{0,1:T(8,128)(2,1)S(1)}, bf16[2048,576]{0,1:T(8,128)(2,1)}, bf16[2048,576]{0,1:T(8,128)(2,1)S(1)}) fusion(f32[2048,576]{0,1:T(8,128)} %fusion.77, f32[2048,576]{0,1:T(8,128)} %fusion.71, bf16[896,1728]{1,0:T(8,128)(2,1)S(1)} %constant_dynamic-update-slice_fusion.8, ...), kind=kOutput, calls=%fused_computation.72 | convolution fusion | flops 2146304000 | bytes 21331968 | tf_op jit(solution)/shard_map/dot_general | solution.py:317
  247.4 2.6 fusion.117
  252.3 2.6 fusion.121
  257.2 2.6 fusion.119
  261.2 5.6 fusion.75
  266.8 5.4 fusion.67
  272.2 8.2 %fusion.84 = f32[2048,640]{1,0:T(8,128)} fusion(bf16[896,1920]{1,0:T(8,128)(2,1)S(1)} %constant_dynamic-update-slice_fusion, bf16[512,896]{1,0:T(8,128)(2,1)S(1)} %collective-permute-done.22, bf16[512,896]{1,0:T(8,128)(2,1)S(1)} %collective-permute-done.21, bf16[512,896]{1,0:T(8,128)(2,1)S(1)} %collective-permute-done.20, ...), kind=kOutput, calls=%fused_computation.169 | convolution fusion | flops 2363490304 | bytes 10059776 | tf_op jit(solution)/shard_map/dot_general | solution.py:316
  280.4 8.0 %fusion.88 = f32[2048,640]{1,0:T(8,128)} fusion(bf16[896,1920]{1,0:T(8,128)(2,1)S(1)} %constant_dynamic-update-slice_fusion, bf16[512,896]{1,0:T(8,128)(2,1)S(1)} %collective-permute-done.22, bf16[512,896]{1,0:T(8,128)(2,1)S(1)} %collective-permute-done.21, bf16[512,896]{1,0:T(8,128)(2,1)S(1)} %collective-permute-done.20, ...), kind=kOutput, calls=%fused_computation.173 | convolution fusion | flops 2363490304 | bytes 10059776 | tf_op jit(solution)/shard_map/dot_general | solution.py:315
  288.5 13.1 %multiply_convert_fusion.2 = (bf16[2048,640]{1,0:T(8,128)(2,1)}, bf16[2048,640]{1,0:T(8,128)(2,1)}, bf16[2048,640]{1,0:T(8,128)(2,1)S(1)}) fusion(f32[2048,640]{1,0:T(8,128)} %fusion.88, f32[2048,640]{1,0:T(8,128)} %fusion.84, bf16[896,1920]{1,0:T(8,128)(2,1)S(1)} %constant_dynamic-update-slice_fusion, bf16[512,896]{1,0:T(8,128)(2,1)S(1)} %copy-done.83, ...), kind=kOutput, calls=%fused_computation.67 | convolution fusion | flops 2383151104 | bytes 23166976 | tf_op jit(solution)/shard_map/dot_general | solution.py:317
  301.6 3.1 fusion.118
  307.4 2.7 copy.78
  313.9 8.4 %fusion.82 = f32[2048,896]{1,0:T(8,128)} fusion(bf16[2048,640]{1,0:T(8,128)(2,1)} %get-tuple-element.303, bf16[896,1920]{1,0:T(8,128)(2,1)} %copy-done.43), kind=kOutput, calls=%fused_computation.167 | convolution fusion | flops 2348810240 | bytes 11108352 | tf_op jit(solution)/shard_map/tf,df->td/dot_general | solution.py:331
  322.3 3.1 fusion.120
  328.0 2.7 copy.77
  334.5 8.9 %fusion.86 = f32[2048,896]{1,0:T(8,128)} fusion(bf16[2048,640]{1,0:T(8,128)(2,1)} %get-tuple-element.304, bf16[896,1920]{1,0:T(8,128)(2,1)} %copy-done.43), kind=kOutput, calls=%fused_computation.171 | convolution fusion | flops 2348810240 | bytes 11108352 | tf_op jit(solution)/shard_map/tf,df->td/dot_general | solution.py:330
  343.5 3.1 fusion.122
  349.1 2.7 copy.76
  352.9 7.3 %fusion.136 = (bf16[2048,896]{1,0:T(8,128)(2,1)}, f32[2048,896]{1,0:T(8,128)S(1)}) fusion(f32[2048,896]{1,0:T(8,128)} %fusion.67, bf16[2048,640]{1,0:T(8,128)(2,1)S(1)} %get-tuple-element.305, bf16[896,1920]{1,0:T(8,128)(2,1)} %copy-done.43), kind=kOutput, calls=%fused_computation.336 | convolution fusion | flops 2352480256 | bytes 22118400 | tf_op jit(solution)/shard_map/tf,df->td/dot_general | solution.py:325
  360.2 17.3 %fusion.137 = (bf16[2048,896]{1,0:T(8,128)(2,1)}, f32[2048,896]{1,0:T(8,128)S(1)}) fusion(bf16[2048,576]{0,1:T(8,128)(2,1)} %copy-done.18, bf16[896,1728]{1,0:T(8,128)(2,1)} %copy-done.41, f32[2048,896]{1,0:T(8,128)} %fusion.75, f32[2048,896]{1,0:T(8,128)} %fusion.86, f32[2048,896]{1,0:T(8,128)} %fusion.82), kind=kOutput, calls=%fused_computation.337 | convolution fusion | flops 2121269248 | bytes 36536320 | tf_op jit(solution)/shard_map/tf,df->td/dot_general | solution.py:331
  377.4 3.1 fusion.127
  388.1 7.6 %collective-permute-done.66 = bf16[448,576]{1,0:T(8,128)(2,1)S(1)} collective-permute-done((bf16[448,576]{1,0:T(8,128)(2,1)S(1)}, bf16[448,576]{1,0:T(8,128)(2,1)S(1)}, u32[]{:S(2)}, u32[]{:S(2)}) %collective-permute-start.66) | collective-permute-done | bytes 516128 | tf_op jit(solution)/shard_map/ppermute | solution.py:17
  402.4 5.1 collective-permute-done.79
  409.0 4.7 collective-permute-done.73
  415.1 4.7 collective-permute-done.67
  421.4 4.6 collective-permute-done.76
  427.4 4.7 collective-permute-done.70
  432.1 5.2 collective-permute-done.64
  437.4 3.5 collective-permute-start.80
  441.0 6.1 collective-permute-done.80
  447.2 9.0 %collective-permute-done.74 = bf16[112,576]{1,0:T(8,128)(2,1)S(1)} collective-permute-done((bf16[112,576]{1,0:T(8,128)(2,1)S(1)}, bf16[112,576]{1,0:T(8,128)(2,1)S(1)}, u32[]{:S(2)}, u32[]{:S(2)}) %collective-permute-start.74) | collective-permute-done | bytes 129056 | tf_op jit(solution)/shard_map/ppermute | solution.py:17
  456.2 7.7 %collective-permute-done.68 = bf16[112,576]{1,0:T(8,128)(2,1)S(1)} collective-permute-done((bf16[112,576]{1,0:T(8,128)(2,1)S(1)}, bf16[112,576]{1,0:T(8,128)(2,1)S(1)}, u32[]{:S(2)}, u32[]{:S(2)}) %collective-permute-start.68) | collective-permute-done | bytes 129056 | tf_op jit(solution)/shard_map/ppermute | solution.py:17
  463.9 3.0 collective-permute-start.71
  468.4 11.0 %collective-permute-done.77 = bf16[112,640]{1,0:T(8,128)(2,1)S(1)} collective-permute-done((bf16[112,640]{1,0:T(8,128)(2,1)S(1)}, bf16[112,640]{1,0:T(8,128)(2,1)S(1)}, u32[]{:S(2)}, u32[]{:S(2)}) %collective-permute-start.77) | collective-permute-done | bytes 143392 | tf_op jit(solution)/shard_map/ppermute | solution.py:17
  488.1 14.6 %collective-permute-done.45 = bf16[512,896]{1,0:T(8,128)(2,1)S(1)} collective-permute-done((bf16[512,896]{1,0:T(8,128)(2,1)S(1)}, bf16[512,896]{1,0:T(8,128)(2,1)S(1)}, u32[]{:S(2)}, u32[]{:S(2)}) %collective-permute-start.45) | collective-permute-done | bytes 917536 | tf_op jit(solution)/shard_map/ppermute | solution.py:17
  505.9 15.4 %collective-permute-done.39 = bf16[512,896]{1,0:T(8,128)(2,1)} collective-permute-done((bf16[512,896]{1,0:T(8,128)(2,1)}, bf16[512,896]{1,0:T(8,128)(2,1)}, u32[]{:S(2)}, u32[]{:S(2)}) %collective-permute-start.39) | collective-permute-done | bytes 917536 | tf_op jit(solution)/shard_map/ppermute | solution.py:17
  521.4 4.3 fusion.61
  525.7 2.9 fusion.96
  530.8 2.6 convolution_convert_fusion
  535.1 109.2 %while.32 = (s32[]{:T(128)}, f32[1024,64]{0,1:T(8,128)}, f32[1024,64]{0,1:T(8,128)}, f32[7,1024,64]{1,2,0:T(8,128)}, bf16[7,1024,64]{2,1,0:T(8,128)(2,1)}, /*ind...) while((s32[]{:T(128)}, f32[1024,64]{0,1:T(8,128)}, ...), condition=%wide.region_12.13_spmd.clone.clone, body=%wide.region_9.12_spmd.clone.sunk.clone | while | flops 512425472 | bytes 32141988 | solution.py:185
  648.7 3.0 fusion.95
  661.9 6.8 collective-permute-done.53
  680.3 2.9 collective-permute-done.62
  689.2 4.6 collective-permute-done.55
  701.9 4.9 fusion.62
  (692 shorter events, 339.5 us)
Async XLA Ops:
  1.8 27.0 %collective-permute-start.1 = (bf16[112,512]{0,1:T(8,128)(2,1)S(1)}, bf16[112,512]{0,1:T(8,128)(2,1)S(1)}, u32[]{:S(2)}, u32[]{:S(2)}) collective-permute-start(bf16[112,512]{0,1:T(8,128)(2,1)S(1)} %pad_maximum_fusion.10), channel_id=1, source_target_pairs={{0,0},{1,2},{2,1},{3,3},{4,4},{5,6},{6,5},{7,7},{8,8},{9,10},{10,9... | collective-permute-start | bytes 344072 | tf_op jit(solution)/shard_map/ppermute | solution.py:86
  2.4 26.3 %collective-permute-start.2 = (bf16[112,512]{0,1:T(8,128)(2,1)S(1)}, bf16[112,512]{0,1:T(8,128)(2,1)S(1)}, u32[]{:S(2)}, u32[]{:S(2)}) collective-permute-start(bf16[112,512]{0,1:T(8,128)(2,1)S(1)} %pad_maximum_fusion.10), channel_id=1, source_target_pairs={{0,2},{1,0},{2,3},{3,1},{4,6},{5,4},{6,7},{7,5},{8,10},{9,8},{10,1... | collective-permute-start | bytes 344072 | tf_op jit(solution)/shard_map/ppermute | solution.py:87
  7.3 21.9 %collective-permute-start.10 = (bf16[1,288]{1,0:T(2,128)(2,1)S(1)}, bf16[1,288]{1,0:T(2,128)(2,1)S(1)}, u32[]{:S(2)}, u32[]{:S(2)}) collective-permute-start(bf16[1,288]{1,0:T(2,128)(2,1)S(1)} %broadcast_in_dim.62), channel_id=1, source_target_pairs={{0,0},{1,2},{2,1},{3,3},{4,4},{5,6},{6,5},{7,7},{8,8},{9,10},{10,9... | collective-permute-start | bytes 1736 | tf_op jit(solution)/shard_map/ppermute | solution.py:86
  8.0 22.9 %collective-permute-start.11 = (bf16[1,288]{1,0:T(2,128)(2,1)S(1)}, bf16[1,288]{1,0:T(2,128)(2,1)S(1)}, u32[]{:S(2)}, u32[]{:S(2)}) collective-permute-start(bf16[1,288]{1,0:T(2,128)(2,1)S(1)} %broadcast_in_dim.62), channel_id=1, source_target_pairs={{0,2},{1,0},{2,3},{3,1},{4,6},{5,4},{6,7},{7,5},{8,10},{9,8},{10,1... | collective-permute-start | bytes 1736 | tf_op jit(solution)/shard_map/ppermute | solution.py:87
  14.7 47.1 %collective-permute-start.30 = (bf16[112,1728]{1,0:T(8,128)(2,1)}, bf16[112,1728]{1,0:T(8,128)(2,1)}, u32[]{:S(2)}, u32[]{:S(2)}) collective-permute-start(bf16[112,1728]{1,0:T(8,128)(2,1)} %concatenate.157), channel_id=1, source_target_pairs={{0,16},{4,20},{8,24},{12,28},{16,0},{20,4},{24,8},{28,12},{1,17},{... | collective-permute-start | bytes 1161224 | tf_op jit(solution)/shard_map/ppermute | solution.py:17
  28.7 56.0 %collective-permute-start = (bf16[512,896]{1,0:T(8,128)(2,1)S(1)}, bf16[512,896]{1,0:T(8,128)(2,1)}, u32[]{:S(2)}, u32[]{:S(2)}) collective-permute-start(bf16[512,896]{1,0:T(8,128)(2,1)S(1)} %fusion.49), channel_id=1, source_target_pairs={{0,1},{1,0},{2,3},{3,2},{4,5},{5,4},{6,7},{7,6},{8,9},{9,8},{10,11... | collective-permute-start | bytes 2752520 | tf_op jit(solution)/shard_map/ppermute | solution.py:17
  28.9 14.3 %collective-permute-start.12 = (bf16[112,448]{0,1:T(8,128)(2,1)S(1)}, bf16[112,448]{0,1:T(8,128)(2,1)S(1)}, u32[]{:S(2)}, u32[]{:S(2)}) collective-permute-start(bf16[112,448]{0,1:T(8,128)(2,1)S(1)} %pad_maximum_fusion.12), channel_id=1, source_target_pairs={{0,16},{4,20},{8,24},{12,28},{16,0},{20,4},{24,8},{28,12},{1,17},{... | collective-permute-start | bytes 301064 | tf_op jit(solution)/shard_map/ppermute | solution.py:17
  29.3 13.9 %collective-permute-start.13 = (bf16[112,448]{0,1:T(8,128)(2,1)S(1)}, bf16[112,448]{0,1:T(8,128)(2,1)S(1)}, u32[]{:S(2)}, u32[]{:S(2)}) collective-permute-start(bf16[112,448]{0,1:T(8,128)(2,1)S(1)} %pad_maximum_fusion.12), channel_id=1, source_target_pairs={{0,8},{4,12},{8,0},{12,4},{16,24},{20,28},{24,16},{28,20},{1,9},{5... | collective-permute-start | bytes 301064 | tf_op jit(solution)/shard_map/ppermute | solution.py:17
  30.9 19.2 %collective-permute-start.3 = (bf16[112,576]{0,1:T(8,128)(2,1)S(1)}, bf16[112,576]{0,1:T(8,128)(2,1)S(1)}, u32[]{:S(2)}, u32[]{:S(2)}) collective-permute-start(bf16[112,576]{0,1:T(8,128)(2,1)S(1)} %pad_maximum_fusion.9), channel_id=1, source_target_pairs={{0,16},{4,20},{8,24},{12,28},{16,0},{20,4},{24,8},{28,12},{1,17},{... | collective-permute-start | bytes 387080 | tf_op jit(solution)/shard_map/ppermute | solution.py:17
  47.9 20.2 %collective-permute-start.31 = (bf16[112,1728]{1,0:T(8,128)(2,1)}, bf16[112,1728]{1,0:T(8,128)(2,1)S(1)}, u32[]{:S(2)}, u32[]{:S(2)}) collective-permute-start(bf16[112,1728]{1,0:T(8,128)(2,1)} %concatenate.157), channel_id=1, source_target_pairs={{0,8},{4,12},{8,0},{12,4},{16,24},{20,28},{24,16},{28,20},{1,9},{5... | collective-permute-start | bytes 1161224 | tf_op jit(solution)/shard_map/ppermute | solution.py:17
  50.2 9.9 %collective-permute-start.14 = (bf16[112,448]{0,1:T(8,128)(2,1)S(1)}, bf16[112,448]{0,1:T(8,128)(2,1)S(1)}, u32[]{:S(2)}, u32[]{:S(2)}) collective-permute-start(bf16[112,448]{0,1:T(8,128)(2,1)S(1)} %collective-permute-done.12), channel_id=1, source_target_pairs={{0,8},{4,12},{8,0},{12,4},{16,24},{20,28},{24,16},{28,20},{1,9},{5... | collective-permute-start | bytes 301064 | tf_op jit(solution)/shard_map/ppermute | solution.py:17
  50.2 11.3 %collective-permute-start.16 = (bf16[112,448]{0,1:T(8,128)(2,1)S(1)}, bf16[112,448]{0,1:T(8,128)(2,1)S(1)}, u32[]{:S(2)}, u32[]{:S(2)}) collective-permute-start(bf16[112,448]{0,1:T(8,128)(2,1)S(1)} %collective-permute-done.12), channel_id=1, source_target_pairs={{0,4},{4,0},{8,12},{12,8},{16,20},{20,16},{24,28},{28,24},{1,5},{5... | collective-permute-start | bytes 301064 | tf_op jit(solution)/shard_map/ppermute | solution.py:17
  68.1 11.1 %collective-permute-start.8 = (bf16[112,576]{0,1:T(8,128)(2,1)S(1)}, bf16[112,576]{0,1:T(8,128)(2,1)S(1)}, u32[]{:S(2)}, u32[]{:S(2)}) collective-permute-start(bf16[112,576]{0,1:T(8,128)(2,1)S(1)} %collective-permute-done.4), channel_id=1, source_target_pairs={{0,4},{4,0},{8,12},{12,8},{16,20},{20,16},{24,28},{28,24},{1,5},{5... | collective-permute-start | bytes 387080 | tf_op jit(solution)/shard_map/ppermute | solution.py:17
  69.6 12.7 %collective-permute-start.9 = (bf16[112,576]{0,1:T(8,128)(2,1)S(1)}, bf16[112,576]{0,1:T(8,128)(2,1)S(1)}, u32[]{:S(2)}, u32[]{:S(2)}) collective-permute-start(bf16[112,576]{0,1:T(8,128)(2,1)S(1)} %collective-permute-done.5), channel_id=1, source_target_pairs={{0,4},{4,0},{8,12},{12,8},{16,20},{20,16},{24,28},{28,24},{1,5},{5... | collective-permute-start | bytes 387080 | tf_op jit(solution)/shard_map/ppermute | solution.py:17
  72.9 81.0 %collective-permute-start.23 = (bf16[112,1920]{1,0:T(8,128)(2,1)}, bf16[112,1920]{1,0:T(8,128)(2,1)}, u32[]{:S(2)}, u32[]{:S(2)}) collective-permute-start(bf16[112,1920]{1,0:T(8,128)(2,1)} %get-tuple-element.319), channel_id=1, source_target_pairs={{0,16},{4,20},{8,24},{12,28},{16,0},{20,4},{24,8},{28,12},{1,17},{... | collective-permute-start | bytes 1290248 | tf_op jit(solution)/shard_map/ppermute | solution.py:17
  76.0 79.1 %collective-permute-start.24 = (bf16[112,1920]{1,0:T(8,128)(2,1)}, bf16[112,1920]{1,0:T(8,128)(2,1)}, u32[]{:S(2)}, u32[]{:S(2)}) collective-permute-start(bf16[112,1920]{1,0:T(8,128)(2,1)} %get-tuple-element.319), channel_id=1, source_target_pairs={{0,8},{4,12},{8,0},{12,4},{16,24},{20,28},{24,16},{28,20},{1,9},{5... | collective-permute-start | bytes 1290248 | tf_op jit(solution)/shard_map/ppermute | solution.py:17
  79.2 101.4 %collective-permute-start.26 = (bf16[112,1920]{1,0:T(8,128)(2,1)}, bf16[112,1920]{1,0:T(8,128)(2,1)}, u32[]{:S(2)}, u32[]{:S(2)}) collective-permute-start(bf16[112,1920]{1,0:T(8,128)(2,1)} %get-tuple-element.319), channel_id=1, source_target_pairs={{0,4},{4,0},{8,12},{12,8},{16,20},{20,16},{24,28},{28,24},{1,5},{5... | collective-permute-start | bytes 1290248 | tf_op jit(solution)/shard_map/ppermute | solution.py:17
  82.3 77.3 %collective-permute-start.33 = (bf16[112,1728]{1,0:T(8,128)(2,1)}, bf16[112,1728]{1,0:T(8,128)(2,1)}, u32[]{:S(2)}, u32[]{:S(2)}) collective-permute-start(bf16[112,1728]{1,0:T(8,128)(2,1)} %concatenate.157), channel_id=1, source_target_pairs={{0,4},{4,0},{8,12},{12,8},{16,20},{20,16},{24,28},{28,24},{1,5},{5... | collective-permute-start | bytes 1161224 | tf_op jit(solution)/shard_map/ppermute | solution.py:17
  84.8 73.5 %collective-permute-start.32 = (bf16[112,1728]{1,0:T(8,128)(2,1)}, bf16[112,1728]{1,0:T(8,128)(2,1)}, u32[]{:S(2)}, u32[]{:S(2)}) collective-permute-start(bf16[112,1728]{1,0:T(8,128)(2,1)} %collective-permute-done.30), channel_id=1, source_target_pairs={{0,8},{4,12},{8,0},{12,4},{16,24},{20,28},{24,16},{28,20},{1,9},{5... | collective-permute-start | bytes 1161224 | tf_op jit(solution)/shard_map/ppermute | solution.py:17
  153.8 8.7 %collective-permute-start.19 = (bf16[512,896]{1,0:T(8,128)(2,1)S(1)}, bf16[512,896]{1,0:T(8,128)(2,1)S(1)}, u32[]{:S(2)}, u32[]{:S(2)}) collective-permute-start(bf16[512,896]{1,0:T(8,128)(2,1)S(1)} %dynamic-slice_convert_fusion.1), channel_id=1, source_target_pairs={{0,1},{1,0},{2,3},{3,2},{4,5},{5,4},{6,7},{7,6},{8,9},{9,8},{10,11... | collective-permute-start | bytes 2752520 | tf_op jit(solution)/shard_map/ppermute | solution.py:17
  155.1 45.9 %collective-permute-start.41 = (bf16[512,896]{1,0:T(8,128)(2,1)S(1)}, bf16[512,896]{1,0:T(8,128)(2,1)S(1)}, u32[]{:S(2)}, u32[]{:S(2)}) collective-permute-start(bf16[512,896]{1,0:T(8,128)(2,1)S(1)} %copy-done.72), channel_id=1, source_target_pairs={{0,2},{1,3},{2,0},{3,1},{4,6},{5,7},{6,4},{7,5},{8,10},{9,11},{10,... | collective-permute-start | bytes 2752520 | tf_op jit(solution)/shard_map/ppermute | solution.py:17
  158.3 12.4 %collective-permute-start.34 = (bf16[112,1728]{1,0:T(8,128)(2,1)}, bf16[112,1728]{1,0:T(8,128)(2,1)S(1)}, u32[]{:S(2)}, u32[]{:S(2)}) collective-permute-start(bf16[112,1728]{1,0:T(8,128)(2,1)} %collective-permute-done.30), channel_id=1, source_target_pairs={{0,4},{4,0},{8,12},{12,8},{16,20},{20,16},{24,28},{28,24},{1,5},{5... | collective-permute-start | bytes 1161224 | tf_op jit(solution)/shard_map/ppermute | solution.py:17
  159.6 18.8 %collective-permute-start.35 = (bf16[112,1728]{1,0:T(8,128)(2,1)S(1)}, bf16[112,1728]{1,0:T(8,128)(2,1)S(1)}, u32[]{:S(2)}, u32[]{:S(2)}) collective-permute-start(bf16[112,1728]{1,0:T(8,128)(2,1)S(1)} %copy-done.49), channel_id=1, source_target_pairs={{0,4},{4,0},{8,12},{12,8},{16,20},{20,16},{24,28},{28,24},{1,5},{5... | collective-permute-start | bytes 1161224 | tf_op jit(solution)/shard_map/ppermute | solution.py:17
  162.5 16.2 %collective-permute-start.25 = (bf16[112,1920]{1,0:T(8,128)(2,1)}, bf16[112,1920]{1,0:T(8,128)(2,1)S(1)}, u32[]{:S(2)}, u32[]{:S(2)}) collective-permute-start(bf16[112,1920]{1,0:T(8,128)(2,1)} %collective-permute-done.23), channel_id=1, source_target_pairs={{0,8},{4,12},{8,0},{12,4},{16,24},{20,28},{24,16},{28,20},{1,9},{5... | collective-permute-start | bytes 1290248 | tf_op jit(solution)/shard_map/ppermute | solution.py:17
  170.7 27.1 %collective-permute-start.21 = (bf16[512,896]{1,0:T(8,128)(2,1)S(1)}, bf16[512,896]{1,0:T(8,128)(2,1)S(1)}, u32[]{:S(2)}, u32[]{:S(2)}) collective-permute-start(bf16[512,896]{1,0:T(8,128)(2,1)S(1)} %multiply_convert_fusion.8), channel_id=1, source_target_pairs={{0,2},{1,3},{2,0},{3,1},{4,6},{5,7},{6,4},{7,5},{8,10},{9,11},{10,... | collective-permute-start | bytes 2752520 | tf_op jit(solution)/shard_map/ppermute | solution.py:17
  178.4 13.1 %collective-permute-start.27 = (bf16[112,1920]{1,0:T(8,128)(2,1)}, bf16[112,1920]{1,0:T(8,128)(2,1)S(1)}, u32[]{:S(2)}, u32[]{:S(2)}) collective-permute-start(bf16[112,1920]{1,0:T(8,128)(2,1)} %collective-permute-done.23), channel_id=1, source_target_pairs={{0,4},{4,0},{8,12},{12,8},{16,20},{20,16},{24,28},{28,24},{1,5},{5... | collective-permute-start | bytes 1290248 | tf_op jit(solution)/shard_map/ppermute | solution.py:17
  178.7 21.9 %collective-permute-start.28 = (bf16[112,1920]{1,0:T(8,128)(2,1)}, bf16[112,1920]{1,0:T(8,128)(2,1)S(1)}, u32[]{:S(2)}, u32[]{:S(2)}) collective-permute-start(bf16[112,1920]{1,0:T(8,128)(2,1)} %collective-permute-done.24), channel_id=1, source_target_pairs={{0,4},{4,0},{8,12},{12,8},{16,20},{20,16},{24,28},{28,24},{1,5},{5... | collective-permute-start | bytes 1290248 | tf_op jit(solution)/shard_map/ppermute | solution.py:17
  180.6 28.7 %collective-permute-start.36 = (bf16[112,1728]{1,0:T(8,128)(2,1)}, bf16[112,1728]{1,0:T(8,128)(2,1)S(1)}, u32[]{:S(2)}, u32[]{:S(2)}) collective-permute-start(bf16[112,1728]{1,0:T(8,128)(2,1)} %collective-permute-done.32), channel_id=1, source_target_pairs={{0,4},{4,0},{8,12},{12,8},{16,20},{20,16},{24,28},{28,24},{1,5},{5... | collective-permute-start | bytes 1161224 | tf_op jit(solution)/shard_map/ppermute | solution.py:17
  191.5 25.3 %collective-permute-start.20 = (bf16[512,896]{1,0:T(8,128)(2,1)S(1)}, bf16[512,896]{1,0:T(8,128)(2,1)S(1)}, u32[]{:S(2)}, u32[]{:S(2)}) collective-permute-start(bf16[512,896]{1,0:T(8,128)(2,1)S(1)} %multiply_convert_fusion.8), channel_id=1, source_target_pairs={{0,1},{1,0},{2,3},{3,2},{4,5},{5,4},{6,7},{7,6},{8,9},{9,8},{10,11... | collective-permute-start | bytes 2752520 | tf_op jit(solution)/shard_map/ppermute | solution.py:17
  197.7 19.0 %collective-permute-start.22 = (bf16[512,896]{1,0:T(8,128)(2,1)S(1)}, bf16[512,896]{1,0:T(8,128)(2,1)S(1)}, u32[]{:S(2)}, u32[]{:S(2)}) collective-permute-start(bf16[512,896]{1,0:T(8,128)(2,1)S(1)} %collective-permute-done.21), channel_id=1, source_target_pairs={{0,1},{1,0},{2,3},{3,2},{4,5},{5,4},{6,7},{7,6},{8,9},{9,8},{10,11... | collective-permute-start | bytes 2752520 | tf_op jit(solution)/shard_map/ppermute | solution.py:17
  200.7 16.0 %collective-permute-start.29 = (bf16[112,1920]{1,0:T(8,128)(2,1)S(1)}, bf16[112,1920]{1,0:T(8,128)(2,1)S(1)}, u32[]{:S(2)}, u32[]{:S(2)}) collective-permute-start(bf16[112,1920]{1,0:T(8,128)(2,1)S(1)} %collective-permute-done.25), channel_id=1, source_target_pairs={{0,4},{4,0},{8,12},{12,8},{16,20},{20,16},{24,28},{28,24},{1,5},{5... | collective-permute-start | bytes 1290248 | tf_op jit(solution)/shard_map/ppermute | solution.py:17
  201.0 32.8 %collective-permute-start.40 = (bf16[512,896]{1,0:T(8,128)(2,1)S(1)}, bf16[512,896]{1,0:T(8,128)(2,1)S(1)}, u32[]{:S(2)}, u32[]{:S(2)}) collective-permute-start(bf16[512,896]{1,0:T(8,128)(2,1)S(1)} %copy-done.72), channel_id=1, source_target_pairs={{0,1},{1,0},{2,3},{3,2},{4,5},{5,4},{6,7},{7,6},{8,9},{9,8},{10,11... | collective-permute-start | bytes 2752520 | tf_op jit(solution)/shard_map/ppermute | solution.py:17
  209.3 24.5 %collective-permute-start.42 = (bf16[512,896]{1,0:T(8,128)(2,1)S(1)}, bf16[512,896]{1,0:T(8,128)(2,1)S(1)}, u32[]{:S(2)}, u32[]{:S(2)}) collective-permute-start(bf16[512,896]{1,0:T(8,128)(2,1)S(1)} %collective-permute-done.41), channel_id=1, source_target_pairs={{0,1},{1,0},{2,3},{3,2},{4,5},{5,4},{6,7},{7,6},{8,9},{9,8},{10,11... | collective-permute-start | bytes 2752520 | tf_op jit(solution)/shard_map/ppermute | solution.py:17
  307.1 88.8 %collective-permute-start.75 = (bf16[448,640]{1,0:T(8,128)(2,1)}, bf16[448,640]{1,0:T(8,128)(2,1)}, u32[]{:S(2)}, u32[]{:S(2)}) collective-permute-start(bf16[448,640]{1,0:T(8,128)(2,1)} %slice.846), channel_id=1, source_target_pairs={{0,4},{4,0},{8,12},{12,8},{16,20},{20,16},{24,28},{28,24},{1,5},{5... | collective-permute-start | bytes 1720328 | tf_op jit(solution)/shard_map/ppermute | solution.py:17
  312.2 71.5 %collective-permute-start.78 = (bf16[448,576]{1,0:T(8,128)(2,1)}, bf16[448,576]{1,0:T(8,128)(2,1)}, u32[]{:S(2)}, u32[]{:S(2)}) collective-permute-start(bf16[448,576]{1,0:T(8,128)(2,1)} %copy.75), channel_id=1, source_target_pairs={{0,4},{4,0},{8,12},{12,8},{16,20},{20,16},{24,28},{28,24},{1,5},{5... | collective-permute-start | bytes 1548296 | tf_op jit(solution)/shard_map/ppermute | solution.py:17
  327.7 70.1 %collective-permute-start.69 = (bf16[448,640]{1,0:T(8,128)(2,1)}, bf16[448,640]{1,0:T(8,128)(2,1)}, u32[]{:S(2)}, u32[]{:S(2)}) collective-permute-start(bf16[448,640]{1,0:T(8,128)(2,1)} %slice.847), channel_id=1, source_target_pairs={{0,4},{4,0},{8,12},{12,8},{16,20},{20,16},{24,28},{28,24},{1,5},{5... | collective-permute-start | bytes 1720328 | tf_op jit(solution)/shard_map/ppermute | solution.py:17
  332.8 53.9 %collective-permute-start.72 = (bf16[448,576]{1,0:T(8,128)(2,1)}, bf16[448,576]{1,0:T(8,128)(2,1)}, u32[]{:S(2)}, u32[]{:S(2)}) collective-permute-start(bf16[448,576]{1,0:T(8,128)(2,1)} %copy.73), channel_id=1, source_target_pairs={{0,4},{4,0},{8,12},{12,8},{16,20},{20,16},{24,28},{28,24},{1,5},{5... | collective-permute-start | bytes 1548296 | tf_op jit(solution)/shard_map/ppermute | solution.py:17
  348.8 51.7 %collective-permute-start.63 = (bf16[448,640]{1,0:T(8,128)(2,1)}, bf16[448,640]{1,0:T(8,128)(2,1)}, u32[]{:S(2)}, u32[]{:S(2)}) collective-permute-start(bf16[448,640]{1,0:T(8,128)(2,1)} %slice.848), channel_id=1, source_target_pairs={{0,4},{4,0},{8,12},{12,8},{16,20},{20,16},{24,28},{28,24},{1,5},{5... | collective-permute-start | bytes 1720328 | tf_op jit(solution)/shard_map/ppermute | solution.py:17
  383.7 11.9 %collective-permute-start.66 = (bf16[448,576]{1,0:T(8,128)(2,1)S(1)}, bf16[448,576]{1,0:T(8,128)(2,1)S(1)}, u32[]{:S(2)}, u32[]{:S(2)}) collective-permute-start(bf16[448,576]{1,0:T(8,128)(2,1)S(1)} %copy-done.44), channel_id=1, source_target_pairs={{0,4},{4,0},{8,12},{12,8},{16,20},{20,16},{24,28},{28,24},{1,5},{5... | collective-permute-start | bytes 1548296 | tf_op jit(solution)/shard_map/ppermute | solution.py:17
  386.7 77.2 %collective-permute-start.44 = (bf16[512,896]{1,0:T(8,128)(2,1)S(1)}, bf16[512,896]{1,0:T(8,128)(2,1)S(1)}, u32[]{:S(2)}, u32[]{:S(2)}) collective-permute-start(bf16[512,896]{1,0:T(8,128)(2,1)S(1)} %get-tuple-element.310), channel_id=1, source_target_pairs={{0,1},{1,0},{2,3},{3,2},{4,5},{5,4},{6,7},{7,6},{8,9},{9,8},{10,11... | collective-permute-start | bytes 2752520 | tf_op jit(solution)/shard_map/ppermute | solution.py:17
  395.7 92.4 %collective-permute-start.43 = (bf16[512,896]{1,0:T(8,128)(2,1)S(1)}, bf16[512,896]{1,0:T(8,128)(2,1)S(1)}, u32[]{:S(2)}, u32[]{:S(2)}) collective-permute-start(bf16[512,896]{1,0:T(8,128)(2,1)S(1)} %get-tuple-element.309), channel_id=1, source_target_pairs={{0,1},{1,0},{2,3},{3,2},{4,5},{5,4},{6,7},{7,6},{8,9},{9,8},{10,11... | collective-permute-start | bytes 2752520 | tf_op jit(solution)/shard_map/ppermute | solution.py:17
  395.9 71.3 %collective-permute-start.38 = (bf16[512,896]{1,0:T(8,128)(2,1)S(1)}, bf16[512,896]{1,0:T(8,128)(2,1)S(1)}, u32[]{:S(2)}, u32[]{:S(2)}) collective-permute-start(bf16[512,896]{1,0:T(8,128)(2,1)S(1)} %get-tuple-element.312), channel_id=1, source_target_pairs={{0,1},{1,0},{2,3},{3,2},{4,5},{5,4},{6,7},{7,6},{8,9},{9,8},{10,11... | collective-permute-start | bytes 2752520 | tf_op jit(solution)/shard_map/ppermute | solution.py:17
  397.8 9.7 %collective-permute-start.79 = (bf16[224,576]{1,0:T(8,128)(2,1)S(1)}, bf16[224,576]{1,0:T(8,128)(2,1)S(1)}, u32[]{:S(2)}, u32[]{:S(2)}) collective-permute-start(bf16[224,576]{1,0:T(8,128)(2,1)S(1)} %slice.851), channel_id=1, source_target_pairs={{0,8},{4,12},{8,0},{12,4},{16,24},{20,28},{24,16},{28,20},{1,9},{5... | collective-permute-start | bytes 774152 | tf_op jit(solution)/shard_map/ppermute | solution.py:17
  400.5 13.2 %collective-permute-start.73 = (bf16[224,576]{1,0:T(8,128)(2,1)S(1)}, bf16[224,576]{1,0:T(8,128)(2,1)S(1)}, u32[]{:S(2)}, u32[]{:S(2)}) collective-permute-start(bf16[224,576]{1,0:T(8,128)(2,1)S(1)} %slice.853), channel_id=1, source_target_pairs={{0,8},{4,12},{8,0},{12,4},{16,24},{20,28},{24,16},{28,20},{1,9},{5... | collective-permute-start | bytes 774152 | tf_op jit(solution)/shard_map/ppermute | solution.py:17
  407.5 12.3 %collective-permute-start.67 = (bf16[224,576]{1,0:T(8,128)(2,1)S(1)}, bf16[224,576]{1,0:T(8,128)(2,1)S(1)}, u32[]{:S(2)}, u32[]{:S(2)}) collective-permute-start(bf16[224,576]{1,0:T(8,128)(2,1)S(1)} %slice.855), channel_id=1, source_target_pairs={{0,8},{4,12},{8,0},{12,4},{16,24},{20,28},{24,16},{28,20},{1,9},{5... | collective-permute-start | bytes 774152 | tf_op jit(solution)/shard_map/ppermute | solution.py:17
  413.7 12.3 %collective-permute-start.76 = (bf16[224,640]{1,0:T(8,128)(2,1)S(1)}, bf16[224,640]{1,0:T(8,128)(2,1)S(1)}, u32[]{:S(2)}, u32[]{:S(2)}) collective-permute-start(bf16[224,640]{1,0:T(8,128)(2,1)S(1)} %slice.852), channel_id=1, source_target_pairs={{0,8},{4,12},{8,0},{12,4},{16,24},{20,28},{24,16},{28,20},{1,9},{5... | collective-permute-start | bytes 860168 | tf_op jit(solution)/shard_map/ppermute | solution.py:17
  419.8 12.3 %collective-permute-start.70 = (bf16[224,640]{1,0:T(8,128)(2,1)S(1)}, bf16[224,640]{1,0:T(8,128)(2,1)S(1)}, u32[]{:S(2)}, u32[]{:S(2)}) collective-permute-start(bf16[224,640]{1,0:T(8,128)(2,1)S(1)} %slice.854), channel_id=1, source_target_pairs={{0,8},{4,12},{8,0},{12,4},{16,24},{20,28},{24,16},{28,20},{1,9},{5... | collective-permute-start | bytes 860168 | tf_op jit(solution)/shard_map/ppermute | solution.py:17
  425.9 11.4 %collective-permute-start.64 = (bf16[224,640]{1,0:T(8,128)(2,1)S(1)}, bf16[224,640]{1,0:T(8,128)(2,1)S(1)}, u32[]{:S(2)}, u32[]{:S(2)}) collective-permute-start(bf16[224,640]{1,0:T(8,128)(2,1)S(1)} %slice.856), channel_id=1, source_target_pairs={{0,8},{4,12},{8,0},{12,4},{16,24},{20,28},{24,16},{28,20},{1,9},{5... | collective-permute-start | bytes 860168 | tf_op jit(solution)/shard_map/ppermute | solution.py:17
  432.1 73.8 %collective-permute-start.37 = (bf16[512,896]{1,0:T(8,128)(2,1)}, bf16[512,896]{1,0:T(8,128)(2,1)}, u32[]{:S(2)}, u32[]{:S(2)}) collective-permute-start(bf16[512,896]{1,0:T(8,128)(2,1)} %get-tuple-element.311), channel_id=1, source_target_pairs={{0,1},{1,0},{2,3},{3,2},{4,5},{5,4},{6,7},{7,6},{8,9},{9,8},{10,11... | collective-permute-start | bytes 2752520 | tf_op jit(solution)/shard_map/ppermute | solution.py:17
  437.4 9.8 %collective-permute-start.80 = (bf16[112,576]{1,0:T(8,128)(2,1)S(1)}, bf16[112,576]{1,0:T(8,128)(2,1)S(1)}, u32[]{:S(2)}, u32[]{:S(2)}) collective-permute-start(bf16[112,576]{1,0:T(8,128)(2,1)S(1)} %slice.859), channel_id=1, source_target_pairs={{0,16},{4,20},{8,24},{12,28},{16,0},{20,4},{24,8},{28,12},{1,17},{... | collective-permute-start | bytes 387080 | tf_op jit(solution)/shard_map/ppermute | solution.py:17
  447.2 9.0 %collective-permute-start.74 = (bf16[112,576]{1,0:T(8,128)(2,1)S(1)}, bf16[112,576]{1,0:T(8,128)(2,1)S(1)}, u32[]{:S(2)}, u32[]{:S(2)}) collective-permute-start(bf16[112,576]{1,0:T(8,128)(2,1)S(1)} %slice.861), channel_id=1, source_target_pairs={{0,16},{4,20},{8,24},{12,28},{16,0},{20,4},{24,8},{28,12},{1,17},{... | collective-permute-start | bytes 387080 | tf_op jit(solution)/shard_map/ppermute | solution.py:17
  463.9 15.5 %collective-permute-start.77 = (bf16[112,640]{1,0:T(8,128)(2,1)S(1)}, bf16[112,640]{1,0:T(8,128)(2,1)S(1)}, u32[]{:S(2)}, u32[]{:S(2)}) collective-permute-start(bf16[112,640]{1,0:T(8,128)(2,1)S(1)} %slice.860), channel_id=1, source_target_pairs={{0,16},{4,20},{8,24},{12,28},{16,0},{20,4},{24,8},{28,12},{1,17},{... | collective-permute-start | bytes 430088 | tf_op jit(solution)/shard_map/ppermute | solution.py:17
  463.9 18.5 %collective-permute-start.71 = (bf16[112,640]{1,0:T(8,128)(2,1)S(1)}, bf16[112,640]{1,0:T(8,128)(2,1)S(1)}, u32[]{:S(2)}, u32[]{:S(2)}) collective-permute-start(bf16[112,640]{1,0:T(8,128)(2,1)S(1)} %slice.862), channel_id=1, source_target_pairs={{0,16},{4,20},{8,24},{12,28},{16,0},{20,4},{24,8},{28,12},{1,17},{... | collective-permute-start | bytes 430088 | tf_op jit(solution)/shard_map/ppermute | solution.py:17
  467.2 18.3 %collective-permute-start.65 = (bf16[112,640]{1,0:T(8,128)(2,1)S(1)}, bf16[112,640]{1,0:T(8,128)(2,1)S(1)}, u32[]{:S(2)}, u32[]{:S(2)}) collective-permute-start(bf16[112,640]{1,0:T(8,128)(2,1)S(1)} %slice.864), channel_id=1, source_target_pairs={{0,16},{4,20},{8,24},{12,28},{16,0},{20,4},{24,8},{28,12},{1,17},{... | collective-permute-start | bytes 430088 | tf_op jit(solution)/shard_map/ppermute | solution.py:17
  479.4 23.2 %collective-permute-start.45 = (bf16[512,896]{1,0:T(8,128)(2,1)S(1)}, bf16[512,896]{1,0:T(8,128)(2,1)S(1)}, u32[]{:S(2)}, u32[]{:S(2)}) collective-permute-start(bf16[512,896]{1,0:T(8,128)(2,1)S(1)} %fusion.40), channel_id=1, source_target_pairs={{0,2},{1,3},{2,0},{3,1},{4,6},{5,7},{6,4},{7,5},{8,10},{9,11},{10,... | collective-permute-start | bytes 2752520 | tf_op jit(solution)/shard_map/ppermute | solution.py:17
  482.5 38.9 %collective-permute-start.39 = (bf16[512,896]{1,0:T(8,128)(2,1)}, bf16[512,896]{1,0:T(8,128)(2,1)}, u32[]{:S(2)}, u32[]{:S(2)}) collective-permute-start(bf16[512,896]{1,0:T(8,128)(2,1)} %fusion.42), channel_id=1, source_target_pairs={{0,2},{1,3},{2,0},{3,1},{4,6},{5,7},{6,4},{7,5},{8,10},{9,11},{10,... | collective-permute-start | bytes 2752520 | tf_op jit(solution)/shard_map/ppermute | solution.py:17
  505.4 20.3 %collective-permute-start.46 = (bf16[512,896]{1,0:T(8,128)(2,1)S(1)}, bf16[512,896]{1,0:T(8,128)(2,1)}, u32[]{:S(2)}, u32[]{:S(2)}) collective-permute-start(bf16[512,896]{1,0:T(8,128)(2,1)S(1)} %get-tuple-element.287), channel_id=1, source_target_pairs={{0,1},{1,0},{2,3},{3,2},{4,5},{5,4},{6,7},{7,6},{8,9},{9,8},{10,11... | collective-permute-start | bytes 2752520 | tf_op jit(solution)/shard_map/ppermute | solution.py:17
  530.8 125.6 %collective-permute-start.58 = (bf16[448,448]{0,1:T(8,128)(2,1)}, bf16[448,448]{0,1:T(8,128)(2,1)}, u32[]{:S(2)}, u32[]{:S(2)}) collective-permute-start(bf16[448,448]{0,1:T(8,128)(2,1)} %slice.849), channel_id=1, source_target_pairs={{0,4},{4,0},{8,12},{12,8},{16,20},{20,16},{24,28},{28,24},{1,5},{5... | collective-permute-start | bytes 1204232 | tf_op jit(solution)/shard_map/ppermute | solution.py:17
  654.4 14.3 %collective-permute-start.53 = (bf16[448,576]{1,0:T(8,128)(2,1)}, bf16[448,576]{1,0:T(8,128)(2,1)}, u32[]{:S(2)}, u32[]{:S(2)}) collective-permute-start(bf16[448,576]{1,0:T(8,128)(2,1)} %copy.68), channel_id=1, source_target_pairs={{0,4},{4,0},{8,12},{12,8},{16,20},{20,16},{24,28},{28,24},{1,5},{5... | collective-permute-start | bytes 1548296 | tf_op jit(solution)/shard_map/ppermute | solution.py:17
  657.7 12.3 %collective-permute-start.59 = (bf16[224,448]{0,1:T(8,128)(2,1)S(1)}, bf16[224,448]{0,1:T(8,128)(2,1)S(1)}, u32[]{:S(2)}, u32[]{:S(2)}) collective-permute-start(bf16[224,448]{0,1:T(8,128)(2,1)S(1)} %slice.857), channel_id=1, source_target_pairs={{0,8},{4,12},{8,0},{12,4},{16,24},{20,28},{24,16},{28,20},{1,9},{5... | collective-permute-start | bytes 602120 | tf_op jit(solution)/shard_map/ppermute | solution.py:17
  660.8 25.3 %collective-permute-start.47 = (bf16[512,896]{1,0:T(8,128)(2,1)}, bf16[512,896]{1,0:T(8,128)(2,1)}, u32[]{:S(2)}, u32[]{:S(2)}) collective-permute-start(bf16[512,896]{1,0:T(8,128)(2,1)} %dynamic-slice_convert_fusion), channel_id=1, source_target_pairs={{0,1},{1,0},{2,3},{3,2},{4,5},{5,4},{6,7},{7,6},{8,9},{9,8},{10,11... | collective-permute-start | bytes 2752520 | tf_op jit(solution)/shard_map/ppermute | solution.py:17
  672.9 11.9 %collective-permute-start.54 = (bf16[224,576]{0,1:T(8,128)(2,1)S(1)}, bf16[224,576]{0,1:T(8,128)(2,1)S(1)}, u32[]{:S(2)}, u32[]{:S(2)}) collective-permute-start(bf16[224,576]{0,1:T(8,128)(2,1)S(1)} %slice.850), channel_id=1, source_target_pairs={{0,8},{4,12},{8,0},{12,4},{16,24},{20,28},{24,16},{28,20},{1,9},{5... | collective-permute-start | bytes 774152 | tf_op jit(solution)/shard_map/ppermute | solution.py:17
  696.0 13.0 %collective-permute-start.56 = (bf16[112,288]{0,1:T(8,128)(2,1)S(1)}, bf16[112,288]{0,1:T(8,128)(2,1)S(1)}, u32[]{:S(2)}, u32[]{:S(2)}) collective-permute-start(bf16[112,288]{0,1:T(8,128)(2,1)S(1)} %get-tuple-element.327), channel_id=1, source_target_pairs={{0,0},{1,2},{2,1},{3,3},{4,4},{5,6},{6,5},{7,7},{8,8},{9,10},{10,9... | collective-permute-start | bytes 193544 | tf_op jit(solution)/shard_map/ppermute | solution.py:94
  696.7 12.4 %collective-permute-start.57 = (bf16[112,288]{0,1:T(8,128)(2,1)S(1)}, bf16[112,288]{0,1:T(8,128)(2,1)S(1)}, u32[]{:S(2)}, u32[]{:S(2)}) collective-permute-start(bf16[112,288]{0,1:T(8,128)(2,1)S(1)} %get-tuple-element.328), channel_id=1, source_target_pairs={{0,1},{1,3},{2,0},{3,2},{4,5},{5,7},{6,4},{7,6},{8,9},{9,11},{10,8... | collective-permute-start | bytes 193544 | tf_op jit(solution)/shard_map/ppermute | solution.py:95
  (115 other events, 1712.0 us)

commit v2 on v1

v2 whole, which is shorter than its diff:
```python
import functools
import math

import jax
import jax.numpy as jnp
from jax import lax
from jax.experimental import pallas as pl
from jax.experimental.pallas import tpu as pltpu
from jax.sharding import PartitionSpec as P

HD = 64
eps = 1e-06
theta_base = 1000000.0
bf16 = jnp.bfloat16
f32 = jnp.float32
NT = (((1,), (1,)), ((), ()))
TN = (((0,), (0,)), ((), ()))


def flip(block, axis, bit):
    count = lax.axis_size(axis)
    return lax.ppermute(block, axis, [(i, i ^ 1 << bit) for i in range(count)])


def bit_reversed(value, bits):
    return sum((value >> b & 1) << (bits - 1 - b) for b in range(bits))


def halves_turned(block):
    lane = lax.broadcasted_iota(jnp.int32, block.shape, 1)
    return jnp.where(lane % HD < HD // 2, pltpu.roll(block, 128 - HD // 2, 1), pltpu.roll(block, HD // 2, 1))

def attend_kernel(norm_ref, w_ref, bias_ref, cos_ref, sin_ref, qk_ref, v_ref, att_ref, lse_ref, kpad, vpad, lse_cols, *, block):
    step = pl.program_id(0)
    length = norm_ref.shape[0]
    wide = qk_ref.shape[1]
    pairs = wide // 128
    lane = lax.broadcasted_iota(jnp.int32, (1, 128), 1)
    @pl.when(step == 0)
    def _():
        for r in range(0, length, block):
            rows = pl.ds(r, block)
            mixed = (jnp.dot(norm_ref[rows, :], w_ref[...], preferred_element_type=f32) + bias_ref[...]).astype(bf16).astype(f32)
            cos, sin = cos_ref[rows, :], sin_ref[rows, :]
            for p in range(pairs):
                u = mixed[:, p * 128:(p + 1) * 128]
                turned = (u * cos + halves_turned(u) * sin).astype(bf16)
                qk_ref[rows, p * 128:(p + 1) * 128] = turned
            value = mixed[:, wide:]
            v_ref[rows, :] = value.astype(bf16)
            zero = jnp.zeros_like(value)
            vpad[0, rows, :] = jnp.concatenate([value, zero], 1).astype(bf16)
            vpad[1, rows, :] = jnp.concatenate([zero, value], 1).astype(bf16)
            last = turned.astype(f32)
            kpad[1, rows, :] = jnp.where(lane >= HD, last, 0.0).astype(bf16)
            kpad[0, rows, :] = jnp.where(lane < HD, pltpu.roll(last, HD, 1), 0.0).astype(bf16)
        lse_cols[...] = jnp.zeros_like(lse_cols)

    factor = HD ** -0.5 * math.log2(math.e)
    cols = pl.ds(pl.multiple_of(step * 128, 128), 128)
    row_i = lax.broadcasted_iota(jnp.int32, (block, block), 0)
    col_i = lax.broadcasted_iota(jnp.int32, (block, block), 1)
    for r in range(0, length, block):
        rows = pl.ds(r, block)
        q = qk_ref[rows, cols]

        def head(odd):
            scores = lax.dot_general(q, kpad[odd, :r + block, :], (((1,), (1,)), ((), ())), preferred_element_type=f32)
            diag = jnp.where(col_i <= row_i, scores[:, r:], -1e30)
            scores = jnp.concatenate([scores[:, :r], diag], 1) if r else diag
            top = jnp.max(scores, 1, keepdims=True)
            e = jnp.exp2((scores - top) * factor)
            total = jnp.sum(e, 1, keepdims=True)
            out = jnp.dot(e.astype(bf16), vpad[odd, :r + block, :], preferred_element_type=f32)
            lse = top * factor + jnp.log2(total)
            at = lax.broadcasted_iota(jnp.int32, (1, 128), 1) == 2 * step + odd
            lse_cols[rows, :] = jnp.where(at, lse, lse_cols[rows, :])
            return out / total

        even = head(0)

        @pl.when(step < pairs - 1)
        def _():
            att_ref[rows, :] = (even + head(1)).astype(bf16)

        @pl.when(step == pairs - 1)
        def _():
            att_ref[rows, :] = even.astype(bf16)

    @pl.when(step == pairs - 1)
    def _():
        lse_ref[...] = lse_cols[...].T[:lse_ref.shape[0], :]

def attend(normed, weight, bias, cos, sin):
    length, depth = normed.shape
    group = weight.shape[1]
    wide = group - HD
    pairs = wide // 128
    block = min(256, length)
    whole = lambda shape: pl.BlockSpec(shape, lambda p: (0, 0))
    return pl.pallas_call(
        functools.partial(attend_kernel, block=block),
        grid=(pairs,),
        in_specs=[whole(normed.shape), whole(weight.shape), whole(bias.shape), whole(cos.shape), whole(sin.shape)],
        out_specs=[whole((length, wide)), whole((length, HD)), pl.BlockSpec((length, 128), lambda p: (0, p)), whole((8, length))],
        out_shape=[jax.ShapeDtypeStruct((length, wide), bf16), jax.ShapeDtypeStruct((length, HD), bf16),
                   jax.ShapeDtypeStruct((length, wide), bf16), jax.ShapeDtypeStruct((8, length), f32)],
        scratch_shapes=[pltpu.VMEM((2, length, 128), bf16), pltpu.VMEM((2, length, 128), bf16), pltpu.VMEM((length, 128), f32)],
        compiler_params=pltpu.CompilerParams(vmem_limit_bytes=50*1024*1024),
        cost_estimate=pl.CostEstimate(flops=6*10**9, bytes_accessed=6*10**6, transcendentals=5*10**6),
    )(normed, weight, bias, cos, sin)

def attend_back_kernel(grad_ref, w_ref, qk_ref, v_ref, lse_ref, cos_ref, sin_ref, mixed_ref, bias_ref, kpad, vpad, gatt, dq_acc, dk, dv, *, block):
    step = pl.program_id(0)
    length = grad_ref.shape[0]
    wide = qk_ref.shape[1]
    pairs = wide // 128
    lane = lax.broadcasted_iota(jnp.int32, (1, 128), 1)
    @pl.when(step == 0)
    def _():
        for r in range(0, length, block):
            rows = pl.ds(r, block)
            got = jnp.dot(grad_ref[rows, :], w_ref[...], preferred_element_type=f32)
            gatt[rows, :wide - HD] = got.astype(bf16)
            gatt[rows, wide - HD:] = jnp.zeros((block, HD), bf16)
            value = v_ref[rows, :].astype(f32)
            zero = jnp.zeros_like(value)
            vpad[0, rows, :] = jnp.concatenate([value, zero], 1).astype(bf16)
            vpad[1, rows, :] = jnp.concatenate([zero, value], 1).astype(bf16)
            last = qk_ref[rows, wide - 128:].astype(f32)
            kpad[1, rows, :] = jnp.where(lane >= HD, last, 0.0).astype(bf16)
            kpad[0, rows, :] = jnp.where(lane < HD, pltpu.roll(last, HD, 1), 0.0).astype(bf16)
        dk[...] = jnp.zeros_like(dk)
        dv[...] = jnp.zeros_like(dv)

    factor = HD ** -0.5 * math.log2(math.e)
    cols = pl.ds(pl.multiple_of(step * 128, 128), 128)
    key_i = lax.broadcasted_iota(jnp.int32, (block, block), 0)
    query_i = lax.broadcasted_iota(jnp.int32, (block, block), 1)
    for r in range(0, length, block):
        rows = pl.ds(r, block)
        q = qk_ref[rows, cols]
        g = gatt[rows, cols]

        def head(odd):
            lse = lse_ref[pl.ds(2 * step + odd, 1), rows]
            probs, grads = [], []
            inner = jnp.zeros((1, block), f32)
            for c in range(0, r + block, block):
                scores = lax.dot_general(kpad[odd, c:c + block, :], q, NT, preferred_element_type=f32)
                p = jnp.exp2(scores * factor - lse)
                if c == r:
                    p = jnp.where(key_i <= query_i, p, 0.0)
                dp = lax.dot_general(vpad[odd, c:c + block, :], g, NT, preferred_element_type=f32)
                inner = inner + jnp.sum(p * dp, 0, keepdims=True)
                probs.append(p)
                grads.append(dp)
            dq = 0.0
            for i, c in enumerate(range(0, r + block, block)):
                keys = pl.ds(c, block)
                ds = (probs[i] * (grads[i] - inner)).astype(bf16)
                half = lane >= HD if odd else lane < HD
                dk[keys, :] += jnp.where(half, jnp.dot(ds, q, preferred_element_type=f32), 0.0)
                dv[keys, :] += jnp.where(half, jnp.dot(probs[i].astype(bf16), g, preferred_element_type=f32), 0.0)
                dq = dq + lax.dot_general(ds, kpad[odd, c:c + block, :], TN, preferred_element_type=f32)
            return dq

        dq_acc[rows, :] = head(0)

        @pl.when(step < pairs - 1)
        def _():
            dq_acc[rows, :] += head(1)

    def back(u, rows):
        return u * cos_ref[rows, :] - halves_turned(u) * sin_ref[rows, :]
    scale = HD ** -0.5
    for r in range(0, length, block):
        rows = pl.ds(r, block)
        @pl.when(step < pairs - 1)
        def _():
            mixed_ref[rows, cols] = back(dq_acc[rows, :] * scale, rows).astype(bf16)
        @pl.when(step == pairs - 1)
        def _():
            k = dk[rows, :]
            k = jnp.where(lane >= HD, k + pltpu.roll(k, HD, 1), dq_acc[rows, :]) * scale
            mixed_ref[rows, wide - 128:wide] = back(k, rows).astype(bf16)
            v = dv[rows, :]
            v = v + pltpu.roll(v, HD, 1)
            mixed_ref[rows, wide:] = v[:, :HD].astype(bf16)
    @pl.when(step == pairs - 1)
    def _():
        total = jnp.zeros((1, mixed_ref.shape[1]), f32)
        for r in range(0, length, block):
            total = total + jnp.sum(mixed_ref[pl.ds(r, block), :].astype(f32), 0, keepdims=True)
        bias_ref[...] = total

def attend_back(grad, weight, qk, v, lse, cos, sin):
    length, depth = grad.shape
    wide = qk.shape[1]
    group = wide + HD
    pairs = wide // 128
    block = min(256, length)
    whole = lambda shape: pl.BlockSpec(shape, lambda p: (0, 0))
    ins = (grad, weight, qk, v, lse, cos, sin)
    return pl.pallas_call(
        functools.partial(attend_back_kernel, block=block),
        grid=(pairs,),
        in_specs=[whole(a.shape) for a in ins],
        out_specs=[whole((length, group)), whole((1, group))],
        out_shape=[jax.ShapeDtypeStruct((length, group), bf16), jax.ShapeDtypeStruct((1, group), f32)],
        scratch_shapes=[pltpu.VMEM((2, length, 128), bf16), pltpu.VMEM((2, length, 128), bf16), pltpu.VMEM((length, wide), bf16),
                        pltpu.VMEM((length, 128), f32), pltpu.VMEM((length, 128), f32), pltpu.VMEM((length, 128), f32)],
        compiler_params=pltpu.CompilerParams(vmem_limit_bytes=50*1024*1024),
        cost_estimate=pl.CostEstimate(flops=12*10**9, bytes_accessed=8*10**6, transcendentals=5*10**6),
    )(*ins)

def rope_tables(length):
    inverse = theta_base ** (-(jnp.arange(HD // 2, dtype=f32) * 2.0 / HD))
    angles = jnp.arange(length, dtype=f32)[:, None] * inverse[None, :]
    c, s = jnp.cos(angles), jnp.sin(angles)
    return jnp.concatenate([c] * 4, 1), jnp.concatenate([-s, s, -s, s], 1)


def mlp_kernel(x_ref, g_ref, wg_ref, wu_ref, wd_ref, *rest, add):
    if add: down_in, ngrad_in, hid_ref, gg_ref, gu_ref, down_ref, ngrad_ref = rest
    else: hid_ref, gg_ref, gu_ref, down_ref, ngrad_ref = rest
    x, g = x_ref[...], g_ref[...]
    gate = jnp.dot(x, wg_ref[...], preferred_element_type=f32)
    up = jnp.dot(x, wu_ref[...], preferred_element_type=f32)
    gh = jnp.dot(g, wd_ref[...], preferred_element_type=f32)
    sig = 1.0 / (1.0 + jnp.exp(-gate))
    silu = gate * sig
    hid = (silu * up).astype(bf16)
    ghs = gh * sig
    gg = (ghs * up * (1.0 + gate - silu)).astype(bf16)
    gu = (ghs * gate).astype(bf16)
    hid_ref[...] = hid[:, :hid_ref.shape[1]]
    gg_ref[...] = gg[:, :gg_ref.shape[1]]
    gu_ref[...] = gu[:, :gu_ref.shape[1]]
    down = lax.dot_general(hid, wd_ref[...], NT, preferred_element_type=f32)
    ngrad = lax.dot_general(gg, wg_ref[...], NT, preferred_element_type=f32) + lax.dot_general(gu, wu_ref[...], NT, preferred_element_type=f32)
    if add:
        down = down + down_in[...].astype(f32); ngrad = ngrad + ngrad_in[...].astype(f32)
    down_ref[...] = down.astype(bf16)
    ngrad_ref[...] = ngrad.astype(bf16)

def mlp(x, g, joined, width, sums=None, tile=512):
    t, d = x.shape
    n = joined.shape[1] // 3
    tile = min(tile, t)
    tok = pl.BlockSpec((tile, d), lambda i: (i, 0)); tn = pl.BlockSpec((tile, width), lambda i: (i, 0))
    w = [pl.BlockSpec((d, n), lambda i, k=k: (0, k)) for k in range(3)]
    add = sums is not None
    return pl.pallas_call(functools.partial(mlp_kernel, add=add), grid=(t // tile,),
        in_specs=[tok, tok, *w] + [tok, tok] * add, out_specs=[tn, tn, tn, tok, tok],
        out_shape=[jax.ShapeDtypeStruct((t, width), bf16)] * 3 + [jax.ShapeDtypeStruct((t, d), bf16)] * 2,
        compiler_params=pltpu.CompilerParams(vmem_limit_bytes=56*1024*1024),
        cost_estimate=pl.CostEstimate(flops=12 * t * d * n, bytes_accessed=2 * (3 * d * n + 3 * t * n + 4 * t * d), transcendentals=2 * t * n),
    )(x, g, joined, joined, joined, *(sums or ()))


def gather_rows(block, bits):
    pieces = [block]
    beside = [flip(block, "row", 0)]
    for bit in reversed(range(1, bits)):
        got = flip(jnp.concatenate(pieces, 0), "row", bit)
        beside.append(flip(got, "row", 0))
        pieces.append(got)
    return jnp.concatenate(pieces + beside, 0)


def scatter_rows(total, first, bits):
    for bit in range(first, bits):
        half = total.shape[0] // 2
        got = flip(total[half:].astype(bf16), "row", bit)
        total = total[:half] + got.astype(f32)
    return total


def in_order(first, second, parity, axis=0):
    return jnp.where(
        parity == 0,
        jnp.concatenate([first, second], axis),
        jnp.concatenate([second, first], axis),
    )


def pair(block, parity):
    return in_order(block, flip(block, "col", 0), parity)


def keep_half(partial, parity):
    half = partial.shape[0] // 2
    outgoing = lax.dynamic_slice_in_dim(partial, (1 - parity) * half, half, 0).astype(bf16)
    staying = lax.dynamic_slice_in_dim(partial, parity * half, half, 0)
    return staying + flip(outgoing, "col", 0).astype(f32)


def to_pairs(block):
    first = lax.ppermute(block, "col", [(2 * a + b, 2 * b + a) for a in range(2) for b in range(2)])
    second = lax.ppermute(
        block, "col", [(2 * a + b, 2 * (1 - b) + a) for a in range(2) for b in range(2)]
    )
    return first, second


def from_pairs(same, other):
    first = lax.ppermute(same, "col", [(2 * a + b, 2 * b + a) for a in range(2) for b in range(2)])
    second = lax.ppermute(
        other, "col", [(2 * a + b, 2 * b + 1 - a) for a in range(2) for b in range(2)]
    )
    return first, second


def cuts(width):
    first = min(512, width)
    return [(0, first), (first, width)] if first < width else [(0, width)]


def shards(
    layer_input,
    gain_attn,
    qkv_weight,
    qkv_bias,
    out_weight,
    gain_mlp,
    gate_weight,
    up_weight,
    down_weight,
    cotangent,
):
    row = lax.axis_index("row")
    column = lax.axis_index("col")
    row_count = lax.axis_size("row")
    bits = row_count.bit_length() - 1
    core = column % 2
    sequence = column // 2
    tok_local, model_width = layer_input.shape
    length = tok_local * 2
    deep = model_width // row_count
    ff_cols = gate_weight.shape[1]
    qkv_cols = qkv_weight.shape[1]
    out_cols = out_weight.shape[0]
    group_width = 2 * qkv_cols
    query_width = group_width - 2 * HD

    first, second = to_pairs(jnp.concatenate([qkv_weight, out_weight.T], 1))
    low = jnp.where(sequence == 0, first, second)
    high = jnp.where(sequence == 0, second, first)
    qkv_full = gather_rows(jnp.concatenate([low[:, :qkv_cols], high[:, :qkv_cols]], 1), bits)
    out_full = gather_rows(jnp.concatenate([low[:, qkv_cols:], high[:, qkv_cols:]], 1), bits)
    first, second = to_pairs(qkv_bias[None, :])
    bias_full = in_order(first, second, sequence, 1).astype(f32)

    place = jnp.arange(model_width, dtype=jnp.int32)
    masks = jnp.array([bit_reversed(p, bits) for p in range(row_count)], jnp.int32)
    source = jnp.repeat(masks ^ row, deep) * deep + place % deep
    to_stored = (place[:, None] == source[None, :]).astype(bf16)

    def stored(block):
        return jnp.dot(block, to_stored, preferred_element_type=f32)

    def unstored(block):
        return jnp.einsum("ts,fs->tf", block, to_stored, preferred_element_type=f32).astype(bf16)

    def unstored_row(vector):
        blocks = vector.reshape(row_count, deep)
        blocks = jnp.concatenate(
            [blocks[bit_reversed(m, bits)][None] for m in range(row_count)], 0
        )
        for bit in range(bits):
            wide = blocks.reshape(-1, 2, 1 << bit, deep)
            turned = jnp.concatenate([wide[:, 1:], wide[:, :1]], 1).reshape(row_count, deep)
            blocks = jnp.where((row >> bit) % 2 == 1, turned, blocks)
        return blocks.reshape(model_width)

    input_rows = stored(layer_input)
    grad_out = stored(cotangent)
    gain_one = stored(gain_attn[None, :])
    gain_two = stored(gain_mlp[None, :])

    scale_one = lax.rsqrt(jnp.mean(input_rows * input_rows, axis=1) + eps)
    normed_one_blk = (input_rows * scale_one[:, None] * gain_one).astype(bf16)
    normed_one = pair(normed_one_blk, core)
    cosine, sine_part = rope_tables(length)
    qk_rows, value_rows, att_group, log_totals = attend(
        normed_one, qkv_full, bias_full, cosine, sine_part
    )
    att_group = att_group[:, :query_width]
    attn_partial = jnp.einsum("ta,da->td", att_group, out_full, preferred_element_type=f32)
    middle = input_rows + keep_half(attn_partial, core)
    scale_two = lax.rsqrt(jnp.mean(middle * middle, axis=1) + eps)
    normed_two_blk = (middle * scale_two[:, None] * gain_two).astype(bf16)

    def widen(block):
        beside = flip(block, "col", 0)
        across = flip(block, "col", 1)
        return jnp.concatenate([block, beside, across, flip(across, "col", 0)], 0)

    def narrow(partial):
        own, beside, across, far = jnp.split(partial, 4, 0)
        across = across.astype(f32) + flip(far, "col", 0).astype(f32)
        return (
            own.astype(f32)
            + flip(beside, "col", 0).astype(f32)
            + flip(across.astype(bf16), "col", 1).astype(f32)
        )

    normed_two = widen(normed_two_blk)
    grad_full = widen(grad_out.astype(bf16))
    down_flipped = down_weight.T
    sums = None
    totals = []
    for start, stop in cuts(ff_cols):
        width = stop - start
        padded = -(-width // 256) * 256
        pieces = [
            jnp.pad(part[:, start:stop], ((0, 0), (0, padded - width)))
            for part in (gate_weight, up_weight, down_flipped)
        ]
        joined = gather_rows(jnp.concatenate(pieces, 1), bits)
        hidden, grad_gate, grad_up, *sums = mlp(normed_two, grad_full, joined, width, sums)
        half = model_width // 2

        def products(columns):
            return [
                jnp.einsum("td,tf->df", rows[:, columns], right, preferred_element_type=f32)
                for rows, right in (
                    (normed_two, grad_gate),
                    (normed_two, grad_up),
                    (grad_full, hidden),
                )
            ]

        sent = jnp.concatenate([part.astype(bf16) for part in products(slice(half, None))], 1)
        kept = jnp.concatenate(products(slice(0, half)), 1)
        total = kept + flip(sent, "row", 0).astype(f32)
        total = scatter_rows(total, 1, bits)
        totals.append([total[:, :width], total[:, width : 2 * width], total[:, 2 * width :]])
    down_sum, normed_sum = sums
    gate_total, up_total, down_total = zip(*totals)
    grad_normed_two = narrow(normed_sum)
    layer_output = unstored((middle + narrow(down_sum)).astype(bf16))
    scaled_two = gain_two * grad_normed_two
    inner_two = jnp.sum(scaled_two * middle, axis=1)
    grad_middle = (
        grad_out
        + scale_two[:, None] * scaled_two
        - middle * (scale_two**3 * inner_two / model_width)[:, None]
    )
    gain_two_grad = jnp.sum(grad_normed_two * middle * scale_two[:, None], axis=0)
    grad_branch = pair(grad_middle.astype(bf16), core)
    out_grad = jnp.einsum("td,ta->da", grad_branch, att_group, preferred_element_type=f32)
    grad_mixed, bias_grad = attend_back(
        grad_branch, out_full, qk_rows, value_rows, log_totals, cosine, sine_part
    )
    bias_grad = bias_grad[0]
    qkv_grad = jnp.einsum("td,tc->dc", normed_one, grad_mixed, preferred_element_type=f32)
    grad_normed_one = keep_half(
        jnp.einsum("tc,dc->td", grad_mixed, qkv_full, preferred_element_type=f32), core
    )
    scaled_one = gain_one * grad_normed_one
    inner_one = jnp.sum(scaled_one * input_rows, axis=1)
    input_grad = unstored(
        (
            grad_middle
            + scale_one[:, None] * scaled_one
            - input_rows * (scale_one**3 * inner_one / model_width)[:, None]
        ).astype(bf16)
    )
    gain_one_grad = jnp.sum(grad_normed_one * input_rows * scale_one[:, None], axis=0)

    def to_columns(total):
        half = total.shape[1] // 2
        low, high = total[:, :half].astype(bf16), total[:, half:].astype(bf16)
        first, second = from_pairs(
            jnp.where(sequence == 0, low, high), jnp.where(sequence == 0, high, low)
        )
        return first.astype(f32) + second.astype(f32)

    out_total = to_columns(scatter_rows(out_grad, 0, bits))
    qkv_total = to_columns(scatter_rows(qkv_grad, 0, bits))
    bias_row = lax.dynamic_update_slice_in_dim(
        jnp.zeros((group_width * 2,), f32), bias_grad, core * group_width, 0
    )
    small = jnp.concatenate([unstored_row(gain_one_grad), unstored_row(gain_two_grad), bias_row])
    small = jnp.pad(small, (0, -small.shape[0] % 128)).reshape(-1, 128)
    for bit in range(2):
        small = small + flip(small, "col", bit)
    for bit in range(bits):
        small = small + flip(small, "row", bit)
    small = small.reshape(-1)
    gain_one_total = small[:model_width]
    gain_two_total = small[model_width : 2 * model_width]
    bias_total = lax.dynamic_slice_in_dim(small, 2 * model_width + column * qkv_cols, qkv_cols, 0)
    return (
        layer_output,
        input_grad,
        gain_one_total,
        qkv_total,
        bias_total,
        out_total.T,
        gain_two_total,
        jnp.concatenate(gate_total, 1),
        jnp.concatenate(up_total, 1),
        jnp.concatenate(down_total, 1).T,
    )


def solution(mesh):
    in_specs = (
        P(("row", "col"), None),
        P(),
        P("row", "col"),
        P("col"),
        P("col", "row"),
        P(),
        P("row", "col"),
        P("row", "col"),
        P("col", "row"),
        P(("row", "col"), None),
    )
    out_specs = (
        P(("row", "col"), None),
        P(("row", "col"), None),
        P(),
        P("row", "col"),
        P("col"),
        P("col", "row"),
        P(),
        P("row", "col"),
        P("row", "col"),
        P("col", "row"),
    )
    return jax.shard_map(shards, mesh=mesh, in_specs=in_specs, out_specs=out_specs, check_vma=False)
```

time: 722 us -> 508 us (0.70)
  matrix products: 293 us -> 56.5 us
  Pallas kernels: 0 us -> 94.8 us
  local copies, waits for them, and re-layouts: 84.7 us -> 40.2 us
  starting transfers between devices: 81.1 us -> 51.2 us
  other arithmetic: 52.4 us -> 66.1 us
    dot_general x118 -> x12, matrix products: 268 us -> 32.2 us  [products(): jnp.einsum('td,tf->df', rows[:, columns], right, preferred_element_type=f32)]
    pallas_call x0 -> x4, Pallas kernels: none -> 94.8 us  [the longest x2 46.1 us: mlp(): pl.pallas_call(functools.partial(mlp_kernel, add=add), grid=(t // tile,),...]
    ppermute x73 -> x53, starting transfers between devices: 67.7 us -> 36.9 us  [flip(): return lax.ppermute(block, axis, [(i, i ^ 1 << bit) for i in range(count)])]
    concatenate x12 -> x10, other arithmetic: 1.3 us -> 24.7 us  [the longest x2 17.6 us: widen(): return jnp.concatenate([block, beside, across, flip(across, 'col', 0)], 0)]
    unnamed x196 -> x146, local copies, waits for them, and re-layouts: 29.6 us -> 11.9 us
    slice x19 -> x10, local copies, waits for them, and re-layouts: 13.7 us -> 2.34 us  [the longest x8 1.35 us: shards(): part[:, start:stop]]
    dynamic_update_slice x7 -> x0, local copies, waits for them, and re-layouts: 9.79 us -> none  [attention_forward(): lax.map(lambda query_one: head_forward(query_one, key_rows, value_rows, b...]
    dynamic_update_slice x14 -> x0, other arithmetic: 9.78 us -> none  [attention_forward(): lax.map(lambda query_one: head_forward(query_one, key_rows, value_rows, b...]
  transfers between devices with their start and end apart: 81 -> 61, of which waited for: 35 -> 24; matrix products, arithmetic and copies ran while one was open for 48% -> 23% of each run, Pallas kernels for 0% -> 10%
where the time goes in v2:
time: 508 us; the launch traced here: 504 us
  waiting for transfers between devices  193 us (38%)
  Pallas kernels  94.8 us (19%)
  other arithmetic  66.1 us (13%)
  matrix products  56.5 us (11%)
  starting transfers between devices  51.2 us (10%)
  local copies, waits for them, and re-layouts  40.2 us (8%)
    ppermute x53, waiting for transfers between devices, flip(): return lax.ppermute(block, axis, [(i, i ^ 1 << bit) for i in range(count)])  190 us
    pallas_call x2, Pallas kernels, mlp(): pl.pallas_call(functools.partial(mlp_kernel, add=add), grid=(t // tile,),...  46.1 us
    ppermute x53, starting transfers between devices, flip(): return lax.ppermute(block, axis, [(i, i ^ 1 << bit) for i in range(count)])  36.9 us
    dot_general x12, matrix products, products(): jnp.einsum('td,tf->df', rows[:, columns], right, preferred_element_type=f32)  32.2 us
    pallas_call x1, Pallas kernels, attend_back(): pl.pallas_call(functools.partial(attend_back_kernel, block=block), grid=(...  29.2 us
    pallas_call x1, Pallas kernels, attend(): pl.pallas_call(functools.partial(attend_kernel, block=block), grid=(pairs...  19.5 us
    concatenate x2, other arithmetic, widen(): return jnp.concatenate([block, beside, across, flip(across, 'col', 0)], 0)  17.6 us
    unnamed x146, local copies, waits for them, and re-layouts  11.9 us
  transfers between devices with their start and end apart: 61, of which 24 were waited for; matrix products, arithmetic and copies ran while one was open for 23% of the time, Pallas kernels for 10%

profile of v2, /device:TPU:0, one launch (start us, length us, event | category | flops | bytes accessed | tf_op | source)
XLA Modules:
  0.0 503.8 jit_solution(13598099045306795033)
XLA Ops:
  3.4 2.1 collective-permute-start.1
  5.5 2.8 collective-permute-start.2
  9.6 3.0 collective-permute-start.9
  13.5 2.5 fusion.15
  19.0 3.2 fusion.72
  22.9 2.8 bitcast_convert_fusion
  26.5 2.7 pad_maximum_fusion.7
  32.3 2.6 collective-permute-start.27
  36.7 2.7 collective-permute-start.10
  39.4 38.8 %collective-permute-done.10 = bf16[112,448]{1,0:T(8,128)(2,1)S(1)} collective-permute-done((bf16[112,448]{1,0:T(8,128)(2,1)S(1)}, bf16[112,448]{1,0:T(8,128)(2,1)S(1)}, u32[]{:S(2)}, u32[]{:S(2)}) %collective-permute-start.10) | collective-permute-done | bytes 100384 | tf_op jit(solution)/shard_map/ppermute | solution.py:22
  78.4 9.2 %collective-permute-done.3 = bf16[112,576]{1,0:T(8,128)(2,1)S(1)} collective-permute-done((bf16[112,576]{1,0:T(8,128)(2,1)S(1)}, bf16[112,576]{1,0:T(8,128)(2,1)S(1)}, u32[]{:S(2)}, u32[]{:S(2)}) %collective-permute-start.3) | collective-permute-done | bytes 129056 | tf_op jit(solution)/shard_map/ppermute | solution.py:22
  90.1 5.2 %collective-permute-done.11 = bf16[224,448]{1,0:T(8,128)(2,1)S(1)} collective-permute-done((bf16[224,448]{1,0:T(8,128)(2,1)S(1)}, bf16[224,448]{1,0:T(8,128)(2,1)S(1)}, u32[]{:S(2)}, u32[]{:S(2)}) %collective-permute-start.11) | collective-permute-done | bytes 200736 | tf_op jit(solution)/shard_map/ppermute | solution.py:22
  96.2 5.2 %collective-permute-done.13 = bf16[112,448]{1,0:T(8,128)(2,1)S(1)} collective-permute-done((bf16[112,448]{1,0:T(8,128)(2,1)S(1)}, bf16[112,448]{1,0:T(8,128)(2,1)S(1)}, u32[]{:S(2)}, u32[]{:S(2)}) %collective-permute-start.13) | collective-permute-done | bytes 100384 | tf_op jit(solution)/shard_map/ppermute | solution.py:22
  103.6 2.9 collective-permute-done.5
  110.3 6.3 %collective-permute-done.14 = bf16[224,448]{1,0:T(8,128)(2,1)S(1)} collective-permute-done((bf16[224,448]{1,0:T(8,128)(2,1)S(1)}, bf16[224,448]{1,0:T(8,128)(2,1)S(1)}, u32[]{:S(2)}, u32[]{:S(2)}) %collective-permute-start.14) | collective-permute-done | bytes 200736 | tf_op jit(solution)/shard_map/ppermute | solution.py:22
  117.2 5.5 %collective-permute-done.7 = bf16[224,576]{1,0:T(8,128)(2,1)S(1)} collective-permute-done((bf16[224,576]{1,0:T(8,128)(2,1)S(1)}, bf16[224,576]{1,0:T(8,128)(2,1)S(1)}, u32[]{:S(2)}, u32[]{:S(2)}) %collective-permute-start.7) | collective-permute-done | bytes 258080 | tf_op jit(solution)/shard_map/ppermute | solution.py:22
  122.7 2.0 collective-permute-start.28
  124.8 3.7 maximum_select_fusion.norm_ref
  128.5 19.5 %shard_map.186 = (bf16[1024,512]{1,0:T(8,128)(2,1)S(1)}, bf16[1024,64]{1,0:T(8,128)(2,1)S(1)}, bf16[1024,512]{1,0:T(8,128)(2,1)S(1)}, f32[8,1024]{1,0:T(8,128)S(1)}) custom-call(bf16[1024,896]{1,0:T(8,128)(2,1)} %maximum_select_fusion.norm_ref, bf16[896,576]{1,0:T(8,128)(2,1)} %copy-done.53, f32[1,576]{1,0:T(1,128)S(1)} %fusion.77.bias_ref, ...), custom_call_target="tpu_custom_call" | custom-call | flops 6000000000 | bytes 6000000 | tf_op jit(solution)/shard_map/pallas_call | solution.py:101
  152.9 8.8 %collective-permute-done.30 = bf16[112,1536]{1,0:T(8,128)(2,1)S(1)} collective-permute-done((bf16[112,1536]{1,0:T(8,128)(2,1)S(1)}, bf16[112,1536]{1,0:T(8,128)(2,1)S(1)}, u32[]{:S(2)}, u32[]{:S(2)}) %collective-permute-start.30) | collective-permute-done | bytes 344096 | tf_op jit(solution)/shard_map/ppermute | solution.py:22
  163.1 20.3 %collective-permute-done.23 = bf16[224,2304]{1,0:T(8,128)(2,1)S(1)} collective-permute-done((bf16[224,2304]{1,0:T(8,128)(2,1)S(1)}, bf16[224,2304]{1,0:T(8,128)(2,1)S(1)}, u32[]{:S(2)}, u32[]{:S(2)}) %collective-permute-start.23) | collective-permute-done | bytes 1032224 | tf_op jit(solution)/shard_map/ppermute | solution.py:22
  183.4 2.2 collective-permute-start.17
  187.9 16.3 %collective-permute-done.31 = bf16[224,1536]{1,0:T(8,128)(2,1)S(1)} collective-permute-done((bf16[224,1536]{1,0:T(8,128)(2,1)S(1)}, bf16[224,1536]{1,0:T(8,128)(2,1)S(1)}, u32[]{:S(2)}, u32[]{:S(2)}) %collective-permute-start.31) | collective-permute-done | bytes 688160 | tf_op jit(solution)/shard_map/ppermute | solution.py:22
  204.8 8.8 %pad_maximum_fusion.1.g_ref = bf16[2048,896]{1,0:T(8,128)(2,1)} fusion(bf16[512,896]{1,0:T(8,128)(2,1)S(1)} %collective-permute-done.21, bf16[512,896]{1,0:T(8,128)(2,1)S(1)} %collective-permute-done.20, bf16[512,896]{1,0:T(8,128)(2,1)S(1)} %collective-permute-done.19, bf16[512,896]{1,0:T(8,128)(2,1)S(1)} %copy-done.43), kind=kLoop, calls=%fused_computation.2 | loop fusion | flops 14680064 | bytes 7340032 | tf_op jit(solution)/shard_map/concatenate | solution.py:398
  213.6 7.4 %collective-permute-done.26 = bf16[224,2304]{1,0:T(8,128)(2,1)S(1)} collective-permute-done((bf16[224,2304]{1,0:T(8,128)(2,1)S(1)}, bf16[224,2304]{1,0:T(8,128)(2,1)S(1)}, u32[]{:S(2)}, u32[]{:S(2)}) %collective-permute-start.26) | collective-permute-done | bytes 1032224 | tf_op jit(solution)/shard_map/ppermute | solution.py:22
  221.2 2.0 copy-done.50
  223.1 8.7 %pad_maximum_fusion.x_ref = bf16[2048,896]{1,0:T(8,128)(2,1)} fusion(bf16[512,896]{1,0:T(8,128)(2,1)S(1)} %collective-permute-done.18, bf16[512,896]{1,0:T(8,128)(2,1)S(1)} %collective-permute-done.17, bf16[512,896]{1,0:T(8,128)(2,1)S(1)} %collective-permute-done.16, bf16[512,896]{1,0:T(8,128)(2,1)S(1)} %multiply_convert_fusion), kind=kLoop, calls=%fused_computation.1 | loop fusion | flops 14680064 | bytes 7340032 | tf_op jit(solution)/shard_map/concatenate | solution.py:398
  231.9 18.5 %shard_map.187 = (bf16[2048,512]{1,0:T(8,128)(2,1)}, bf16[2048,512]{1,0:T(8,128)(2,1)}, bf16[2048,512]{1,0:T(8,128)(2,1)}, bf16[2048,896]{1,0:T(8,128)(2,1)}, bf16[2048,896]{1,0:T(8,128)(2,1)}) custom-call(bf16[2048,896]{1,0:T(8,128)(2,1)} %pad_maximum_fusion.x_ref, bf16[2048,896]{1,0:T(8,128)(2,1)} %pad_maximum_fusion.1.g_ref, ...), custom_call_target="tpu_custom_call" | custom-call | flops 11274289152 | bytes 23724032 | tf_op jit(solution)/shard_map/pallas_call | solution.py:254
  250.4 3.4 fusion.51
  253.8 2.1 fusion.44
  255.9 27.6 %shard_map.188 = (bf16[2048,704]{1,0:T(8,128)(2,1)}, bf16[2048,704]{1,0:T(8,128)(2,1)}, bf16[2048,704]{1,0:T(8,128)(2,1)}, bf16[2048,896]{1,0:T(8,128)(2,1)}, bf16[2048,896]{1,0:T(8,128)(2,1)}) custom-call(bf16[2048,896]{1,0:T(8,128)(2,1)} %pad_maximum_fusion.x_ref, bf16[2048,896]{1,0:T(8,128)(2,1)} %pad_maximum_fusion.1.g_ref, ...), custom_call_target="tpu_custom_call" | custom-call | flops 16911433728 | bytes 28246016 | tf_op jit(solution)/shard_map/pallas_call | solution.py:254
  283.5 4.9 convolution_convert_fusion
  288.4 2.8 fusion.40
  291.2 2.9 convolution_convert_fusion.1
  294.1 2.8 fusion.42
  302.4 2.7 fusion.10
  308.9 3.1 fusion.31
  312.0 2.1 fusion.46
  315.6 2.1 fusion.12
  317.6 4.1 concatenate.186
  323.2 4.8 concatenate.185
  328.1 2.7 add_convert_fusion.2
  330.8 2.4 collective-permute-done.55
  338.7 2.3 multiply_reduce_fusion
  341.0 3.7 fusion.83
  345.3 12.7 %collective-permute-done.34 = bf16[512,896]{1,0:T(8,128)(2,1)} collective-permute-done((bf16[512,896]{1,0:T(8,128)(2,1)}, bf16[512,896]{1,0:T(8,128)(2,1)}, u32[]{:S(2)}, u32[]{:S(2)}) %collective-permute-start.34) | collective-permute-done | bytes 917536 | tf_op jit(solution)/shard_map/ppermute | solution.py:22
  358.0 4.7 fusion.29
  364.2 6.7 %collective-permute-done.58 = bf16[448,2112]{1,0:T(8,128)(2,1)} collective-permute-done((bf16[448,2112]{1,0:T(8,128)(2,1)}, bf16[448,2112]{1,0:T(8,128)(2,1)}, u32[]{:S(2)}, u32[]{:S(2)}) %collective-permute-start.58) | collective-permute-done | bytes 1892384 | tf_op jit(solution)/shard_map/ppermute | solution.py:22
  370.9 1.9 convert_add_fusion
  375.2 7.0 %collective-permute-done.57 = bf16[112,1536]{1,0:T(8,128)(2,1)S(1)} collective-permute-done((bf16[112,1536]{1,0:T(8,128)(2,1)S(1)}, bf16[112,1536]{1,0:T(8,128)(2,1)S(1)}, u32[]{:S(2)}, u32[]{:S(2)}) %collective-permute-start.57) | collective-permute-done | bytes 344096 | tf_op jit(solution)/shard_map/ppermute | solution.py:22
  383.2 2.6 maximum_select_fusion.1.grad_ref
  389.6 29.2 %shard_map.189 = (bf16[1024,576]{1,0:T(8,128)(2,1)}, f32[1,576]{1,0:T(1,128)S(1)}) custom-call(bf16[1024,896]{1,0:T(8,128)(2,1)} %copy-done.30, bf16[896,448]{1,0:T(8,128)(2,1)S(1)} %constant_dynamic-update-slice_fusion.6.w_ref, bf16[1024,512]{1,0:T(8,128)(2,1)S(1)} %copy-done.3, bf16[1024,64]{1,0:T(8,128)(2,1)S(1)} %get-tuple-element.32.v_ref, ...), custom_call_target="tpu_custom_call" | custom-call | flops 12000000000 | bytes 8000000 | tf_op jit(solution)/shard_map/pallas_call | solution.py:205
  418.7 2.7 fusion.96
  424.7 3.0 fusion.95
  431.2 2.1 slice_add_fusion
  438.3 2.1 copy.26
  442.3 15.5 %collective-permute-done.60 = bf16[112,2112]{1,0:T(8,128)(2,1)} collective-permute-done((bf16[112,2112]{1,0:T(8,128)(2,1)}, bf16[112,2112]{1,0:T(8,128)(2,1)}, u32[]{:S(2)}, u32[]{:S(2)}) %collective-permute-start.60) | collective-permute-done | bytes 473120 | tf_op jit(solution)/shard_map/ppermute | solution.py:22
  462.3 7.2 %collective-permute-done.52 = bf16[112,448]{0,1:T(8,128)(2,1)S(1)} collective-permute-done((bf16[112,448]{0,1:T(8,128)(2,1)S(1)}, bf16[112,448]{0,1:T(8,128)(2,1)S(1)}, u32[]{:S(2)}, u32[]{:S(2)}) %collective-permute-start.52) | collective-permute-done | bytes 100384 | tf_op jit(solution)/shard_map/ppermute | solution.py:22
  472.9 3.1 collective-permute-done.54
  479.4 5.3 %collective-permute-done.47 = bf16[112,576]{0,1:T(8,128)(2,1)S(1)} collective-permute-done((bf16[112,576]{0,1:T(8,128)(2,1)S(1)}, bf16[112,576]{0,1:T(8,128)(2,1)S(1)}, u32[]{:S(2)}, u32[]{:S(2)}) %collective-permute-start.47) | collective-permute-done | bytes 129056 | tf_op jit(solution)/shard_map/ppermute | solution.py:22
  486.3 2.7 collective-permute-start.49
  490.5 2.2 collective-permute-done.42
  492.8 4.9 fusion.30
  497.7 3.0 collective-permute-start.44
  (365 shorter events, 90.3 us)
Async XLA Ops:
  3.4 31.6 %collective-permute-start.1 = (bf16[112,512]{1,0:T(8,128)(2,1)}, bf16[112,512]{1,0:T(8,128)(2,1)}, u32[]{:S(2)}, u32[]{:S(2)}) collective-permute-start(bf16[112,512]{1,0:T(8,128)(2,1)} %pad_maximum_fusion.14), channel_id=1, source_target_pairs={{0,0},{1,2},{2,1},{3,3},{4,4},{5,6},{6,5},{7,7},{8,8},{9,10},{10,9... | collective-permute-start | bytes 344072 | tf_op jit(solution)/shard_map/ppermute | solution.py:300
  5.5 29.8 %collective-permute-start.2 = (bf16[112,512]{1,0:T(8,128)(2,1)}, bf16[112,512]{1,0:T(8,128)(2,1)}, u32[]{:S(2)}, u32[]{:S(2)}) collective-permute-start(bf16[112,512]{1,0:T(8,128)(2,1)} %pad_maximum_fusion.14), channel_id=1, source_target_pairs={{0,2},{1,0},{2,3},{3,1},{4,6},{5,4},{6,7},{7,5},{8,10},{9,8},{10,1... | collective-permute-start | bytes 344072 | tf_op jit(solution)/shard_map/ppermute | solution.py:301
  9.0 23.2 %collective-permute-start.8 = (bf16[1,288]{1,0:T(2,128)(2,1)S(1)}, bf16[1,288]{1,0:T(2,128)(2,1)S(1)}, u32[]{:S(2)}, u32[]{:S(2)}) collective-permute-start(bf16[1,288]{1,0:T(2,128)(2,1)S(1)} %broadcast_in_dim.7), channel_id=1, source_target_pairs={{0,0},{1,2},{2,1},{3,3},{4,4},{5,6},{6,5},{7,7},{8,8},{9,10},{10,9... | collective-permute-start | bytes 1736 | tf_op jit(solution)/shard_map/ppermute | solution.py:300
  9.6 22.7 %collective-permute-start.9 = (bf16[1,288]{1,0:T(2,128)(2,1)S(1)}, bf16[1,288]{1,0:T(2,128)(2,1)S(1)}, u32[]{:S(2)}, u32[]{:S(2)}) collective-permute-start(bf16[1,288]{1,0:T(2,128)(2,1)S(1)} %broadcast_in_dim.7), channel_id=1, source_target_pairs={{0,2},{1,0},{2,3},{3,1},{4,6},{5,4},{6,7},{7,5},{8,10},{9,8},{10,1... | collective-permute-start | bytes 1736 | tf_op jit(solution)/shard_map/ppermute | solution.py:301
  17.5 107.3 %collective-permute-start = (bf16[512,896]{1,0:T(8,128)(2,1)S(1)}, bf16[512,896]{1,0:T(8,128)(2,1)}, u32[]{:S(2)}, u32[]{:S(2)}) collective-permute-start(bf16[512,896]{1,0:T(8,128)(2,1)S(1)} %fusion.17), channel_id=1, source_target_pairs={{0,1},{1,0},{2,3},{3,2},{4,5},{5,4},{6,7},{7,6},{8,9},{9,8},{10,11... | collective-permute-start | bytes 2752520 | tf_op jit(solution)/shard_map/ppermute | solution.py:22
  32.1 57.1 %copy-start.41 = (bf16[112,512]{1,0:T(8,128)(2,1)S(1)}, bf16[112,512]{1,0:T(8,128)(2,1)}, u32[]{:S(2)}) copy-start(bf16[112,512]{1,0:T(8,128)(2,1)} %slice.309) | copy-start | bytes 344068
  32.1 57.2 %copy-start.42 = (bf16[112,512]{1,0:T(8,128)(2,1)S(1)}, bf16[112,512]{1,0:T(8,128)(2,1)}, u32[]{:S(2)}) copy-start(bf16[112,512]{1,0:T(8,128)(2,1)} %slice.310) | copy-start | bytes 344068
  32.2 129.6 %collective-permute-start.20 = (bf16[512,896]{1,0:T(8,128)(2,1)}, bf16[512,896]{1,0:T(8,128)(2,1)S(1)}, u32[]{:S(2)}, u32[]{:S(2)}) collective-permute-start(bf16[512,896]{1,0:T(8,128)(2,1)} %get-tuple-element.109), channel_id=1, source_target_pairs={{0,2},{1,3},{2,0},{3,1},{4,6},{5,7},{6,4},{7,5},{8,10},{9,11},{10,... | collective-permute-start | bytes 2752520 | tf_op jit(solution)/shard_map/ppermute | solution.py:22
  32.3 56.9 %collective-permute-start.27 = (bf16[112,1536]{1,0:T(8,128)(2,1)}, bf16[112,1536]{1,0:T(8,128)(2,1)S(1)}, u32[]{:S(2)}, u32[]{:S(2)}) collective-permute-start(bf16[112,1536]{1,0:T(8,128)(2,1)} %get-tuple-element.64), channel_id=1, source_target_pairs={{0,16},{4,20},{8,24},{12,28},{16,0},{20,4},{24,8},{28,12},{1,17},{... | collective-permute-start | bytes 1032200 | tf_op jit(solution)/shard_map/ppermute | solution.py:22
  35.0 73.7 %collective-permute-start.22 = (bf16[112,2304]{1,0:T(8,128)(2,1)}, bf16[112,2304]{1,0:T(8,128)(2,1)S(1)}, u32[]{:S(2)}, u32[]{:S(2)}) collective-permute-start(bf16[112,2304]{1,0:T(8,128)(2,1)} %get-tuple-element.62), channel_id=1, source_target_pairs={{0,16},{4,20},{8,24},{12,28},{16,0},{20,4},{24,8},{28,12},{1,17},{... | collective-permute-start | bytes 1548296 | tf_op jit(solution)/shard_map/ppermute | solution.py:22
  36.7 41.6 %collective-permute-start.10 = (bf16[112,448]{1,0:T(8,128)(2,1)S(1)}, bf16[112,448]{1,0:T(8,128)(2,1)S(1)}, u32[]{:S(2)}, u32[]{:S(2)}) collective-permute-start(bf16[112,448]{1,0:T(8,128)(2,1)S(1)} %get-tuple-element.72), channel_id=1, source_target_pairs={{0,16},{4,20},{8,24},{12,28},{16,0},{20,4},{24,8},{28,12},{1,17},{... | collective-permute-start | bytes 301064 | tf_op jit(solution)/shard_map/ppermute | solution.py:22
  78.3 9.3 %collective-permute-start.3 = (bf16[112,576]{1,0:T(8,128)(2,1)S(1)}, bf16[112,576]{1,0:T(8,128)(2,1)S(1)}, u32[]{:S(2)}, u32[]{:S(2)}) collective-permute-start(bf16[112,576]{1,0:T(8,128)(2,1)S(1)} %get-tuple-element.51), channel_id=1, source_target_pairs={{0,16},{4,20},{8,24},{12,28},{16,0},{20,4},{24,8},{28,12},{1,17},{... | collective-permute-start | bytes 387080 | tf_op jit(solution)/shard_map/ppermute | solution.py:22
  87.5 8.0 %collective-permute-start.12 = (bf16[112,448]{1,0:T(8,128)(2,1)S(1)}, bf16[112,448]{1,0:T(8,128)(2,1)S(1)}, u32[]{:S(2)}, u32[]{:S(2)}) collective-permute-start(bf16[112,448]{1,0:T(8,128)(2,1)S(1)} %get-tuple-element.72), channel_id=1, source_target_pairs={{0,4},{4,0},{8,12},{12,8},{16,20},{20,16},{24,28},{28,24},{1,5},{5... | collective-permute-start | bytes 301064 | tf_op jit(solution)/shard_map/ppermute | solution.py:22
  89.2 6.1 %collective-permute-start.11 = (bf16[224,448]{1,0:T(8,128)(2,1)S(1)}, bf16[224,448]{1,0:T(8,128)(2,1)S(1)}, u32[]{:S(2)}, u32[]{:S(2)}) collective-permute-start(bf16[224,448]{1,0:T(8,128)(2,1)S(1)} %pad_maximum_fusion.12), channel_id=1, source_target_pairs={{0,8},{4,12},{8,0},{12,4},{16,24},{20,28},{24,16},{28,20},{1,9},{5... | collective-permute-start | bytes 602120 | tf_op jit(solution)/shard_map/ppermute | solution.py:22
  95.3 6.7 %collective-permute-start.4 = (bf16[224,576]{1,0:T(8,128)(2,1)S(1)}, bf16[224,576]{1,0:T(8,128)(2,1)S(1)}, u32[]{:S(2)}, u32[]{:S(2)}) collective-permute-start(bf16[224,576]{1,0:T(8,128)(2,1)S(1)} %pad_maximum_fusion.11), channel_id=1, source_target_pairs={{0,8},{4,12},{8,0},{12,4},{16,24},{20,28},{24,16},{28,20},{1,9},{5... | collective-permute-start | bytes 774152 | tf_op jit(solution)/shard_map/ppermute | solution.py:22
  95.6 5.9 %collective-permute-start.13 = (bf16[112,448]{1,0:T(8,128)(2,1)S(1)}, bf16[112,448]{1,0:T(8,128)(2,1)S(1)}, u32[]{:S(2)}, u32[]{:S(2)}) collective-permute-start(bf16[112,448]{1,0:T(8,128)(2,1)S(1)} %collective-permute-done.10), channel_id=1, source_target_pairs={{0,4},{4,0},{8,12},{12,8},{16,20},{20,16},{24,28},{28,24},{1,5},{5... | collective-permute-start | bytes 301064 | tf_op jit(solution)/shard_map/ppermute | solution.py:22
  101.4 5.1 %collective-permute-start.5 = (bf16[112,576]{1,0:T(8,128)(2,1)S(1)}, bf16[112,576]{1,0:T(8,128)(2,1)S(1)}, u32[]{:S(2)}, u32[]{:S(2)}) collective-permute-start(bf16[112,576]{1,0:T(8,128)(2,1)S(1)} %get-tuple-element.51), channel_id=1, source_target_pairs={{0,4},{4,0},{8,12},{12,8},{16,20},{20,16},{24,28},{28,24},{1,5},{5... | collective-permute-start | bytes 387080 | tf_op jit(solution)/shard_map/ppermute | solution.py:22
  102.0 6.1 %collective-permute-start.6 = (bf16[112,576]{1,0:T(8,128)(2,1)S(1)}, bf16[112,576]{1,0:T(8,128)(2,1)S(1)}, u32[]{:S(2)}, u32[]{:S(2)}) collective-permute-start(bf16[112,576]{1,0:T(8,128)(2,1)S(1)} %collective-permute-done.3), channel_id=1, source_target_pairs={{0,4},{4,0},{8,12},{12,8},{16,20},{20,16},{24,28},{28,24},{1,5},{5... | collective-permute-start | bytes 387080 | tf_op jit(solution)/shard_map/ppermute | solution.py:22
  106.5 98.2 %collective-permute-start.19 = (bf16[512,896]{1,0:T(8,128)(2,1)S(1)}, bf16[512,896]{1,0:T(8,128)(2,1)S(1)}, u32[]{:S(2)}, u32[]{:S(2)}) collective-permute-start(bf16[512,896]{1,0:T(8,128)(2,1)S(1)} %copy-done.43), channel_id=1, source_target_pairs={{0,1},{1,0},{2,3},{3,2},{4,5},{5,4},{6,7},{7,6},{8,9},{9,8},{10,11... | collective-permute-start | bytes 2752520 | tf_op jit(solution)/shard_map/ppermute | solution.py:22
  108.1 8.5 %collective-permute-start.14 = (bf16[224,448]{1,0:T(8,128)(2,1)S(1)}, bf16[224,448]{1,0:T(8,128)(2,1)S(1)}, u32[]{:S(2)}, u32[]{:S(2)}) collective-permute-start(bf16[224,448]{1,0:T(8,128)(2,1)S(1)} %collective-permute-done.11), channel_id=1, source_target_pairs={{0,4},{4,0},{8,12},{12,8},{16,20},{20,16},{24,28},{28,24},{1,5},{5... | collective-permute-start | bytes 602120 | tf_op jit(solution)/shard_map/ppermute | solution.py:22
  108.7 14.1 %collective-permute-start.7 = (bf16[224,576]{1,0:T(8,128)(2,1)S(1)}, bf16[224,576]{1,0:T(8,128)(2,1)S(1)}, u32[]{:S(2)}, u32[]{:S(2)}) collective-permute-start(bf16[224,576]{1,0:T(8,128)(2,1)S(1)} %collective-permute-done.4), channel_id=1, source_target_pairs={{0,4},{4,0},{8,12},{12,8},{16,20},{20,16},{24,28},{28,24},{1,5},{5... | collective-permute-start | bytes 774152 | tf_op jit(solution)/shard_map/ppermute | solution.py:22
  116.6 35.2 %collective-permute-start.29 = (bf16[112,1536]{1,0:T(8,128)(2,1)}, bf16[112,1536]{1,0:T(8,128)(2,1)S(1)}, u32[]{:S(2)}, u32[]{:S(2)}) collective-permute-start(bf16[112,1536]{1,0:T(8,128)(2,1)} %get-tuple-element.64), channel_id=1, source_target_pairs={{0,4},{4,0},{8,12},{12,8},{16,20},{20,16},{24,28},{28,24},{1,5},{5... | collective-permute-start | bytes 1032200 | tf_op jit(solution)/shard_map/ppermute | solution.py:22
  122.7 27.9 %collective-permute-start.28 = (bf16[224,1536]{1,0:T(8,128)(2,1)S(1)}, bf16[224,1536]{1,0:T(8,128)(2,1)S(1)}, u32[]{:S(2)}, u32[]{:S(2)}) collective-permute-start(bf16[224,1536]{1,0:T(8,128)(2,1)S(1)} %pad_maximum_fusion.4), channel_id=1, source_target_pairs={{0,8},{4,12},{8,0},{12,4},{16,24},{20,28},{24,16},{28,20},{1,9},{5... | collective-permute-start | bytes 2064392 | tf_op jit(solution)/shard_map/ppermute | solution.py:22
  149.5 12.9 %collective-permute-start.15 = (bf16[512,896]{1,0:T(8,128)(2,1)S(1)}, bf16[512,896]{1,0:T(8,128)(2,1)S(1)}, u32[]{:S(2)}, u32[]{:S(2)}) collective-permute-start(bf16[512,896]{1,0:T(8,128)(2,1)S(1)} %dynamic-slice_convert_fusion.1), channel_id=1, source_target_pairs={{0,1},{1,0},{2,3},{3,2},{4,5},{5,4},{6,7},{7,6},{8,9},{9,8},{10,11... | collective-permute-start | bytes 2752520 | tf_op jit(solution)/shard_map/ppermute | solution.py:22
  150.7 11.1 %collective-permute-start.30 = (bf16[112,1536]{1,0:T(8,128)(2,1)S(1)}, bf16[112,1536]{1,0:T(8,128)(2,1)S(1)}, u32[]{:S(2)}, u32[]{:S(2)}) collective-permute-start(bf16[112,1536]{1,0:T(8,128)(2,1)S(1)} %collective-permute-done.27), channel_id=1, source_target_pairs={{0,4},{4,0},{8,12},{12,8},{16,20},{20,16},{24,28},{28,24},{1,5},{5... | collective-permute-start | bytes 1032200 | tf_op jit(solution)/shard_map/ppermute | solution.py:22
  151.8 33.9 %collective-permute-start.24 = (bf16[112,2304]{1,0:T(8,128)(2,1)}, bf16[112,2304]{1,0:T(8,128)(2,1)S(1)}, u32[]{:S(2)}, u32[]{:S(2)}) collective-permute-start(bf16[112,2304]{1,0:T(8,128)(2,1)} %get-tuple-element.62), channel_id=1, source_target_pairs={{0,4},{4,0},{8,12},{12,8},{16,20},{20,16},{24,28},{28,24},{1,5},{5... | collective-permute-start | bytes 1548296 | tf_op jit(solution)/shard_map/ppermute | solution.py:22
  161.7 21.7 %collective-permute-start.23 = (bf16[224,2304]{1,0:T(8,128)(2,1)S(1)}, bf16[224,2304]{1,0:T(8,128)(2,1)S(1)}, u32[]{:S(2)}, u32[]{:S(2)}) collective-permute-start(bf16[224,2304]{1,0:T(8,128)(2,1)S(1)} %pad_maximum_fusion.3), channel_id=1, source_target_pairs={{0,8},{4,12},{8,0},{12,4},{16,24},{20,28},{24,16},{28,20},{1,9},{5... | collective-permute-start | bytes 3096584 | tf_op jit(solution)/shard_map/ppermute | solution.py:22
  161.8 24.6 %collective-permute-start.25 = (bf16[112,2304]{1,0:T(8,128)(2,1)S(1)}, bf16[112,2304]{1,0:T(8,128)(2,1)S(1)}, u32[]{:S(2)}, u32[]{:S(2)}) collective-permute-start(bf16[112,2304]{1,0:T(8,128)(2,1)S(1)} %collective-permute-done.22), channel_id=1, source_target_pairs={{0,4},{4,0},{8,12},{12,8},{16,20},{20,16},{24,28},{28,24},{1,5},{5... | collective-permute-start | bytes 1548296 | tf_op jit(solution)/shard_map/ppermute | solution.py:22
  162.4 42.3 %collective-permute-start.21 = (bf16[512,896]{1,0:T(8,128)(2,1)S(1)}, bf16[512,896]{1,0:T(8,128)(2,1)S(1)}, u32[]{:S(2)}, u32[]{:S(2)}) collective-permute-start(bf16[512,896]{1,0:T(8,128)(2,1)S(1)} %collective-permute-done.20), channel_id=1, source_target_pairs={{0,1},{1,0},{2,3},{3,2},{4,5},{5,4},{6,7},{7,6},{8,9},{9,8},{10,11... | collective-permute-start | bytes 2752520 | tf_op jit(solution)/shard_map/ppermute | solution.py:22
  183.4 20.7 %collective-permute-start.17 = (bf16[512,896]{1,0:T(8,128)(2,1)S(1)}, bf16[512,896]{1,0:T(8,128)(2,1)S(1)}, u32[]{:S(2)}, u32[]{:S(2)}) collective-permute-start(bf16[512,896]{1,0:T(8,128)(2,1)S(1)} %multiply_convert_fusion), channel_id=1, source_target_pairs={{0,2},{1,3},{2,0},{3,1},{4,6},{5,7},{6,4},{7,5},{8,10},{9,11},{10,... | collective-permute-start | bytes 2752520 | tf_op jit(solution)/shard_map/ppermute | solution.py:22
  185.7 18.4 %collective-permute-start.31 = (bf16[224,1536]{1,0:T(8,128)(2,1)S(1)}, bf16[224,1536]{1,0:T(8,128)(2,1)S(1)}, u32[]{:S(2)}, u32[]{:S(2)}) collective-permute-start(bf16[224,1536]{1,0:T(8,128)(2,1)S(1)} %collective-permute-done.28), channel_id=1, source_target_pairs={{0,4},{4,0},{8,12},{12,8},{16,20},{20,16},{24,28},{28,24},{1,5},{5... | collective-permute-start | bytes 2064392 | tf_op jit(solution)/shard_map/ppermute | solution.py:22
  186.4 34.7 %collective-permute-start.26 = (bf16[224,2304]{1,0:T(8,128)(2,1)S(1)}, bf16[224,2304]{1,0:T(8,128)(2,1)S(1)}, u32[]{:S(2)}, u32[]{:S(2)}) collective-permute-start(bf16[224,2304]{1,0:T(8,128)(2,1)S(1)} %collective-permute-done.23), channel_id=1, source_target_pairs={{0,4},{4,0},{8,12},{12,8},{16,20},{20,16},{24,28},{28,24},{1,5},{5... | collective-permute-start | bytes 3096584 | tf_op jit(solution)/shard_map/ppermute | solution.py:22
  204.2 17.0 %collective-permute-start.16 = (bf16[512,896]{1,0:T(8,128)(2,1)S(1)}, bf16[512,896]{1,0:T(8,128)(2,1)S(1)}, u32[]{:S(2)}, u32[]{:S(2)}) collective-permute-start(bf16[512,896]{1,0:T(8,128)(2,1)S(1)} %multiply_convert_fusion), channel_id=1, source_target_pairs={{0,1},{1,0},{2,3},{3,2},{4,5},{5,4},{6,7},{7,6},{8,9},{9,8},{10,11... | collective-permute-start | bytes 2752520 | tf_op jit(solution)/shard_map/ppermute | solution.py:22
  204.2 17.0 %collective-permute-start.18 = (bf16[512,896]{1,0:T(8,128)(2,1)S(1)}, bf16[512,896]{1,0:T(8,128)(2,1)S(1)}, u32[]{:S(2)}, u32[]{:S(2)}) collective-permute-start(bf16[512,896]{1,0:T(8,128)(2,1)S(1)} %collective-permute-done.17), channel_id=1, source_target_pairs={{0,1},{1,0},{2,3},{3,2},{4,5},{5,4},{6,7},{7,6},{8,9},{9,8},{10,11... | collective-permute-start | bytes 2752520 | tf_op jit(solution)/shard_map/ppermute | solution.py:22
  301.8 31.4 %collective-permute-start.55 = (bf16[448,1536]{1,0:T(8,128)(2,1)}, bf16[448,1536]{1,0:T(8,128)(2,1)}, u32[]{:S(2)}, u32[]{:S(2)}) collective-permute-start(bf16[448,1536]{1,0:T(8,128)(2,1)} %pad_maximum_fusion.2), channel_id=1, source_target_pairs={{0,4},{4,0},{8,12},{12,8},{16,20},{20,16},{24,28},{28,24},{1,5},{5... | collective-permute-start | bytes 4128776 | tf_op jit(solution)/shard_map/ppermute | solution.py:22
  306.2 7.8 %collective-permute-start.36 = (bf16[512,896]{1,0:T(8,128)(2,1)S(1)}, bf16[512,896]{1,0:T(8,128)(2,1)S(1)}, u32[]{:S(2)}, u32[]{:S(2)}) collective-permute-start(bf16[512,896]{1,0:T(8,128)(2,1)S(1)} %get-tuple-element.53), channel_id=1, source_target_pairs={{0,1},{1,0},{2,3},{3,2},{4,5},{5,4},{6,7},{7,6},{8,9},{9,8},{10,11... | collective-permute-start | bytes 2752520 | tf_op jit(solution)/shard_map/ppermute | solution.py:22
  306.2 30.0 %collective-permute-start.35 = (bf16[512,896]{1,0:T(8,128)(2,1)}, bf16[512,896]{1,0:T(8,128)(2,1)}, u32[]{:S(2)}, u32[]{:S(2)}) collective-permute-start(bf16[512,896]{1,0:T(8,128)(2,1)} %get-tuple-element.52), channel_id=1, source_target_pairs={{0,1},{1,0},{2,3},{3,2},{4,5},{5,4},{6,7},{7,6},{8,9},{9,8},{10,11... | collective-permute-start | bytes 2752520 | tf_op jit(solution)/shard_map/ppermute | solution.py:22
  308.9 19.1 %collective-permute-start.33 = (bf16[512,896]{1,0:T(8,128)(2,1)}, bf16[512,896]{1,0:T(8,128)(2,1)}, u32[]{:S(2)}, u32[]{:S(2)}) collective-permute-start(bf16[512,896]{1,0:T(8,128)(2,1)} %get-tuple-element.55), channel_id=1, source_target_pairs={{0,1},{1,0},{2,3},{3,2},{4,5},{5,4},{6,7},{7,6},{8,9},{9,8},{10,11... | collective-permute-start | bytes 2752520 | tf_op jit(solution)/shard_map/ppermute | solution.py:22
  315.3 23.5 %collective-permute-start.37 = (bf16[512,896]{1,0:T(8,128)(2,1)}, bf16[512,896]{1,0:T(8,128)(2,1)}, u32[]{:S(2)}, u32[]{:S(2)}) collective-permute-start(bf16[512,896]{1,0:T(8,128)(2,1)} %add_convert_fusion), channel_id=1, source_target_pairs={{0,2},{1,3},{2,0},{3,1},{4,6},{5,7},{6,4},{7,5},{8,10},{9,11},{10,... | collective-permute-start | bytes 2752520 | tf_op jit(solution)/shard_map/ppermute | solution.py:22
  321.8 49.1 %collective-permute-start.58 = (bf16[448,2112]{1,0:T(8,128)(2,1)}, bf16[448,2112]{1,0:T(8,128)(2,1)}, u32[]{:S(2)}, u32[]{:S(2)}) collective-permute-start(bf16[448,2112]{1,0:T(8,128)(2,1)} %concatenate.186), channel_id=1, source_target_pairs={{0,4},{4,0},{8,12},{12,8},{16,20},{20,16},{24,28},{28,24},{1,5},{5... | collective-permute-start | bytes 5677064 | tf_op jit(solution)/shard_map/ppermute | solution.py:22
  328.0 17.3 %collective-permute-start.32 = (bf16[512,896]{1,0:T(8,128)(2,1)}, bf16[512,896]{1,0:T(8,128)(2,1)}, u32[]{:S(2)}, u32[]{:S(2)}) collective-permute-start(bf16[512,896]{1,0:T(8,128)(2,1)} %get-tuple-element.54), channel_id=1, source_target_pairs={{0,1},{1,0},{2,3},{3,2},{4,5},{5,4},{6,7},{7,6},{8,9},{9,8},{10,11... | collective-permute-start | bytes 2752520 | tf_op jit(solution)/shard_map/ppermute | solution.py:22
  333.2 24.7 %collective-permute-start.34 = (bf16[512,896]{1,0:T(8,128)(2,1)}, bf16[512,896]{1,0:T(8,128)(2,1)}, u32[]{:S(2)}, u32[]{:S(2)}) collective-permute-start(bf16[512,896]{1,0:T(8,128)(2,1)} %add_convert_fusion.2), channel_id=1, source_target_pairs={{0,2},{1,3},{2,0},{3,1},{4,6},{5,7},{6,4},{7,5},{8,10},{9,11},{10,... | collective-permute-start | bytes 2752520 | tf_op jit(solution)/shard_map/ppermute | solution.py:22
  336.2 26.4 %collective-permute-start.56 = (bf16[224,1536]{1,0:T(8,128)(2,1)}, bf16[224,1536]{1,0:T(8,128)(2,1)}, u32[]{:S(2)}, u32[]{:S(2)}) collective-permute-start(bf16[224,1536]{1,0:T(8,128)(2,1)} %slice.535), channel_id=1, source_target_pairs={{0,8},{4,12},{8,0},{12,4},{16,24},{20,28},{24,16},{28,20},{1,9},{5... | collective-permute-start | bytes 2064392 | tf_op jit(solution)/shard_map/ppermute | solution.py:22
  344.8 38.4 %collective-permute-start.38 = (bf16[512,896]{1,0:T(8,128)(2,1)}, bf16[512,896]{1,0:T(8,128)(2,1)}, u32[]{:S(2)}, u32[]{:S(2)}) collective-permute-start(bf16[512,896]{1,0:T(8,128)(2,1)} %get-tuple-element.46), channel_id=1, source_target_pairs={{0,1},{1,0},{2,3},{3,2},{4,5},{5,4},{6,7},{7,6},{8,9},{9,8},{10,11... | collective-permute-start | bytes 2752520 | tf_op jit(solution)/shard_map/ppermute | solution.py:22
  364.1 18.1 %collective-permute-start.57 = (bf16[112,1536]{1,0:T(8,128)(2,1)S(1)}, bf16[112,1536]{1,0:T(8,128)(2,1)S(1)}, u32[]{:S(2)}, u32[]{:S(2)}) collective-permute-start(bf16[112,1536]{1,0:T(8,128)(2,1)S(1)} %slice.539), channel_id=1, source_target_pairs={{0,16},{4,20},{8,24},{12,28},{16,0},{20,4},{24,8},{28,12},{1,17},{... | collective-permute-start | bytes 1032200 | tf_op jit(solution)/shard_map/ppermute | solution.py:22
  374.0 57.2 %collective-permute-start.59 = (bf16[224,2112]{1,0:T(8,128)(2,1)}, bf16[224,2112]{1,0:T(8,128)(2,1)}, u32[]{:S(2)}, u32[]{:S(2)}) collective-permute-start(bf16[224,2112]{1,0:T(8,128)(2,1)} %slice.534), channel_id=1, source_target_pairs={{0,8},{4,12},{8,0},{12,4},{16,24},{20,28},{24,16},{28,20},{1,9},{5... | collective-permute-start | bytes 2838536 | tf_op jit(solution)/shard_map/ppermute | solution.py:22
  388.1 46.1 %collective-permute-start.50 = (bf16[448,448]{0,1:T(8,128)(2,1)}, bf16[448,448]{0,1:T(8,128)(2,1)}, u32[]{:S(2)}, u32[]{:S(2)}) collective-permute-start(bf16[448,448]{0,1:T(8,128)(2,1)} %slice.538), channel_id=1, source_target_pairs={{0,4},{4,0},{8,12},{12,8},{16,20},{20,16},{24,28},{28,24},{1,5},{5... | collective-permute-start | bytes 1204232 | tf_op jit(solution)/shard_map/ppermute | solution.py:22
  389.5 29.2 %copy-start.29 = (bf16[1024,896]{1,0:T(8,128)(2,1)S(1)}, bf16[1024,896]{1,0:T(8,128)(2,1)}, u32[]{:S(2)}) copy-start(bf16[1024,896]{1,0:T(8,128)(2,1)} %maximum_select_fusion.norm_ref) | copy-start | bytes 5505028
  424.1 14.2 %collective-permute-start.45 = (bf16[448,576]{1,0:T(8,128)(2,1)}, bf16[448,576]{1,0:T(8,128)(2,1)}, u32[]{:S(2)}, u32[]{:S(2)}) collective-permute-start(bf16[448,576]{1,0:T(8,128)(2,1)} %copy.25), channel_id=1, source_target_pairs={{0,4},{4,0},{8,12},{12,8},{16,20},{20,16},{24,28},{28,24},{1,5},{5... | collective-permute-start | bytes 1548296 | tf_op jit(solution)/shard_map/ppermute | solution.py:22
  430.7 46.3 %collective-permute-start.39 = (bf16[512,896]{1,0:T(8,128)(2,1)}, bf16[512,896]{1,0:T(8,128)(2,1)}, u32[]{:S(2)}, u32[]{:S(2)}) collective-permute-start(bf16[512,896]{1,0:T(8,128)(2,1)} %dynamic-slice_convert_fusion), channel_id=1, source_target_pairs={{0,1},{1,0},{2,3},{3,2},{4,5},{5,4},{6,7},{7,6},{8,9},{9,8},{10,11... | collective-permute-start | bytes 2752520 | tf_op jit(solution)/shard_map/ppermute | solution.py:22
  434.1 23.6 %collective-permute-start.60 = (bf16[112,2112]{1,0:T(8,128)(2,1)}, bf16[112,2112]{1,0:T(8,128)(2,1)}, u32[]{:S(2)}, u32[]{:S(2)}) collective-permute-start(bf16[112,2112]{1,0:T(8,128)(2,1)} %slice.537), channel_id=1, source_target_pairs={{0,16},{4,20},{8,24},{12,28},{16,0},{20,4},{24,8},{28,12},{1,17},{... | collective-permute-start | bytes 1419272 | tf_op jit(solution)/shard_map/ppermute | solution.py:22
  436.3 23.7 %collective-permute-start.51 = (bf16[224,448]{0,1:T(8,128)(2,1)}, bf16[224,448]{0,1:T(8,128)(2,1)}, u32[]{:S(2)}, u32[]{:S(2)}) collective-permute-start(bf16[224,448]{0,1:T(8,128)(2,1)} %slice.541), channel_id=1, source_target_pairs={{0,8},{4,12},{8,0},{12,4},{16,24},{20,28},{24,16},{28,20},{1,9},{5... | collective-permute-start | bytes 602120 | tf_op jit(solution)/shard_map/ppermute | solution.py:22
  442.2 34.4 %collective-permute-start.46 = (bf16[224,576]{0,1:T(8,128)(2,1)S(1)}, bf16[224,576]{0,1:T(8,128)(2,1)S(1)}, u32[]{:S(2)}, u32[]{:S(2)}) collective-permute-start(bf16[224,576]{0,1:T(8,128)(2,1)S(1)} %slice.540), channel_id=1, source_target_pairs={{0,8},{4,12},{8,0},{12,4},{16,24},{20,28},{24,16},{28,20},{1,9},{5... | collective-permute-start | bytes 774152 | tf_op jit(solution)/shard_map/ppermute | solution.py:22
  461.4 8.2 %collective-permute-start.52 = (bf16[112,448]{0,1:T(8,128)(2,1)S(1)}, bf16[112,448]{0,1:T(8,128)(2,1)S(1)}, u32[]{:S(2)}, u32[]{:S(2)}) collective-permute-start(bf16[112,448]{0,1:T(8,128)(2,1)S(1)} %slice.543), channel_id=1, source_target_pairs={{0,16},{4,20},{8,24},{12,28},{16,0},{20,4},{24,8},{28,12},{1,17},{... | collective-permute-start | bytes 301064 | tf_op jit(solution)/shard_map/ppermute | solution.py:22
  469.6 3.2 collective-permute-start.53
  470.3 5.6 %collective-permute-start.54 = (bf16[112,224]{0,1:T(8,128)(2,1)S(1)}, bf16[112,224]{0,1:T(8,128)(2,1)S(1)}, u32[]{:S(2)}, u32[]{:S(2)}) collective-permute-start(bf16[112,224]{0,1:T(8,128)(2,1)S(1)} %get-tuple-element.71), channel_id=1, source_target_pairs={{0,1},{1,3},{2,0},{3,2},{4,5},{5,7},{6,4},{7,6},{8,9},{9,11},{10,8... | collective-permute-start | bytes 150536 | tf_op jit(solution)/shard_map/ppermute | solution.py:309
  476.8 7.9 %collective-permute-start.47 = (bf16[112,576]{0,1:T(8,128)(2,1)S(1)}, bf16[112,576]{0,1:T(8,128)(2,1)S(1)}, u32[]{:S(2)}, u32[]{:S(2)}) collective-permute-start(bf16[112,576]{0,1:T(8,128)(2,1)S(1)} %slice.542), channel_id=1, source_target_pairs={{0,16},{4,20},{8,24},{12,28},{16,0},{20,4},{24,8},{28,12},{1,17},{... | collective-permute-start | bytes 387080 | tf_op jit(solution)/shard_map/ppermute | solution.py:22
  479.4 5.4 %collective-permute-start.40 = (f32[23,128]{1,0:T(8,128)S(1)}, f32[23,128]{1,0:T(8,128)S(1)}, u32[]{:S(2)}, u32[]{:S(2)}) collective-permute-start(f32[23,128]{1,0:T(8,128)S(1)} %maximum_bitcast_fusion.1), channel_id=1, source_target_pairs={{0,1},{1,0},{2,3},{3,2},{4,5},{5,4},{6,7},{7,6},{8,9},{9,8},{10,11... | collective-permute-start | bytes 35336 | tf_op jit(solution)/shard_map/ppermute | solution.py:22
  484.8 4.2 collective-permute-start.41
  485.6 15.0 %collective-permute-start.48 = (bf16[112,288]{0,1:T(8,128)(2,1)S(1)}, bf16[112,288]{0,1:T(8,128)(2,1)S(1)}, u32[]{:S(2)}, u32[]{:S(2)}) collective-permute-start(bf16[112,288]{0,1:T(8,128)(2,1)S(1)} %get-tuple-element.68), channel_id=1, source_target_pairs={{0,0},{1,2},{2,1},{3,3},{4,4},{5,6},{6,5},{7,7},{8,8},{9,10},{10,9... | collective-permute-start | bytes 193544 | tf_op jit(solution)/shard_map/ppermute | solution.py:308
  486.3 14.3 %collective-permute-start.49 = (bf16[112,288]{0,1:T(8,128)(2,1)S(1)}, bf16[112,288]{0,1:T(8,128)(2,1)S(1)}, u32[]{:S(2)}, u32[]{:S(2)}) collective-permute-start(bf16[112,288]{0,1:T(8,128)(2,1)S(1)} %get-tuple-element.69), channel_id=1, source_target_pairs={{0,1},{1,3},{2,0},{3,2},{4,5},{5,7},{6,4},{7,6},{8,9},{9,11},{10,8... | collective-permute-start | bytes 193544 | tf_op jit(solution)/shard_map/ppermute | solution.py:309
  489.0 3.8 collective-permute-start.42
  492.8 4.9 collective-permute-start.43
  497.7 4.7 collective-permute-start.44
  (62 other events, 480.7 us)

commit v3 on v2

v3 whole, which is shorter than its diff:
```python
import functools
import math

import jax
import jax.numpy as jnp
from jax import lax
from jax.experimental import pallas as pl
from jax.experimental.pallas import tpu as pltpu
from jax.sharding import PartitionSpec as P

HD = 64
eps = 1e-06
theta_base = 1000000.0
bf16 = jnp.bfloat16
f32 = jnp.float32
NT = (((1,), (1,)), ((), ()))
TN = (((0,), (0,)), ((), ()))
MIB = 1024 * 1024


def flip(block, axis, bit):
    count = lax.axis_size(axis)
    return lax.ppermute(block, axis, [(i, i ^ 1 << bit) for i in range(count)])


def bit_reversed(value, bits):
    return sum((value >> b & 1) << (bits - 1 - b) for b in range(bits))


def after(value, *earlier):
    return lax.optimization_barrier((value, *earlier))[0]


def kernel_params(mib):
    return pltpu.CompilerParams(vmem_limit_bytes=mib * MIB)


def cost(flops, nbytes, exps=0):
    return pl.CostEstimate(flops=int(flops), bytes_accessed=int(nbytes), transcendentals=int(exps))


def whole(array):
    return pl.BlockSpec(array.shape, lambda *_: (0,) * len(array.shape))


def in_place(block):
    return pl.BlockSpec(memory_space=pl.ANY)


def assemble(pieces, held, sems):
    copies = []
    at = 0
    for i, piece in enumerate(pieces):
        rows = piece.shape[0]
        copies.append(pltpu.make_async_copy(piece, held.at[pl.ds(at, rows)], sems.at[i]))
        at += rows
    for copy in copies:
        copy.start()
    for copy in copies:
        copy.wait()


def halves_turned(block):
    lane = lax.broadcasted_iota(jnp.int32, block.shape, 1)
    up = pltpu.roll(block, 128 - HD // 2, 1)
    return jnp.where(lane % HD < HD // 2, up, pltpu.roll(block, HD // 2, 1))


def side_rows(r, block, half, parity):
    side = (r // half) ^ parity
    return pl.ds(pl.multiple_of(side * half + r % half, block), block)


def pad_heads(key_value, rows, value, last):
    lane = lax.broadcasted_iota(jnp.int32, (1, 128), 1)
    kpad, vpad = key_value
    zero = jnp.zeros_like(value)
    vpad[0, rows, :] = jnp.concatenate([value, zero], 1).astype(bf16)
    vpad[1, rows, :] = jnp.concatenate([zero, value], 1).astype(bf16)
    kpad[1, rows, :] = jnp.where(lane >= HD, last, 0.0).astype(bf16)
    kpad[0, rows, :] = jnp.where(lane < HD, pltpu.roll(last, HD, 1), 0.0).astype(bf16)


def attend_kernel(parity_ref, own_ref, other_ref, bias_ref, cos_ref, sin_ref, *rest, block, count):
    pieces = rest[:count]
    qk_ref, v_ref, att_ref, lse_ref, held, kpad, vpad, lse_cols, sems = rest[count:]
    step = pl.program_id(0)
    half = own_ref.shape[0]
    length = 2 * half
    wide = qk_ref.shape[1]
    pairs = wide // 128
    parity = parity_ref[0]

    @pl.when(step == 0)
    def _():
        assemble(pieces, held, sems)
        for side, rows_ref in enumerate((own_ref, other_ref)):
            for r in range(0, half, block):
                at = pl.multiple_of((side ^ parity) * half + r, block)
                rows = pl.ds(at, block)
                mixed = jnp.dot(rows_ref[r : r + block, :], held[...], preferred_element_type=f32)
                mixed = (mixed + bias_ref[...]).astype(bf16).astype(f32)
                cos, sin = cos_ref[rows, :], sin_ref[rows, :]
                for p in range(pairs):
                    u = mixed[:, p * 128 : (p + 1) * 128]
                    turned = (u * cos + halves_turned(u) * sin).astype(bf16)
                    qk_ref[rows, p * 128 : (p + 1) * 128] = turned
                v_ref[rows, :] = mixed[:, wide:].astype(bf16)
                pad_heads((kpad, vpad), rows, mixed[:, wide:], turned.astype(f32))
        lse_cols[...] = jnp.zeros_like(lse_cols)

    factor = HD**-0.5 * math.log2(math.e)
    cols = pl.ds(pl.multiple_of(step * 128, 128), 128)
    row_i = lax.broadcasted_iota(jnp.int32, (block, block), 0)
    col_i = lax.broadcasted_iota(jnp.int32, (block, block), 1)
    for r in range(0, length, block):
        rows = pl.ds(r, block)
        to = side_rows(r, block, half, parity)
        q = qk_ref[rows, cols]

        def head(odd):
            keys = kpad[odd, : r + block, :]
            scores = lax.dot_general(q, keys, NT, preferred_element_type=f32)
            diag = jnp.where(col_i <= row_i, scores[:, r:], -1e30)
            scores = jnp.concatenate([scores[:, :r], diag], 1) if r else diag
            top = jnp.max(scores, 1, keepdims=True)
            e = jnp.exp2((scores - top) * factor)
            total = jnp.sum(e, 1, keepdims=True)
            out = jnp.dot(e.astype(bf16), vpad[odd, : r + block, :], preferred_element_type=f32)
            lse = top * factor + jnp.log2(total)
            at = lax.broadcasted_iota(jnp.int32, (1, 128), 1) == 2 * step + odd
            lse_cols[rows, :] = jnp.where(at, lse, lse_cols[rows, :])
            return out / total

        even = head(0)

        @pl.when(step < pairs - 1)
        def _():
            att_ref[to, :] = (even + head(1)).astype(bf16)

        @pl.when(step == pairs - 1)
        def _():
            att_ref[to, :] = even.astype(bf16)

    @pl.when(step == pairs - 1)
    def _():
        lse_ref[...] = lse_cols[...].T[: lse_ref.shape[0], :]


def attend(parity, own, other, pieces, bias, cos, sin):
    half, depth = own.shape
    length = 2 * half
    group = bias.shape[1]
    wide = group - HD
    pairs = wide // 128
    block = min(256, half)
    return pl.pallas_call(
        functools.partial(attend_kernel, block=block, count=len(pieces)),
        grid=(pairs,),
        in_specs=[pl.BlockSpec(memory_space=pltpu.SMEM)]
        + [whole(a) for a in (own, other, bias, cos, sin)]
        + [in_place(piece) for piece in pieces],
        out_specs=[
            pl.BlockSpec((length, wide), lambda p: (0, 0)),
            pl.BlockSpec((length, HD), lambda p: (0, 0)),
            pl.BlockSpec((length, 128), lambda p: (0, p)),
            pl.BlockSpec((8, length), lambda p: (0, 0)),
        ],
        out_shape=[
            jax.ShapeDtypeStruct((length, wide), bf16),
            jax.ShapeDtypeStruct((length, HD), bf16),
            jax.ShapeDtypeStruct((length, wide), bf16),
            jax.ShapeDtypeStruct((8, length), f32),
        ],
        scratch_shapes=[
            pltpu.VMEM((depth, group), bf16),
            pltpu.VMEM((2, length, 128), bf16),
            pltpu.VMEM((2, length, 128), bf16),
            pltpu.VMEM((length, 128), f32),
            pltpu.SemaphoreType.DMA((len(pieces),)),
        ],
        compiler_params=kernel_params(40),
        cost_estimate=cost(12e9, 8e6, 5e6),
    )(parity, own, other, bias, cos, sin, *pieces)


def project_kernel(att_ref, *rest, count):
    pieces = rest[:count]
    own_ref, other_ref, held, sems = rest[count:]
    half = own_ref.shape[0]
    assemble(pieces, held, sems)
    for side, ref in enumerate((own_ref, other_ref)):
        rows = att_ref[side * half : (side + 1) * half, :]
        ref[...] = lax.dot_general(rows, held[...], NT, preferred_element_type=f32).astype(ref.dtype)


def project(att, pieces):
    length, wide = att.shape
    depth = sum(piece.shape[0] for piece in pieces)
    return pl.pallas_call(
        functools.partial(project_kernel, count=len(pieces)),
        in_specs=[pl.BlockSpec(memory_space=pltpu.VMEM)] + [in_place(piece) for piece in pieces],
        out_specs=[pl.BlockSpec(memory_space=pltpu.VMEM)] * 2,
        out_shape=[
            jax.ShapeDtypeStruct((length // 2, depth), f32),
            jax.ShapeDtypeStruct((length // 2, depth), bf16),
        ],
        scratch_shapes=[
            pltpu.VMEM((depth, wide), bf16),
            pltpu.SemaphoreType.DMA((len(pieces),)),
        ],
        compiler_params=kernel_params(40),
        cost_estimate=cost(2 * length * depth * wide, 6e6),
    )(att, *pieces)


def attend_back_kernel(
    parity_ref, own_ref, other_ref, qk_ref, v_ref, lse_ref, cos_ref, sin_ref, *rest, block, count
):
    pieces = rest[:count]
    mixed_ref, bias_ref, held, kpad, vpad, gatt, dq_acc, dk, dv, sems = rest[count:]
    step = pl.program_id(0)
    half_rows = own_ref.shape[0]
    length = 2 * half_rows
    wide = qk_ref.shape[1]
    pairs = wide // 128
    parity = parity_ref[0]
    lane = lax.broadcasted_iota(jnp.int32, (1, 128), 1)

    @pl.when(step == 0)
    def _():
        assemble(pieces, held, sems)
        for side, rows_ref in enumerate((own_ref, other_ref)):
            for r in range(0, half_rows, block):
                rows = pl.ds(pl.multiple_of((side ^ parity) * half_rows + r, block), block)
                got = jnp.dot(rows_ref[r : r + block, :], held[...], preferred_element_type=f32)
                gatt[rows, :] = got.astype(bf16)
        for r in range(0, length, block):
            rows = pl.ds(r, block)
            last = qk_ref[rows, wide - 128 :].astype(f32)
            pad_heads((kpad, vpad), rows, v_ref[rows, :].astype(f32), last)
        dk[...] = jnp.zeros_like(dk)
        dv[...] = jnp.zeros_like(dv)

    factor = HD**-0.5 * math.log2(math.e)
    cols = pl.ds(pl.multiple_of(step * 128, 128), 128)
    key_i = lax.broadcasted_iota(jnp.int32, (block, block), 0)
    query_i = lax.broadcasted_iota(jnp.int32, (block, block), 1)
    for r in range(0, length, block):
        rows = pl.ds(r, block)
        q = qk_ref[rows, cols]
        g = gatt[rows, cols]

        def head(odd):
            lse = lse_ref[pl.ds(2 * step + odd, 1), rows]
            probs, grads = [], []
            inner = jnp.zeros((1, block), f32)
            for c in range(0, r + block, block):
                scores = lax.dot_general(
                    kpad[odd, c : c + block, :], q, NT, preferred_element_type=f32
                )
                p = jnp.exp2(scores * factor - lse)
                if c == r:
                    p = jnp.where(key_i <= query_i, p, 0.0)
                dp = lax.dot_general(vpad[odd, c : c + block, :], g, NT, preferred_element_type=f32)
                inner = inner + jnp.sum(p * dp, 0, keepdims=True)
                probs.append(p)
                grads.append(dp)
            dq = 0.0
            half = lane >= HD if odd else lane < HD
            for i, c in enumerate(range(0, r + block, block)):
                keys = pl.ds(c, block)
                ds = (probs[i] * (grads[i] - inner)).astype(bf16)
                p = probs[i].astype(bf16)
                dk[keys, :] += jnp.where(half, jnp.dot(ds, q, preferred_element_type=f32), 0.0)
                dv[keys, :] += jnp.where(half, jnp.dot(p, g, preferred_element_type=f32), 0.0)
                dq = dq + lax.dot_general(
                    ds, kpad[odd, c : c + block, :], TN, preferred_element_type=f32
                )
            return dq

        dq_acc[rows, :] = head(0)

        @pl.when(step < pairs - 1)
        def _():
            dq_acc[rows, :] += head(1)

    def back(u, rows):
        return u * cos_ref[rows, :] - halves_turned(u) * sin_ref[rows, :]

    scale = HD**-0.5
    for r in range(0, length, block):
        rows = pl.ds(r, block)
        to = side_rows(r, block, half_rows, parity)

        @pl.when(step < pairs - 1)
        def _():
            mixed_ref[to, cols] = back(dq_acc[rows, :] * scale, rows).astype(bf16)

        @pl.when(step == pairs - 1)
        def _():
            k = dk[rows, :]
            k = jnp.where(lane >= HD, k + pltpu.roll(k, HD, 1), dq_acc[rows, :]) * scale
            mixed_ref[to, wide - 128 : wide] = back(k, rows).astype(bf16)
            v = dv[rows, :]
            v = v + pltpu.roll(v, HD, 1)
            mixed_ref[to, wide:] = v[:, :HD].astype(bf16)

    @pl.when(step == pairs - 1)
    def _():
        total = jnp.zeros((1, mixed_ref.shape[1]), f32)
        for r in range(0, length, block):
            part = mixed_ref[pl.ds(r, block), :].astype(f32)
            total = total + jnp.sum(part, 0, keepdims=True)
        bias_ref[...] = total


def attend_back(parity, own, other, pieces, qk, v, lse, cos, sin):
    half, depth = own.shape
    length = 2 * half
    wide = qk.shape[1]
    group = wide + HD
    pairs = wide // 128
    block = min(256, half)
    ins = (own, other, qk, v, lse, cos, sin)
    return pl.pallas_call(
        functools.partial(attend_back_kernel, block=block, count=len(pieces)),
        grid=(pairs,),
        in_specs=[pl.BlockSpec(memory_space=pltpu.SMEM)]
        + [whole(a) for a in ins]
        + [in_place(piece) for piece in pieces],
        out_specs=[
            pl.BlockSpec((length, group), lambda p: (0, 0)),
            pl.BlockSpec((1, group), lambda p: (0, 0)),
        ],
        out_shape=[
            jax.ShapeDtypeStruct((length, group), bf16),
            jax.ShapeDtypeStruct((1, group), f32),
        ],
        scratch_shapes=[
            pltpu.VMEM((depth, wide), bf16),
            pltpu.VMEM((2, length, 128), bf16),
            pltpu.VMEM((2, length, 128), bf16),
            pltpu.VMEM((length, wide), bf16),
            pltpu.VMEM((length, 128), f32),
            pltpu.VMEM((length, 128), f32),
            pltpu.VMEM((length, 128), f32),
            pltpu.SemaphoreType.DMA((len(pieces),)),
        ],
        compiler_params=kernel_params(50),
        cost_estimate=cost(25e9, 8e6, 5e6),
    )(parity, *ins, *pieces)


def mlp_kernel(x0_ref, x1_ref, g0_ref, g1_ref, *rest, count, add):
    pieces = rest[:count]
    rest = rest[count:]
    if add:
        near_in, far_in, act_ref, near_ref, far_ref, held, sems = rest
    else:
        act_ref, near_ref, far_ref, held, sems = rest
    n = held.shape[1] // 3
    step = pl.program_id(0)

    @pl.when(step == 0)
    def _():
        assemble(pieces, held, sems)

    wg, wu, wd = (held[:, k * n : (k + 1) * n] for k in range(3))
    x = jnp.where(step == 0, x0_ref[...], x1_ref[...])
    g = jnp.where(step == 0, g0_ref[...], g1_ref[...])
    gate = jnp.dot(x, wg, preferred_element_type=f32)
    up = jnp.dot(x, wu, preferred_element_type=f32)
    gh = jnp.dot(g, wd, preferred_element_type=f32)
    sig = 1.0 / (1.0 + jnp.exp(-gate))
    silu = gate * sig
    hid = (silu * up).astype(bf16)
    ghs = gh * sig
    gg = (ghs * up * (1.0 + gate - silu)).astype(bf16)
    gu = (ghs * gate).astype(bf16)
    act_ref[:, :n] = gg
    act_ref[:, n : 2 * n] = gu
    act_ref[:, 2 * n :] = hid
    ngrad = lax.dot_general(gg, wg, NT, preferred_element_type=f32)
    ngrad = ngrad + lax.dot_general(gu, wu, NT, preferred_element_type=f32)
    down = lax.dot_general(hid, wd, NT, preferred_element_type=f32)

    @pl.when(step == 0)
    def _():
        near_ref[0] = (ngrad + near_in[0].astype(f32) if add else ngrad).astype(bf16)
        near_ref[1] = (down + near_in[1].astype(f32) if add else down).astype(bf16)

    @pl.when(step == 1)
    def _():
        far_ref[0] = (ngrad + far_in[0].astype(f32) if add else ngrad).astype(bf16)
        far_ref[1] = (down + far_in[1].astype(f32) if add else down).astype(bf16)


def mlp(rows, grads, pieces, sums=None):
    t, d = rows[0].shape
    columns = pieces[0].shape[1]
    add = sums is not None
    ins = (*rows, *grads)
    sums = tuple(sums or ())
    both = pl.BlockSpec((2, t, d), lambda i: (0, 0, 0))
    return pl.pallas_call(
        functools.partial(mlp_kernel, count=len(pieces), add=add),
        grid=(2,),
        in_specs=[whole(a) for a in ins] + [in_place(p) for p in pieces] + [both] * len(sums),
        out_specs=[pl.BlockSpec((t, columns), lambda i: (i, 0)), both, both],
        out_shape=[
            jax.ShapeDtypeStruct((2 * t, columns), bf16),
            jax.ShapeDtypeStruct((2, t, d), bf16),
            jax.ShapeDtypeStruct((2, t, d), bf16),
        ],
        scratch_shapes=[
            pltpu.VMEM((d, columns), bf16),
            pltpu.SemaphoreType.DMA((len(pieces),)),
        ],
        compiler_params=kernel_params(58),
        cost_estimate=cost(8 * t * d * columns, 30 * MIB, 2 * t * columns),
    )(*ins, *pieces, *sums)


def outer_kernel(*refs, groups, blocks):
    rights = refs[groups * blocks : -2]
    sent_ref, kept_ref = refs[-2:]
    half = kept_ref.shape[0]
    t = refs[0].shape[0]

    def fill(lefts):
        for part, ref in ((slice(half, 2 * half), sent_ref), (slice(0, half), kept_ref)):
            total = 0.0
            for i, left in enumerate(lefts):
                right = rights[i * t // rights[0].shape[0]]
                at = i * t % right.shape[0]
                total = total + lax.dot_general(
                    left[:, part], right[at : at + t, :], TN, preferred_element_type=f32
                )
            ref[...] = total.astype(ref.dtype)

    step = pl.program_id(0)
    if groups == 1:
        fill(refs[:blocks])
    else:
        @pl.when(step < 2)
        def _():
            fill(refs[:blocks])

        @pl.when(step == 2)
        def _():
            fill(refs[blocks : 2 * blocks])


def outer(lefts, rights):
    groups, blocks = len(lefts), len(lefts[0])
    steps = 1 if groups == 1 else 3
    t, d = lefts[0][0].shape
    rows = rights[0].shape[0]
    columns = rights[0].shape[1]
    n = columns // steps
    flat = [left for group in lefts for left in group]
    out = pl.BlockSpec((d // 2, n), lambda k: (0, k))
    return pl.pallas_call(
        functools.partial(outer_kernel, groups=groups, blocks=blocks),
        grid=(steps,),
        in_specs=[whole(left) for left in flat]
        + [pl.BlockSpec((rows, n), lambda k: (0, k)) for _ in rights],
        out_specs=[out, out],
        out_shape=[
            jax.ShapeDtypeStruct((d // 2, columns), bf16),
            jax.ShapeDtypeStruct((d // 2, columns), f32),
        ],
        compiler_params=kernel_params(58),
        cost_estimate=cost(2 * t * blocks * d * columns, 20 * MIB),
    )(*flat, *rights)


def rope_tables(length):
    inverse = theta_base ** (-(jnp.arange(HD // 2, dtype=f32) * 2.0 / HD))
    angles = jnp.arange(length, dtype=f32)[:, None] * inverse[None, :]
    c, s = jnp.cos(angles), jnp.sin(angles)
    return jnp.concatenate([c] * 4, 1), jnp.concatenate([-s, s, -s, s], 1)


class Gather:
    def __init__(self, block, bits):
        self.bits = bits
        self.left = bits - 1
        self.pieces = [block]
        self.beside = []
        self.fresh = block

    def ready(self, *earlier):
        self.fresh = after(self.fresh, *earlier)
        self.pieces[-1] = self.fresh

    def step(self):
        self.beside.append(flip(self.fresh, "row", 0))
        if self.left > 0:
            held = jnp.concatenate(self.pieces, 0) if len(self.pieces) > 1 else self.pieces[0]
            self.fresh = flip(held, "row", self.left)
            self.pieces.append(self.fresh)
            self.left -= 1

    def all(self):
        while len(self.beside) < self.bits:
            self.step()
        out = self.pieces + self.beside
        return out if out[0].shape[0] % 16 == 0 else [jnp.concatenate(out, 0)]


def halve(kept, got, bits, bit):
    half = kept.shape[0] // 2
    sent = (kept[half:] + got[half:].astype(f32)).astype(bf16)
    return sent, kept[:half] + got[:half].astype(f32)


class Scatter:
    def __init__(self, sent, kept, bits):
        self.bits, self.bit = bits, 0
        self.kept = kept
        self.got = flip(sent, "row", 0)

    def step(self):
        if self.bit == self.bits - 1:
            return
        self.bit += 1
        sent, self.kept = halve(self.kept, self.got, self.bits, self.bit)
        self.got = flip(sent, "row", self.bit)

    def total(self):
        while self.bit < self.bits - 1:
            self.step()
        return self.kept + self.got.astype(f32)


def turned_pairs(block):
    first = [(2 * a + b, 2 * b + a) for a in range(2) for b in range(2)]
    second = [(2 * a + b, 2 * (1 - b) + a) for a in range(2) for b in range(2)]
    return lax.ppermute(block, "col", first), lax.ppermute(block, "col", second)


def from_pairs(same, other):
    first = [(2 * a + b, 2 * b + a) for a in range(2) for b in range(2)]
    second = [(2 * a + b, 2 * b + 1 - a) for a in range(2) for b in range(2)]
    return lax.ppermute(same, "col", first), lax.ppermute(other, "col", second)


def cuts(width):
    first = min(512, width)
    return [(0, first), (first, width)] if first < width else [(0, width)]


def shards(
    layer_input,
    gain_attn,
    qkv_weight,
    qkv_bias,
    out_weight,
    gain_mlp,
    gate_weight,
    up_weight,
    down_weight,
    cotangent,
):
    row = lax.axis_index("row")
    column = lax.axis_index("col")
    row_count = lax.axis_size("row")
    bits = row_count.bit_length() - 1
    core = column % 2
    sequence = column // 2
    parity = core.astype(jnp.int32).reshape(1)
    tok_local, model_width = layer_input.shape
    length = tok_local * 2
    deep = model_width // row_count
    ff_cols = gate_weight.shape[1]
    qkv_cols = qkv_weight.shape[1]
    out_cols = out_weight.shape[0]
    group_width = 2 * qkv_cols
    query_width = group_width - 2 * HD

    bias_rows = jnp.pad(qkv_bias[None, :], ((0, 15), (0, 0)))
    first, second = turned_pairs(
        jnp.concatenate(
            [
                jnp.concatenate([qkv_weight, bias_rows], 0),
                jnp.pad(out_weight.T, ((0, 16), (0, 0))),
            ],
            1,
        )
    )
    low = jnp.where(sequence == 0, first, second)
    high = jnp.where(sequence == 0, second, first)
    qkv_own = jnp.concatenate([low[:, :qkv_cols], high[:, :qkv_cols]], 1)
    bias_full = qkv_own[deep : deep + 1].astype(f32)
    out_own = jnp.concatenate([low[:deep, qkv_cols:], high[:deep, qkv_cols:]], 1)
    out_own = jnp.pad(out_own, ((0, 0), (0, HD)))
    qkv_gather = Gather(qkv_own[:deep], bits)
    out_gather = Gather(out_own, bits)
    down_flipped = down_weight.T
    mlp_gathers = []
    for start, stop in cuts(ff_cols):
        padded = -(-(stop - start) // 256) * 256
        pieces = [
            jnp.pad(part[:, start:stop], ((0, 0), (0, padded - (stop - start))))
            for part in (gate_weight, up_weight, down_flipped)
        ]
        mlp_gathers.append(Gather(jnp.concatenate(pieces, 1), bits))
    qkv_gather.step()
    out_gather.ready(qkv_gather.fresh)
    qkv_gather.step()
    out_gather.step()
    mlp_gathers[0].ready(qkv_gather.fresh, out_gather.fresh)
    qkv_pieces = qkv_gather.all()
    out_gather.step()
    mlp_gathers[0].step()
    mlp_gathers[1].ready(qkv_pieces[-1], out_gather.fresh)
    out_pieces = out_gather.all()
    mlp_gathers[1].step()

    place = jnp.arange(model_width, dtype=jnp.int32)
    masks = jnp.array([bit_reversed(p, bits) for p in range(row_count)], jnp.int32)
    source = jnp.repeat(masks ^ row, deep) * deep + place % deep
    to_stored = (place[:, None] == source[None, :]).astype(bf16)

    def stored(block):
        return jnp.dot(block, to_stored, preferred_element_type=f32)

    def unstored(block):
        return jnp.einsum("ts,fs->tf", block, to_stored, preferred_element_type=f32).astype(bf16)

    def unstored_row(vector):
        blocks = vector.reshape(row_count, deep)
        blocks = jnp.concatenate(
            [blocks[bit_reversed(m, bits)][None] for m in range(row_count)], 0
        )
        for bit in range(bits):
            wide = blocks.reshape(-1, 2, 1 << bit, deep)
            turned = jnp.concatenate([wide[:, 1:], wide[:, :1]], 1).reshape(row_count, deep)
            blocks = jnp.where((row >> bit) % 2 == 1, turned, blocks)
        return blocks.reshape(model_width)

    input_rows = stored(layer_input)
    grad_out = stored(cotangent)
    gain_one = stored(gain_attn[None, :])
    gain_two = stored(gain_mlp[None, :])

    scale_one = lax.rsqrt(jnp.mean(input_rows * input_rows, axis=1) + eps)
    normed_own = (input_rows * scale_one[:, None] * gain_one).astype(bf16)
    normed_other = flip(normed_own, "col", 0)
    grad_blocks = [grad_out.astype(bf16)]
    grad_blocks.append(flip(grad_blocks[0], "col", 0))
    across = flip(grad_blocks[0], "col", 1)
    grad_blocks += [across, flip(across, "col", 0)]
    cosine, sine_part = rope_tables(length)
    qk_rows, value_rows, att_rows, log_totals = attend(
        parity,
        normed_own,
        normed_other,
        qkv_pieces,
        bias_full,
        cosine,
        sine_part,
    )
    att_own, att_other = project(att_rows, out_pieces)
    middle = input_rows + att_own + flip(att_other, "col", 0).astype(f32)
    scale_two = lax.rsqrt(jnp.mean(middle * middle, axis=1) + eps)
    blocks = [(middle * scale_two[:, None] * gain_two).astype(bf16)]
    across = flip(blocks[0], "col", 1)
    blocks.append(flip(blocks[0], "col", 0))
    blocks += [across, flip(across, "col", 0)]

    first_pieces, second_pieces = (gather.all() for gather in mlp_gathers)
    act_own, *sums_own = mlp(blocks[:2], grad_blocks[:2], first_pieces)
    act_far, *sums_far = mlp(blocks[2:], grad_blocks[2:], first_pieces)
    first_scatter = Scatter(*outer([blocks, grad_blocks], [act_own, act_far]), bits)
    start_far = after(blocks[2], first_scatter.kept)
    act_far, near_far, far_far = mlp(
        [start_far, blocks[3]], grad_blocks[2:], second_pieces, sums_far
    )
    across = near_far.astype(f32) + flip(far_far, "col", 0).astype(f32)
    across = across.astype(bf16)
    normed_back = flip(across[0], "col", 1)
    act_own, near_own, far_own = mlp(
        [after(blocks[0], across), blocks[1]], grad_blocks[:2], second_pieces, sums_own
    )
    beside = flip(far_own, "col", 0)
    first_scatter.step()
    second_scatter = Scatter(*outer([blocks, grad_blocks], [act_own, act_far]), bits)
    down_back = flip(after(across[1], normed_back), "col", 1)

    def summed(k, back):
        return near_own[k].astype(f32) + beside[k].astype(f32) + back.astype(f32)

    grad_normed_two = summed(0, normed_back)
    scaled_two = gain_two * grad_normed_two
    inner_two = jnp.sum(scaled_two * middle, axis=1)
    grad_middle = (
        grad_out
        + scale_two[:, None] * scaled_two
        - middle * (scale_two**3 * inner_two / model_width)[:, None]
    )
    gain_two_grad = jnp.sum(grad_normed_two * middle * scale_two[:, None], axis=0)
    branch_own = grad_middle.astype(bf16)
    branch_other = flip(branch_own, "col", 0)
    out_scatter = Scatter(*outer([[branch_own, branch_other]], [att_rows]), bits)
    layer_output = unstored((middle + summed(1, down_back)).astype(bf16))
    grad_mixed, bias_grad = attend_back(
        parity,
        branch_own,
        branch_other,
        out_pieces,
        qk_rows,
        value_rows,
        log_totals,
        cosine,
        sine_part,
    )
    bias_grad = bias_grad[0]
    qkv_scatter = Scatter(*outer([[normed_own, normed_other]], [grad_mixed]), bits)
    qkv_full = jnp.concatenate(qkv_pieces, 0)
    partial = jnp.einsum("tc,dc->td", grad_mixed, qkv_full, preferred_element_type=f32)
    grad_normed_one = partial[:tok_local] + flip(
        partial[tok_local:].astype(bf16), "col", 0
    ).astype(f32)
    scaled_one = gain_one * grad_normed_one
    inner_one = jnp.sum(scaled_one * input_rows, axis=1)
    input_grad = unstored(
        (
            grad_middle
            + scale_one[:, None] * scaled_one
            - input_rows * (scale_one**3 * inner_one / model_width)[:, None]
        ).astype(bf16)
    )
    gain_one_grad = jnp.sum(grad_normed_one * input_rows * scale_one[:, None], axis=0)

    def to_columns(total, width):
        low, high = total[:, :width].astype(bf16), total[:, width : 2 * width].astype(bf16)
        first, second = from_pairs(
            jnp.where(sequence == 0, low, high), jnp.where(sequence == 0, high, low)
        )
        return first.astype(f32) + second.astype(f32)

    qkv_total = to_columns(qkv_scatter.total(), qkv_cols)
    out_total = to_columns(out_scatter.total(), out_cols)
    mlp_totals = []
    for scatter, (start, stop) in zip((first_scatter, second_scatter), cuts(ff_cols)):
        total = scatter.total()
        padded = total.shape[1] // 3
        mlp_totals.append(
            [total[:, k * padded : k * padded + stop - start] for k in range(3)]
        )
    gate_total, up_total, down_total = (jnp.concatenate(parts, 1) for parts in zip(*mlp_totals))
    bias_row = lax.dynamic_update_slice_in_dim(
        jnp.zeros((group_width * 2,), f32), bias_grad, core * group_width, 0
    )
    small = jnp.concatenate([unstored_row(gain_one_grad), unstored_row(gain_two_grad), bias_row])
    small = jnp.pad(small, (0, -small.shape[0] % 128)).reshape(-1, 128)
    for bit in range(2):
        small = small + flip(small, "col", bit)
    for bit in range(bits):
        small = small + flip(small, "row", bit)
    small = small.reshape(-1)
    gain_one_total = small[:model_width]
    gain_two_total = small[model_width : 2 * model_width]
    bias_total = lax.dynamic_slice_in_dim(small, 2 * model_width + column * qkv_cols, qkv_cols, 0)
    return (
        layer_output,
        input_grad,
        gain_one_total,
        qkv_total,
        bias_total,
        out_total.T,
        gain_two_total,
        gate_total,
        up_total,
        down_total.T,
    )


def solution(mesh):
    in_specs = (
        P(("row", "col"), None),
        P(),
        P("row", "col"),
        P("col"),
        P("col", "row"),
        P(),
        P("row", "col"),
        P("row", "col"),
        P("col", "row"),
        P(("row", "col"), None),
    )
    out_specs = (
        P(("row", "col"), None),
        P(("row", "col"), None),
        P(),
        P("row", "col"),
        P("col"),
        P("col", "row"),
        P(),
        P("row", "col"),
        P("row", "col"),
        P("col", "row"),
    )
    return jax.shard_map(shards, mesh=mesh, in_specs=in_specs, out_specs=out_specs, check_vma=False)
```

time: 508 us -> 449 us (0.88)
  Pallas kernels: 94.8 us -> 163 us
  waiting for transfers between devices: 193 us -> 139 us
  matrix products: 56.5 us -> 17.2 us
  other arithmetic: 66.1 us -> 34.2 us
  local copies, waits for them, and re-layouts: 40.2 us -> 27.5 us
  starting transfers between devices: 51.2 us -> 59.7 us
    pallas_call x4 -> x11, Pallas kernels: 94.8 us -> 163 us  [the longest x4 68.4 us: mlp(): pl.pallas_call(functools.partial(mlp_kernel, count=len(pieces), add=add),...]
    ppermute x53 -> x51, waiting for transfers between devices: 190 us -> 137 us  [flip(): return lax.ppermute(block, axis, [(i, i ^ 1 << bit) for i in range(count)])]
    dot_general x15 -> x0, matrix products: 37.4 us -> none  [the longest x12 32.2 us: products(): jnp.einsum('td,tf->df', rows[:, columns], right, preferred_element_type=f32)]
    concatenate x13 -> x10, other arithmetic: 24.5 us -> 2.79 us  [the longest x2 1.69 us: shards(): jnp.concatenate(parts, 1)]
    ppermute x53 -> x51, starting transfers between devices: 36.9 us -> 50 us  [flip(): return lax.ppermute(block, axis, [(i, i ^ 1 << bit) for i in range(count)])]
    add x10 -> x2, other arithmetic: 12.5 us -> 2.57 us  [total(): return self.kept + self.got.astype(f32)]
    convert_element_type x6 -> x13, other arithmetic: 8.14 us -> 17.8 us  [the longest x8 9.97 us: halve(): sent = (kept[half:] + got[half:].astype(f32)).astype(bf16)]
    concatenate x6 -> x1, local copies, waits for them, and re-layouts: 9.08 us -> 0.72 us  [shards(): qkv_full = jnp.concatenate(qkv_pieces, 0)]
  transfers between devices with their start and end apart: 61 -> 57, of which waited for: 24 -> 19; matrix products, arithmetic and copies ran while one was open for 23% -> 15% of each run, Pallas kernels for 10% -> 37%
where the time goes in v3:
time: 449 us; the launch traced here: 442 us
  Pallas kernels  163 us (36%)
  waiting for transfers between devices  139 us (31%)
  starting transfers between devices  59.7 us (13%)
  other arithmetic  34.2 us (8%)
  local copies, waits for them, and re-layouts  27.5 us (6%)
  matrix products  17.2 us (4%)
    ppermute x51, waiting for transfers between devices, flip(): return lax.ppermute(block, axis, [(i, i ^ 1 << bit) for i in range(count)])  137 us
    pallas_call x4, Pallas kernels, mlp(): pl.pallas_call(functools.partial(mlp_kernel, count=len(pieces), add=add),...  68.4 us
    ppermute x51, starting transfers between devices, flip(): return lax.ppermute(block, axis, [(i, i ^ 1 << bit) for i in range(count)])  50 us
    pallas_call x4, Pallas kernels, outer(): pl.pallas_call(functools.partial(outer_kernel, groups=groups, blocks=bloc...  39.8 us
    pallas_call x1, Pallas kernels, attend_back(): pl.pallas_call(functools.partial(attend_back_kernel, block=block, count=l...  30.9 us
    pallas_call x1, Pallas kernels, attend(): pl.pallas_call(functools.partial(attend_kernel, block=block, count=len(pi...  20 us
    unnamed x114, local copies, waits for them, and re-layouts  16.6 us
    convert_element_type x8, other arithmetic, halve(): sent = (kept[half:] + got[half:].astype(f32)).astype(bf16)  9.97 us
  transfers between devices with their start and end apart: 57, of which 19 were waited for; matrix products, arithmetic and copies ran while one was open for 15% of the time, Pallas kernels for 37%

profile of v3, /device:TPU:0, one launch (start us, length us, event | category | flops | bytes accessed | tf_op | source)
XLA Modules:
  0.0 442.1 jit_solution(8195071543479972456)
XLA Ops:
  3.4 3.0 collective-permute-start.2
  9.2 2.5 fusion.9
  13.3 1.4 collective-permute-start
  14.8 2.8 bitcast_convert_fusion
  18.4 2.6 collective-permute-start.3
  21.3 6.8 %collective-permute-done.3.rest_1_ = bf16[112,576]{1,0:T(8,128)(2,1)S(1)} collective-permute-done((bf16[112,576]{1,0:T(8,128)(2,1)S(1)}, bf16[112,576]{1,0:T(8,128)(2,1)S(1)}, u32[]{:S(2)}, u32[]{:S(2)}) %collective-permute-start.3) | collective-permute-done | bytes 129056 | tf_op jit(solution)/shard_map/ppermute | solution.py:23
  28.1 4.1 collective-permute-start.4
  32.2 2.0 fusion.59
  34.2 1.6 collective-permute-start.5
  36.3 3.9 collective-permute-done.4.rest_2_
  40.1 1.5 collective-permute-start.7
  43.8 1.6 slice.449
  45.3 1.6 slice.450
  49.7 1.5 collective-permute-start.11
  51.7 20.0 %shard_map.186 = (bf16[1024,512]{1,0:T(8,128)(2,1)S(1)}, bf16[1024,64]{1,0:T(8,128)(2,1)S(1)}, bf16[1024,512]{1,0:T(8,128)(2,1)S(1)}, f32[8,1024]{1,0:T(8,128)S(1)}) custom-call(s32[1]{0:T(128)} %bitcast.1.parity_ref, bf16[512,896]{1,0:T(8,128)(2,1)S(1)} %fusion.11.own_ref.refs_0_, bf16[512,896]{1,0:T(8,128)(2,1)} %collective-permute-done.other_ref.refs_1_, ...), custom_call_target="tpu_custom_call" | custom-call | flops 12000000000 | bytes 8000000 | tf_op jit(solution)/shard_map/pallas_call | solution.py:157
  71.9 3.5 shard_map.187
  76.3 2.5 collective-permute-start.20
  78.8 1.6 collective-permute-start.22
  80.4 14.7 %collective-permute-done.20.rest_1_ = bf16[112,1536]{1,0:T(8,128)(2,1)S(1)} collective-permute-done((bf16[112,1536]{1,0:T(8,128)(2,1)S(1)}, bf16[112,1536]{1,0:T(8,128)(2,1)S(1)}, u32[]{:S(2)}, u32[]{:S(2)}) %collective-permute-start.20) | collective-permute-done | bytes 344096 | tf_op jit(solution)/shard_map/ppermute | solution.py:23
  95.2 3.3 collective-permute-start.21
  99.2 21.3 %collective-permute-done.25.rest_1_ = bf16[112,2304]{1,0:T(8,128)(2,1)S(1)} collective-permute-done((bf16[112,2304]{1,0:T(8,128)(2,1)S(1)}, bf16[112,2304]{1,0:T(8,128)(2,1)S(1)}, u32[]{:S(2)}, u32[]{:S(2)}) %collective-permute-start.25) | collective-permute-done | bytes 516128 | tf_op jit(solution)/shard_map/ppermute | solution.py:23
  122.5 1.5 collective-permute-start.23
  124.8 1.6 collective-permute-start.24
  126.4 7.1 %collective-permute-done.23.rest_4_ = bf16[112,1536]{1,0:T(8,128)(2,1)S(1)} collective-permute-done((bf16[112,1536]{1,0:T(8,128)(2,1)S(1)}, bf16[112,1536]{1,0:T(8,128)(2,1)S(1)}, u32[]{:S(2)}, u32[]{:S(2)}) %collective-permute-start.23) | collective-permute-done | bytes 344096 | tf_op jit(solution)/shard_map/ppermute | solution.py:23
  133.4 9.4 %collective-permute-done.14.x0_ref.refs_2_ = bf16[512,896]{1,0:T(8,128)(2,1)} collective-permute-done((bf16[512,896]{1,0:T(8,128)(2,1)S(1)}, bf16[512,896]{1,0:T(8,128)(2,1)}, u32[]{:S(2)}, u32[]{:S(2)}) %collective-permute-start.14) | collective-permute-done | bytes 917536 | tf_op jit(solution)/shard_map/ppermute | solution.py:23
  142.8 4.9 %collective-permute-done.24.rest_5_ = bf16[224,1536]{1,0:T(8,128)(2,1)S(1)} collective-permute-done((bf16[224,1536]{1,0:T(8,128)(2,1)S(1)}, bf16[224,1536]{1,0:T(8,128)(2,1)S(1)}, u32[]{:S(2)}, u32[]{:S(2)}) %collective-permute-start.24) | collective-permute-done | bytes 688160 | tf_op jit(solution)/shard_map/ppermute | solution.py:23
  147.8 1.5 collective-permute-start.27
  150.8 1.5 collective-permute-start.29
  152.2 14.4 %shard_map.188 = (bf16[1024,1536]{1,0:T(8,128)(2,1)}, bf16[2,512,896]{2,1,0:T(8,128)(2,1)}, bf16[2,512,896]{2,1,0:T(8,128)(2,1)}) custom-call(bf16[512,896]{1,0:T(8,128)(2,1)} %copy-done.29, bf16[512,896]{1,0:T(8,128)(2,1)} %copy-done.46, bf16[512,896]{1,0:T(8,128)(2,1)} %get-tuple-element.155.g0_ref.refs_4_, bf16[512,896]{1,0:T(8,128)(2,1)} %copy-done.45, ...), custom_call_target="tpu_custom_call" | custom-call | flops 5637144576 | bytes 31457280 | tf_op jit(solution)/shard_map/pallas_call | solution.py:406
  166.7 13.9 %shard_map.189 = (bf16[1024,1536]{1,0:T(8,128)(2,1)}, bf16[2,512,896]{2,1,0:T(8,128)(2,1)}, bf16[2,512,896]{2,1,0:T(8,128)(2,1)}) custom-call(bf16[512,896]{1,0:T(8,128)(2,1)} %collective-permute-done.14.x0_ref.refs_2_, bf16[512,896]{1,0:T(8,128)(2,1)} %collective-permute-done.16.x1_ref.refs_3_, bf16[512,896]{1,0:T(8,128)(2,1)} %collective-permute-done.18.g0_ref.refs_6_, ...), custom_call_target="tpu_custom_call" | custom-call | flops 5637144576 | bytes 31457280 | tf_op jit(solution)/shard_map/pallas_call | solution.py:406
  180.6 14.4 %shard_map.190 = (bf16[448,1536]{1,0:T(8,128)(2,1)}, f32[448,1536]{1,0:T(8,128)}) custom-call(bf16[512,896]{1,0:T(8,128)(2,1)} %copy-done.29, bf16[512,896]{1,0:T(8,128)(2,1)} %copy-done.46, bf16[512,896]{1,0:T(8,128)(2,1)} %collective-permute-done.14.x0_ref.refs_2_, bf16[512,896]{1,0:T(8,128)(2,1)} %collective-permute-done.16.x1_ref.refs_3_, ...), custom_call_target="tpu_custom_call" | custom-call | flops 5637144576 | bytes 20971520 | tf_op jit(solution)/shard_map/pallas_call | solution.py:464
  196.5 20.1 %shard_map.191 = (bf16[1024,2304]{1,0:T(8,128)(2,1)}, bf16[2,512,896]{2,1,0:T(8,128)(2,1)}, bf16[2,512,896]{2,1,0:T(8,128)(2,1)}) custom-call(bf16[512,896]{1,0:T(8,128)(2,1)} %collective-permute-done.14.x0_ref.refs_2_, bf16[512,896]{1,0:T(8,128)(2,1)} %collective-permute-done.16.x1_ref.refs_3_, bf16[512,896]{1,0:T(8,128)(2,1)} %collective-permute-done.18.g0_ref.refs_6_, ...), custom_call_target="tpu_custom_call" | custom-call | flops 8455716864 | bytes 31457280 | tf_op jit(solution)/shard_map/pallas_call | solution.py:406
  220.2 6.0 %collective-permute-done.51 = bf16[448,1536]{1,0:T(8,128)(2,1)} collective-permute-done((bf16[448,1536]{1,0:T(8,128)(2,1)}, bf16[448,1536]{1,0:T(8,128)(2,1)}, u32[]{:S(2)}, u32[]{:S(2)}) %collective-permute-start.51) | collective-permute-done | bytes 1376288 | tf_op jit(solution)/shard_map/ppermute | solution.py:23
  226.2 2.5 add_convert_fusion.2
  228.7 1.4 collective-permute-start.52
  230.2 2.0 add_convert_fusion
  234.5 19.9 %shard_map.192 = (bf16[1024,2304]{1,0:T(8,128)(2,1)}, bf16[2,512,896]{2,1,0:T(8,128)(2,1)}, bf16[2,512,896]{2,1,0:T(8,128)(2,1)}) custom-call(bf16[512,896]{1,0:T(8,128)(2,1)} %copy-done.29, bf16[512,896]{1,0:T(8,128)(2,1)} %copy-done.46, bf16[512,896]{1,0:T(8,128)(2,1)} %get-tuple-element.155.g0_ref.refs_4_, bf16[512,896]{1,0:T(8,128)(2,1)} %copy-done.45, ...), custom_call_target="tpu_custom_call" | custom-call | flops 8455716864 | bytes 31457280 | tf_op jit(solution)/shard_map/pallas_call | solution.py:406
  255.5 15.7 %shard_map.196 = (bf16[448,2304]{1,0:T(8,128)(2,1)}, f32[448,2304]{1,0:T(8,128)}) custom-call(bf16[512,896]{1,0:T(8,128)(2,1)} %copy-done.29, bf16[512,896]{1,0:T(8,128)(2,1)} %copy-done.46, bf16[512,896]{1,0:T(8,128)(2,1)} %collective-permute-done.14.x0_ref.refs_2_, bf16[512,896]{1,0:T(8,128)(2,1)} %collective-permute-done.16.x1_ref.refs_3_, ...), custom_call_target="tpu_custom_call" | custom-call | flops 8455716864 | bytes 20971520 | tf_op jit(solution)/shard_map/pallas_call | solution.py:464
  271.8 1.8 collective-permute-done.53
  276.6 2.2 multiply_reduce_fusion
  279.4 4.6 %fusion.71 = (bf16[512,896]{1,0:T(8,128)(2,1)}, f32[512,896]{1,0:T(8,128)}) fusion(f32[512,896]{1,0:T(8,128)S(1)} %copy-done.16, f32[512]{0:T(512)S(1)} %fusion.68, bf16[512,896]{1,0:T(8,128)(2,1)} %copy-done.21, bf16[2,512,896]{2,1,0:T(8,128)(2,1)} %collective-permute-done.31, bf16[2,512,896]{2,1,0:T(8,128)(2,1)} %get-tuple-element.61, ...), kind=kLoop, calls=%fused_computation.179 | loop fusion | flops 5046272 | bytes 9182720 | tf_op jit(solution)/shard_map/convert_element_type | solution.py:705
  284.1 14.0 %collective-permute-done.33 = bf16[512,896]{1,0:T(8,128)(2,1)} collective-permute-done((bf16[512,896]{1,0:T(8,128)(2,1)}, bf16[512,896]{1,0:T(8,128)(2,1)}, u32[]{:S(2)}, u32[]{:S(2)}) %collective-permute-start.33) | collective-permute-done | bytes 917536 | tf_op jit(solution)/shard_map/ppermute | solution.py:23
  298.1 4.0 fusion.24
  302.1 16.8 %collective-permute-done.54 = bf16[448,2304]{1,0:T(8,128)(2,1)} collective-permute-done((bf16[448,2304]{1,0:T(8,128)(2,1)}, bf16[448,2304]{1,0:T(8,128)(2,1)}, u32[]{:S(2)}, u32[]{:S(2)}) %collective-permute-start.54) | collective-permute-done | bytes 2064416 | tf_op jit(solution)/shard_map/ppermute | solution.py:23
  318.9 2.9 add_convert_fusion.1
  323.6 4.5 %shard_map.195 = (bf16[448,512]{1,0:T(8,128)(2,1)}, f32[448,512]{1,0:T(8,128)}) custom-call(bf16[512,896]{1,0:T(8,128)(2,1)} %get-tuple-element.94.own_ref.refs_0_, bf16[512,896]{1,0:T(8,128)(2,1)} %copy-done.3, bf16[1024,512]{1,0:T(8,128)(2,1)} %copy-done.11), custom_call_target="tpu_custom_call" | custom-call | flops 939524096 | bytes 20971520 | tf_op jit(solution)/shard_map/pallas_call | solution.py:464
  329.8 30.9 %shard_map.193 = (bf16[1024,576]{1,0:T(8,128)(2,1)}, f32[1,576]{1,0:T(1,128)S(1)}) custom-call(s32[1]{0:T(128)} %bitcast.1.parity_ref, bf16[512,896]{1,0:T(8,128)(2,1)} %get-tuple-element.94.own_ref.refs_0_, bf16[512,896]{1,0:T(8,128)(2,1)S(1)} %copy-done.4, bf16[1024,512]{1,0:T(8,128)(2,1)} %copy-done.12, bf16[1024,64]{1,0:T(8,128)(2,1)S(1)} %copy-done.14, ...), custom_call_target="tpu_custom_call" | custom-call | flops 24999999488 | bytes 8000000 | tf_op jit(solution)/shard_map/pallas_call | solution.py:326
  360.7 5.3 %shard_map.194 = (bf16[448,576]{1,0:T(8,128)(2,1)}, f32[448,576]{1,0:T(8,128)}) custom-call(bf16[512,896]{1,0:T(8,128)(2,1)} %copy-done.2, bf16[512,896]{1,0:T(8,128)(2,1)} %collective-permute-done.other_ref.refs_1_, bf16[1024,576]{1,0:T(8,128)(2,1)} %get-tuple-element.67.refs_2_), custom_call_target="tpu_custom_call" | custom-call | flops 1056964608 | bytes 20971520 | tf_op jit(solution)/shard_map/pallas_call | solution.py:464
  366.0 1.5 collective-permute-start.41
  367.5 1.7 fusion.82
  369.2 1.9 copy-done.22
  372.6 1.5 add_convert_fusion.4
  376.6 2.0 collective-permute-start.56
  378.6 6.8 %collective-permute-done.47 = bf16[224,512]{1,0:T(8,128)(2,1)S(1)} collective-permute-done((bf16[224,512]{1,0:T(8,128)(2,1)S(1)}, bf16[224,512]{1,0:T(8,128)(2,1)S(1)}, u32[]{:S(2)}, u32[]{:S(2)}) %collective-permute-start.47) | collective-permute-done | bytes 229408 | tf_op jit(solution)/shard_map/ppermute | solution.py:23
  387.9 2.5 collective-permute-start.42
  390.5 17.0 %collective-permute-done.48 = bf16[112,512]{1,0:T(8,128)(2,1)S(1)} collective-permute-done((bf16[112,512]{1,0:T(8,128)(2,1)S(1)}, bf16[112,512]{1,0:T(8,128)(2,1)S(1)}, u32[]{:S(2)}, u32[]{:S(2)}) %collective-permute-start.48) | collective-permute-done | bytes 114720 | tf_op jit(solution)/shard_map/ppermute | solution.py:23
  408.3 2.4 collective-permute-start.50
  411.5 1.9 collective-permute-done.50
  418.8 1.9 fusion.17
  424.3 2.3 collective-permute-start.45
  427.3 3.1 collective-permute-done.38
  431.1 4.9 %fusion.25 = bf16[512,896]{1,0:T(8,128)(2,1)} fusion(s32[896]{0:T(1024)S(1)} %fusion.63, f32[896,512]{0,1:T(8,128)S(1)} %copy-done.19, f32[512,896]{1,0:T(8,128)} %get-tuple-element.95, f32[512]{0:T(512)S(1)} %fusion.70, f32[896]{0:T(1024)S(1)} %fusion.26, f32[512]{0:T(512)S(1)} %add_rsqrt_fusion.1, f32[1024,896]{1,0:T(8,128)} %copy-done.22, ...), kind=kOutput, calls=%fused_computation.47 | convolution fusion | flops 827015168 | bytes 7351296 | tf_op jit(solution)/shard_map/ts,fs->tf/dot_general | solution.py:631
  436.0 1.9 collective-permute-start.40
  438.7 1.9 collective-permute-done.40
  (291 shorter events, 56.4 us)
Async XLA Ops:
  3.4 14.1 %collective-permute-start.2 = (bf16[128,512]{1,0:T(8,128)(2,1)S(1)}, bf16[128,512]{1,0:T(8,128)(2,1)S(1)}, u32[]{:S(2)}, u32[]{:S(2)}) collective-permute-start(bf16[128,512]{1,0:T(8,128)(2,1)S(1)} %fusion.60), channel_id=1, source_target_pairs={{0,2},{1,0},{2,3},{3,1},{4,6},{5,4},{6,7},{7,5},{8,10},{9,8},{10,1... | collective-permute-start | bytes 393224 | tf_op jit(solution)/shard_map/ppermute | solution.py:541
  6.4 11.1 %collective-permute-start.1 = (bf16[128,512]{1,0:T(8,128)(2,1)S(1)}, bf16[128,512]{1,0:T(8,128)(2,1)S(1)}, u32[]{:S(2)}, u32[]{:S(2)}) collective-permute-start(bf16[128,512]{1,0:T(8,128)(2,1)S(1)} %fusion.60), channel_id=1, source_target_pairs={{0,0},{1,2},{2,1},{3,3},{4,4},{5,6},{6,5},{7,7},{8,8},{9,10},{10,9... | collective-permute-start | bytes 393224 | tf_op jit(solution)/shard_map/ppermute | solution.py:541
  13.3 38.4 %copy-start.2 = (bf16[512,896]{1,0:T(8,128)(2,1)}, bf16[512,896]{1,0:T(8,128)(2,1)S(1)}, u32[]{:S(2)}) copy-start(bf16[512,896]{1,0:T(8,128)(2,1)S(1)} %fusion.11.own_ref.refs_0_) | copy-start | bytes 2752516
  13.3 37.9 %collective-permute-start = (bf16[512,896]{1,0:T(8,128)(2,1)S(1)}, bf16[512,896]{1,0:T(8,128)(2,1)}, u32[]{:S(2)}, u32[]{:S(2)}) collective-permute-start(bf16[512,896]{1,0:T(8,128)(2,1)S(1)} %fusion.11.own_ref.refs_0_), channel_id=1, source_target_pairs={{0,1},{1,0},{2,3},{3,2},{4,5},{5,4},{6,7},{7,6},{8,9},{9,8},{10,11... | collective-permute-start | bytes 2752520 | tf_op jit(solution)/shard_map/ppermute | solution.py:23
  18.4 9.7 %collective-permute-start.3 = (bf16[112,576]{1,0:T(8,128)(2,1)S(1)}, bf16[112,576]{1,0:T(8,128)(2,1)S(1)}, u32[]{:S(2)}, u32[]{:S(2)}) collective-permute-start(bf16[112,576]{1,0:T(8,128)(2,1)S(1)} %get-tuple-element.93.rest_0_), channel_id=1, source_target_pairs={{0,16},{4,20},{8,24},{12,28},{16,0},{20,4},{24,8},{28,12},{1,17},{... | collective-permute-start | bytes 387080 | tf_op jit(solution)/shard_map/ppermute | solution.py:23
  28.1 13.6 %collective-permute-start.8 = (bf16[112,512]{1,0:T(8,128)(2,1)S(1)}, bf16[112,512]{1,0:T(8,128)(2,1)S(1)}, u32[]{:S(2)}, u32[]{:S(2)}) collective-permute-start(bf16[112,512]{1,0:T(8,128)(2,1)S(1)} %fusion.62.rest_0_), channel_id=1, source_target_pairs={{0,16},{4,20},{8,24},{12,28},{16,0},{20,4},{24,8},{28,12},{1,17},{... | collective-permute-start | bytes 344072 | tf_op jit(solution)/shard_map/ppermute | solution.py:23
  28.1 12.1 %collective-permute-start.4 = (bf16[224,576]{1,0:T(8,128)(2,1)S(1)}, bf16[224,576]{1,0:T(8,128)(2,1)S(1)}, u32[]{:S(2)}, u32[]{:S(2)}) collective-permute-start(bf16[224,576]{1,0:T(8,128)(2,1)S(1)} %pad_maximum_fusion.7), channel_id=1, source_target_pairs={{0,8},{4,12},{8,0},{12,4},{16,24},{20,28},{24,16},{28,20},{1,9},{5... | collective-permute-start | bytes 774152 | tf_op jit(solution)/shard_map/ppermute | solution.py:23
  34.2 13.5 %collective-permute-start.5 = (bf16[112,576]{1,0:T(8,128)(2,1)S(1)}, bf16[112,576]{1,0:T(8,128)(2,1)S(1)}, u32[]{:S(2)}, u32[]{:S(2)}) collective-permute-start(bf16[112,576]{1,0:T(8,128)(2,1)S(1)} %get-tuple-element.93.rest_0_), channel_id=1, source_target_pairs={{0,4},{4,0},{8,12},{12,8},{16,20},{20,16},{24,28},{28,24},{1,5},{5... | collective-permute-start | bytes 387080 | tf_op jit(solution)/shard_map/ppermute | solution.py:23
  35.7 13.0 %collective-permute-start.6 = (bf16[112,576]{1,0:T(8,128)(2,1)S(1)}, bf16[112,576]{1,0:T(8,128)(2,1)S(1)}, u32[]{:S(2)}, u32[]{:S(2)}) collective-permute-start(bf16[112,576]{1,0:T(8,128)(2,1)S(1)} %collective-permute-done.3.rest_1_), channel_id=1, source_target_pairs={{0,4},{4,0},{8,12},{12,8},{16,20},{20,16},{24,28},{28,24},{1,5},{5... | collective-permute-start | bytes 387080 | tf_op jit(solution)/shard_map/ppermute | solution.py:23
  40.1 9.5 %collective-permute-start.7 = (bf16[224,576]{1,0:T(8,128)(2,1)S(1)}, bf16[224,576]{1,0:T(8,128)(2,1)S(1)}, u32[]{:S(2)}, u32[]{:S(2)}) collective-permute-start(bf16[224,576]{1,0:T(8,128)(2,1)S(1)} %collective-permute-done.4.rest_2_), channel_id=1, source_target_pairs={{0,4},{4,0},{8,12},{12,8},{16,20},{20,16},{24,28},{28,24},{1,5},{5... | collective-permute-start | bytes 774152 | tf_op jit(solution)/shard_map/ppermute | solution.py:23
  42.3 6.8 %collective-permute-start.9 = (bf16[224,512]{1,0:T(8,128)(2,1)}, bf16[224,512]{1,0:T(8,128)(2,1)}, u32[]{:S(2)}, u32[]{:S(2)}) collective-permute-start(bf16[224,512]{1,0:T(8,128)(2,1)} %pad_maximum_fusion.8), channel_id=1, source_target_pairs={{0,8},{4,12},{8,0},{12,4},{16,24},{20,28},{24,16},{28,20},{1,9},{5... | collective-permute-start | bytes 688136 | tf_op jit(solution)/shard_map/ppermute | solution.py:23
  47.7 74.7 %collective-permute-start.18 = (bf16[512,896]{1,0:T(8,128)(2,1)}, bf16[512,896]{1,0:T(8,128)(2,1)}, u32[]{:S(2)}, u32[]{:S(2)}) collective-permute-start(bf16[512,896]{1,0:T(8,128)(2,1)} %get-tuple-element.155.g0_ref.refs_4_), channel_id=1, source_target_pairs={{0,2},{1,3},{2,0},{3,1},{4,6},{5,7},{6,4},{7,5},{8,10},{9,11},{10,... | collective-permute-start | bytes 2752520 | tf_op jit(solution)/shard_map/ppermute | solution.py:23
  48.7 73.7 %collective-permute-start.17 = (bf16[512,896]{1,0:T(8,128)(2,1)}, bf16[512,896]{1,0:T(8,128)(2,1)S(1)}, u32[]{:S(2)}, u32[]{:S(2)}) collective-permute-start(bf16[512,896]{1,0:T(8,128)(2,1)} %get-tuple-element.155.g0_ref.refs_4_), channel_id=1, source_target_pairs={{0,1},{1,0},{2,3},{3,2},{4,5},{5,4},{6,7},{7,6},{8,9},{9,8},{10,11... | collective-permute-start | bytes 2752520 | tf_op jit(solution)/shard_map/ppermute | solution.py:23
  49.1 22.7 %collective-permute-start.10 = (bf16[112,512]{1,0:T(8,128)(2,1)S(1)}, bf16[112,512]{1,0:T(8,128)(2,1)S(1)}, u32[]{:S(2)}, u32[]{:S(2)}) collective-permute-start(bf16[112,512]{1,0:T(8,128)(2,1)S(1)} %fusion.62.rest_0_), channel_id=1, source_target_pairs={{0,4},{4,0},{8,12},{12,8},{16,20},{20,16},{24,28},{28,24},{1,5},{5... | collective-permute-start | bytes 344072 | tf_op jit(solution)/shard_map/ppermute | solution.py:23
  49.7 22.1 %collective-permute-start.11 = (bf16[112,512]{1,0:T(8,128)(2,1)S(1)}, bf16[112,512]{1,0:T(8,128)(2,1)S(1)}, u32[]{:S(2)}, u32[]{:S(2)}) collective-permute-start(bf16[112,512]{1,0:T(8,128)(2,1)S(1)} %collective-permute-done.8.rest_1_), channel_id=1, source_target_pairs={{0,4},{4,0},{8,12},{12,8},{16,20},{20,16},{24,28},{28,24},{1,5},{5... | collective-permute-start | bytes 344072 | tf_op jit(solution)/shard_map/ppermute | solution.py:23
  51.2 20.7 %collective-permute-start.12 = (bf16[224,512]{1,0:T(8,128)(2,1)}, bf16[224,512]{1,0:T(8,128)(2,1)S(1)}, u32[]{:S(2)}, u32[]{:S(2)}) collective-permute-start(bf16[224,512]{1,0:T(8,128)(2,1)} %collective-permute-done.9.rest_2_), channel_id=1, source_target_pairs={{0,4},{4,0},{8,12},{12,8},{16,20},{20,16},{24,28},{28,24},{1,5},{5... | collective-permute-start | bytes 688136 | tf_op jit(solution)/shard_map/ppermute | solution.py:23
  75.5 19.7 %collective-permute-start.13 = (bf16[512,896]{1,0:T(8,128)(2,1)S(1)}, bf16[512,896]{1,0:T(8,128)(2,1)S(1)}, u32[]{:S(2)}, u32[]{:S(2)}) collective-permute-start(bf16[512,896]{1,0:T(8,128)(2,1)S(1)} %get-tuple-element.47), channel_id=1, source_target_pairs={{0,1},{1,0},{2,3},{3,2},{4,5},{5,4},{6,7},{7,6},{8,9},{9,8},{10,11... | collective-permute-start | bytes 2752520 | tf_op jit(solution)/shard_map/ppermute | solution.py:23
  76.3 18.8 %collective-permute-start.20 = (bf16[112,1536]{1,0:T(8,128)(2,1)S(1)}, bf16[112,1536]{1,0:T(8,128)(2,1)S(1)}, u32[]{:S(2)}, u32[]{:S(2)}) collective-permute-start(bf16[112,1536]{1,0:T(8,128)(2,1)S(1)} %pad_maximum_fusion.6.rest_0_), channel_id=1, source_target_pairs={{0,16},{4,20},{8,24},{12,28},{16,0},{20,4},{24,8},{28,12},{1,17},{... | collective-permute-start | bytes 1032200 | tf_op jit(solution)/shard_map/ppermute | solution.py:23
  78.8 68.9 %copy-start.24 = (bf16[112,2304]{1,0:T(8,128)(2,1)}, bf16[112,2304]{1,0:T(8,128)(2,1)S(1)}, u32[]{:S(2)}) copy-start(bf16[112,2304]{1,0:T(8,128)(2,1)S(1)} %fusion.46.rest_0_) | copy-start | bytes 1548292
  78.8 42.9 %collective-permute-start.22 = (bf16[112,1536]{1,0:T(8,128)(2,1)S(1)}, bf16[112,1536]{1,0:T(8,128)(2,1)S(1)}, u32[]{:S(2)}, u32[]{:S(2)}) collective-permute-start(bf16[112,1536]{1,0:T(8,128)(2,1)S(1)} %pad_maximum_fusion.6.rest_0_), channel_id=1, source_target_pairs={{0,4},{4,0},{8,12},{12,8},{16,20},{20,16},{24,28},{28,24},{1,5},{5... | collective-permute-start | bytes 1032200 | tf_op jit(solution)/shard_map/ppermute | solution.py:23
  95.1 27.4 %copy-start.39 = (bf16[112,1536]{1,0:T(8,128)(2,1)}, bf16[112,1536]{1,0:T(8,128)(2,1)S(1)}, u32[]{:S(2)}) copy-start(bf16[112,1536]{1,0:T(8,128)(2,1)S(1)} %collective-permute-done.20.rest_1_) | copy-start | bytes 1032196
  95.1 25.4 %collective-permute-start.25 = (bf16[112,2304]{1,0:T(8,128)(2,1)S(1)}, bf16[112,2304]{1,0:T(8,128)(2,1)S(1)}, u32[]{:S(2)}, u32[]{:S(2)}) collective-permute-start(bf16[112,2304]{1,0:T(8,128)(2,1)S(1)} %fusion.46.rest_0_), channel_id=1, source_target_pairs={{0,16},{4,20},{8,24},{12,28},{16,0},{20,4},{24,8},{28,12},{1,17},{... | collective-permute-start | bytes 1548296 | tf_op jit(solution)/shard_map/ppermute | solution.py:23
  95.2 29.6 %collective-permute-start.21 = (bf16[224,1536]{1,0:T(8,128)(2,1)S(1)}, bf16[224,1536]{1,0:T(8,128)(2,1)S(1)}, u32[]{:S(2)}, u32[]{:S(2)}) collective-permute-start(bf16[224,1536]{1,0:T(8,128)(2,1)S(1)} %pad_maximum_fusion.1), channel_id=1, source_target_pairs={{0,8},{4,12},{8,0},{12,4},{16,24},{20,28},{24,16},{28,20},{1,9},{5... | collective-permute-start | bytes 2064392 | tf_op jit(solution)/shard_map/ppermute | solution.py:23
  99.2 53.0 %copy-start.29 = (bf16[512,896]{1,0:T(8,128)(2,1)}, bf16[512,896]{1,0:T(8,128)(2,1)S(1)}, u32[]{:S(2)}) copy-start(bf16[512,896]{1,0:T(8,128)(2,1)S(1)} %multiply_convert_fusion.x0_ref.refs_0_) | copy-start | bytes 2752516
  120.5 46.1 %copy-start.37 = (bf16[112,2304]{1,0:T(8,128)(2,1)}, bf16[112,2304]{1,0:T(8,128)(2,1)S(1)}, u32[]{:S(2)}) copy-start(bf16[112,2304]{1,0:T(8,128)(2,1)S(1)} %collective-permute-done.25.rest_1_) | copy-start | bytes 1548292
  120.5 22.3 %collective-permute-start.14 = (bf16[512,896]{1,0:T(8,128)(2,1)S(1)}, bf16[512,896]{1,0:T(8,128)(2,1)}, u32[]{:S(2)}, u32[]{:S(2)}) collective-permute-start(bf16[512,896]{1,0:T(8,128)(2,1)S(1)} %multiply_convert_fusion.x0_ref.refs_0_), channel_id=1, source_target_pairs={{0,2},{1,3},{2,0},{3,1},{4,6},{5,7},{6,4},{7,5},{8,10},{9,11},{10,... | collective-permute-start | bytes 2752520 | tf_op jit(solution)/shard_map/ppermute | solution.py:23
  121.7 27.5 %collective-permute-start.26 = (bf16[224,2304]{1,0:T(8,128)(2,1)S(1)}, bf16[224,2304]{1,0:T(8,128)(2,1)}, u32[]{:S(2)}, u32[]{:S(2)}) collective-permute-start(bf16[224,2304]{1,0:T(8,128)(2,1)S(1)} %pad_maximum_fusion), channel_id=1, source_target_pairs={{0,8},{4,12},{8,0},{12,4},{16,24},{20,28},{24,16},{28,20},{1,9},{5... | collective-permute-start | bytes 3096584 | tf_op jit(solution)/shard_map/ppermute | solution.py:23
  122.5 27.3 %collective-permute-start.15 = (bf16[512,896]{1,0:T(8,128)(2,1)S(1)}, bf16[512,896]{1,0:T(8,128)(2,1)S(1)}, u32[]{:S(2)}, u32[]{:S(2)}) collective-permute-start(bf16[512,896]{1,0:T(8,128)(2,1)S(1)} %multiply_convert_fusion.x0_ref.refs_0_), channel_id=1, source_target_pairs={{0,1},{1,0},{2,3},{3,2},{4,5},{5,4},{6,7},{7,6},{8,9},{9,8},{10,11... | collective-permute-start | bytes 2752520 | tf_op jit(solution)/shard_map/ppermute | solution.py:23
  122.5 27.3 %copy-start.45 = (bf16[512,896]{1,0:T(8,128)(2,1)}, bf16[512,896]{1,0:T(8,128)(2,1)S(1)}, u32[]{:S(2)}) copy-start(bf16[512,896]{1,0:T(8,128)(2,1)S(1)} %collective-permute-done.17.g1_ref.refs_5_) | copy-start | bytes 2752516
  122.5 10.9 %collective-permute-start.23 = (bf16[112,1536]{1,0:T(8,128)(2,1)S(1)}, bf16[112,1536]{1,0:T(8,128)(2,1)S(1)}, u32[]{:S(2)}, u32[]{:S(2)}) collective-permute-start(bf16[112,1536]{1,0:T(8,128)(2,1)S(1)} %collective-permute-done.20.rest_1_), channel_id=1, source_target_pairs={{0,4},{4,0},{8,12},{12,8},{16,20},{20,16},{24,28},{28,24},{1,5},{5... | collective-permute-start | bytes 1032200 | tf_op jit(solution)/shard_map/ppermute | solution.py:23
  124.8 25.0 %copy-start.47 = (bf16[224,1536]{1,0:T(8,128)(2,1)}, bf16[224,1536]{1,0:T(8,128)(2,1)S(1)}, u32[]{:S(2)}) copy-start(bf16[224,1536]{1,0:T(8,128)(2,1)S(1)} %collective-permute-done.21.rest_2_) | copy-start | bytes 2064388
  124.8 23.0 %collective-permute-start.24 = (bf16[224,1536]{1,0:T(8,128)(2,1)S(1)}, bf16[224,1536]{1,0:T(8,128)(2,1)S(1)}, u32[]{:S(2)}, u32[]{:S(2)}) collective-permute-start(bf16[224,1536]{1,0:T(8,128)(2,1)S(1)} %collective-permute-done.21.rest_2_), channel_id=1, source_target_pairs={{0,4},{4,0},{8,12},{12,8},{16,20},{20,16},{24,28},{28,24},{1,5},{5... | collective-permute-start | bytes 2064392 | tf_op jit(solution)/shard_map/ppermute | solution.py:23
  133.4 33.2 %collective-permute-start.19 = (bf16[512,896]{1,0:T(8,128)(2,1)}, bf16[512,896]{1,0:T(8,128)(2,1)}, u32[]{:S(2)}, u32[]{:S(2)}) collective-permute-start(bf16[512,896]{1,0:T(8,128)(2,1)} %collective-permute-done.18.g0_ref.refs_6_), channel_id=1, source_target_pairs={{0,1},{1,0},{2,3},{3,2},{4,5},{5,4},{6,7},{7,6},{8,9},{9,8},{10,11... | collective-permute-start | bytes 2752520 | tf_op jit(solution)/shard_map/ppermute | solution.py:23
  142.8 23.8 %collective-permute-start.16 = (bf16[512,896]{1,0:T(8,128)(2,1)}, bf16[512,896]{1,0:T(8,128)(2,1)}, u32[]{:S(2)}, u32[]{:S(2)}) collective-permute-start(bf16[512,896]{1,0:T(8,128)(2,1)} %collective-permute-done.14.x0_ref.refs_2_), channel_id=1, source_target_pairs={{0,1},{1,0},{2,3},{3,2},{4,5},{5,4},{6,7},{7,6},{8,9},{9,8},{10,11... | collective-permute-start | bytes 2752520 | tf_op jit(solution)/shard_map/ppermute | solution.py:23
  147.8 47.8 %collective-permute-start.27 = (bf16[112,2304]{1,0:T(8,128)(2,1)S(1)}, bf16[112,2304]{1,0:T(8,128)(2,1)}, u32[]{:S(2)}, u32[]{:S(2)}) collective-permute-start(bf16[112,2304]{1,0:T(8,128)(2,1)S(1)} %fusion.46.rest_0_), channel_id=1, source_target_pairs={{0,4},{4,0},{8,12},{12,8},{16,20},{20,16},{24,28},{28,24},{1,5},{5... | collective-permute-start | bytes 1548296 | tf_op jit(solution)/shard_map/ppermute | solution.py:23
  149.2 46.3 %collective-permute-start.28 = (bf16[112,2304]{1,0:T(8,128)(2,1)S(1)}, bf16[112,2304]{1,0:T(8,128)(2,1)}, u32[]{:S(2)}, u32[]{:S(2)}) collective-permute-start(bf16[112,2304]{1,0:T(8,128)(2,1)S(1)} %collective-permute-done.25.rest_1_), channel_id=1, source_target_pairs={{0,4},{4,0},{8,12},{12,8},{16,20},{20,16},{24,28},{28,24},{1,5},{5... | collective-permute-start | bytes 1548296 | tf_op jit(solution)/shard_map/ppermute | solution.py:23
  150.8 44.8 %collective-permute-start.29 = (bf16[224,2304]{1,0:T(8,128)(2,1)}, bf16[224,2304]{1,0:T(8,128)(2,1)S(1)}, u32[]{:S(2)}, u32[]{:S(2)}) collective-permute-start(bf16[224,2304]{1,0:T(8,128)(2,1)} %collective-permute-done.26.rest_2_), channel_id=1, source_target_pairs={{0,4},{4,0},{8,12},{12,8},{16,20},{20,16},{24,28},{28,24},{1,5},{5... | collective-permute-start | bytes 3096584 | tf_op jit(solution)/shard_map/ppermute | solution.py:23
  195.0 31.3 %collective-permute-start.51 = (bf16[448,1536]{1,0:T(8,128)(2,1)}, bf16[448,1536]{1,0:T(8,128)(2,1)}, u32[]{:S(2)}, u32[]{:S(2)}) collective-permute-start(bf16[448,1536]{1,0:T(8,128)(2,1)} %get-tuple-element.73), channel_id=1, source_target_pairs={{0,4},{4,0},{8,12},{12,8},{16,20},{20,16},{24,28},{28,24},{1,5},{5... | collective-permute-start | bytes 4128776 | tf_op jit(solution)/shard_map/ppermute | solution.py:23
  216.6 13.5 %collective-permute-start.30 = (bf16[2,512,896]{2,1,0:T(8,128)(2,1)}, bf16[2,512,896]{2,1,0:T(8,128)(2,1)}, u32[]{:S(2)}, u32[]{:S(2)}) collective-permute-start(bf16[2,512,896]{2,1,0:T(8,128)(2,1)} %get-tuple-element.57), channel_id=1, source_target_pairs={{0,1},{1,0},{2,3},{3,2},{4,5},{5,4},{6,7},{7,6},{8,9},{9,8},{10,11... | collective-permute-start | bytes 5505032 | tf_op jit(solution)/shard_map/ppermute | solution.py:23
  228.7 25.9 %collective-permute-start.52 = (bf16[224,1536]{1,0:T(8,128)(2,1)S(1)}, bf16[224,1536]{1,0:T(8,128)(2,1)S(1)}, u32[]{:S(2)}, u32[]{:S(2)}) collective-permute-start(bf16[224,1536]{1,0:T(8,128)(2,1)S(1)} %get-tuple-element.100), channel_id=1, source_target_pairs={{0,8},{4,12},{8,0},{12,4},{16,24},{20,28},{24,16},{28,20},{1,9},{5... | collective-permute-start | bytes 2064392 | tf_op jit(solution)/shard_map/ppermute | solution.py:23
  233.5 42.1 %collective-permute-start.32 = (bf16[512,896]{1,0:T(8,128)(2,1)}, bf16[512,896]{1,0:T(8,128)(2,1)S(1)}, u32[]{:S(2)}, u32[]{:S(2)}) collective-permute-start(bf16[512,896]{1,0:T(8,128)(2,1)} %get-tuple-element.102), channel_id=1, source_target_pairs={{0,2},{1,3},{2,0},{3,1},{4,6},{5,7},{6,4},{7,5},{8,10},{9,11},{10,... | collective-permute-start | bytes 2752520 | tf_op jit(solution)/shard_map/ppermute | solution.py:23
  254.5 22.1 %collective-permute-start.31 = (bf16[2,512,896]{2,1,0:T(8,128)(2,1)}, bf16[2,512,896]{2,1,0:T(8,128)(2,1)}, u32[]{:S(2)}, u32[]{:S(2)}) collective-permute-start(bf16[2,512,896]{2,1,0:T(8,128)(2,1)} %get-tuple-element.62), channel_id=1, source_target_pairs={{0,1},{1,0},{2,3},{3,2},{4,5},{5,4},{6,7},{7,6},{8,9},{9,8},{10,11... | collective-permute-start | bytes 5505032 | tf_op jit(solution)/shard_map/ppermute | solution.py:23
  254.7 18.9 %collective-permute-start.53 = (bf16[112,1536]{1,0:T(8,128)(2,1)S(1)}, bf16[112,1536]{1,0:T(8,128)(2,1)}, u32[]{:S(2)}, u32[]{:S(2)}) collective-permute-start(bf16[112,1536]{1,0:T(8,128)(2,1)S(1)} %fusion.41), channel_id=1, source_target_pairs={{0,16},{4,20},{8,24},{12,28},{16,0},{20,4},{24,8},{28,12},{1,17},{... | collective-permute-start | bytes 1032200 | tf_op jit(solution)/shard_map/ppermute | solution.py:23
  271.2 47.7 %collective-permute-start.54 = (bf16[448,2304]{1,0:T(8,128)(2,1)}, bf16[448,2304]{1,0:T(8,128)(2,1)}, u32[]{:S(2)}, u32[]{:S(2)}) collective-permute-start(bf16[448,2304]{1,0:T(8,128)(2,1)} %get-tuple-element.77), channel_id=1, source_target_pairs={{0,4},{4,0},{8,12},{12,8},{16,20},{20,16},{24,28},{28,24},{1,5},{5... | collective-permute-start | bytes 6193160 | tf_op jit(solution)/shard_map/ppermute | solution.py:23
  275.6 22.5 %collective-permute-start.33 = (bf16[512,896]{1,0:T(8,128)(2,1)}, bf16[512,896]{1,0:T(8,128)(2,1)}, u32[]{:S(2)}, u32[]{:S(2)}) collective-permute-start(bf16[512,896]{1,0:T(8,128)(2,1)} %get-tuple-element.63), channel_id=1, source_target_pairs={{0,2},{1,3},{2,0},{3,1},{4,6},{5,7},{6,4},{7,5},{8,10},{9,11},{10,... | collective-permute-start | bytes 2752520 | tf_op jit(solution)/shard_map/ppermute | solution.py:23
  284.1 38.6 %collective-permute-start.34 = (bf16[512,896]{1,0:T(8,128)(2,1)}, bf16[512,896]{1,0:T(8,128)(2,1)S(1)}, u32[]{:S(2)}, u32[]{:S(2)}) collective-permute-start(bf16[512,896]{1,0:T(8,128)(2,1)} %get-tuple-element.94.own_ref.refs_0_), channel_id=1, source_target_pairs={{0,1},{1,0},{2,3},{3,2},{4,5},{5,4},{6,7},{7,6},{8,9},{9,8},{10,11... | collective-permute-start | bytes 2752520 | tf_op jit(solution)/shard_map/ppermute | solution.py:23
  321.8 53.7 %collective-permute-start.55 = (bf16[224,2304]{1,0:T(8,128)(2,1)}, bf16[224,2304]{1,0:T(8,128)(2,1)}, u32[]{:S(2)}, u32[]{:S(2)}) collective-permute-start(bf16[224,2304]{1,0:T(8,128)(2,1)} %get-tuple-element.98), channel_id=1, source_target_pairs={{0,8},{4,12},{8,0},{12,4},{16,24},{20,28},{24,16},{28,20},{1,9},{5... | collective-permute-start | bytes 3096584 | tf_op jit(solution)/shard_map/ppermute | solution.py:23
  328.1 44.5 %collective-permute-start.46 = (bf16[448,512]{1,0:T(8,128)(2,1)}, bf16[448,512]{1,0:T(8,128)(2,1)}, u32[]{:S(2)}, u32[]{:S(2)}) collective-permute-start(bf16[448,512]{1,0:T(8,128)(2,1)} %get-tuple-element.72), channel_id=1, source_target_pairs={{0,4},{4,0},{8,12},{12,8},{16,20},{20,16},{24,28},{28,24},{1,5},{5... | collective-permute-start | bytes 1376264 | tf_op jit(solution)/shard_map/ppermute | solution.py:23
  366.0 20.0 %collective-permute-start.41 = (bf16[448,576]{1,0:T(8,128)(2,1)}, bf16[448,576]{1,0:T(8,128)(2,1)S(1)}, u32[]{:S(2)}, u32[]{:S(2)}) collective-permute-start(bf16[448,576]{1,0:T(8,128)(2,1)} %get-tuple-element.70), channel_id=1, source_target_pairs={{0,4},{4,0},{8,12},{12,8},{16,20},{20,16},{24,28},{28,24},{1,5},{5... | collective-permute-start | bytes 1548296 | tf_op jit(solution)/shard_map/ppermute | solution.py:23
  372.1 46.1 %collective-permute-start.35 = (bf16[512,896]{1,0:T(8,128)(2,1)}, bf16[512,896]{1,0:T(8,128)(2,1)}, u32[]{:S(2)}, u32[]{:S(2)}) collective-permute-start(bf16[512,896]{1,0:T(8,128)(2,1)} %slice.616), channel_id=1, source_target_pairs={{0,1},{1,0},{2,3},{3,2},{4,5},{5,4},{6,7},{7,6},{8,9},{9,8},{10,11... | collective-permute-start | bytes 2752520 | tf_op jit(solution)/shard_map/ppermute | solution.py:23
  374.1 11.2 %collective-permute-start.47 = (bf16[224,512]{1,0:T(8,128)(2,1)S(1)}, bf16[224,512]{1,0:T(8,128)(2,1)S(1)}, u32[]{:S(2)}, u32[]{:S(2)}) collective-permute-start(bf16[224,512]{1,0:T(8,128)(2,1)S(1)} %get-tuple-element.106), channel_id=1, source_target_pairs={{0,8},{4,12},{8,0},{12,4},{16,24},{20,28},{24,16},{28,20},{1,9},{5... | collective-permute-start | bytes 688136 | tf_op jit(solution)/shard_map/ppermute | solution.py:23
  376.6 37.5 %collective-permute-start.56 = (bf16[112,2304]{1,0:T(8,128)(2,1)S(1)}, bf16[112,2304]{1,0:T(8,128)(2,1)}, u32[]{:S(2)}, u32[]{:S(2)}) collective-permute-start(bf16[112,2304]{1,0:T(8,128)(2,1)S(1)} %fusion.28), channel_id=1, source_target_pairs={{0,16},{4,20},{8,24},{12,28},{16,0},{20,4},{24,8},{28,12},{1,17},{... | collective-permute-start | bytes 1548296 | tf_op jit(solution)/shard_map/ppermute | solution.py:23
  385.4 22.1 %collective-permute-start.48 = (bf16[112,512]{1,0:T(8,128)(2,1)S(1)}, bf16[112,512]{1,0:T(8,128)(2,1)S(1)}, u32[]{:S(2)}, u32[]{:S(2)}) collective-permute-start(bf16[112,512]{1,0:T(8,128)(2,1)S(1)} %fusion.54), channel_id=1, source_target_pairs={{0,16},{4,20},{8,24},{12,28},{16,0},{20,4},{24,8},{28,12},{1,17},{... | collective-permute-start | bytes 344072 | tf_op jit(solution)/shard_map/ppermute | solution.py:23
  387.9 22.8 %collective-permute-start.42 = (bf16[224,576]{1,0:T(8,128)(2,1)S(1)}, bf16[224,576]{1,0:T(8,128)(2,1)S(1)}, u32[]{:S(2)}, u32[]{:S(2)}) collective-permute-start(bf16[224,576]{1,0:T(8,128)(2,1)S(1)} %get-tuple-element.104), channel_id=1, source_target_pairs={{0,8},{4,12},{8,0},{12,4},{16,24},{20,28},{24,16},{28,20},{1,9},{5... | collective-permute-start | bytes 774152 | tf_op jit(solution)/shard_map/ppermute | solution.py:23
  407.6 3.8 collective-permute-start.49
  408.3 5.0 %collective-permute-start.50 = (bf16[112,224]{1,0:T(8,128)(2,1)S(1)}, bf16[112,224]{1,0:T(8,128)(2,1)S(1)}, u32[]{:S(2)}, u32[]{:S(2)}) collective-permute-start(bf16[112,224]{1,0:T(8,128)(2,1)S(1)} %get-tuple-element.119), channel_id=1, source_target_pairs={{0,1},{1,3},{2,0},{3,2},{4,5},{5,7},{6,4},{7,6},{8,9},{9,11},{10,8... | collective-permute-start | bytes 150536 | tf_op jit(solution)/shard_map/ppermute | solution.py:547
  411.4 9.8 %collective-permute-start.43 = (bf16[112,576]{1,0:T(8,128)(2,1)}, bf16[112,576]{1,0:T(8,128)(2,1)}, u32[]{:S(2)}, u32[]{:S(2)}) collective-permute-start(bf16[112,576]{1,0:T(8,128)(2,1)} %fusion.47), channel_id=1, source_target_pairs={{0,16},{4,20},{8,24},{12,28},{16,0},{20,4},{24,8},{28,12},{1,17},{... | collective-permute-start | bytes 387080 | tf_op jit(solution)/shard_map/ppermute | solution.py:23
  421.2 1.2 collective-permute-start.36
  422.4 4.2 collective-permute-start.37
  423.6 14.3 %collective-permute-start.44 = (bf16[112,288]{1,0:T(8,128)(2,1)S(1)}, bf16[112,288]{1,0:T(8,128)(2,1)S(1)}, u32[]{:S(2)}, u32[]{:S(2)}) collective-permute-start(bf16[112,288]{1,0:T(8,128)(2,1)S(1)} %get-tuple-element.116), channel_id=1, source_target_pairs={{0,0},{1,2},{2,1},{3,3},{4,4},{5,6},{6,5},{7,7},{8,8},{9,10},{10,9... | collective-permute-start | bytes 193544 | tf_op jit(solution)/shard_map/ppermute | solution.py:547
  424.3 13.6 %collective-permute-start.45 = (bf16[112,288]{1,0:T(8,128)(2,1)S(1)}, bf16[112,288]{1,0:T(8,128)(2,1)S(1)}, u32[]{:S(2)}, u32[]{:S(2)}) collective-permute-start(bf16[112,288]{1,0:T(8,128)(2,1)S(1)} %get-tuple-element.117), channel_id=1, source_target_pairs={{0,1},{1,3},{2,0},{3,2},{4,5},{5,7},{6,4},{7,6},{8,9},{9,11},{10,8... | collective-permute-start | bytes 193544 | tf_op jit(solution)/shard_map/ppermute | solution.py:547
  426.6 3.8 collective-permute-start.38
  430.4 5.6 %collective-permute-start.39 = (f32[23,128]{1,0:T(8,128)S(1)}, f32[23,128]{1,0:T(8,128)S(1)}, u32[]{:S(2)}, u32[]{:S(2)}) collective-permute-start(f32[23,128]{1,0:T(8,128)S(1)} %add.218), channel_id=1, source_target_pairs={{0,8},{4,12},{8,0},{12,4},{16,24},{20,28},{24,16},{28,20},{1,9},{5... | collective-permute-start | bytes 35336 | tf_op jit(solution)/shard_map/ppermute | solution.py:23
  436.0 4.7 %collective-permute-start.40 = (f32[23,128]{1,0:T(8,128)S(1)}, f32[23,128]{1,0:T(8,128)S(1)}, u32[]{:S(2)}, u32[]{:S(2)}) collective-permute-start(f32[23,128]{1,0:T(8,128)S(1)} %add.219), channel_id=1, source_target_pairs={{0,16},{4,20},{8,24},{12,28},{16,0},{20,4},{24,8},{28,12},{1,17},{... | collective-permute-start | bytes 35336 | tf_op jit(solution)/shard_map/ppermute | solution.py:23
  (49 other events, 321.5 us)

commit v4 on v3

--- a/solution.py
+++ b/solution.py
@@ -36,7 +36,9 @@
 
 
 def cost(flops, nbytes, exps=0):
-    return pl.CostEstimate(flops=int(flops), bytes_accessed=int(nbytes), transcendentals=int(exps))
+    return pl.CostEstimate(
+        flops=int(flops), bytes_accessed=int(nbytes), transcendentals=int(exps)
+    )
 
 
 def whole(array):
@@ -215,41 +217,60 @@
 
 
 def attend_back_kernel(
-    parity_ref, own_ref, other_ref, qk_ref, v_ref, lse_ref, cos_ref, sin_ref, *rest, block, count
+    parity_ref,
+    own_ref,
+    other_ref,
+    qk_ref,
+    v_ref,
+    lse_ref,
+    cos_ref,
+    sin_ref,
+    *rest,
+    block,
+    count,
+    first,
+    last,
 ):
     pieces = rest[:count]
-    mixed_ref, bias_ref, held, kpad, vpad, gatt, dq_acc, dk, dv, sems = rest[count:]
-    step = pl.program_id(0)
+    if first == 0:
+        mixed_ref, bias_ref, dk, dv, held, kpad, vpad, gatt, dq_acc, sems = rest[count:]
+    else:
+        dk_in, dv_in, mixed_ref, bias_ref, held, kpad, vpad, gatt, dq_acc, dk, dv, sems = rest[count:]
+    step = pl.program_id(0) + first
     half_rows = own_ref.shape[0]
     length = 2 * half_rows
     wide = qk_ref.shape[1]
     pairs = wide // 128
+    used = slice(first * 128, last * 128)
     parity = parity_ref[0]
     lane = lax.broadcasted_iota(jnp.int32, (1, 128), 1)
 
-    @pl.when(step == 0)
+    @pl.when(step == first)
     def _():
         assemble(pieces, held, sems)
         for side, rows_ref in enumerate((own_ref, other_ref)):
             for r in range(0, half_rows, block):
                 rows = pl.ds(pl.multiple_of((side ^ parity) * half_rows + r, block), block)
-                got = jnp.dot(rows_ref[r : r + block, :], held[...], preferred_element_type=f32)
+                got = jnp.dot(
+                    rows_ref[r : r + block, :], held[:, used], preferred_element_type=f32
+                )
                 gatt[rows, :] = got.astype(bf16)
         for r in range(0, length, block):
             rows = pl.ds(r, block)
-            last = qk_ref[rows, wide - 128 :].astype(f32)
-            pad_heads((kpad, vpad), rows, v_ref[rows, :].astype(f32), last)
-        dk[...] = jnp.zeros_like(dk)
-        dv[...] = jnp.zeros_like(dv)
+            keys = qk_ref[rows, wide - 128 :].astype(f32)
+            pad_heads((kpad, vpad), rows, v_ref[rows, :].astype(f32), keys)
+        dk[...] = dk_in[...] if first else jnp.zeros_like(dk)
+        dv[...] = dv_in[...] if first else jnp.zeros_like(dv)
 
     factor = HD**-0.5 * math.log2(math.e)
     cols = pl.ds(pl.multiple_of(step * 128, 128), 128)
+    here = pl.ds(pl.multiple_of((step - first) * 128, 128), 128)
     key_i = lax.broadcasted_iota(jnp.int32, (block, block), 0)
     query_i = lax.broadcasted_iota(jnp.int32, (block, block), 1)
     for r in range(0, length, block):
         rows = pl.ds(r, block)
         q = qk_ref[rows, cols]
-        g = gatt[rows, cols]
+        g = gatt[rows, here]
 
         def head(odd):
             lse = lse_ref[pl.ds(2 * step + odd, 1), rows]
@@ -295,18 +316,21 @@
 
         @pl.when(step < pairs - 1)
         def _():
-            mixed_ref[to, cols] = back(dq_acc[rows, :] * scale, rows).astype(bf16)
-
-        @pl.when(step == pairs - 1)
-        def _():
-            k = dk[rows, :]
-            k = jnp.where(lane >= HD, k + pltpu.roll(k, HD, 1), dq_acc[rows, :]) * scale
-            mixed_ref[to, wide - 128 : wide] = back(k, rows).astype(bf16)
-            v = dv[rows, :]
-            v = v + pltpu.roll(v, HD, 1)
-            mixed_ref[to, wide:] = v[:, :HD].astype(bf16)
-
-    @pl.when(step == pairs - 1)
+            mixed_ref[to, here] = back(dq_acc[rows, :] * scale, rows).astype(bf16)
+
+        if last == pairs:
+            end = (last - first) * 128
+
+            @pl.when(step == pairs - 1)
+            def _():
+                k = dk[rows, :]
+                k = jnp.where(lane >= HD, k + pltpu.roll(k, HD, 1), dq_acc[rows, :]) * scale
+                mixed_ref[to, end - 128 : end] = back(k, rows).astype(bf16)
+                v = dv[rows, :]
+                v = v + pltpu.roll(v, HD, 1)
+                mixed_ref[to, end:] = v[:, :HD].astype(bf16)
+
+    @pl.when(step == last - 1)
     def _():
         total = jnp.zeros((1, mixed_ref.shape[1]), f32)
         for r in range(0, length, block):
@@ -315,41 +339,47 @@
         bias_ref[...] = total
 
 
-def attend_back(parity, own, other, pieces, qk, v, lse, cos, sin):
+def attend_back(parity, own, other, pieces, qk, v, lse, cos, sin, first, last, earlier=()):
     half, depth = own.shape
     length = 2 * half
     wide = qk.shape[1]
-    group = wide + HD
     pairs = wide // 128
+    group = (last - first) * 128 + (HD if last == pairs else 0)
     block = min(256, half)
     ins = (own, other, qk, v, lse, cos, sin)
+    carried = pl.BlockSpec((length, 128), lambda p: (0, 0))
+    carry = [jax.ShapeDtypeStruct((length, 128), f32)] * 2
     return pl.pallas_call(
-        functools.partial(attend_back_kernel, block=block, count=len(pieces)),
-        grid=(pairs,),
+        functools.partial(
+            attend_back_kernel, block=block, count=len(pieces), first=first, last=last
+        ),
+        grid=(last - first,),
         in_specs=[pl.BlockSpec(memory_space=pltpu.SMEM)]
         + [whole(a) for a in ins]
-        + [in_place(piece) for piece in pieces],
+        + [in_place(piece) for piece in pieces]
+        + [carried] * len(earlier),
         out_specs=[
             pl.BlockSpec((length, group), lambda p: (0, 0)),
             pl.BlockSpec((1, group), lambda p: (0, 0)),
-        ],
+        ]
+        + ([] if first else [carried] * 2),
         out_shape=[
             jax.ShapeDtypeStruct((length, group), bf16),
             jax.ShapeDtypeStruct((1, group), f32),
-        ],
+        ]
+        + ([] if first else carry),
         scratch_shapes=[
             pltpu.VMEM((depth, wide), bf16),
             pltpu.VMEM((2, length, 128), bf16),
             pltpu.VMEM((2, length, 128), bf16),
-            pltpu.VMEM((length, wide), bf16),
+            pltpu.VMEM((length, (last - first) * 128), bf16),
             pltpu.VMEM((length, 128), f32),
-            pltpu.VMEM((length, 128), f32),
-            pltpu.VMEM((length, 128), f32),
-            pltpu.SemaphoreType.DMA((len(pieces),)),
-        ],
+        ]
+        + ([pltpu.VMEM((length, 128), f32)] * 2 if first else [])
+        + [pltpu.SemaphoreType.DMA((len(pieces),))],
         compiler_params=kernel_params(50),
-        cost_estimate=cost(25e9, 8e6, 5e6),
-    )(parity, *ins, *pieces)
+        cost_estimate=cost(12e9, 6e6, 3e6),
+    )(parity, *ins, *pieces, *earlier)
 
 
 def mlp_kernel(x0_ref, x1_ref, g0_ref, g1_ref, *rest, count, add):
@@ -422,58 +452,87 @@
     )(*ins, *pieces, *sums)
 
 
-def outer_kernel(*refs, groups, blocks):
-    rights = refs[groups * blocks : -2]
-    sent_ref, kept_ref = refs[-2:]
+def fill(sent_ref, kept_ref, lefts, rights, second):
     half = kept_ref.shape[0]
-    t = refs[0].shape[0]
-
-    def fill(lefts):
-        for part, ref in ((slice(half, 2 * half), sent_ref), (slice(0, half), kept_ref)):
-            total = 0.0
-            for i, left in enumerate(lefts):
-                right = rights[i * t // rights[0].shape[0]]
-                at = i * t % right.shape[0]
-                total = total + lax.dot_general(
-                    left[:, part], right[at : at + t, :], TN, preferred_element_type=f32
-                )
-            ref[...] = total.astype(ref.dtype)
-
+    t = lefts[0].shape[0]
+    q = half // 2
+    if second:
+        parts = ((sent_ref, 0, q), (sent_ref, q, 3 * q), (kept_ref, 0, 0), (kept_ref, q, 2 * q))
+        size = q
+    else:
+        parts = ((sent_ref, 0, half), (kept_ref, 0, 0))
+        size = half
+    for ref, to, start in parts:
+        total = 0.0
+        for i, left in enumerate(lefts):
+            right = rights[i * t // rights[0].shape[0]]
+            at = i * t % right.shape[0]
+            total = total + lax.dot_general(
+                left[:, start : start + size],
+                right[at : at + t, :],
+                TN,
+                preferred_element_type=f32,
+            )
+        ref[to : to + size, :] = total.astype(ref.dtype)
+
+
+def outer_kernel(*refs, blocks):
+    rows, grads, rights = refs[:blocks], refs[blocks : 2 * blocks], refs[2 * blocks : -4]
+    sent_one, kept_one, sent_two, kept_two = refs[-4:]
     step = pl.program_id(0)
-    if groups == 1:
-        fill(refs[:blocks])
-    else:
-        @pl.when(step < 2)
-        def _():
-            fill(refs[:blocks])
-
-        @pl.when(step == 2)
-        def _():
-            fill(refs[blocks : 2 * blocks])
-
-
-def outer(lefts, rights):
-    groups, blocks = len(lefts), len(lefts[0])
-    steps = 1 if groups == 1 else 3
-    t, d = lefts[0][0].shape
-    rows = rights[0].shape[0]
-    columns = rights[0].shape[1]
-    n = columns // steps
-    flat = [left for group in lefts for left in group]
-    out = pl.BlockSpec((d // 2, n), lambda k: (0, k))
+
+    @pl.when(step < 2)
+    def _():
+        fill(sent_one, kept_one, rows, rights, False)
+
+    @pl.when(step == 2)
+    def _():
+        fill(sent_two, kept_two, grads, rights, True)
+
+
+def outer(rows, grads, acts):
+    t, d = rows[0].shape
+    tall, columns = acts[0].shape
+    n = columns // 3
+    flat = [*rows, *grads]
+    one = pl.BlockSpec((d // 2, n), lambda k: (0, jnp.minimum(k, 1)))
+    two = pl.BlockSpec((d // 2, n), lambda k: (0, 0))
     return pl.pallas_call(
-        functools.partial(outer_kernel, groups=groups, blocks=blocks),
-        grid=(steps,),
+        functools.partial(outer_kernel, blocks=len(rows)),
+        grid=(3,),
         in_specs=[whole(left) for left in flat]
-        + [pl.BlockSpec((rows, n), lambda k: (0, k)) for _ in rights],
-        out_specs=[out, out],
+        + [pl.BlockSpec((tall, n), lambda k: (0, k)) for _ in acts],
+        out_specs=[one, one, two, two],
+        out_shape=[
+            jax.ShapeDtypeStruct((d // 2, 2 * n), bf16),
+            jax.ShapeDtypeStruct((d // 2, 2 * n), f32),
+            jax.ShapeDtypeStruct((d // 2, n), bf16),
+            jax.ShapeDtypeStruct((d // 2, n), f32),
+        ],
+        compiler_params=kernel_params(58),
+        cost_estimate=cost(2 * t * len(rows) * d * columns, 20 * MIB),
+    )(*flat, *acts)
+
+
+def outer_one_kernel(*refs):
+    fill(refs[-2], refs[-1], refs[:-3], refs[-3:-2], False)
+
+
+def outer_one(lefts, right):
+    t, d = lefts[0].shape
+    columns = right.shape[1]
+    vmem = pl.BlockSpec(memory_space=pltpu.VMEM)
+    return pl.pallas_call(
+        outer_one_kernel,
+        in_specs=[vmem] * (len(lefts) + 1),
+        out_specs=[vmem] * 2,
         out_shape=[
             jax.ShapeDtypeStruct((d // 2, columns), bf16),
             jax.ShapeDtypeStruct((d // 2, columns), f32),
         ],
-        compiler_params=kernel_params(58),
-        cost_estimate=cost(2 * t * blocks * d * columns, 20 * MIB),
-    )(*flat, *rights)
+        compiler_params=kernel_params(40),
+        cost_estimate=cost(2 * t * len(lefts) * d * columns, 6 * MIB),
+    )(*lefts, right)
 
 
 def rope_tables(length):
@@ -489,50 +548,73 @@
         self.left = bits - 1
         self.pieces = [block]
         self.beside = []
-        self.fresh = block
 
     def ready(self, *earlier):
-        self.fresh = after(self.fresh, *earlier)
-        self.pieces[-1] = self.fresh
-
-    def step(self):
-        self.beside.append(flip(self.fresh, "row", 0))
-        if self.left > 0:
-            held = jnp.concatenate(self.pieces, 0) if len(self.pieces) > 1 else self.pieces[0]
-            self.fresh = flip(held, "row", self.left)
-            self.pieces.append(self.fresh)
-            self.left -= 1
-
-    def all(self):
-        while len(self.beside) < self.bits:
-            self.step()
+        self.pieces[-1] = after(self.pieces[-1], *earlier)
+
+    def double(self, *earlier):
+        held = jnp.concatenate(self.pieces, 0) if len(self.pieces) > 1 else self.pieces[0]
+        self.pieces.append(flip(after(held, *earlier) if earlier else held, "row", self.left))
+        self.left -= 1
+        return self.pieces[-1]
+
+    def send(self, *earlier):
+        piece = self.pieces[len(self.beside)]
+        self.beside.append(flip(after(piece, *earlier) if earlier else piece, "row", 0))
+        return self.beside[-1]
+
+    def finish(self, *earlier):
+        while self.left > 0:
+            self.double()
+        rest = jnp.concatenate(self.pieces[len(self.beside) :], 0)
+        self.beside.append(flip(after(rest, *earlier), "row", 0))
         out = self.pieces + self.beside
         return out if out[0].shape[0] % 16 == 0 else [jnp.concatenate(out, 0)]
 
-
-def halve(kept, got, bits, bit):
-    half = kept.shape[0] // 2
-    sent = (kept[half:] + got[half:].astype(f32)).astype(bf16)
-    return sent, kept[:half] + got[:half].astype(f32)
+    def all(self):
+        while self.left > 0:
+            self.double()
+        while len(self.beside) < self.bits:
+            self.send()
+        out = self.pieces + self.beside
+        return out if out[0].shape[0] % 16 == 0 else [jnp.concatenate(out, 0)]
 
 
 class Scatter:
-    def __init__(self, sent, kept, bits):
-        self.bits, self.bit = bits, 0
-        self.kept = kept
-        self.got = flip(sent, "row", 0)
+    def __init__(self, parts, bits):
+        self.bits = bits
+        self.orders = [[0, 1], [1, 0]][: len(parts)]
+        self.kept = [kept for _, kept in parts]
+        self.done = 0
+        self.start([sent for sent, _ in parts])
+
+    def start(self, sents):
+        bits = [order[self.done] if self.done < 2 else self.done for order in self.orders]
+        self.got = [flip(sent, "row", bit) for sent, bit in zip(sents, bits)]
+
+    def wait(self, *earlier):
+        self.got = [after(got, *earlier) for got in self.got]
 
     def step(self):
-        if self.bit == self.bits - 1:
+        if self.done == self.bits - 1:
             return
-        self.bit += 1
-        sent, self.kept = halve(self.kept, self.got, self.bits, self.bit)
-        self.got = flip(sent, "row", self.bit)
+        self.done += 1
+        half = self.kept[0].shape[0] // 2
+        sents = [
+            (kept[half:] + got[half:].astype(f32)).astype(bf16)
+            for kept, got in zip(self.kept, self.got)
+        ]
+        self.kept = [kept[:half] + got[:half].astype(f32) for kept, got in zip(self.kept, self.got)]
+        if self.done == 2:
+            sents = [jnp.concatenate(sents, 1)]
+            self.kept = [jnp.concatenate(self.kept, 1)]
+        self.start(sents)
 
     def total(self):
-        while self.bit < self.bits - 1:
+        while self.done < self.bits - 1:
             self.step()
-        return self.kept + self.got.astype(f32)
+        totals = [kept + got.astype(f32) for kept, got in zip(self.kept, self.got)]
+        return jnp.concatenate(totals, 1)
 
 
 def turned_pairs(block):
@@ -607,18 +689,6 @@
             for part in (gate_weight, up_weight, down_flipped)
         ]
         mlp_gathers.append(Gather(jnp.concatenate(pieces, 1), bits))
-    qkv_gather.step()
-    out_gather.ready(qkv_gather.fresh)
-    qkv_gather.step()
-    out_gather.step()
-    mlp_gathers[0].ready(qkv_gather.fresh, out_gather.fresh)
-    qkv_pieces = qkv_gather.all()
-    out_gather.step()
-    mlp_gathers[0].step()
-    mlp_gathers[1].ready(qkv_pieces[-1], out_gather.fresh)
-    out_pieces = out_gather.all()
-    mlp_gathers[1].step()
-
     place = jnp.arange(model_width, dtype=jnp.int32)
     masks = jnp.array([bit_reversed(p, bits) for p in range(row_count)], jnp.int32)
     source = jnp.repeat(masks ^ row, deep) * deep + place % deep
@@ -649,11 +719,26 @@
     scale_one = lax.rsqrt(jnp.mean(input_rows * input_rows, axis=1) + eps)
     normed_own = (input_rows * scale_one[:, None] * gain_one).astype(bf16)
     normed_other = flip(normed_own, "col", 0)
+    cosine, sine_part = rope_tables(length)
     grad_blocks = [grad_out.astype(bf16)]
-    grad_blocks.append(flip(grad_blocks[0], "col", 0))
-    across = flip(grad_blocks[0], "col", 1)
-    grad_blocks += [across, flip(across, "col", 0)]
-    cosine, sine_part = rope_tables(length)
+
+    near, far = mlp_gathers
+    n_four = near.double()
+    n_own = near.send()
+    a_own = qkv_gather.send(n_own)
+    a_four = qkv_gather.double(n_own)
+    a_two = qkv_gather.double(a_own, n_four)
+    a_beside = qkv_gather.send(a_own)
+    o_four = out_gather.double(a_four)
+    a_last = qkv_gather.send(a_beside)
+    qkv_pieces = qkv_gather.all()
+    far.ready(a_two, o_four)
+    f_four = far.double()
+    o_two = out_gather.double(a_two)
+    across = flip(after(grad_blocks[0], a_four), "col", 1)
+    out_pieces = out_gather.finish(a_last, o_two)
+    n_two = near.double(o_two)
+    n_beside = near.send(a_last)
     qk_rows, value_rows, att_rows, log_totals = attend(
         parity,
         normed_own,
@@ -663,31 +748,44 @@
         cosine,
         sine_part,
     )
-    att_own, att_other = project(att_rows, out_pieces)
-    middle = input_rows + att_own + flip(att_other, "col", 0).astype(f32)
+    n_last = near.send(att_rows)
+    att_own, att_other = project(after(att_rows, n_beside, n_two, across, f_four), out_pieces)
+    att_got = flip(att_other, "col", 0)
+    grad_blocks.append(flip(after(grad_blocks[0], att_got), "col", 0))
+    grad_blocks += [across, flip(after(across, att_got), "col", 0)]
+    middle = input_rows + att_own + att_got.astype(f32)
     scale_two = lax.rsqrt(jnp.mean(middle * middle, axis=1) + eps)
     blocks = [(middle * scale_two[:, None] * gain_two).astype(bf16)]
     across = flip(blocks[0], "col", 1)
-    blocks.append(flip(blocks[0], "col", 0))
+    blocks.append(flip(after(blocks[0], n_last), "col", 0))
     blocks += [across, flip(across, "col", 0)]
 
+    f_own = far.send(n_last)
+    f_two = far.double(blocks[0])
+    f_beside = far.send(f_own)
+    f_last = far.send(f_beside)
     first_pieces, second_pieces = (gather.all() for gather in mlp_gathers)
-    act_own, *sums_own = mlp(blocks[:2], grad_blocks[:2], first_pieces)
+    act_own, *sums_own = mlp([after(blocks[0], blocks[2]), blocks[1]], grad_blocks[:2], first_pieces)
     act_far, *sums_far = mlp(blocks[2:], grad_blocks[2:], first_pieces)
-    first_scatter = Scatter(*outer([blocks, grad_blocks], [act_own, act_far]), bits)
-    start_far = after(blocks[2], first_scatter.kept)
+    sent_one, kept_one, sent_two, kept_two = outer(blocks, grad_blocks, [act_own, act_far])
+    first_scatter = Scatter([(sent_one, kept_one), (sent_two, kept_two)], bits)
+    start_far = after(blocks[2], kept_one)
     act_far, near_far, far_far = mlp(
         [start_far, blocks[3]], grad_blocks[2:], second_pieces, sums_far
     )
+    far_far = after(far_far, *first_scatter.got)
     across = near_far.astype(f32) + flip(far_far, "col", 0).astype(f32)
     across = across.astype(bf16)
     normed_back = flip(across[0], "col", 1)
     act_own, near_own, far_own = mlp(
-        [after(blocks[0], across), blocks[1]], grad_blocks[:2], second_pieces, sums_own
-    )
-    beside = flip(far_own, "col", 0)
+        [after(blocks[0], across), blocks[1]],
+        grad_blocks[:2],
+        second_pieces,
+        sums_own,
+    )
     first_scatter.step()
-    second_scatter = Scatter(*outer([blocks, grad_blocks], [act_own, act_far]), bits)
+    beside = flip(after(far_own, normed_back, *first_scatter.got), "col", 0)
+    first_scatter.step()
     down_back = flip(after(across[1], normed_back), "col", 1)
 
     def summed(k, back):
@@ -704,11 +802,17 @@
     gain_two_grad = jnp.sum(grad_normed_two * middle * scale_two[:, None], axis=0)
     branch_own = grad_middle.astype(bf16)
     branch_other = flip(branch_own, "col", 0)
-    out_scatter = Scatter(*outer([[branch_own, branch_other]], [att_rows]), bits)
-    layer_output = unstored((middle + summed(1, down_back)).astype(bf16))
-    grad_mixed, bias_grad = attend_back(
+    sent_one, kept_one, sent_two, kept_two = outer(
+        [after(blocks[0], branch_own, *first_scatter.kept), *blocks[1:]],
+        grad_blocks,
+        [act_own, act_far],
+    )
+    second_scatter = Scatter([(sent_one, kept_one), (sent_two, kept_two)], bits)
+    out_scatter = Scatter([outer_one([after(branch_own, kept_one), branch_other], att_rows)], bits)
+    split = qk_rows.shape[1] // 256
+    mixed_first, bias_first, *carry = attend_back(
         parity,
-        branch_own,
+        after(branch_own, out_scatter.kept[0]),
         branch_other,
         out_pieces,
         qk_rows,
@@ -716,10 +820,39 @@
         log_totals,
         cosine,
         sine_part,
-    )
-    bias_grad = bias_grad[0]
-    qkv_scatter = Scatter(*outer([[normed_own, normed_other]], [grad_mixed]), bits)
+        0,
+        split,
+    )
+    second_scatter.wait(mixed_first)
+    out_scatter.wait(mixed_first)
+    second_scatter.step()
+    out_scatter.step()
+    mixed_last, bias_last = attend_back(
+        parity,
+        after(branch_own, *second_scatter.kept, out_scatter.kept[0]),
+        branch_other,
+        out_pieces,
+        qk_rows,
+        value_rows,
+        log_totals,
+        cosine,
+        sine_part,
+        split,
+        2 * split,
+        carry,
+    )
+    bias_grad = jnp.concatenate([bias_first, bias_last], 1)[0]
+    first_scatter.wait(mixed_last)
+    second_scatter.wait(mixed_last)
+    out_scatter.wait(mixed_last)
+    grad_mixed = jnp.concatenate([mixed_first, mixed_last], 1)
+    passed = [*second_scatter.got, *out_scatter.got]
+    second_scatter.step()
+    out_scatter.step()
+    layer_output = unstored((middle + summed(1, after(down_back, grad_mixed))).astype(bf16))
+    qkv_scatter = Scatter([outer_one([normed_own, normed_other], grad_mixed)], bits)
     qkv_full = jnp.concatenate(qkv_pieces, 0)
+    grad_mixed = after(grad_mixed, qkv_scatter.kept[0], *passed)
     partial = jnp.einsum("tc,dc->td", grad_mixed, qkv_full, preferred_element_type=f32)
     grad_normed_one = partial[:tok_local] + flip(
         partial[tok_local:].astype(bf16), "col", 0

time: 449 us -> 422 us (0.940)
  waiting for transfers between devices: 139 us -> 99.3 us
  local copies, waits for them, and re-layouts: 27.5 us -> 33.3 us
  starting transfers between devices: 59.7 us -> 65.2 us
    ppermute x51 -> x53, waiting for transfers between devices: 137 us -> 98 us  [flip(): return lax.ppermute(block, axis, [(i, i ^ 1 << bit) for i in range(count)])]
    ppermute x51 -> x53, starting transfers between devices: 50 us -> 53.4 us  [flip(): return lax.ppermute(block, axis, [(i, i ^ 1 << bit) for i in range(count)])]
    pallas_call x1 -> x2, Pallas kernels: 30.9 us -> 33 us  [attend_back(): pl.pallas_call(functools.partial(attend_back_kernel, block=block, count=l...]
    unnamed x114 -> x155, local copies, waits for them, and re-layouts: 16.6 us -> 17.1 us
  transfers between devices with their start and end apart: 57 -> 59, of which waited for: 19 -> 17; matrix products, arithmetic and copies ran while one was open for 15% -> 16% of each run, Pallas kernels for 37% -> 38%
where the time goes in v4:
time: 422 us; the launch traced here: 414 us
  Pallas kernels  161 us (38%)
  waiting for transfers between devices  99.3 us (24%)
  starting transfers between devices  65.2 us (15%)
  other arithmetic  35.9 us (9%)
  local copies, waits for them, and re-layouts  33.3 us (8%)
  matrix products  17.2 us (4%)
    ppermute x53, waiting for transfers between devices, flip(): return lax.ppermute(block, axis, [(i, i ^ 1 << bit) for i in range(count)])  98 us
    pallas_call x4, Pallas kernels, mlp(): pl.pallas_call(functools.partial(mlp_kernel, count=len(pieces), add=add),...  68.7 us
    ppermute x53, starting transfers between devices, flip(): return lax.ppermute(block, axis, [(i, i ^ 1 << bit) for i in range(count)])  53.4 us
    pallas_call x2, Pallas kernels, attend_back(): pl.pallas_call(functools.partial(attend_back_kernel, block=block, count=l...  33 us
    pallas_call x2, Pallas kernels, outer(): pl.pallas_call(functools.partial(outer_kernel, blocks=len(rows)), grid=(3...  31.7 us
    pallas_call x1, Pallas kernels, attend(): pl.pallas_call(functools.partial(attend_kernel, block=block, count=len(pi...  19.9 us
    unnamed x155, local copies, waits for them, and re-layouts  17.1 us
  transfers between devices with their start and end apart: 59, of which 17 were waited for; matrix products, arithmetic and copies ran while one was open for 16% of the time, Pallas kernels for 38%

profile of v4, /device:TPU:0, one launch (start us, length us, event | category | flops | bytes accessed | tf_op | source)
XLA Modules:
  0.0 414.1 jit_solution(8523934205234403065)
XLA Ops:
  3.5 3.0 collective-permute-start.2
  10.1 2.7 collective-permute-start.6
  12.7 1.5 collective-permute-start.3
  15.1 1.4 fusion.9
  19.0 2.8 bitcast_convert_fusion
  23.9 2.0 fusion.59
  26.1 1.6 collective-permute-start.5
  27.7 7.4 %collective-permute-done.4.rest_1_ = bf16[112,576]{1,0:T(8,128)(2,1)S(1)} collective-permute-done((bf16[112,576]{1,0:T(8,128)(2,1)S(1)}, bf16[112,576]{1,0:T(8,128)(2,1)S(1)}, u32[]{:S(2)}, u32[]{:S(2)}) %collective-permute-start.4) | collective-permute-done | bytes 129056 | tf_op jit(solution)/shard_map/ppermute | solution.py:23
  36.6 4.3 %collective-permute-start.7 = (bf16[224,576]{1,0:T(8,128)(2,1)}, bf16[224,576]{1,0:T(8,128)(2,1)S(1)}, u32[]{:S(2)}, u32[]{:S(2)}) collective-permute-start(bf16[224,576]{1,0:T(8,128)(2,1)} %pad_maximum_fusion.11), channel_id=1, source_target_pairs={{0,8},{4,12},{8,0},{12,4},{16,24},{20,28},{24,16},{28,20},{1,9},{5... | collective-permute-start | bytes 774152 | tf_op jit(solution)/shard_map/ppermute | solution.py:23
  41.8 1.6 collective-permute-start.8
  43.8 5.4 %collective-permute-done.7.rest_2_ = bf16[224,576]{1,0:T(8,128)(2,1)S(1)} collective-permute-done((bf16[224,576]{1,0:T(8,128)(2,1)}, bf16[224,576]{1,0:T(8,128)(2,1)S(1)}, u32[]{:S(2)}, u32[]{:S(2)}) %collective-permute-start.7) | collective-permute-done | bytes 258080 | tf_op jit(solution)/shard_map/ppermute | solution.py:23
  49.7 1.5 collective-permute-start.9
  52.4 2.1 collective-permute-start.15
  54.5 4.2 %collective-permute-done.12.rest_2_ = bf16[224,512]{1,0:T(8,128)(2,1)S(1)} collective-permute-done((bf16[224,512]{1,0:T(8,128)(2,1)S(1)}, bf16[224,512]{1,0:T(8,128)(2,1)S(1)}, u32[]{:S(2)}, u32[]{:S(2)}) %collective-permute-start.12) | collective-permute-done | bytes 229408 | tf_op jit(solution)/shard_map/ppermute | solution.py:23
  58.7 2.0 collective-permute-start.10
  61.8 19.9 %shard_map.186 = (bf16[1024,512]{1,0:T(8,128)(2,1)S(1)}, bf16[1024,64]{1,0:T(8,128)(2,1)S(1)}, bf16[1024,512]{1,0:T(8,128)(2,1)S(1)}, f32[8,1024]{1,0:T(8,128)S(1)}) custom-call(s32[1]{0:T(128)} %bitcast.1.parity_ref, bf16[512,896]{1,0:T(8,128)(2,1)S(1)} %fusion.11.own_ref.refs_0_, bf16[512,896]{1,0:T(8,128)(2,1)} %collective-permute-done.other_ref.refs_1_, ...), custom_call_target="tpu_custom_call" | custom-call | flops 12000000000 | bytes 8000000 | tf_op jit(solution)/shard_map/pallas_call | solution.py:159
  82.9 2.2 shard_map.187
  85.9 2.2 collective-permute-start.19
  88.9 15.3 %collective-permute-done.19.rest_5_ = bf16[224,1536]{1,0:T(8,128)(2,1)S(1)} collective-permute-done((bf16[224,1536]{1,0:T(8,128)(2,1)S(1)}, bf16[224,1536]{1,0:T(8,128)(2,1)S(1)}, u32[]{:S(2)}, u32[]{:S(2)}) %collective-permute-start.19) | collective-permute-done | bytes 688160 | tf_op jit(solution)/shard_map/ppermute | solution.py:23
  104.7 1.7 collective-permute-start.25
  106.5 1.9 collective-permute-start.24
  108.4 10.0 %collective-permute-done.25.rest_3_ = bf16[112,2304]{1,0:T(8,128)(2,1)S(1)} collective-permute-done((bf16[112,2304]{1,0:T(8,128)(2,1)S(1)}, bf16[112,2304]{1,0:T(8,128)(2,1)S(1)}, u32[]{:S(2)}, u32[]{:S(2)}) %collective-permute-start.25) | collective-permute-done | bytes 516128 | tf_op jit(solution)/shard_map/ppermute | solution.py:23
  118.9 1.8 collective-permute-start.26
  120.7 14.1 %shard_map.188 = (bf16[1024,1536]{1,0:T(8,128)(2,1)}, bf16[2,512,896]{2,1,0:T(8,128)(2,1)}, bf16[2,512,896]{2,1,0:T(8,128)(2,1)}) custom-call(bf16[512,896]{1,0:T(8,128)(2,1)} %copy-done.43, bf16[512,896]{1,0:T(8,128)(2,1)} %copy-done.65, bf16[512,896]{1,0:T(8,128)(2,1)} %get-tuple-element.102.g0_ref.refs_4_, ...), custom_call_target="tpu_custom_call" | custom-call | flops 5637144576 | bytes 31457280 | tf_op jit(solution)/shard_map/pallas_call | solution.py:436
  135.8 14.3 %shard_map.189 = (bf16[1024,1536]{1,0:T(8,128)(2,1)}, bf16[2,512,896]{2,1,0:T(8,128)(2,1)}, bf16[2,512,896]{2,1,0:T(8,128)(2,1)}) custom-call(bf16[512,896]{1,0:T(8,128)(2,1)} %collective-permute-done.18.x0_ref.refs_2_, bf16[512,896]{1,0:T(8,128)(2,1)} %collective-permute-done.21.x1_ref.refs_3_, bf16[512,896]{1,0:T(8,128)(2,1)} %collective-permute-done.14.g0_ref.refs_6_, ...), custom_call_target="tpu_custom_call" | custom-call | flops 5637144576 | bytes 31457280 | tf_op jit(solution)/shard_map/pallas_call | solution.py:436
  150.1 15.4 %shard_map.190 = (bf16[448,1024]{1,0:T(8,128)(2,1)}, f32[448,1024]{1,0:T(8,128)}, bf16[448,512]{1,0:T(8,128)(2,1)}, f32[448,512]{1,0:T(8,128)}) custom-call(bf16[512,896]{1,0:T(8,128)(2,1)} %copy-done.43, bf16[512,896]{1,0:T(8,128)(2,1)} %copy-done.65, bf16[512,896]{1,0:T(8,128)(2,1)} %collective-permute-done.18.x0_ref.refs_2_, ...), custom_call_target="tpu_custom_call" | custom-call | flops 5637144576 | bytes 20971520 | tf_op jit(solution)/shard_map/pallas_call | solution.py:500
  166.8 1.8 collective-permute-start.29
  168.6 20.2 %shard_map.191 = (bf16[1024,2304]{1,0:T(8,128)(2,1)}, bf16[2,512,896]{2,1,0:T(8,128)(2,1)}, bf16[2,512,896]{2,1,0:T(8,128)(2,1)}) custom-call(bf16[512,896]{1,0:T(8,128)(2,1)} %collective-permute-done.18.x0_ref.refs_2_, bf16[512,896]{1,0:T(8,128)(2,1)} %collective-permute-done.21.x1_ref.refs_3_, bf16[512,896]{1,0:T(8,128)(2,1)} %collective-permute-done.14.g0_ref.refs_6_, ...), custom_call_target="tpu_custom_call" | custom-call | flops 8455716864 | bytes 31457280 | tf_op jit(solution)/shard_map/pallas_call | solution.py:436
  189.9 2.9 collective-permute-done.30
  197.2 20.1 %shard_map.192 = (bf16[1024,2304]{1,0:T(8,128)(2,1)}, bf16[2,512,896]{2,1,0:T(8,128)(2,1)}, bf16[2,512,896]{2,1,0:T(8,128)(2,1)}) custom-call(bf16[512,896]{1,0:T(8,128)(2,1)} %copy-done.43, bf16[512,896]{1,0:T(8,128)(2,1)} %copy-done.65, bf16[512,896]{1,0:T(8,128)(2,1)} %get-tuple-element.102.g0_ref.refs_4_, ...), custom_call_target="tpu_custom_call" | custom-call | flops 8455716864 | bytes 31457280 | tf_op jit(solution)/shard_map/pallas_call | solution.py:436
  221.8 1.9 slice_add_fusion.13
  225.3 1.6 collective-permute-start.57
  226.9 1.3 collective-permute-start.35
  228.1 2.4 multiply_reduce_fusion
  230.5 3.4 fusion.71
  235.4 16.3 %shard_map.193 = (bf16[448,1536]{1,0:T(8,128)(2,1)}, f32[448,1536]{1,0:T(8,128)}, bf16[448,768]{1,0:T(8,128)(2,1)}, f32[448,768]{1,0:T(8,128)}) custom-call(bf16[512,896]{1,0:T(8,128)(2,1)} %copy-done.43, bf16[512,896]{1,0:T(8,128)(2,1)} %copy-done.65, bf16[512,896]{1,0:T(8,128)(2,1)} %collective-permute-done.18.x0_ref.refs_2_, ...), custom_call_target="tpu_custom_call" | custom-call | flops 8455716864 | bytes 20971520 | tf_op jit(solution)/shard_map/pallas_call | solution.py:500
  255.1 1.3 collective-permute-start.38
  261.3 1.7 shard_map.194
  263.0 1.3 collective-permute-start.39
  266.3 18.0 %shard_map.195 = (bf16[1024,256]{1,0:T(8,128)(2,1)S(1)}, f32[1,256]{1,0:T(1,128)S(1)}, f32[1024,128]{1,0:T(8,128)S(1)}, f32[1024,128]{1,0:T(8,128)S(1)}) custom-call(s32[1]{0:T(128)} %bitcast.1.parity_ref, bf16[512,896]{1,0:T(8,128)(2,1)} %copy-done.2, bf16[512,896]{1,0:T(8,128)(2,1)} %copy-done.14, bf16[1024,512]{1,0:T(8,128)(2,1)} %copy-done.20, ...), custom_call_target="tpu_custom_call" | custom-call | flops 12000000000 | bytes 6000000 | tf_op jit(solution)/shard_map/pallas_call | solution.py:352
  286.0 13.5 %collective-permute-done.39 = bf16[448,512]{1,0:T(8,128)(2,1)S(1)} collective-permute-done((bf16[448,512]{1,0:T(8,128)(2,1)S(1)}, bf16[448,512]{1,0:T(8,128)(2,1)S(1)}, u32[]{:S(2)}, u32[]{:S(2)}) %collective-permute-start.39) | collective-permute-done | bytes 458784 | tf_op jit(solution)/shard_map/ppermute | solution.py:23
  299.7 3.0 add_convert_fusion.1
  302.7 15.0 %shard_map.196 = (bf16[1024,320]{1,0:T(8,128)(2,1)S(1)}, f32[1,320]{1,0:T(1,128)S(1)}) custom-call(s32[1]{0:T(128)} %bitcast.1.parity_ref, bf16[512,896]{1,0:T(8,128)(2,1)} %copy-done.2, bf16[512,896]{1,0:T(8,128)(2,1)} %copy-done.14, bf16[1024,512]{1,0:T(8,128)(2,1)} %copy-done.20, bf16[1024,64]{1,0:T(8,128)(2,1)S(1)} %copy-done.22, ...), custom_call_target="tpu_custom_call" | custom-call | flops 12000000000 | bytes 6000000 | tf_op jit(solution)/shard_map/pallas_call | solution.py:352
  318.5 1.3 collective-permute-start.40
  320.0 3.8 shard_map.197
  326.3 1.3 collective-permute-start.54
  327.7 3.9 fusion.24
  331.6 7.7 %collective-permute-done.54 = bf16[112,512]{1,0:T(8,128)(2,1)S(1)} collective-permute-done((bf16[112,512]{1,0:T(8,128)(2,1)S(1)}, bf16[112,512]{1,0:T(8,128)(2,1)S(1)}, u32[]{:S(2)}, u32[]{:S(2)}) %collective-permute-start.54) | collective-permute-done | bytes 114720 | tf_op jit(solution)/shard_map/ppermute | solution.py:23
  340.1 2.0 collective-permute-start.56
  346.7 3.2 collective-permute-start.50
  349.8 1.6 fusion.39
  351.5 4.5 %collective-permute-done.50 = bf16[224,576]{1,0:T(8,128)(2,1)S(1)} collective-permute-done((bf16[224,576]{1,0:T(8,128)(2,1)S(1)}, bf16[224,576]{1,0:T(8,128)(2,1)S(1)}, u32[]{:S(2)}, u32[]{:S(2)}) %collective-permute-start.50) | collective-permute-done | bytes 258080 | tf_op jit(solution)/shard_map/ppermute | solution.py:23
  356.1 2.1 collective-permute-start.51
  359.2 17.3 %collective-permute-done.51 = bf16[112,576]{1,0:T(8,128)(2,1)S(1)} collective-permute-done((bf16[112,576]{1,0:T(8,128)(2,1)S(1)}, bf16[112,576]{1,0:T(8,128)(2,1)S(1)}, u32[]{:S(2)}, u32[]{:S(2)}) %collective-permute-start.51) | collective-permute-done | bytes 129056 | tf_op jit(solution)/shard_map/ppermute | solution.py:23
  377.3 4.8 %collective-permute-start.53 = (bf16[112,288]{1,0:T(8,128)(2,1)S(1)}, bf16[112,288]{1,0:T(8,128)(2,1)S(1)}, u32[]{:S(2)}, u32[]{:S(2)}) collective-permute-start(bf16[112,288]{1,0:T(8,128)(2,1)S(1)} %get-tuple-element.211), channel_id=1, source_target_pairs={{0,1},{1,3},{2,0},{3,2},{4,5},{5,7},{6,4},{7,6},{8,9},{9,11},{10,8... | collective-permute-start | bytes 193544 | tf_op jit(solution)/shard_map/ppermute | solution.py:629
  382.1 3.5 fusion.82
  385.6 2.5 slice.696
  389.8 1.3 maximum_add_fusion
  391.4 2.4 fusion.17
  394.9 1.8 maximum_bitcast_fusion
  398.1 2.4 collective-permute-done.45
  402.1 2.1 collective-permute-done.46
  404.3 3.7 collective-permute-done.47
  408.2 4.3 %fusion.25 = bf16[512,896]{1,0:T(8,128)(2,1)} fusion(s32[896]{0:T(1024)S(1)} %copy-done.60, f32[896,512]{0,1:T(8,128)S(1)} %copy-done.28, f32[512,896]{1,0:T(8,128)S(1)} %copy-done.34, f32[512]{0:T(512)S(1)} %fusion.70, f32[896]{0:T(1024)S(1)} %copy-done.56, f32[512]{0:T(512)S(1)} %add_rsqrt_fusion.1, f32[1024,896]{1,0:T(8,128)} %fusion.82, ...), kind=kOutput, calls=%fused_computation.45 | convolution fusion | flops 827015168 | bytes 7351296 | tf_op jit(solution)/shard_map/ts,fs->tf/dot_general | solution.py:701
  (343 shorter events, 66.8 us)
Async XLA Ops:
  3.5 18.3 %collective-permute-start.2 = (bf16[128,512]{1,0:T(8,128)(2,1)S(1)}, bf16[128,512]{1,0:T(8,128)(2,1)S(1)}, u32[]{:S(2)}, u32[]{:S(2)}) collective-permute-start(bf16[128,512]{1,0:T(8,128)(2,1)S(1)} %fusion.60), channel_id=1, source_target_pairs={{0,2},{1,0},{2,3},{3,1},{4,6},{5,4},{6,7},{7,5},{8,10},{9,8},{10,1... | collective-permute-start | bytes 393224 | tf_op jit(solution)/shard_map/ppermute | solution.py:623
  6.5 15.3 %collective-permute-start.1 = (bf16[128,512]{1,0:T(8,128)(2,1)S(1)}, bf16[128,512]{1,0:T(8,128)(2,1)S(1)}, u32[]{:S(2)}, u32[]{:S(2)}) collective-permute-start(bf16[128,512]{1,0:T(8,128)(2,1)S(1)} %fusion.60), channel_id=1, source_target_pairs={{0,0},{1,2},{2,1},{3,3},{4,4},{5,6},{6,5},{7,7},{8,8},{9,10},{10,9... | collective-permute-start | bytes 393224 | tf_op jit(solution)/shard_map/ppermute | solution.py:623
  10.1 25.8 %collective-permute-start.6 = (bf16[112,1536]{1,0:T(8,128)(2,1)S(1)}, bf16[112,1536]{1,0:T(8,128)(2,1)}, u32[]{:S(2)}, u32[]{:S(2)}) collective-permute-start(bf16[112,1536]{1,0:T(8,128)(2,1)S(1)} %pad_maximum_fusion.9.rest_0_), channel_id=1, source_target_pairs={{0,16},{4,20},{8,24},{12,28},{16,0},{20,4},{24,8},{28,12},{1,17},{... | collective-permute-start | bytes 1032200 | tf_op jit(solution)/shard_map/ppermute | solution.py:23
  12.7 10.9 %collective-permute-start.3 = (bf16[112,1536]{1,0:T(8,128)(2,1)S(1)}, bf16[112,1536]{1,0:T(8,128)(2,1)}, u32[]{:S(2)}, u32[]{:S(2)}) collective-permute-start(bf16[112,1536]{1,0:T(8,128)(2,1)S(1)} %pad_maximum_fusion.9.rest_0_), channel_id=1, source_target_pairs={{0,4},{4,0},{8,12},{12,8},{16,20},{20,16},{24,28},{28,24},{1,5},{5... | collective-permute-start | bytes 1032200 | tf_op jit(solution)/shard_map/ppermute | solution.py:23
  14.4 70.8 %copy-start.59 = (s32[896]{0:T(1024)}, s32[896]{0:T(1024)S(1)}, u32[]{:S(2)}) copy-start(s32[896]{0:T(1024)S(1)} %fusion.63) | copy-start | bytes 10756
  16.7 44.0 %collective-permute-start = (bf16[512,896]{1,0:T(8,128)(2,1)S(1)}, bf16[512,896]{1,0:T(8,128)(2,1)}, u32[]{:S(2)}, u32[]{:S(2)}) collective-permute-start(bf16[512,896]{1,0:T(8,128)(2,1)S(1)} %fusion.11.own_ref.refs_0_), channel_id=1, source_target_pairs={{0,1},{1,0},{2,3},{3,2},{4,5},{5,4},{6,7},{7,6},{8,9},{9,8},{10,11... | collective-permute-start | bytes 2752520 | tf_op jit(solution)/shard_map/ppermute | solution.py:23
  23.6 11.5 %collective-permute-start.4 = (bf16[112,576]{1,0:T(8,128)(2,1)S(1)}, bf16[112,576]{1,0:T(8,128)(2,1)S(1)}, u32[]{:S(2)}, u32[]{:S(2)}) collective-permute-start(bf16[112,576]{1,0:T(8,128)(2,1)S(1)} %get-tuple-element.85.rest_0_), channel_id=1, source_target_pairs={{0,16},{4,20},{8,24},{12,28},{16,0},{20,4},{24,8},{28,12},{1,17},{... | collective-permute-start | bytes 387080 | tf_op jit(solution)/shard_map/ppermute | solution.py:23
  26.1 9.8 %collective-permute-start.5 = (bf16[112,576]{1,0:T(8,128)(2,1)S(1)}, bf16[112,576]{1,0:T(8,128)(2,1)S(1)}, u32[]{:S(2)}, u32[]{:S(2)}) collective-permute-start(bf16[112,576]{1,0:T(8,128)(2,1)S(1)} %get-tuple-element.85.rest_0_), channel_id=1, source_target_pairs={{0,4},{4,0},{8,12},{12,8},{16,20},{20,16},{24,28},{28,24},{1,5},{5... | collective-permute-start | bytes 387080 | tf_op jit(solution)/shard_map/ppermute | solution.py:23
  35.1 8.7 %collective-permute-start.11 = (bf16[112,512]{1,0:T(8,128)(2,1)S(1)}, bf16[112,512]{1,0:T(8,128)(2,1)S(1)}, u32[]{:S(2)}, u32[]{:S(2)}) collective-permute-start(bf16[112,512]{1,0:T(8,128)(2,1)S(1)} %fusion.62.rest_0_), channel_id=1, source_target_pairs={{0,16},{4,20},{8,24},{12,28},{16,0},{20,4},{24,8},{28,12},{1,17},{... | collective-permute-start | bytes 344072 | tf_op jit(solution)/shard_map/ppermute | solution.py:23
  36.6 12.6 %collective-permute-start.7 = (bf16[224,576]{1,0:T(8,128)(2,1)}, bf16[224,576]{1,0:T(8,128)(2,1)S(1)}, u32[]{:S(2)}, u32[]{:S(2)}) collective-permute-start(bf16[224,576]{1,0:T(8,128)(2,1)} %pad_maximum_fusion.11), channel_id=1, source_target_pairs={{0,8},{4,12},{8,0},{12,4},{16,24},{20,28},{24,16},{28,20},{1,9},{5... | collective-permute-start | bytes 774152 | tf_op jit(solution)/shard_map/ppermute | solution.py:23
  41.8 39.9 %copy-start.3 = (f32[1024,128]{1,0:T(8,128)}, f32[1024,128]{1,0:T(8,128)S(1)}, u32[]{:S(2)}) copy-start(f32[1024,128]{1,0:T(8,128)S(1)} %get-tuple-element.252.sin_ref) | copy-start | bytes 1572868
  41.8 7.4 %collective-permute-start.8 = (bf16[112,576]{1,0:T(8,128)(2,1)S(1)}, bf16[112,576]{1,0:T(8,128)(2,1)S(1)}, u32[]{:S(2)}, u32[]{:S(2)}) collective-permute-start(bf16[112,576]{1,0:T(8,128)(2,1)S(1)} %collective-permute-done.4.rest_1_), channel_id=1, source_target_pairs={{0,4},{4,0},{8,12},{12,8},{16,20},{20,16},{24,28},{28,24},{1,5},{5... | collective-permute-start | bytes 387080 | tf_op jit(solution)/shard_map/ppermute | solution.py:23
  49.2 32.5 %copy-start.12 = (bf16[112,576]{1,0:T(8,128)(2,1)}, bf16[112,576]{1,0:T(8,128)(2,1)S(1)}, u32[]{:S(2)}) copy-start(bf16[112,576]{1,0:T(8,128)(2,1)S(1)} %collective-permute-done.8.rest_4_) | copy-start | bytes 387076
  49.2 9.5 %collective-permute-start.12 = (bf16[224,512]{1,0:T(8,128)(2,1)S(1)}, bf16[224,512]{1,0:T(8,128)(2,1)S(1)}, u32[]{:S(2)}, u32[]{:S(2)}) collective-permute-start(bf16[224,512]{1,0:T(8,128)(2,1)S(1)} %pad_maximum_fusion.12), channel_id=1, source_target_pairs={{0,8},{4,12},{8,0},{12,4},{16,24},{20,28},{24,16},{28,20},{1,9},{5... | collective-permute-start | bytes 688136 | tf_op jit(solution)/shard_map/ppermute | solution.py:23
  49.7 9.0 %collective-permute-start.9 = (bf16[224,576]{1,0:T(8,128)(2,1)S(1)}, bf16[224,576]{1,0:T(8,128)(2,1)S(1)}, u32[]{:S(2)}, u32[]{:S(2)}) collective-permute-start(bf16[224,576]{1,0:T(8,128)(2,1)S(1)} %collective-permute-done.7.rest_2_), channel_id=1, source_target_pairs={{0,4},{4,0},{8,12},{12,8},{16,20},{20,16},{24,28},{28,24},{1,5},{5... | collective-permute-start | bytes 774152 | tf_op jit(solution)/shard_map/ppermute | solution.py:23
  52.4 30.5 %collective-permute-start.14 = (bf16[512,896]{1,0:T(8,128)(2,1)S(1)}, bf16[512,896]{1,0:T(8,128)(2,1)}, u32[]{:S(2)}, u32[]{:S(2)}) collective-permute-start(bf16[512,896]{1,0:T(8,128)(2,1)S(1)} %copy-done.64), channel_id=1, source_target_pairs={{0,2},{1,3},{2,0},{3,1},{4,6},{5,7},{6,4},{7,5},{8,10},{9,11},{10,... | collective-permute-start | bytes 2752520 | tf_op jit(solution)/shard_map/ppermute | solution.py:23
  52.4 30.4 %collective-permute-start.15 = (bf16[112,2304]{1,0:T(8,128)(2,1)}, bf16[112,2304]{1,0:T(8,128)(2,1)S(1)}, u32[]{:S(2)}, u32[]{:S(2)}) collective-permute-start(bf16[112,2304]{1,0:T(8,128)(2,1)} %fusion.43.rest_0_), channel_id=1, source_target_pairs={{0,16},{4,20},{8,24},{12,28},{16,0},{20,4},{24,8},{28,12},{1,17},{... | collective-permute-start | bytes 1548296 | tf_op jit(solution)/shard_map/ppermute | solution.py:23
  58.7 24.1 %collective-permute-start.13 = (bf16[224,1536]{1,0:T(8,128)(2,1)S(1)}, bf16[224,1536]{1,0:T(8,128)(2,1)S(1)}, u32[]{:S(2)}, u32[]{:S(2)}) collective-permute-start(bf16[224,1536]{1,0:T(8,128)(2,1)S(1)} %pad_maximum_fusion.1), channel_id=1, source_target_pairs={{0,8},{4,12},{8,0},{12,4},{16,24},{20,28},{24,16},{28,20},{1,9},{5... | collective-permute-start | bytes 2064392 | tf_op jit(solution)/shard_map/ppermute | solution.py:23
  58.7 24.1 %collective-permute-start.10 = (bf16[112,1536]{1,0:T(8,128)(2,1)}, bf16[112,1536]{1,0:T(8,128)(2,1)S(1)}, u32[]{:S(2)}, u32[]{:S(2)}) collective-permute-start(bf16[112,1536]{1,0:T(8,128)(2,1)} %collective-permute-done.6.rest_1_), channel_id=1, source_target_pairs={{0,4},{4,0},{8,12},{12,8},{16,20},{20,16},{24,28},{28,24},{1,5},{5... | collective-permute-start | bytes 1032200 | tf_op jit(solution)/shard_map/ppermute | solution.py:23
  60.8 22.1 %collective-permute-start.16 = (bf16[448,512]{1,0:T(8,128)(2,1)S(1)}, bf16[448,512]{1,0:T(8,128)(2,1)S(1)}, u32[]{:S(2)}, u32[]{:S(2)}) collective-permute-start(bf16[448,512]{1,0:T(8,128)(2,1)S(1)} %pad_maximum_fusion.8), channel_id=1, source_target_pairs={{0,4},{4,0},{8,12},{12,8},{16,20},{20,16},{24,28},{28,24},{1,5},{5... | collective-permute-start | bytes 1376264 | tf_op jit(solution)/shard_map/ppermute | solution.py:23
  82.8 36.1 %copy-start.48 = (bf16[112,2304]{1,0:T(8,128)(2,1)}, bf16[112,2304]{1,0:T(8,128)(2,1)S(1)}, u32[]{:S(2)}) copy-start(bf16[112,2304]{1,0:T(8,128)(2,1)S(1)} %collective-permute-done.15.rest_1_) | copy-start | bytes 1548292
  85.1 3.0 collective-permute-start.17
  85.9 18.3 %collective-permute-start.19 = (bf16[224,1536]{1,0:T(8,128)(2,1)S(1)}, bf16[224,1536]{1,0:T(8,128)(2,1)S(1)}, u32[]{:S(2)}, u32[]{:S(2)}) collective-permute-start(bf16[224,1536]{1,0:T(8,128)(2,1)S(1)} %collective-permute-done.13.rest_2_), channel_id=1, source_target_pairs={{0,4},{4,0},{8,12},{12,8},{16,20},{20,16},{24,28},{28,24},{1,5},{5... | collective-permute-start | bytes 2064392 | tf_op jit(solution)/shard_map/ppermute | solution.py:23
  88.8 31.9 %copy-start.43 = (bf16[512,896]{1,0:T(8,128)(2,1)}, bf16[512,896]{1,0:T(8,128)(2,1)S(1)}, u32[]{:S(2)}) copy-start(bf16[512,896]{1,0:T(8,128)(2,1)S(1)} %multiply_convert_fusion.x0_ref.refs_0_) | copy-start | bytes 2752516
  88.8 29.5 %collective-permute-start.18 = (bf16[512,896]{1,0:T(8,128)(2,1)S(1)}, bf16[512,896]{1,0:T(8,128)(2,1)}, u32[]{:S(2)}, u32[]{:S(2)}) collective-permute-start(bf16[512,896]{1,0:T(8,128)(2,1)S(1)} %multiply_convert_fusion.x0_ref.refs_0_), channel_id=1, source_target_pairs={{0,2},{1,3},{2,0},{3,1},{4,6},{5,7},{6,4},{7,5},{8,10},{9,11},{10,... | collective-permute-start | bytes 2752520 | tf_op jit(solution)/shard_map/ppermute | solution.py:23
  104.2 14.7 %collective-permute-start.20 = (bf16[512,896]{1,0:T(8,128)(2,1)S(1)}, bf16[512,896]{1,0:T(8,128)(2,1)S(1)}, u32[]{:S(2)}, u32[]{:S(2)}) collective-permute-start(bf16[512,896]{1,0:T(8,128)(2,1)S(1)} %multiply_convert_fusion.x0_ref.refs_0_), channel_id=1, source_target_pairs={{0,1},{1,0},{2,3},{3,2},{4,5},{5,4},{6,7},{7,6},{8,9},{9,8},{10,11... | collective-permute-start | bytes 2752520 | tf_op jit(solution)/shard_map/ppermute | solution.py:23
  104.2 16.5 %collective-permute-start.22 = (bf16[512,896]{1,0:T(8,128)(2,1)S(1)}, bf16[512,896]{1,0:T(8,128)(2,1)}, u32[]{:S(2)}, u32[]{:S(2)}) collective-permute-start(bf16[512,896]{1,0:T(8,128)(2,1)S(1)} %copy-done.64), channel_id=1, source_target_pairs={{0,1},{1,0},{2,3},{3,2},{4,5},{5,4},{6,7},{7,6},{8,9},{9,8},{10,11... | collective-permute-start | bytes 2752520 | tf_op jit(solution)/shard_map/ppermute | solution.py:23
  104.7 13.7 %collective-permute-start.25 = (bf16[112,2304]{1,0:T(8,128)(2,1)S(1)}, bf16[112,2304]{1,0:T(8,128)(2,1)S(1)}, u32[]{:S(2)}, u32[]{:S(2)}) collective-permute-start(bf16[112,2304]{1,0:T(8,128)(2,1)S(1)} %copy-done.31), channel_id=1, source_target_pairs={{0,4},{4,0},{8,12},{12,8},{16,20},{20,16},{24,28},{28,24},{1,5},{5... | collective-permute-start | bytes 1548296 | tf_op jit(solution)/shard_map/ppermute | solution.py:23
  106.5 28.3 %collective-permute-start.24 = (bf16[224,2304]{1,0:T(8,128)(2,1)S(1)}, bf16[224,2304]{1,0:T(8,128)(2,1)}, u32[]{:S(2)}, u32[]{:S(2)}) collective-permute-start(bf16[224,2304]{1,0:T(8,128)(2,1)S(1)} %pad_maximum_fusion), channel_id=1, source_target_pairs={{0,8},{4,12},{8,0},{12,4},{16,24},{20,28},{24,16},{28,20},{1,9},{5... | collective-permute-start | bytes 3096584 | tf_op jit(solution)/shard_map/ppermute | solution.py:23
  118.4 17.4 %collective-permute-start.23 = (bf16[512,896]{1,0:T(8,128)(2,1)}, bf16[512,896]{1,0:T(8,128)(2,1)}, u32[]{:S(2)}, u32[]{:S(2)}) collective-permute-start(bf16[512,896]{1,0:T(8,128)(2,1)} %collective-permute-done.14.g0_ref.refs_6_), channel_id=1, source_target_pairs={{0,1},{1,0},{2,3},{3,2},{4,5},{5,4},{6,7},{7,6},{8,9},{9,8},{10,11... | collective-permute-start | bytes 2752520 | tf_op jit(solution)/shard_map/ppermute | solution.py:23
  118.4 17.4 %collective-permute-start.21 = (bf16[512,896]{1,0:T(8,128)(2,1)}, bf16[512,896]{1,0:T(8,128)(2,1)}, u32[]{:S(2)}, u32[]{:S(2)}) collective-permute-start(bf16[512,896]{1,0:T(8,128)(2,1)} %collective-permute-done.18.x0_ref.refs_2_), channel_id=1, source_target_pairs={{0,1},{1,0},{2,3},{3,2},{4,5},{5,4},{6,7},{7,6},{8,9},{9,8},{10,11... | collective-permute-start | bytes 2752520 | tf_op jit(solution)/shard_map/ppermute | solution.py:23
  118.9 15.9 %collective-permute-start.26 = (bf16[112,2304]{1,0:T(8,128)(2,1)S(1)}, bf16[112,2304]{1,0:T(8,128)(2,1)S(1)}, u32[]{:S(2)}, u32[]{:S(2)}) collective-permute-start(bf16[112,2304]{1,0:T(8,128)(2,1)S(1)} %collective-permute-done.15.rest_1_), channel_id=1, source_target_pairs={{0,4},{4,0},{8,12},{12,8},{16,20},{20,16},{24,28},{28,24},{1,5},{5... | collective-permute-start | bytes 1548296 | tf_op jit(solution)/shard_map/ppermute | solution.py:23
  134.8 33.7 %collective-permute-start.27 = (bf16[224,2304]{1,0:T(8,128)(2,1)}, bf16[224,2304]{1,0:T(8,128)(2,1)}, u32[]{:S(2)}, u32[]{:S(2)}) collective-permute-start(bf16[224,2304]{1,0:T(8,128)(2,1)} %collective-permute-done.24.rest_2_), channel_id=1, source_target_pairs={{0,4},{4,0},{8,12},{12,8},{16,20},{20,16},{24,28},{28,24},{1,5},{5... | collective-permute-start | bytes 3096584 | tf_op jit(solution)/shard_map/ppermute | solution.py:23
  165.5 23.3 %collective-permute-start.28 = (bf16[448,1024]{1,0:T(8,128)(2,1)}, bf16[448,1024]{1,0:T(8,128)(2,1)S(1)}, u32[]{:S(2)}, u32[]{:S(2)}) collective-permute-start(bf16[448,1024]{1,0:T(8,128)(2,1)} %get-tuple-element.117), channel_id=1, source_target_pairs={{0,4},{4,0},{8,12},{12,8},{16,20},{20,16},{24,28},{28,24},{1,5},{5... | collective-permute-start | bytes 2752520 | tf_op jit(solution)/shard_map/ppermute | solution.py:23
  166.8 22.0 %collective-permute-start.29 = (bf16[448,512]{1,0:T(8,128)(2,1)}, bf16[448,512]{1,0:T(8,128)(2,1)S(1)}, u32[]{:S(2)}, u32[]{:S(2)}) collective-permute-start(bf16[448,512]{1,0:T(8,128)(2,1)} %get-tuple-element.118), channel_id=1, source_target_pairs={{0,8},{4,12},{8,0},{12,4},{16,24},{20,28},{24,16},{28,20},{1,9},{5... | collective-permute-start | bytes 1376264 | tf_op jit(solution)/shard_map/ppermute | solution.py:23
  188.8 4.1 collective-permute-start.30
  189.0 28.4 %collective-permute-start.33 = (bf16[224,512]{1,0:T(8,128)(2,1)S(1)}, bf16[224,512]{1,0:T(8,128)(2,1)S(1)}, u32[]{:S(2)}, u32[]{:S(2)}) collective-permute-start(bf16[224,512]{1,0:T(8,128)(2,1)S(1)} %get-tuple-element.195), channel_id=1, source_target_pairs={{0,4},{4,0},{8,12},{12,8},{16,20},{20,16},{24,28},{28,24},{1,5},{5... | collective-permute-start | bytes 688136 | tf_op jit(solution)/shard_map/ppermute | solution.py:23
  194.4 23.0 %collective-permute-start.31 = (bf16[512,896]{1,0:T(8,128)(2,1)S(1)}, bf16[512,896]{1,0:T(8,128)(2,1)}, u32[]{:S(2)}, u32[]{:S(2)}) collective-permute-start(bf16[512,896]{1,0:T(8,128)(2,1)S(1)} %get-tuple-element.188), channel_id=1, source_target_pairs={{0,2},{1,3},{2,0},{3,1},{4,6},{5,7},{6,4},{7,5},{8,10},{9,11},{10,... | collective-permute-start | bytes 2752520 | tf_op jit(solution)/shard_map/ppermute | solution.py:23
  196.4 21.0 %collective-permute-start.32 = (bf16[224,1024]{1,0:T(8,128)(2,1)S(1)}, bf16[224,1024]{1,0:T(8,128)(2,1)S(1)}, u32[]{:S(2)}, u32[]{:S(2)}) collective-permute-start(bf16[224,1024]{1,0:T(8,128)(2,1)S(1)} %get-tuple-element.183), channel_id=1, source_target_pairs={{0,8},{4,12},{8,0},{12,4},{16,24},{20,28},{24,16},{28,20},{1,9},{5... | collective-permute-start | bytes 1376264 | tf_op jit(solution)/shard_map/ppermute | solution.py:23
  218.2 9.9 %collective-permute-start.34 = (bf16[2,512,896]{2,1,0:T(8,128)(2,1)}, bf16[2,512,896]{2,1,0:T(8,128)(2,1)}, u32[]{:S(2)}, u32[]{:S(2)}) collective-permute-start(bf16[2,512,896]{2,1,0:T(8,128)(2,1)} %get-tuple-element.126), channel_id=1, source_target_pairs={{0,1},{1,0},{2,3},{3,2},{4,5},{5,4},{6,7},{7,6},{8,9},{9,8},{10,11... | collective-permute-start | bytes 5505032 | tf_op jit(solution)/shard_map/ppermute | solution.py:23
  225.3 92.4 %collective-permute-start.57 = (bf16[112,1536]{1,0:T(8,128)(2,1)}, bf16[112,1536]{1,0:T(8,128)(2,1)}, u32[]{:S(2)}, u32[]{:S(2)}) collective-permute-start(bf16[112,1536]{1,0:T(8,128)(2,1)} %pad_maximum_fusion.10), channel_id=1, source_target_pairs={{0,16},{4,20},{8,24},{12,28},{16,0},{20,4},{24,8},{28,12},{1,17},{... | collective-permute-start | bytes 1032200 | tf_op jit(solution)/shard_map/ppermute | solution.py:23
  226.9 93.1 %collective-permute-start.35 = (bf16[512,896]{1,0:T(8,128)(2,1)}, bf16[512,896]{1,0:T(8,128)(2,1)}, u32[]{:S(2)}, u32[]{:S(2)}) collective-permute-start(bf16[512,896]{1,0:T(8,128)(2,1)} %get-tuple-element.127), channel_id=1, source_target_pairs={{0,2},{1,3},{2,0},{3,1},{4,6},{5,7},{6,4},{7,5},{8,10},{9,11},{10,... | collective-permute-start | bytes 2752520 | tf_op jit(solution)/shard_map/ppermute | solution.py:23
  233.9 24.0 %collective-permute-start.36 = (bf16[512,896]{1,0:T(8,128)(2,1)S(1)}, bf16[512,896]{1,0:T(8,128)(2,1)S(1)}, u32[]{:S(2)}, u32[]{:S(2)}) collective-permute-start(bf16[512,896]{1,0:T(8,128)(2,1)S(1)} %get-tuple-element.146.refs_0_.own_ref), channel_id=1, source_target_pairs={{0,1},{1,0},{2,3},{3,2},{4,5},{5,4},{6,7},{7,6},{8,9},{9,8},{10,11... | collective-permute-start | bytes 2752520 | tf_op jit(solution)/shard_map/ppermute | solution.py:23
  255.1 29.1 %collective-permute-start.38 = (bf16[448,768]{1,0:T(8,128)(2,1)}, bf16[448,768]{1,0:T(8,128)(2,1)S(1)}, u32[]{:S(2)}, u32[]{:S(2)}) collective-permute-start(bf16[448,768]{1,0:T(8,128)(2,1)} %get-tuple-element.142), channel_id=1, source_target_pairs={{0,8},{4,12},{8,0},{12,4},{16,24},{20,28},{24,16},{28,20},{1,9},{5... | collective-permute-start | bytes 2064392 | tf_op jit(solution)/shard_map/ppermute | solution.py:23
  256.4 43.2 %collective-permute-start.37 = (bf16[448,1536]{1,0:T(8,128)(2,1)}, bf16[448,1536]{1,0:T(8,128)(2,1)}, u32[]{:S(2)}, u32[]{:S(2)}) collective-permute-start(bf16[448,1536]{1,0:T(8,128)(2,1)} %get-tuple-element.139), channel_id=1, source_target_pairs={{0,4},{4,0},{8,12},{12,8},{16,20},{20,16},{24,28},{28,24},{1,5},{5... | collective-permute-start | bytes 4128776 | tf_op jit(solution)/shard_map/ppermute | solution.py:23
  263.0 36.5 %collective-permute-start.39 = (bf16[448,512]{1,0:T(8,128)(2,1)S(1)}, bf16[448,512]{1,0:T(8,128)(2,1)S(1)}, u32[]{:S(2)}, u32[]{:S(2)}) collective-permute-start(bf16[448,512]{1,0:T(8,128)(2,1)S(1)} %get-tuple-element.144), channel_id=1, source_target_pairs={{0,4},{4,0},{8,12},{12,8},{16,20},{20,16},{24,28},{28,24},{1,5},{5... | collective-permute-start | bytes 1376264 | tf_op jit(solution)/shard_map/ppermute | solution.py:23
  285.2 33.4 %collective-permute-start.41 = (bf16[224,768]{1,0:T(8,128)(2,1)}, bf16[224,768]{1,0:T(8,128)(2,1)S(1)}, u32[]{:S(2)}, u32[]{:S(2)}) collective-permute-start(bf16[224,768]{1,0:T(8,128)(2,1)} %get-tuple-element.186), channel_id=1, source_target_pairs={{0,4},{4,0},{8,12},{12,8},{16,20},{20,16},{24,28},{28,24},{1,5},{5... | collective-permute-start | bytes 1032200 | tf_op jit(solution)/shard_map/ppermute | solution.py:23
  317.7 8.6 %collective-permute-start.42 = (bf16[224,512]{1,0:T(8,128)(2,1)S(1)}, bf16[224,512]{1,0:T(8,128)(2,1)S(1)}, u32[]{:S(2)}, u32[]{:S(2)}) collective-permute-start(bf16[224,512]{1,0:T(8,128)(2,1)S(1)} %get-tuple-element.196), channel_id=1, source_target_pairs={{0,8},{4,12},{8,0},{12,4},{16,24},{20,28},{24,16},{28,20},{1,9},{5... | collective-permute-start | bytes 688136 | tf_op jit(solution)/shard_map/ppermute | solution.py:23
  318.5 31.3 %collective-permute-start.40 = (bf16[224,1536]{1,0:T(8,128)(2,1)}, bf16[224,1536]{1,0:T(8,128)(2,1)}, u32[]{:S(2)}, u32[]{:S(2)}) collective-permute-start(bf16[224,1536]{1,0:T(8,128)(2,1)} %get-tuple-element.180), channel_id=1, source_target_pairs={{0,8},{4,12},{8,0},{12,4},{16,24},{20,28},{24,16},{28,20},{1,9},{5... | collective-permute-start | bytes 2064392 | tf_op jit(solution)/shard_map/ppermute | solution.py:23
  323.8 21.7 %collective-permute-start.49 = (bf16[448,576]{1,0:T(8,128)(2,1)S(1)}, bf16[448,576]{1,0:T(8,128)(2,1)}, u32[]{:S(2)}, u32[]{:S(2)}) collective-permute-start(bf16[448,576]{1,0:T(8,128)(2,1)S(1)} %get-tuple-element.158), channel_id=1, source_target_pairs={{0,4},{4,0},{8,12},{12,8},{16,20},{20,16},{24,28},{28,24},{1,5},{5... | collective-permute-start | bytes 1548296 | tf_op jit(solution)/shard_map/ppermute | solution.py:23
  326.3 12.9 %collective-permute-start.54 = (bf16[112,512]{1,0:T(8,128)(2,1)S(1)}, bf16[112,512]{1,0:T(8,128)(2,1)S(1)}, u32[]{:S(2)}, u32[]{:S(2)}) collective-permute-start(bf16[112,512]{1,0:T(8,128)(2,1)S(1)} %fusion.54), channel_id=1, source_target_pairs={{0,16},{4,20},{8,24},{12,28},{16,0},{20,4},{24,8},{28,12},{1,17},{... | collective-permute-start | bytes 344072 | tf_op jit(solution)/shard_map/ppermute | solution.py:23
  339.4 4.1 collective-permute-start.55
  340.1 4.7 %collective-permute-start.56 = (bf16[112,224]{1,0:T(8,128)(2,1)S(1)}, bf16[112,224]{1,0:T(8,128)(2,1)S(1)}, u32[]{:S(2)}, u32[]{:S(2)}) collective-permute-start(bf16[112,224]{1,0:T(8,128)(2,1)S(1)} %get-tuple-element.213), channel_id=1, source_target_pairs={{0,1},{1,3},{2,0},{3,2},{4,5},{5,7},{6,4},{7,6},{8,9},{9,11},{10,8... | collective-permute-start | bytes 150536 | tf_op jit(solution)/shard_map/ppermute | solution.py:629
  346.7 9.4 %collective-permute-start.50 = (bf16[224,576]{1,0:T(8,128)(2,1)S(1)}, bf16[224,576]{1,0:T(8,128)(2,1)S(1)}, u32[]{:S(2)}, u32[]{:S(2)}) collective-permute-start(bf16[224,576]{1,0:T(8,128)(2,1)S(1)} %get-tuple-element.190), channel_id=1, source_target_pairs={{0,8},{4,12},{8,0},{12,4},{16,24},{20,28},{24,16},{28,20},{1,9},{5... | collective-permute-start | bytes 774152 | tf_op jit(solution)/shard_map/ppermute | solution.py:23
  356.1 20.4 %collective-permute-start.51 = (bf16[112,576]{1,0:T(8,128)(2,1)S(1)}, bf16[112,576]{1,0:T(8,128)(2,1)S(1)}, u32[]{:S(2)}, u32[]{:S(2)}) collective-permute-start(bf16[112,576]{1,0:T(8,128)(2,1)S(1)} %fusion.46), channel_id=1, source_target_pairs={{0,16},{4,20},{8,24},{12,28},{16,0},{20,4},{24,8},{28,12},{1,17},{... | collective-permute-start | bytes 387080 | tf_op jit(solution)/shard_map/ppermute | solution.py:23
  358.2 30.8 %collective-permute-start.58 = (bf16[112,2304]{1,0:T(8,128)(2,1)S(1)}, bf16[112,2304]{1,0:T(8,128)(2,1)S(1)}, u32[]{:S(2)}, u32[]{:S(2)}) collective-permute-start(bf16[112,2304]{1,0:T(8,128)(2,1)S(1)} %pad_maximum_fusion.7), channel_id=1, source_target_pairs={{0,16},{4,20},{8,24},{12,28},{16,0},{20,4},{24,8},{28,12},{1,17},{... | collective-permute-start | bytes 1548296 | tf_op jit(solution)/shard_map/ppermute | solution.py:23
  376.6 11.5 %collective-permute-start.52 = (bf16[112,288]{1,0:T(8,128)(2,1)S(1)}, bf16[112,288]{1,0:T(8,128)(2,1)S(1)}, u32[]{:S(2)}, u32[]{:S(2)}) collective-permute-start(bf16[112,288]{1,0:T(8,128)(2,1)S(1)} %get-tuple-element.210), channel_id=1, source_target_pairs={{0,0},{1,2},{2,1},{3,3},{4,4},{5,6},{6,5},{7,7},{8,8},{9,10},{10,9... | collective-permute-start | bytes 193544 | tf_op jit(solution)/shard_map/ppermute | solution.py:629
  377.3 10.9 %collective-permute-start.53 = (bf16[112,288]{1,0:T(8,128)(2,1)S(1)}, bf16[112,288]{1,0:T(8,128)(2,1)S(1)}, u32[]{:S(2)}, u32[]{:S(2)}) collective-permute-start(bf16[112,288]{1,0:T(8,128)(2,1)S(1)} %get-tuple-element.211), channel_id=1, source_target_pairs={{0,1},{1,3},{2,0},{3,2},{4,5},{5,7},{6,4},{7,6},{8,9},{9,11},{10,8... | collective-permute-start | bytes 193544 | tf_op jit(solution)/shard_map/ppermute | solution.py:629
  388.1 3.0 collective-permute-start.43
  394.4 2.3 collective-permute-start.44
  396.7 3.8 collective-permute-start.45
  400.5 3.8 collective-permute-start.46
  404.2 3.7 collective-permute-start.47
  407.9 4.6 %collective-permute-start.48 = (f32[23,128]{1,0:T(8,128)S(1)}, f32[23,128]{1,0:T(8,128)S(1)}, u32[]{:S(2)}, u32[]{:S(2)}) collective-permute-start(f32[23,128]{1,0:T(8,128)S(1)} %add.255), channel_id=1, source_target_pairs={{0,16},{4,20},{8,24},{12,28},{16,0},{20,4},{24,8},{28,12},{1,17},{... | collective-permute-start | bytes 35336 | tf_op jit(solution)/shard_map/ppermute | solution.py:23
  (69 other events, 503.8 us)

commit v5 on v4

--- a/solution.py
+++ b/solution.py
@@ -547,6 +547,7 @@
         self.bits = bits
         self.left = bits - 1
         self.pieces = [block]
+        self.sent = 0
         self.beside = []
 
     def ready(self, *earlier):
@@ -559,22 +560,28 @@
         return self.pieces[-1]
 
     def send(self, *earlier):
-        piece = self.pieces[len(self.beside)]
+        piece = self.pieces[self.sent]
+        self.sent += 1
         self.beside.append(flip(after(piece, *earlier) if earlier else piece, "row", 0))
+        return self.beside[-1]
+
+    def catch_up(self, *earlier):
+        rest = jnp.concatenate(self.pieces[self.sent :], 0)
+        self.sent = len(self.pieces)
+        self.beside.append(flip(after(rest, *earlier), "row", 0))
         return self.beside[-1]
 
     def finish(self, *earlier):
         while self.left > 0:
             self.double()
-        rest = jnp.concatenate(self.pieces[len(self.beside) :], 0)
-        self.beside.append(flip(after(rest, *earlier), "row", 0))
+        self.catch_up(*earlier)
         out = self.pieces + self.beside
         return out if out[0].shape[0] % 16 == 0 else [jnp.concatenate(out, 0)]
 
     def all(self):
         while self.left > 0:
             self.double()
-        while len(self.beside) < self.bits:
+        while self.sent < len(self.pieces):
             self.send()
         out = self.pieces + self.beside
         return out if out[0].shape[0] % 16 == 0 else [jnp.concatenate(out, 0)]
@@ -693,12 +700,13 @@
     masks = jnp.array([bit_reversed(p, bits) for p in range(row_count)], jnp.int32)
     source = jnp.repeat(masks ^ row, deep) * deep + place % deep
     to_stored = (place[:, None] == source[None, :]).astype(bf16)
+    from_stored = (source[:, None] == place[None, :]).astype(bf16)
 
     def stored(block):
         return jnp.dot(block, to_stored, preferred_element_type=f32)
 
     def unstored(block):
-        return jnp.einsum("ts,fs->tf", block, to_stored, preferred_element_type=f32).astype(bf16)
+        return jnp.dot(block, from_stored, preferred_element_type=f32).astype(bf16)
 
     def unstored_row(vector):
         blocks = vector.reshape(row_count, deep)
@@ -711,7 +719,7 @@
             blocks = jnp.where((row >> bit) % 2 == 1, turned, blocks)
         return blocks.reshape(model_width)
 
-    input_rows = stored(layer_input)
+    input_rows = stored(after(layer_input, first, second))
     grad_out = stored(cotangent)
     gain_one = stored(gain_attn[None, :])
     gain_two = stored(gain_mlp[None, :])
@@ -725,12 +733,12 @@
     near, far = mlp_gathers
     n_four = near.double()
     n_own = near.send()
-    a_own = qkv_gather.send(n_own)
-    a_four = qkv_gather.double(n_own)
-    a_two = qkv_gather.double(a_own, n_four)
+    a_own = qkv_gather.send()
+    a_four = qkv_gather.double()
+    a_two = qkv_gather.double(a_own)
     a_beside = qkv_gather.send(a_own)
     o_four = out_gather.double(a_four)
-    a_last = qkv_gather.send(a_beside)
+    a_last = qkv_gather.send(a_beside, n_own)
     qkv_pieces = qkv_gather.all()
     far.ready(a_two, o_four)
     f_four = far.double()
@@ -760,9 +768,8 @@
     blocks.append(flip(after(blocks[0], n_last), "col", 0))
     blocks += [across, flip(across, "col", 0)]
 
-    f_own = far.send(n_last)
-    f_two = far.double(blocks[0])
-    f_beside = far.send(f_own)
+    f_beside = far.catch_up(n_last)
+    f_two = far.double(blocks[2])
     f_last = far.send(f_beside)
     first_pieces, second_pieces = (gather.all() for gather in mlp_gathers)
     act_own, *sums_own = mlp([after(blocks[0], blocks[2]), blocks[1]], grad_blocks[:2], first_pieces)
@@ -802,17 +809,19 @@
     gain_two_grad = jnp.sum(grad_normed_two * middle * scale_two[:, None], axis=0)
     branch_own = grad_middle.astype(bf16)
     branch_other = flip(branch_own, "col", 0)
+    out_scatter = Scatter([outer_one([branch_own, branch_other], att_rows)], bits)
     sent_one, kept_one, sent_two, kept_two = outer(
-        [after(blocks[0], branch_own, *first_scatter.kept), *blocks[1:]],
+        [after(blocks[0], out_scatter.kept[0], *first_scatter.kept), *blocks[1:]],
         grad_blocks,
         [act_own, act_far],
     )
     second_scatter = Scatter([(sent_one, kept_one), (sent_two, kept_two)], bits)
-    out_scatter = Scatter([outer_one([after(branch_own, kept_one), branch_other], att_rows)], bits)
+    out_scatter.wait(kept_one)
+    out_scatter.step()
     split = qk_rows.shape[1] // 256
     mixed_first, bias_first, *carry = attend_back(
         parity,
-        after(branch_own, out_scatter.kept[0]),
+        after(branch_own, kept_one, out_scatter.kept[0]),
         branch_other,
         out_pieces,
         qk_rows,
@@ -823,13 +832,10 @@
         0,
         split,
     )
-    second_scatter.wait(mixed_first)
     out_scatter.wait(mixed_first)
-    second_scatter.step()
-    out_scatter.step()
     mixed_last, bias_last = attend_back(
         parity,
-        after(branch_own, *second_scatter.kept, out_scatter.kept[0]),
+        after(branch_own, mixed_first),
         branch_other,
         out_pieces,
         qk_rows,
@@ -846,13 +852,13 @@
     second_scatter.wait(mixed_last)
     out_scatter.wait(mixed_last)
     grad_mixed = jnp.concatenate([mixed_first, mixed_last], 1)
-    passed = [*second_scatter.got, *out_scatter.got]
     second_scatter.step()
+    layer_output = unstored((middle + summed(1, after(down_back, grad_mixed))).astype(bf16))
+    qkv_scatter = Scatter([outer_one([normed_own, normed_other], after(grad_mixed, second_scatter.kept[0]))], bits)
+    qkv_full = jnp.concatenate(qkv_pieces, 0)
+    grad_mixed = after(grad_mixed, qkv_scatter.kept[0])
+    out_scatter.wait(qkv_scatter.kept[0])
     out_scatter.step()
-    layer_output = unstored((middle + summed(1, after(down_back, grad_mixed))).astype(bf16))
-    qkv_scatter = Scatter([outer_one([normed_own, normed_other], grad_mixed)], bits)
-    qkv_full = jnp.concatenate(qkv_pieces, 0)
-    grad_mixed = after(grad_mixed, qkv_scatter.kept[0], *passed)
     partial = jnp.einsum("tc,dc->td", grad_mixed, qkv_full, preferred_element_type=f32)
     grad_normed_one = partial[:tok_local] + flip(
         partial[tok_local:].astype(bf16), "col", 0
@@ -875,6 +881,17 @@
         )
         return first.astype(f32) + second.astype(f32)
 
+    bias_row = lax.dynamic_update_slice_in_dim(
+        jnp.zeros((group_width * 2,), f32), bias_grad, core * group_width, 0
+    )
+    small = jnp.concatenate([unstored_row(gain_one_grad), unstored_row(gain_two_grad), bias_row])
+    small = jnp.pad(small, (0, -small.shape[0] % 128)).reshape(-1, 128)
+    small = after(small, *second_scatter.got)
+    second_scatter.step()
+    for bit in range(2):
+        small = small + flip(small, "col", bit)
+    for bit in range(bits):
+        small = small + flip(small, "row", bit)
     qkv_total = to_columns(qkv_scatter.total(), qkv_cols)
     out_total = to_columns(out_scatter.total(), out_cols)
     mlp_totals = []
@@ -885,15 +902,6 @@
             [total[:, k * padded : k * padded + stop - start] for k in range(3)]
         )
     gate_total, up_total, down_total = (jnp.concatenate(parts, 1) for parts in zip(*mlp_totals))
-    bias_row = lax.dynamic_update_slice_in_dim(
-        jnp.zeros((group_width * 2,), f32), bias_grad, core * group_width, 0
-    )
-    small = jnp.concatenate([unstored_row(gain_one_grad), unstored_row(gain_two_grad), bias_row])
-    small = jnp.pad(small, (0, -small.shape[0] % 128)).reshape(-1, 128)
-    for bit in range(2):
-        small = small + flip(small, "col", bit)
-    for bit in range(bits):
-        small = small + flip(small, "row", bit)
     small = small.reshape(-1)
     gain_one_total = small[:model_width]
     gain_two_total = small[model_width : 2 * model_width]

time: 422 us -> 405 us (0.960)
  waiting for transfers between devices: 99.3 us -> 79.4 us
    ppermute x53 -> x52, waiting for transfers between devices: 98 us -> 79.3 us  [flip(): return lax.ppermute(block, axis, [(i, i ^ 1 << bit) for i in range(count)])]
    unnamed x155 -> x168, local copies, waits for them, and re-layouts: 17.1 us -> 18.4 us
    ppermute x53 -> x52, starting transfers between devices: 53.4 us -> 53.5 us  [flip(): return lax.ppermute(block, axis, [(i, i ^ 1 << bit) for i in range(count)])]
  transfers between devices with their start and end apart: 59 -> 58, of which waited for: 17 -> 15; matrix products, arithmetic and copies ran while one was open for 16% -> 19% of each run, Pallas kernels for 38% -> 40%
where the time goes in v5:
time: 405 us; the launch traced here: 398 us
  Pallas kernels  161 us (40%)
  waiting for transfers between devices  79.4 us (20%)
  starting transfers between devices  63.3 us (16%)
  other arithmetic  39.2 us (10%)
  local copies, waits for them, and re-layouts  34.3 us (8%)
  matrix products  18.6 us (5%)
    ppermute x52, waiting for transfers between devices, flip(): return lax.ppermute(block, axis, [(i, i ^ 1 << bit) for i in range(count)])  79.3 us
    pallas_call x4, Pallas kernels, mlp(): pl.pallas_call(functools.partial(mlp_kernel, count=len(pieces), add=add),...  68.4 us
    ppermute x52, starting transfers between devices, flip(): return lax.ppermute(block, axis, [(i, i ^ 1 << bit) for i in range(count)])  53.5 us
    pallas_call x2, Pallas kernels, attend_back(): pl.pallas_call(functools.partial(attend_back_kernel, block=block, count=l...  33 us
    pallas_call x2, Pallas kernels, outer(): pl.pallas_call(functools.partial(outer_kernel, blocks=len(rows)), grid=(3...  31.7 us
    pallas_call x1, Pallas kernels, attend(): pl.pallas_call(functools.partial(attend_kernel, block=block, count=len(pi...  19.9 us
    unnamed x168, local copies, waits for them, and re-layouts  18.4 us
    dot_general x2, matrix products, unstored(): return jnp.dot(block, from_stored, preferred_element_type=f32).astype(bf16)  9.71 us
  transfers between devices with their start and end apart: 58, of which 15 were waited for; matrix products, arithmetic and copies ran while one was open for 19% of the time, Pallas kernels for 40%

profile of v5, /device:TPU:0, one launch (start us, length us, event | category | flops | bytes accessed | tf_op | source)
XLA Modules:
  0.0 397.7 jit_solution(7279806855545343705)
XLA Ops:
  3.5 3.0 collective-permute-start.1
  10.8 2.6 collective-permute-start.9
  13.4 1.5 collective-permute-start.7
  15.1 2.0 fusion.49
  17.1 2.8 bitcast_convert_fusion
  23.3 1.3 multiply_reduce_fusion.5
  25.4 10.6 %collective-permute-done.3.rest_1_ = bf16[112,576]{1,0:T(8,128)(2,1)S(1)} collective-permute-done((bf16[112,576]{1,0:T(8,128)(2,1)S(1)}, bf16[112,576]{1,0:T(8,128)(2,1)S(1)}, u32[]{:S(2)}, u32[]{:S(2)}) %collective-permute-start.3) | collective-permute-done | bytes 129056 | tf_op jit(solution)/shard_map/ppermute | solution.py:23
  37.4 4.3 %collective-permute-start.5 = (bf16[224,576]{1,0:T(8,128)(2,1)}, bf16[224,576]{1,0:T(8,128)(2,1)S(1)}, u32[]{:S(2)}, u32[]{:S(2)}) collective-permute-start(bf16[224,576]{1,0:T(8,128)(2,1)} %pad_maximum_fusion.10), channel_id=1, source_target_pairs={{0,8},{4,12},{8,0},{12,4},{16,24},{20,28},{24,16},{28,20},{1,9},{5... | collective-permute-start | bytes 774152 | tf_op jit(solution)/shard_map/ppermute | solution.py:23
  42.7 2.0 collective-permute-done.11.rest_1_
  44.7 1.5 collective-permute-start.6
  46.3 3.8 collective-permute-done.5.rest_2_
  50.6 1.5 collective-permute-start.8
  53.3 2.1 collective-permute-start.15
  55.4 4.4 %collective-permute-done.12.rest_2_ = bf16[224,512]{1,0:T(8,128)(2,1)S(1)} collective-permute-done((bf16[224,512]{1,0:T(8,128)(2,1)S(1)}, bf16[224,512]{1,0:T(8,128)(2,1)S(1)}, u32[]{:S(2)}, u32[]{:S(2)}) %collective-permute-start.12) | collective-permute-done | bytes 229408 | tf_op jit(solution)/shard_map/ppermute | solution.py:23
  59.8 2.0 collective-permute-start.10
  62.8 19.9 %shard_map.186 = (bf16[1024,512]{1,0:T(8,128)(2,1)S(1)}, bf16[1024,64]{1,0:T(8,128)(2,1)S(1)}, bf16[1024,512]{1,0:T(8,128)(2,1)S(1)}, f32[8,1024]{1,0:T(8,128)S(1)}) custom-call(s32[1]{0:T(128)} %bitcast.1.parity_ref, bf16[512,896]{1,0:T(8,128)(2,1)S(1)} %multiply_convert_fusion.1.own_ref.refs_0_, bf16[512,896]{1,0:T(8,128)(2,1)} %collective-permute-done.2.other_ref.refs_1_, ...), custom_call_target="tpu_custom_call" | custom-call | flops 12000000000 | bytes 8000000 | tf_op jit(solution)/shard_map/pallas_call | solution.py:159
  83.9 2.2 shard_map.187
  86.9 2.1 collective-permute-start.19
  91.0 1.7 collective-permute-start.18
  92.7 12.4 %collective-permute-done.19.rest_5_ = bf16[224,1536]{1,0:T(8,128)(2,1)S(1)} collective-permute-done((bf16[224,1536]{1,0:T(8,128)(2,1)S(1)}, bf16[224,1536]{1,0:T(8,128)(2,1)S(1)}, u32[]{:S(2)}, u32[]{:S(2)}) %collective-permute-start.19) | collective-permute-done | bytes 688160 | tf_op jit(solution)/shard_map/ppermute | solution.py:23
  107.3 1.7 collective-permute-start.25
  109.0 4.5 %collective-permute-done.18.x0_ref.refs_2_ = bf16[512,896]{1,0:T(8,128)(2,1)} collective-permute-done((bf16[512,896]{1,0:T(8,128)(2,1)S(1)}, bf16[512,896]{1,0:T(8,128)(2,1)}, u32[]{:S(2)}, u32[]{:S(2)}) %collective-permute-start.18) | collective-permute-done | bytes 917536 | tf_op jit(solution)/shard_map/ppermute | solution.py:23
  113.6 1.9 collective-permute-start.24
  117.0 13.9 %shard_map.188 = (bf16[1024,1536]{1,0:T(8,128)(2,1)}, bf16[2,512,896]{2,1,0:T(8,128)(2,1)}, bf16[2,512,896]{2,1,0:T(8,128)(2,1)}) custom-call(bf16[512,896]{1,0:T(8,128)(2,1)} %copy-done.43, bf16[512,896]{1,0:T(8,128)(2,1)} %copy-done.73, bf16[512,896]{1,0:T(8,128)(2,1)} %get-tuple-element.102.g0_ref.refs_4_, ...), custom_call_target="tpu_custom_call" | custom-call | flops 5637144576 | bytes 31457280 | tf_op jit(solution)/shard_map/pallas_call | solution.py:436
  130.9 1.5 collective-permute-done.25.rest_3_
  132.4 5.8 %collective-permute-done.24.rest_2_ = bf16[224,2304]{1,0:T(8,128)(2,1)} collective-permute-done((bf16[224,2304]{1,0:T(8,128)(2,1)}, bf16[224,2304]{1,0:T(8,128)(2,1)}, u32[]{:S(2)}, u32[]{:S(2)}) %collective-permute-start.24) | collective-permute-done | bytes 1032224 | tf_op jit(solution)/shard_map/ppermute | solution.py:23
  138.2 1.6 collective-permute-start.26
  139.7 14.2 %shard_map.189 = (bf16[1024,1536]{1,0:T(8,128)(2,1)}, bf16[2,512,896]{2,1,0:T(8,128)(2,1)}, bf16[2,512,896]{2,1,0:T(8,128)(2,1)}) custom-call(bf16[512,896]{1,0:T(8,128)(2,1)} %collective-permute-done.18.x0_ref.refs_2_, bf16[512,896]{1,0:T(8,128)(2,1)} %collective-permute-done.21.x1_ref.refs_3_, bf16[512,896]{1,0:T(8,128)(2,1)} %collective-permute-done.14.g0_ref.refs_6_, ...), custom_call_target="tpu_custom_call" | custom-call | flops 5637144576 | bytes 31457280 | tf_op jit(solution)/shard_map/pallas_call | solution.py:436
  154.0 15.4 %shard_map.190 = (bf16[448,1024]{1,0:T(8,128)(2,1)}, f32[448,1024]{1,0:T(8,128)}, bf16[448,512]{1,0:T(8,128)(2,1)}, f32[448,512]{1,0:T(8,128)}) custom-call(bf16[512,896]{1,0:T(8,128)(2,1)} %copy-done.43, bf16[512,896]{1,0:T(8,128)(2,1)} %copy-done.73, bf16[512,896]{1,0:T(8,128)(2,1)} %collective-permute-done.18.x0_ref.refs_2_, ...), custom_call_target="tpu_custom_call" | custom-call | flops 5637144576 | bytes 20971520 | tf_op jit(solution)/shard_map/pallas_call | solution.py:500
  169.9 1.7 collective-permute-start.28
  171.6 20.1 %shard_map.191 = (bf16[1024,2304]{1,0:T(8,128)(2,1)}, bf16[2,512,896]{2,1,0:T(8,128)(2,1)}, bf16[2,512,896]{2,1,0:T(8,128)(2,1)}) custom-call(bf16[512,896]{1,0:T(8,128)(2,1)} %collective-permute-done.18.x0_ref.refs_2_, bf16[512,896]{1,0:T(8,128)(2,1)} %collective-permute-done.21.x1_ref.refs_3_, bf16[512,896]{1,0:T(8,128)(2,1)} %collective-permute-done.14.g0_ref.refs_6_, ...), custom_call_target="tpu_custom_call" | custom-call | flops 8455716864 | bytes 31457280 | tf_op jit(solution)/shard_map/pallas_call | solution.py:436
  192.0 1.6 collective-permute-start.32
  193.6 2.2 collective-permute-done.29
  197.4 1.7 collective-permute-start.30
  200.7 20.2 %shard_map.192 = (bf16[1024,2304]{1,0:T(8,128)(2,1)}, bf16[2,512,896]{2,1,0:T(8,128)(2,1)}, bf16[2,512,896]{2,1,0:T(8,128)(2,1)}) custom-call(bf16[512,896]{1,0:T(8,128)(2,1)} %copy-done.43, bf16[512,896]{1,0:T(8,128)(2,1)} %copy-done.73, bf16[512,896]{1,0:T(8,128)(2,1)} %get-tuple-element.102.g0_ref.refs_4_, ...), custom_call_target="tpu_custom_call" | custom-call | flops 8455716864 | bytes 31457280 | tf_op jit(solution)/shard_map/pallas_call | solution.py:436
  225.2 1.8 slice_add_fusion.13
  228.7 1.7 collective-permute-start.56
  231.2 2.3 multiply_reduce_fusion
  233.6 4.8 %fusion.61 = (bf16[512,896]{1,0:T(8,128)(2,1)S(1)}, f32[512,896]{1,0:T(8,128)}) fusion(f32[512,896]{1,0:T(8,128)} %copy-done.21, f32[512]{0:T(512)S(1)} %fusion.58, bf16[512,896]{1,0:T(8,128)(2,1)} %collective-permute-done.30, bf16[2,512,896]{2,1,0:T(8,128)(2,1)} %collective-permute-done.33, bf16[2,512,896]{2,1,0:T(8,128)(2,1)} %get-tuple-element.122, ...), kind=kLoop, calls=%fused_computation.189 | loop fusion | flops 5046272 | bytes 9182720 | tf_op jit(solution)/shard_map/convert_element_type | solution.py:810
  245.4 1.7 shard_map.193
  247.1 2.3 collective-permute-start.36
  249.4 16.3 %shard_map.194 = (bf16[448,1536]{1,0:T(8,128)(2,1)}, f32[448,1536]{1,0:T(8,128)}, bf16[448,768]{1,0:T(8,128)(2,1)}, f32[448,768]{1,0:T(8,128)}) custom-call(bf16[512,896]{1,0:T(8,128)(2,1)} %copy-done.43, bf16[512,896]{1,0:T(8,128)(2,1)} %copy-done.73, bf16[512,896]{1,0:T(8,128)(2,1)} %collective-permute-done.18.x0_ref.refs_2_, ...), custom_call_target="tpu_custom_call" | custom-call | flops 8455716864 | bytes 20971520 | tf_op jit(solution)/shard_map/pallas_call | solution.py:500
  265.8 1.3 collective-permute-start.40
  268.9 17.9 %shard_map.195 = (bf16[1024,256]{1,0:T(8,128)(2,1)S(1)}, f32[1,256]{1,0:T(1,128)S(1)}, f32[1024,128]{1,0:T(8,128)S(1)}, f32[1024,128]{1,0:T(8,128)S(1)}) custom-call(s32[1]{0:T(128)} %bitcast.1.parity_ref, bf16[512,896]{1,0:T(8,128)(2,1)} %copy-done.2, bf16[512,896]{1,0:T(8,128)(2,1)} %copy-done.12, bf16[1024,512]{1,0:T(8,128)(2,1)} %copy-done.18, ...), custom_call_target="tpu_custom_call" | custom-call | flops 12000000000 | bytes 6000000 | tf_op jit(solution)/shard_map/pallas_call | solution.py:352
  286.9 15.1 %shard_map.196 = (bf16[1024,320]{1,0:T(8,128)(2,1)S(1)}, f32[1,320]{1,0:T(1,128)S(1)}) custom-call(s32[1]{0:T(128)} %bitcast.1.parity_ref, bf16[512,896]{1,0:T(8,128)(2,1)} %copy-done.2, bf16[512,896]{1,0:T(8,128)(2,1)} %copy-done.12, bf16[1024,512]{1,0:T(8,128)(2,1)} %copy-done.18, bf16[1024,64]{1,0:T(8,128)(2,1)S(1)} %copy-done.20, ...), custom_call_target="tpu_custom_call" | custom-call | flops 12000000000 | bytes 6000000 | tf_op jit(solution)/shard_map/pallas_call | solution.py:352
  303.8 4.7 %fusion.15 = bf16[512,896]{1,0:T(8,128)(2,1)} fusion(s32[896]{0:T(1024)S(1)} %copy-done.68, f32[512,896]{1,0:T(8,128)} %copy-done.21, bf16[512,896]{1,0:T(8,128)(2,1)} %collective-permute-done.34, bf16[2,512,896]{2,1,0:T(8,128)(2,1)} %collective-permute-done.33, bf16[2,512,896]{2,1,0:T(8,128)(2,1)} %get-tuple-element.122), kind=kOutput, calls=%fused_computation.36 | convolution fusion | flops 826556416 | bytes 5508608 | tf_op jit(solution)/shard_map/dot_general | solution.py:709
  310.1 1.5 convert_add_fusion.3
  311.6 2.1 collective-permute-start.41
  313.7 3.0 add_convert_fusion.1
  316.7 3.7 shard_map.197
  322.5 1.8 collective-permute-start.39
  325.0 3.0 collective-permute-done.53
  328.7 2.6 collective-permute-start.55
  331.4 3.5 fusion.71
  334.9 2.5 slice.700
  339.0 1.7 collective-permute-done.39
  340.7 2.1 fusion.29
  344.8 5.0 %collective-permute-done.48 = bf16[224,576]{1,0:T(8,128)(2,1)S(1)} collective-permute-done((bf16[224,576]{1,0:T(8,128)(2,1)S(1)}, bf16[224,576]{1,0:T(8,128)(2,1)S(1)}, u32[]{:S(2)}, u32[]{:S(2)}) %collective-permute-start.48) | collective-permute-done | bytes 258080 | tf_op jit(solution)/shard_map/ppermute | solution.py:23
  350.6 3.0 multiply_reduce_fusion.1
  355.4 19.1 %collective-permute-done.49 = bf16[112,576]{1,0:T(8,128)(2,1)S(1)} collective-permute-done((bf16[112,576]{1,0:T(8,128)(2,1)S(1)}, bf16[112,576]{1,0:T(8,128)(2,1)S(1)}, u32[]{:S(2)}, u32[]{:S(2)}) %collective-permute-start.49) | collective-permute-done | bytes 129056 | tf_op jit(solution)/shard_map/ppermute | solution.py:23
  376.6 2.2 collective-permute-start.51
  380.2 2.4 collective-permute-done.44
  382.6 5.0 %fusion.16 = bf16[512,896]{1,0:T(8,128)(2,1)} fusion(s32[896]{0:T(1024)} %copy-done.67, f32[512,896]{1,0:T(8,128)S(1)} %copy-done.25, f32[512,896]{1,0:T(8,128)} %get-tuple-element.177, f32[512]{0:T(512)S(1)} %fusion.60, f32[896]{0:T(1024)S(1)} %copy-done.65, f32[512]{0:T(512)S(1)} %copy-done.60, f32[1024,896]{1,0:T(8,128)} %fusion.71, ...), kind=kOutput, calls=%fused_computation.37 | convolution fusion | flops 827015168 | bytes 7351808 | tf_op jit(solution)/shard_map/dot_general | solution.py:709
  387.6 3.4 collective-permute-start.46
  (354 shorter events, 66.0 us)
Async XLA Ops:
  3.5 17.9 %collective-permute-start.1 = (bf16[128,512]{1,0:T(8,128)(2,1)S(1)}, bf16[128,512]{1,0:T(8,128)(2,1)S(1)}, u32[]{:S(2)}, u32[]{:S(2)}) collective-permute-start(bf16[128,512]{1,0:T(8,128)(2,1)S(1)} %fusion.50), channel_id=1, source_target_pairs={{0,2},{1,0},{2,3},{3,1},{4,6},{5,4},{6,7},{7,5},{8,10},{9,8},{10,1... | collective-permute-start | bytes 393224 | tf_op jit(solution)/shard_map/ppermute | solution.py:630
  6.5 14.9 %collective-permute-start = (bf16[128,512]{1,0:T(8,128)(2,1)S(1)}, bf16[128,512]{1,0:T(8,128)(2,1)S(1)}, u32[]{:S(2)}, u32[]{:S(2)}) collective-permute-start(bf16[128,512]{1,0:T(8,128)(2,1)S(1)} %fusion.50), channel_id=1, source_target_pairs={{0,0},{1,2},{2,1},{3,3},{4,4},{5,6},{6,5},{7,7},{8,8},{9,10},{10,9... | collective-permute-start | bytes 393224 | tf_op jit(solution)/shard_map/ppermute | solution.py:630
  10.8 41.4 %collective-permute-start.9 = (bf16[112,1536]{1,0:T(8,128)(2,1)}, bf16[112,1536]{1,0:T(8,128)(2,1)}, u32[]{:S(2)}, u32[]{:S(2)}) collective-permute-start(bf16[112,1536]{1,0:T(8,128)(2,1)} %pad_maximum_fusion.8.rest_0_), channel_id=1, source_target_pairs={{0,16},{4,20},{8,24},{12,28},{16,0},{20,4},{24,8},{28,12},{1,17},{... | collective-permute-start | bytes 1032200 | tf_op jit(solution)/shard_map/ppermute | solution.py:23
  13.4 36.7 %collective-permute-start.7 = (bf16[112,1536]{1,0:T(8,128)(2,1)}, bf16[112,1536]{1,0:T(8,128)(2,1)}, u32[]{:S(2)}, u32[]{:S(2)}) collective-permute-start(bf16[112,1536]{1,0:T(8,128)(2,1)} %pad_maximum_fusion.8.rest_0_), channel_id=1, source_target_pairs={{0,4},{4,0},{8,12},{12,8},{16,20},{20,16},{24,28},{28,24},{1,5},{5... | collective-permute-start | bytes 1032200 | tf_op jit(solution)/shard_map/ppermute | solution.py:23
  15.1 71.1 %copy-start.67 = (s32[896]{0:T(1024)}, s32[896]{0:T(1024)S(1)}, u32[]{:S(2)}) copy-start(s32[896]{0:T(1024)S(1)} %fusion.53) | copy-start | bytes 10756
  22.4 14.3 %collective-permute-start.4 = (bf16[112,576]{1,0:T(8,128)(2,1)S(1)}, bf16[112,576]{1,0:T(8,128)(2,1)S(1)}, u32[]{:S(2)}, u32[]{:S(2)}) collective-permute-start(bf16[112,576]{1,0:T(8,128)(2,1)S(1)} %get-tuple-element.175.rest_0_), channel_id=1, source_target_pairs={{0,4},{4,0},{8,12},{12,8},{16,20},{20,16},{24,28},{28,24},{1,5},{5... | collective-permute-start | bytes 387080 | tf_op jit(solution)/shard_map/ppermute | solution.py:23
  23.0 13.0 %collective-permute-start.3 = (bf16[112,576]{1,0:T(8,128)(2,1)S(1)}, bf16[112,576]{1,0:T(8,128)(2,1)S(1)}, u32[]{:S(2)}, u32[]{:S(2)}) collective-permute-start(bf16[112,576]{1,0:T(8,128)(2,1)S(1)} %get-tuple-element.175.rest_0_), channel_id=1, source_target_pairs={{0,16},{4,20},{8,24},{12,28},{16,0},{20,4},{24,8},{28,12},{1,17},{... | collective-permute-start | bytes 387080 | tf_op jit(solution)/shard_map/ppermute | solution.py:23
  24.9 36.9 %collective-permute-start.2 = (bf16[512,896]{1,0:T(8,128)(2,1)S(1)}, bf16[512,896]{1,0:T(8,128)(2,1)}, u32[]{:S(2)}, u32[]{:S(2)}) collective-permute-start(bf16[512,896]{1,0:T(8,128)(2,1)S(1)} %multiply_convert_fusion.1.own_ref.refs_0_), channel_id=1, source_target_pairs={{0,1},{1,0},{2,3},{3,2},{4,5},{5,4},{6,7},{7,6},{8,9},{9,8},{10,11... | collective-permute-start | bytes 2752520 | tf_op jit(solution)/shard_map/ppermute | solution.py:23
  36.0 8.7 %collective-permute-start.11 = (bf16[112,512]{1,0:T(8,128)(2,1)S(1)}, bf16[112,512]{1,0:T(8,128)(2,1)S(1)}, u32[]{:S(2)}, u32[]{:S(2)}) collective-permute-start(bf16[112,512]{1,0:T(8,128)(2,1)S(1)} %fusion.52.rest_0_), channel_id=1, source_target_pairs={{0,16},{4,20},{8,24},{12,28},{16,0},{20,4},{24,8},{28,12},{1,17},{... | collective-permute-start | bytes 344072 | tf_op jit(solution)/shard_map/ppermute | solution.py:23
  37.4 12.6 %collective-permute-start.5 = (bf16[224,576]{1,0:T(8,128)(2,1)}, bf16[224,576]{1,0:T(8,128)(2,1)S(1)}, u32[]{:S(2)}, u32[]{:S(2)}) collective-permute-start(bf16[224,576]{1,0:T(8,128)(2,1)} %pad_maximum_fusion.10), channel_id=1, source_target_pairs={{0,8},{4,12},{8,0},{12,4},{16,24},{20,28},{24,16},{28,20},{1,9},{5... | collective-permute-start | bytes 774152 | tf_op jit(solution)/shard_map/ppermute | solution.py:23
  42.6 40.1 %copy-start.3 = (f32[1024,128]{1,0:T(8,128)}, f32[1024,128]{1,0:T(8,128)S(1)}, u32[]{:S(2)}) copy-start(f32[1024,128]{1,0:T(8,128)S(1)} %get-tuple-element.252.sin_ref) | copy-start | bytes 1572868
  44.7 5.4 %collective-permute-start.6 = (bf16[112,576]{1,0:T(8,128)(2,1)S(1)}, bf16[112,576]{1,0:T(8,128)(2,1)S(1)}, u32[]{:S(2)}, u32[]{:S(2)}) collective-permute-start(bf16[112,576]{1,0:T(8,128)(2,1)S(1)} %collective-permute-done.3.rest_1_), channel_id=1, source_target_pairs={{0,4},{4,0},{8,12},{12,8},{16,20},{20,16},{24,28},{28,24},{1,5},{5... | collective-permute-start | bytes 387080 | tf_op jit(solution)/shard_map/ppermute | solution.py:23
  50.0 33.8 %collective-permute-start.14 = (bf16[512,896]{1,0:T(8,128)(2,1)}, bf16[512,896]{1,0:T(8,128)(2,1)}, u32[]{:S(2)}, u32[]{:S(2)}) collective-permute-start(bf16[512,896]{1,0:T(8,128)(2,1)} %get-tuple-element.102.g0_ref.refs_4_), channel_id=1, source_target_pairs={{0,2},{1,3},{2,0},{3,1},{4,6},{5,7},{6,4},{7,5},{8,10},{9,11},{10,... | collective-permute-start | bytes 2752520 | tf_op jit(solution)/shard_map/ppermute | solution.py:23
  50.1 32.7 %copy-start.10 = (bf16[112,576]{1,0:T(8,128)(2,1)}, bf16[112,576]{1,0:T(8,128)(2,1)S(1)}, u32[]{:S(2)}) copy-start(bf16[112,576]{1,0:T(8,128)(2,1)S(1)} %collective-permute-done.6.rest_4_) | copy-start | bytes 387076
  50.1 9.6 %collective-permute-start.12 = (bf16[224,512]{1,0:T(8,128)(2,1)S(1)}, bf16[224,512]{1,0:T(8,128)(2,1)S(1)}, u32[]{:S(2)}, u32[]{:S(2)}) collective-permute-start(bf16[224,512]{1,0:T(8,128)(2,1)S(1)} %pad_maximum_fusion.11), channel_id=1, source_target_pairs={{0,8},{4,12},{8,0},{12,4},{16,24},{20,28},{24,16},{28,20},{1,9},{5... | collective-permute-start | bytes 688136 | tf_op jit(solution)/shard_map/ppermute | solution.py:23
  50.6 9.1 %collective-permute-start.8 = (bf16[224,576]{1,0:T(8,128)(2,1)S(1)}, bf16[224,576]{1,0:T(8,128)(2,1)S(1)}, u32[]{:S(2)}, u32[]{:S(2)}) collective-permute-start(bf16[224,576]{1,0:T(8,128)(2,1)S(1)} %collective-permute-done.5.rest_2_), channel_id=1, source_target_pairs={{0,4},{4,0},{8,12},{12,8},{16,20},{20,16},{24,28},{28,24},{1,5},{5... | collective-permute-start | bytes 774152 | tf_op jit(solution)/shard_map/ppermute | solution.py:23
  53.3 30.5 %collective-permute-start.15 = (bf16[112,2304]{1,0:T(8,128)(2,1)}, bf16[112,2304]{1,0:T(8,128)(2,1)S(1)}, u32[]{:S(2)}, u32[]{:S(2)}) collective-permute-start(bf16[112,2304]{1,0:T(8,128)(2,1)} %fusion.33.rest_0_), channel_id=1, source_target_pairs={{0,16},{4,20},{8,24},{12,28},{16,0},{20,4},{24,8},{28,12},{1,17},{... | collective-permute-start | bytes 1548296 | tf_op jit(solution)/shard_map/ppermute | solution.py:23
  59.7 24.1 %collective-permute-start.13 = (bf16[224,1536]{1,0:T(8,128)(2,1)S(1)}, bf16[224,1536]{1,0:T(8,128)(2,1)S(1)}, u32[]{:S(2)}, u32[]{:S(2)}) collective-permute-start(bf16[224,1536]{1,0:T(8,128)(2,1)S(1)} %pad_maximum_fusion), channel_id=1, source_target_pairs={{0,8},{4,12},{8,0},{12,4},{16,24},{20,28},{24,16},{28,20},{1,9},{5... | collective-permute-start | bytes 2064392 | tf_op jit(solution)/shard_map/ppermute | solution.py:23
  59.8 24.1 %collective-permute-start.10 = (bf16[112,1536]{1,0:T(8,128)(2,1)}, bf16[112,1536]{1,0:T(8,128)(2,1)S(1)}, u32[]{:S(2)}, u32[]{:S(2)}) collective-permute-start(bf16[112,1536]{1,0:T(8,128)(2,1)} %collective-permute-done.9.rest_1_), channel_id=1, source_target_pairs={{0,4},{4,0},{8,12},{12,8},{16,20},{20,16},{24,28},{28,24},{1,5},{5... | collective-permute-start | bytes 1032200 | tf_op jit(solution)/shard_map/ppermute | solution.py:23
  61.8 22.1 %collective-permute-start.16 = (bf16[448,512]{1,0:T(8,128)(2,1)S(1)}, bf16[448,512]{1,0:T(8,128)(2,1)S(1)}, u32[]{:S(2)}, u32[]{:S(2)}) collective-permute-start(bf16[448,512]{1,0:T(8,128)(2,1)S(1)} %pad_maximum_fusion.7), channel_id=1, source_target_pairs={{0,4},{4,0},{8,12},{12,8},{16,20},{20,16},{24,28},{28,24},{1,5},{5... | collective-permute-start | bytes 1376264 | tf_op jit(solution)/shard_map/ppermute | solution.py:23
  86.1 2.9 collective-permute-start.17
  86.9 18.2 %collective-permute-start.19 = (bf16[224,1536]{1,0:T(8,128)(2,1)S(1)}, bf16[224,1536]{1,0:T(8,128)(2,1)S(1)}, u32[]{:S(2)}, u32[]{:S(2)}) collective-permute-start(bf16[224,1536]{1,0:T(8,128)(2,1)S(1)} %collective-permute-done.13.rest_2_), channel_id=1, source_target_pairs={{0,4},{4,0},{8,12},{12,8},{16,20},{20,16},{24,28},{28,24},{1,5},{5... | collective-permute-start | bytes 2064392 | tf_op jit(solution)/shard_map/ppermute | solution.py:23
  91.0 22.6 %collective-permute-start.18 = (bf16[512,896]{1,0:T(8,128)(2,1)S(1)}, bf16[512,896]{1,0:T(8,128)(2,1)}, u32[]{:S(2)}, u32[]{:S(2)}) collective-permute-start(bf16[512,896]{1,0:T(8,128)(2,1)S(1)} %multiply_convert_fusion.x0_ref.refs_0_), channel_id=1, source_target_pairs={{0,2},{1,3},{2,0},{3,1},{4,6},{5,7},{6,4},{7,5},{8,10},{9,11},{10,... | collective-permute-start | bytes 2752520 | tf_op jit(solution)/shard_map/ppermute | solution.py:23
  105.1 10.4 %collective-permute-start.20 = (bf16[512,896]{1,0:T(8,128)(2,1)S(1)}, bf16[512,896]{1,0:T(8,128)(2,1)S(1)}, u32[]{:S(2)}, u32[]{:S(2)}) collective-permute-start(bf16[512,896]{1,0:T(8,128)(2,1)S(1)} %multiply_convert_fusion.x0_ref.refs_0_), channel_id=1, source_target_pairs={{0,1},{1,0},{2,3},{3,2},{4,5},{5,4},{6,7},{7,6},{8,9},{9,8},{10,11... | collective-permute-start | bytes 2752520 | tf_op jit(solution)/shard_map/ppermute | solution.py:23
  105.1 11.9 %collective-permute-start.22 = (bf16[512,896]{1,0:T(8,128)(2,1)S(1)}, bf16[512,896]{1,0:T(8,128)(2,1)}, u32[]{:S(2)}, u32[]{:S(2)}) collective-permute-start(bf16[512,896]{1,0:T(8,128)(2,1)S(1)} %copy-done.72), channel_id=1, source_target_pairs={{0,1},{1,0},{2,3},{3,2},{4,5},{5,4},{6,7},{7,6},{8,9},{9,8},{10,11... | collective-permute-start | bytes 2752520 | tf_op jit(solution)/shard_map/ppermute | solution.py:23
  107.3 25.1 %collective-permute-start.25 = (bf16[224,2304]{1,0:T(8,128)(2,1)}, bf16[224,2304]{1,0:T(8,128)(2,1)}, u32[]{:S(2)}, u32[]{:S(2)}) collective-permute-start(bf16[224,2304]{1,0:T(8,128)(2,1)} %constant_dynamic-update-slice_fusion), channel_id=1, source_target_pairs={{0,4},{4,0},{8,12},{12,8},{16,20},{20,16},{24,28},{28,24},{1,5},{5... | collective-permute-start | bytes 3096584 | tf_op jit(solution)/shard_map/ppermute | solution.py:23
  113.6 24.6 %collective-permute-start.24 = (bf16[224,2304]{1,0:T(8,128)(2,1)}, bf16[224,2304]{1,0:T(8,128)(2,1)}, u32[]{:S(2)}, u32[]{:S(2)}) collective-permute-start(bf16[224,2304]{1,0:T(8,128)(2,1)} %constant_dynamic-update-slice_fusion), channel_id=1, source_target_pairs={{0,8},{4,12},{8,0},{12,4},{16,24},{20,28},{24,16},{28,20},{1,9},{5... | collective-permute-start | bytes 3096584 | tf_op jit(solution)/shard_map/ppermute | solution.py:23
  115.5 24.2 %collective-permute-start.23 = (bf16[512,896]{1,0:T(8,128)(2,1)}, bf16[512,896]{1,0:T(8,128)(2,1)}, u32[]{:S(2)}, u32[]{:S(2)}) collective-permute-start(bf16[512,896]{1,0:T(8,128)(2,1)} %collective-permute-done.14.g0_ref.refs_6_), channel_id=1, source_target_pairs={{0,1},{1,0},{2,3},{3,2},{4,5},{5,4},{6,7},{7,6},{8,9},{9,8},{10,11... | collective-permute-start | bytes 2752520 | tf_op jit(solution)/shard_map/ppermute | solution.py:23
  116.5 23.3 %collective-permute-start.21 = (bf16[512,896]{1,0:T(8,128)(2,1)}, bf16[512,896]{1,0:T(8,128)(2,1)}, u32[]{:S(2)}, u32[]{:S(2)}) collective-permute-start(bf16[512,896]{1,0:T(8,128)(2,1)} %collective-permute-done.18.x0_ref.refs_2_), channel_id=1, source_target_pairs={{0,1},{1,0},{2,3},{3,2},{4,5},{5,4},{6,7},{7,6},{8,9},{9,8},{10,11... | collective-permute-start | bytes 2752520 | tf_op jit(solution)/shard_map/ppermute | solution.py:23
  138.2 33.5 %collective-permute-start.26 = (bf16[224,2304]{1,0:T(8,128)(2,1)}, bf16[224,2304]{1,0:T(8,128)(2,1)}, u32[]{:S(2)}, u32[]{:S(2)}) collective-permute-start(bf16[224,2304]{1,0:T(8,128)(2,1)} %collective-permute-done.24.rest_2_), channel_id=1, source_target_pairs={{0,4},{4,0},{8,12},{12,8},{16,20},{20,16},{24,28},{28,24},{1,5},{5... | collective-permute-start | bytes 3096584 | tf_op jit(solution)/shard_map/ppermute | solution.py:23
  169.4 22.4 %collective-permute-start.27 = (bf16[448,1024]{1,0:T(8,128)(2,1)}, bf16[448,1024]{1,0:T(8,128)(2,1)S(1)}, u32[]{:S(2)}, u32[]{:S(2)}) collective-permute-start(bf16[448,1024]{1,0:T(8,128)(2,1)} %get-tuple-element.116), channel_id=1, source_target_pairs={{0,4},{4,0},{8,12},{12,8},{16,20},{20,16},{24,28},{28,24},{1,5},{5... | collective-permute-start | bytes 2752520 | tf_op jit(solution)/shard_map/ppermute | solution.py:23
  169.9 21.8 %collective-permute-start.28 = (bf16[448,512]{1,0:T(8,128)(2,1)}, bf16[448,512]{1,0:T(8,128)(2,1)S(1)}, u32[]{:S(2)}, u32[]{:S(2)}) collective-permute-start(bf16[448,512]{1,0:T(8,128)(2,1)} %get-tuple-element.117), channel_id=1, source_target_pairs={{0,8},{4,12},{8,0},{12,4},{16,24},{20,28},{24,16},{28,20},{1,9},{5... | collective-permute-start | bytes 1376264 | tf_op jit(solution)/shard_map/ppermute | solution.py:23
  191.8 4.1 %collective-permute-start.29 = (bf16[2,512,896]{2,1,0:T(8,128)(2,1)}, bf16[2,512,896]{2,1,0:T(8,128)(2,1)S(1)}, u32[]{:S(2)}, u32[]{:S(2)}) collective-permute-start(bf16[2,512,896]{2,1,0:T(8,128)(2,1)} %get-tuple-element.118), channel_id=1, source_target_pairs={{0,1},{1,0},{2,3},{3,2},{4,5},{5,4},{6,7},{7,6},{8,9},{9,8},{10,11... | collective-permute-start | bytes 5505032 | tf_op jit(solution)/shard_map/ppermute | solution.py:23
  192.0 28.8 %collective-permute-start.32 = (bf16[224,512]{1,0:T(8,128)(2,1)S(1)}, bf16[224,512]{1,0:T(8,128)(2,1)S(1)}, u32[]{:S(2)}, u32[]{:S(2)}) collective-permute-start(bf16[224,512]{1,0:T(8,128)(2,1)S(1)} %get-tuple-element.195), channel_id=1, source_target_pairs={{0,4},{4,0},{8,12},{12,8},{16,20},{20,16},{24,28},{28,24},{1,5},{5... | collective-permute-start | bytes 688136 | tf_op jit(solution)/shard_map/ppermute | solution.py:23
  197.4 23.5 %collective-permute-start.30 = (bf16[512,896]{1,0:T(8,128)(2,1)S(1)}, bf16[512,896]{1,0:T(8,128)(2,1)}, u32[]{:S(2)}, u32[]{:S(2)}) collective-permute-start(bf16[512,896]{1,0:T(8,128)(2,1)S(1)} %get-tuple-element.188), channel_id=1, source_target_pairs={{0,2},{1,3},{2,0},{3,1},{4,6},{5,7},{6,4},{7,5},{8,10},{9,11},{10,... | collective-permute-start | bytes 2752520 | tf_op jit(solution)/shard_map/ppermute | solution.py:23
  200.4 20.5 %collective-permute-start.31 = (bf16[224,1024]{1,0:T(8,128)(2,1)S(1)}, bf16[224,1024]{1,0:T(8,128)(2,1)S(1)}, u32[]{:S(2)}, u32[]{:S(2)}) collective-permute-start(bf16[224,1024]{1,0:T(8,128)(2,1)S(1)} %get-tuple-element.183), channel_id=1, source_target_pairs={{0,8},{4,12},{8,0},{12,4},{16,24},{20,28},{24,16},{28,20},{1,9},{5... | collective-permute-start | bytes 1376264 | tf_op jit(solution)/shard_map/ppermute | solution.py:23
  221.7 9.5 %collective-permute-start.33 = (bf16[2,512,896]{2,1,0:T(8,128)(2,1)}, bf16[2,512,896]{2,1,0:T(8,128)(2,1)}, u32[]{:S(2)}, u32[]{:S(2)}) collective-permute-start(bf16[2,512,896]{2,1,0:T(8,128)(2,1)} %get-tuple-element.125), channel_id=1, source_target_pairs={{0,1},{1,0},{2,3},{3,2},{4,5},{5,4},{6,7},{7,6},{8,9},{9,8},{10,11... | collective-permute-start | bytes 5505032 | tf_op jit(solution)/shard_map/ppermute | solution.py:23
  228.7 73.3 %collective-permute-start.56 = (bf16[112,1536]{1,0:T(8,128)(2,1)}, bf16[112,1536]{1,0:T(8,128)(2,1)}, u32[]{:S(2)}, u32[]{:S(2)}) collective-permute-start(bf16[112,1536]{1,0:T(8,128)(2,1)} %pad_maximum_fusion.9), channel_id=1, source_target_pairs={{0,16},{4,20},{8,24},{12,28},{16,0},{20,4},{24,8},{28,12},{1,17},{... | collective-permute-start | bytes 1032200 | tf_op jit(solution)/shard_map/ppermute | solution.py:23
  230.4 72.9 %collective-permute-start.34 = (bf16[512,896]{1,0:T(8,128)(2,1)}, bf16[512,896]{1,0:T(8,128)(2,1)}, u32[]{:S(2)}, u32[]{:S(2)}) collective-permute-start(bf16[512,896]{1,0:T(8,128)(2,1)} %get-tuple-element.126), channel_id=1, source_target_pairs={{0,2},{1,3},{2,0},{3,1},{4,6},{5,7},{6,4},{7,5},{8,10},{9,11},{10,... | collective-permute-start | bytes 2752520 | tf_op jit(solution)/shard_map/ppermute | solution.py:23
  238.4 27.3 %copy-start.2 = (bf16[512,896]{1,0:T(8,128)(2,1)}, bf16[512,896]{1,0:T(8,128)(2,1)S(1)}, u32[]{:S(2)}) copy-start(bf16[512,896]{1,0:T(8,128)(2,1)S(1)} %get-tuple-element.139.refs_0_.own_ref) | copy-start | bytes 2752516
  238.4 3.5 collective-permute-start.35
  247.1 20.4 %collective-permute-start.36 = (bf16[448,512]{1,0:T(8,128)(2,1)S(1)}, bf16[448,512]{1,0:T(8,128)(2,1)S(1)}, u32[]{:S(2)}, u32[]{:S(2)}) collective-permute-start(bf16[448,512]{1,0:T(8,128)(2,1)S(1)} %get-tuple-element.132), channel_id=1, source_target_pairs={{0,4},{4,0},{8,12},{12,8},{16,20},{20,16},{24,28},{28,24},{1,5},{5... | collective-permute-start | bytes 1376264 | tf_op jit(solution)/shard_map/ppermute | solution.py:23
  265.8 43.7 %collective-permute-start.40 = (bf16[448,768]{1,0:T(8,128)(2,1)}, bf16[448,768]{1,0:T(8,128)(2,1)}, u32[]{:S(2)}, u32[]{:S(2)}) collective-permute-start(bf16[448,768]{1,0:T(8,128)(2,1)} %get-tuple-element.152), channel_id=1, source_target_pairs={{0,8},{4,12},{8,0},{12,4},{16,24},{20,28},{24,16},{28,20},{1,9},{5... | collective-permute-start | bytes 2064392 | tf_op jit(solution)/shard_map/ppermute | solution.py:23
  267.1 46.6 %collective-permute-start.37 = (bf16[448,1536]{1,0:T(8,128)(2,1)}, bf16[448,1536]{1,0:T(8,128)(2,1)}, u32[]{:S(2)}, u32[]{:S(2)}) collective-permute-start(bf16[448,1536]{1,0:T(8,128)(2,1)} %get-tuple-element.144), channel_id=1, source_target_pairs={{0,4},{4,0},{8,12},{12,8},{16,20},{20,16},{24,28},{28,24},{1,5},{5... | collective-permute-start | bytes 4128776 | tf_op jit(solution)/shard_map/ppermute | solution.py:23
  268.5 41.0 %collective-permute-start.52 = (bf16[224,512]{1,0:T(8,128)(2,1)}, bf16[224,512]{1,0:T(8,128)(2,1)S(1)}, u32[]{:S(2)}, u32[]{:S(2)}) collective-permute-start(bf16[224,512]{1,0:T(8,128)(2,1)} %get-tuple-element.196), channel_id=1, source_target_pairs={{0,8},{4,12},{8,0},{12,4},{16,24},{20,28},{24,16},{28,20},{1,9},{5... | collective-permute-start | bytes 688136 | tf_op jit(solution)/shard_map/ppermute | solution.py:23
  311.6 10.1 %collective-permute-start.41 = (bf16[224,768]{1,0:T(8,128)(2,1)S(1)}, bf16[224,768]{1,0:T(8,128)(2,1)S(1)}, u32[]{:S(2)}, u32[]{:S(2)}) collective-permute-start(bf16[224,768]{1,0:T(8,128)(2,1)S(1)} %get-tuple-element.187), channel_id=1, source_target_pairs={{0,4},{4,0},{8,12},{12,8},{16,20},{20,16},{24,28},{28,24},{1,5},{5... | collective-permute-start | bytes 1032200 | tf_op jit(solution)/shard_map/ppermute | solution.py:23
  320.4 7.5 %collective-permute-start.53 = (bf16[112,512]{1,0:T(8,128)(2,1)S(1)}, bf16[112,512]{1,0:T(8,128)(2,1)S(1)}, u32[]{:S(2)}, u32[]{:S(2)}) collective-permute-start(bf16[112,512]{1,0:T(8,128)(2,1)S(1)} %fusion.44), channel_id=1, source_target_pairs={{0,16},{4,20},{8,24},{12,28},{16,0},{20,4},{24,8},{28,12},{1,17},{... | collective-permute-start | bytes 344072 | tf_op jit(solution)/shard_map/ppermute | solution.py:23
  322.5 18.2 %collective-permute-start.39 = (bf16[224,1536]{1,0:T(8,128)(2,1)}, bf16[224,1536]{1,0:T(8,128)(2,1)}, u32[]{:S(2)}, u32[]{:S(2)}) collective-permute-start(bf16[224,1536]{1,0:T(8,128)(2,1)} %get-tuple-element.180), channel_id=1, source_target_pairs={{0,8},{4,12},{8,0},{12,4},{16,24},{20,28},{24,16},{28,20},{1,9},{5... | collective-permute-start | bytes 2064392 | tf_op jit(solution)/shard_map/ppermute | solution.py:23
  324.3 14.0 %collective-permute-start.47 = (bf16[448,576]{1,0:T(8,128)(2,1)}, bf16[448,576]{1,0:T(8,128)(2,1)S(1)}, u32[]{:S(2)}, u32[]{:S(2)}) collective-permute-start(bf16[448,576]{1,0:T(8,128)(2,1)} %get-tuple-element.155), channel_id=1, source_target_pairs={{0,4},{4,0},{8,12},{12,8},{16,20},{20,16},{24,28},{28,24},{1,5},{5... | collective-permute-start | bytes 1548296 | tf_op jit(solution)/shard_map/ppermute | solution.py:23
  328.1 9.4 %collective-permute-start.54 = (bf16[112,224]{1,0:T(8,128)(2,1)S(1)}, bf16[112,224]{1,0:T(8,128)(2,1)S(1)}, u32[]{:S(2)}, u32[]{:S(2)}) collective-permute-start(bf16[112,224]{1,0:T(8,128)(2,1)S(1)} %get-tuple-element.212), channel_id=1, source_target_pairs={{0,0},{1,2},{2,1},{3,3},{4,4},{5,6},{6,5},{7,7},{8,8},{9,10},{10,9... | collective-permute-start | bytes 150536 | tf_op jit(solution)/shard_map/ppermute | solution.py:636
  328.7 8.7 %collective-permute-start.55 = (bf16[112,224]{1,0:T(8,128)(2,1)S(1)}, bf16[112,224]{1,0:T(8,128)(2,1)S(1)}, u32[]{:S(2)}, u32[]{:S(2)}) collective-permute-start(bf16[112,224]{1,0:T(8,128)(2,1)S(1)} %get-tuple-element.213), channel_id=1, source_target_pairs={{0,1},{1,3},{2,0},{3,2},{4,5},{5,7},{6,4},{7,6},{8,9},{9,11},{10,8... | collective-permute-start | bytes 150536 | tf_op jit(solution)/shard_map/ppermute | solution.py:636
  337.4 13.1 %collective-permute-start.38 = (bf16[512,896]{1,0:T(8,128)(2,1)}, bf16[512,896]{1,0:T(8,128)(2,1)}, u32[]{:S(2)}, u32[]{:S(2)}) collective-permute-start(bf16[512,896]{1,0:T(8,128)(2,1)} %slice.700), channel_id=1, source_target_pairs={{0,1},{1,0},{2,3},{3,2},{4,5},{5,4},{6,7},{7,6},{8,9},{9,8},{10,11... | collective-permute-start | bytes 2752520 | tf_op jit(solution)/shard_map/ppermute | solution.py:23
  338.4 11.4 %collective-permute-start.48 = (bf16[224,576]{1,0:T(8,128)(2,1)S(1)}, bf16[224,576]{1,0:T(8,128)(2,1)S(1)}, u32[]{:S(2)}, u32[]{:S(2)}) collective-permute-start(bf16[224,576]{1,0:T(8,128)(2,1)S(1)} %get-tuple-element.190), channel_id=1, source_target_pairs={{0,8},{4,12},{8,0},{12,4},{16,24},{20,28},{24,16},{28,20},{1,9},{5... | collective-permute-start | bytes 774152 | tf_op jit(solution)/shard_map/ppermute | solution.py:23
  343.6 50.4 %collective-permute-start.57 = (bf16[112,2304]{1,0:T(8,128)(2,1)}, bf16[112,2304]{1,0:T(8,128)(2,1)S(1)}, u32[]{:S(2)}, u32[]{:S(2)}) collective-permute-start(bf16[112,2304]{1,0:T(8,128)(2,1)} %pad_maximum_fusion.6), channel_id=1, source_target_pairs={{0,16},{4,20},{8,24},{12,28},{16,0},{20,4},{24,8},{28,12},{1,17},{... | collective-permute-start | bytes 1548296 | tf_op jit(solution)/shard_map/ppermute | solution.py:23
  350.5 32.2 %copy-start.60 = (f32[512]{0:T(512)S(1)}, f32[512]{0:T(512)}, u32[]{:S(2)}) copy-start(f32[512]{0:T(512)} %copy-done.58) | copy-start | bytes 6148
  350.5 32.2 %copy-start.65 = (f32[896]{0:T(1024)S(1)}, f32[896]{0:T(1024)}, u32[]{:S(2)}) copy-start(f32[896]{0:T(1024)} %copy-done.63) | copy-start | bytes 10756
  350.5 24.1 %collective-permute-start.49 = (bf16[112,576]{1,0:T(8,128)(2,1)S(1)}, bf16[112,576]{1,0:T(8,128)(2,1)S(1)}, u32[]{:S(2)}, u32[]{:S(2)}) collective-permute-start(bf16[112,576]{1,0:T(8,128)(2,1)S(1)} %fusion.36), channel_id=1, source_target_pairs={{0,16},{4,20},{8,24},{12,28},{16,0},{20,4},{24,8},{28,12},{1,17},{... | collective-permute-start | bytes 387080 | tf_op jit(solution)/shard_map/ppermute | solution.py:23
  355.4 19.2 %collective-permute-start.42 = (f32[23,128]{1,0:T(8,128)S(1)}, f32[23,128]{1,0:T(8,128)S(1)}, u32[]{:S(2)}, u32[]{:S(2)}) collective-permute-start(f32[23,128]{1,0:T(8,128)S(1)} %maximum_bitcast_fusion.1), channel_id=1, source_target_pairs={{0,1},{1,0},{2,3},{3,2},{4,5},{5,4},{6,7},{7,6},{8,9},{9,8},{10,11... | collective-permute-start | bytes 35336 | tf_op jit(solution)/shard_map/ppermute | solution.py:23
  374.6 4.2 %collective-permute-start.43 = (f32[23,128]{1,0:T(8,128)S(1)}, f32[23,128]{1,0:T(8,128)S(1)}, u32[]{:S(2)}, u32[]{:S(2)}) collective-permute-start(f32[23,128]{1,0:T(8,128)S(1)} %add.258), channel_id=1, source_target_pairs={{0,2},{1,3},{2,0},{3,1},{4,6},{5,7},{6,4},{7,5},{8,10},{9,11},{10,... | collective-permute-start | bytes 35336 | tf_op jit(solution)/shard_map/ppermute | solution.py:23
  376.0 15.1 %collective-permute-start.50 = (bf16[112,288]{1,0:T(8,128)(2,1)S(1)}, bf16[112,288]{1,0:T(8,128)(2,1)S(1)}, u32[]{:S(2)}, u32[]{:S(2)}) collective-permute-start(bf16[112,288]{1,0:T(8,128)(2,1)S(1)} %get-tuple-element.210), channel_id=1, source_target_pairs={{0,0},{1,2},{2,1},{3,3},{4,4},{5,6},{6,5},{7,7},{8,8},{9,10},{10,9... | collective-permute-start | bytes 193544 | tf_op jit(solution)/shard_map/ppermute | solution.py:636
  376.6 14.4 %collective-permute-start.51 = (bf16[112,288]{1,0:T(8,128)(2,1)S(1)}, bf16[112,288]{1,0:T(8,128)(2,1)S(1)}, u32[]{:S(2)}, u32[]{:S(2)}) collective-permute-start(bf16[112,288]{1,0:T(8,128)(2,1)S(1)} %get-tuple-element.211), channel_id=1, source_target_pairs={{0,1},{1,3},{2,0},{3,2},{4,5},{5,7},{6,4},{7,6},{8,9},{9,11},{10,8... | collective-permute-start | bytes 193544 | tf_op jit(solution)/shard_map/ppermute | solution.py:636
  378.9 3.7 collective-permute-start.44
  382.6 5.0 %collective-permute-start.45 = (f32[23,128]{1,0:T(8,128)S(1)}, f32[23,128]{1,0:T(8,128)S(1)}, u32[]{:S(2)}, u32[]{:S(2)}) collective-permute-start(f32[23,128]{1,0:T(8,128)S(1)} %add.260), channel_id=1, source_target_pairs={{0,8},{4,12},{8,0},{12,4},{16,24},{20,28},{24,16},{28,20},{1,9},{5... | collective-permute-start | bytes 35336 | tf_op jit(solution)/shard_map/ppermute | solution.py:23
  387.6 5.1 %collective-permute-start.46 = (f32[23,128]{1,0:T(8,128)S(1)}, f32[23,128]{1,0:T(8,128)S(1)}, u32[]{:S(2)}, u32[]{:S(2)}) collective-permute-start(f32[23,128]{1,0:T(8,128)S(1)} %add.261), channel_id=1, source_target_pairs={{0,16},{4,20},{8,24},{12,28},{16,0},{20,4},{24,8},{28,12},{1,17},{... | collective-permute-start | bytes 35336 | tf_op jit(solution)/shard_map/ppermute | solution.py:23
  (74 other events, 585.4 us)

commit v6 on v5

--- a/solution.py
+++ b/solution.py
@@ -83,18 +83,28 @@
     kpad[0, rows, :] = jnp.where(lane < HD, pltpu.roll(last, HD, 1), 0.0).astype(bf16)
 
 
-def attend_kernel(parity_ref, own_ref, other_ref, bias_ref, cos_ref, sin_ref, *rest, block, count):
-    pieces = rest[:count]
-    qk_ref, v_ref, att_ref, lse_ref, held, kpad, vpad, lse_cols, sems = rest[count:]
-    step = pl.program_id(0)
-    half = own_ref.shape[0]
-    length = 2 * half
-    wide = qk_ref.shape[1]
+def attend_kernel(parity_ref, *rest, block, count, first, last):
+    if first == 0:
+        own_ref, other_ref, bias_ref, cos_ref, sin_ref = rest[:5]
+        pieces = rest[5 : 5 + count]
+        qk_ref, v_ref, att_ref, lse_ref, held, kpad, vpad, lse_cols, sems = rest[5 + count :]
+    else:
+        qk_ref, v_ref, att_ref, lse_ref, kpad, vpad, lse_cols = rest
+    step = pl.program_id(0) + first
+    length, wide = qk_ref.shape
+    half = length // 2
     pairs = wide // 128
     parity = parity_ref[0]
 
-    @pl.when(step == 0)
+    @pl.when(step == first)
     def _():
+        lse_cols[...] = jnp.zeros_like(lse_cols)
+        if first:
+            for r in range(0, length, block):
+                rows = pl.ds(r, block)
+                keys = qk_ref[rows, wide - 128 :].astype(f32)
+                pad_heads((kpad, vpad), rows, v_ref[rows, :].astype(f32), keys)
+            return
         assemble(pieces, held, sems)
         for side, rows_ref in enumerate((own_ref, other_ref)):
             for r in range(0, half, block):
@@ -109,7 +119,6 @@
                     qk_ref[rows, p * 128 : (p + 1) * 128] = turned
                 v_ref[rows, :] = mixed[:, wide:].astype(bf16)
                 pad_heads((kpad, vpad), rows, mixed[:, wide:], turned.astype(f32))
-        lse_cols[...] = jnp.zeros_like(lse_cols)
 
     factor = HD**-0.5 * math.log2(math.e)
     cols = pl.ds(pl.multiple_of(step * 128, 128), 128)
@@ -144,21 +153,20 @@
         def _():
             att_ref[to, :] = even.astype(bf16)
 
-    @pl.when(step == pairs - 1)
+    @pl.when(step == last - 1)
     def _():
         lse_ref[...] = lse_cols[...].T[: lse_ref.shape[0], :]
 
 
-def attend(parity, own, other, pieces, bias, cos, sin):
+def attend(parity, own, other, pieces, bias, cos, sin, last):
     half, depth = own.shape
     length = 2 * half
     group = bias.shape[1]
     wide = group - HD
-    pairs = wide // 128
     block = min(256, half)
     return pl.pallas_call(
-        functools.partial(attend_kernel, block=block, count=len(pieces)),
-        grid=(pairs,),
+        functools.partial(attend_kernel, block=block, count=len(pieces), first=0, last=last),
+        grid=(last,),
         in_specs=[pl.BlockSpec(memory_space=pltpu.SMEM)]
         + [whole(a) for a in (own, other, bias, cos, sin)]
         + [in_place(piece) for piece in pieces],
@@ -171,7 +179,7 @@
         out_shape=[
             jax.ShapeDtypeStruct((length, wide), bf16),
             jax.ShapeDtypeStruct((length, HD), bf16),
-            jax.ShapeDtypeStruct((length, wide), bf16),
+            jax.ShapeDtypeStruct((length, last * 128), bf16),
             jax.ShapeDtypeStruct((8, length), f32),
         ],
         scratch_shapes=[
@@ -182,26 +190,60 @@
             pltpu.SemaphoreType.DMA((len(pieces),)),
         ],
         compiler_params=kernel_params(40),
-        cost_estimate=cost(12e9, 8e6, 5e6),
+        cost_estimate=cost(8e9, 6e6, 3e6),
     )(parity, own, other, bias, cos, sin, *pieces)
 
 
-def project_kernel(att_ref, *rest, count):
+def attend_rest(parity, qk, v, first):
+    length, wide = qk.shape
+    pairs = wide // 128
+    block = min(256, length // 2)
+    return pl.pallas_call(
+        functools.partial(attend_kernel, block=block, count=0, first=first, last=pairs),
+        grid=(pairs - first,),
+        in_specs=[pl.BlockSpec(memory_space=pltpu.SMEM), whole(qk), whole(v)],
+        out_specs=[
+            pl.BlockSpec((length, 128), lambda p: (0, p)),
+            pl.BlockSpec((8, length), lambda p: (0, 0)),
+        ],
+        out_shape=[
+            jax.ShapeDtypeStruct((length, (pairs - first) * 128), bf16),
+            jax.ShapeDtypeStruct((8, length), f32),
+        ],
+        scratch_shapes=[
+            pltpu.VMEM((2, length, 128), bf16),
+            pltpu.VMEM((2, length, 128), bf16),
+            pltpu.VMEM((length, 128), f32),
+        ],
+        compiler_params=kernel_params(40),
+        cost_estimate=cost(6e9, 4e6, 3e6),
+    )(parity, qk, v)
+
+
+def project_kernel(first_ref, last_ref, *rest, count):
     pieces = rest[:count]
     own_ref, other_ref, held, sems = rest[count:]
     half = own_ref.shape[0]
     assemble(pieces, held, sems)
     for side, ref in enumerate((own_ref, other_ref)):
-        rows = att_ref[side * half : (side + 1) * half, :]
-        ref[...] = lax.dot_general(rows, held[...], NT, preferred_element_type=f32).astype(ref.dtype)
-
-
-def project(att, pieces):
-    length, wide = att.shape
+        total = 0.0
+        at = 0
+        for part_ref in (first_ref, last_ref):
+            rows = part_ref[side * half : (side + 1) * half, :]
+            weight = held[:, at : at + rows.shape[1]]
+            total = total + lax.dot_general(rows, weight, NT, preferred_element_type=f32)
+            at += rows.shape[1]
+        ref[...] = total.astype(ref.dtype)
+
+
+def project(first, last, pieces):
+    length = first.shape[0]
+    wide = first.shape[1] + last.shape[1]
     depth = sum(piece.shape[0] for piece in pieces)
     return pl.pallas_call(
         functools.partial(project_kernel, count=len(pieces)),
-        in_specs=[pl.BlockSpec(memory_space=pltpu.VMEM)] + [in_place(piece) for piece in pieces],
+        in_specs=[pl.BlockSpec(memory_space=pltpu.VMEM)] * 2
+        + [in_place(piece) for piece in pieces],
         out_specs=[pl.BlockSpec(memory_space=pltpu.VMEM)] * 2,
         out_shape=[
             jax.ShapeDtypeStruct((length // 2, depth), f32),
@@ -213,7 +255,7 @@
         ],
         compiler_params=kernel_params(40),
         cost_estimate=cost(2 * length * depth * wide, 6e6),
-    )(att, *pieces)
+    )(first, last, *pieces)
 
 
 def attend_back_kernel(
@@ -559,6 +601,11 @@
         self.left -= 1
         return self.pieces[-1]
 
+    def double_all(self):
+        while self.left > 0:
+            self.double()
+        return self.pieces[-1]
+
     def send(self, *earlier):
         piece = self.pieces[self.sent]
         self.sent += 1
@@ -622,6 +669,14 @@
             self.step()
         totals = [kept + got.astype(f32) for kept, got in zip(self.kept, self.got)]
         return jnp.concatenate(totals, 1)
+
+
+def in_order(first, second, parity, axis=0):
+    return jnp.where(
+        parity == 0,
+        jnp.concatenate([first, second], axis),
+        jnp.concatenate([second, first], axis),
+    )
 
 
 def turned_pairs(block):
@@ -669,24 +724,13 @@
     group_width = 2 * qkv_cols
     query_width = group_width - 2 * HD
 
-    bias_rows = jnp.pad(qkv_bias[None, :], ((0, 15), (0, 0)))
-    first, second = turned_pairs(
-        jnp.concatenate(
-            [
-                jnp.concatenate([qkv_weight, bias_rows], 0),
-                jnp.pad(out_weight.T, ((0, 16), (0, 0))),
-            ],
-            1,
-        )
-    )
-    low = jnp.where(sequence == 0, first, second)
-    high = jnp.where(sequence == 0, second, first)
-    qkv_own = jnp.concatenate([low[:, :qkv_cols], high[:, :qkv_cols]], 1)
-    bias_full = qkv_own[deep : deep + 1].astype(f32)
-    out_own = jnp.concatenate([low[:deep, qkv_cols:], high[:deep, qkv_cols:]], 1)
-    out_own = jnp.pad(out_own, ((0, 0), (0, HD)))
-    qkv_gather = Gather(qkv_own[:deep], bits)
-    out_gather = Gather(out_own, bits)
+    qkv_gather = Gather(qkv_weight, bits)
+    out_gather = Gather(out_weight.T, bits)
+
+    def both(block):
+        first, second = turned_pairs(block)
+        return in_order(first, second, sequence, 1)
+
     down_flipped = down_weight.T
     mlp_gathers = []
     for start, stop in cuts(ff_cols):
@@ -719,7 +763,7 @@
             blocks = jnp.where((row >> bit) % 2 == 1, turned, blocks)
         return blocks.reshape(model_width)
 
-    input_rows = stored(after(layer_input, first, second))
+    input_rows = stored(layer_input)
     grad_out = stored(cotangent)
     gain_one = stored(gain_attn[None, :])
     gain_two = stored(gain_mlp[None, :])
@@ -731,33 +775,36 @@
     grad_blocks = [grad_out.astype(bf16)]
 
     near, far = mlp_gathers
-    n_four = near.double()
-    n_own = near.send()
-    a_own = qkv_gather.send()
     a_four = qkv_gather.double()
-    a_two = qkv_gather.double(a_own)
-    a_beside = qkv_gather.send(a_own)
-    o_four = out_gather.double(a_four)
-    a_last = qkv_gather.send(a_beside, n_own)
-    qkv_pieces = qkv_gather.all()
-    far.ready(a_two, o_four)
+    n_four = near.double(a_four)
+    a_two = qkv_gather.double_all()
+    a_rows = jnp.concatenate(qkv_gather.pieces, 0)
+    a_beside = qkv_gather.catch_up()
+    bias_rows = jnp.pad(qkv_bias[None, :], ((0, 15), (0, 0)))
+    a_first = both(jnp.concatenate([a_rows, bias_rows], 0))
+    bias_full = a_first[-16:-15].astype(f32)
+    across = flip(grad_blocks[0], "col", 1)
+    a_last = both(after(a_beside, across))
+    qkv_pieces = [a_first[:-16], a_last]
+    o_four = out_gather.double(a_beside)
+    n_own = near.send(a_beside)
+    o_two = out_gather.double_all()
+    o_beside = out_gather.catch_up(n_own)
+    o_rows = jnp.concatenate([*out_gather.pieces, o_beside], 0)
+    n_two = near.double(o_two)
+    n_beside = near.send(n_own)
+    far.ready(a_last, n_four, o_four)
     f_four = far.double()
-    o_two = out_gather.double(a_two)
-    across = flip(after(grad_blocks[0], a_four), "col", 1)
-    out_pieces = out_gather.finish(a_last, o_two)
-    n_two = near.double(o_two)
-    n_beside = near.send(a_last)
-    qk_rows, value_rows, att_rows, log_totals = attend(
-        parity,
-        normed_own,
-        normed_other,
-        qkv_pieces,
-        bias_full,
-        cosine,
-        sine_part,
-    )
-    n_last = near.send(att_rows)
-    att_own, att_other = project(after(att_rows, n_beside, n_two, across, f_four), out_pieces)
+    out_full = jnp.pad(both(after(o_rows, a_last)), ((0, 0), (0, HD)))
+    out_pieces = [out_full]
+    split = -(-(query_width + HD) // 256)
+    qk_rows, value_rows, att_first, log_first = attend(
+        parity, normed_own, normed_other, qkv_pieces, bias_full, cosine, sine_part, split
+    )
+    n_last = near.send(n_beside, att_first)
+    att_last, log_last = attend_rest(parity, after(qk_rows, n_beside, n_two), value_rows, split)
+    log_totals = log_first + log_last
+    att_own, att_other = project(att_first, after(att_last, f_four), out_pieces)
     att_got = flip(att_other, "col", 0)
     grad_blocks.append(flip(after(grad_blocks[0], att_got), "col", 0))
     grad_blocks += [across, flip(after(across, att_got), "col", 0)]
@@ -769,10 +816,10 @@
     blocks += [across, flip(across, "col", 0)]
 
     f_beside = far.catch_up(n_last)
-    f_two = far.double(blocks[2])
+    f_two = far.double(blocks[0])
     f_last = far.send(f_beside)
     first_pieces, second_pieces = (gather.all() for gather in mlp_gathers)
-    act_own, *sums_own = mlp([after(blocks[0], blocks[2]), blocks[1]], grad_blocks[:2], first_pieces)
+    act_own, *sums_own = mlp(blocks[:2], grad_blocks[:2], first_pieces)
     act_far, *sums_far = mlp(blocks[2:], grad_blocks[2:], first_pieces)
     sent_one, kept_one, sent_two, kept_two = outer(blocks, grad_blocks, [act_own, act_far])
     first_scatter = Scatter([(sent_one, kept_one), (sent_two, kept_two)], bits)
@@ -791,7 +838,9 @@
         sums_own,
     )
     first_scatter.step()
-    beside = flip(after(far_own, normed_back, *first_scatter.got), "col", 0)
+    far_own = after(far_own, normed_back, *first_scatter.got)
+    beside = [flip(far_own[0], "col", 0)]
+    beside.append(flip(after(far_own[1], beside[0]), "col", 0))
     first_scatter.step()
     down_back = flip(after(across[1], normed_back), "col", 1)
 
@@ -809,7 +858,7 @@
     gain_two_grad = jnp.sum(grad_normed_two * middle * scale_two[:, None], axis=0)
     branch_own = grad_middle.astype(bf16)
     branch_other = flip(branch_own, "col", 0)
-    out_scatter = Scatter([outer_one([branch_own, branch_other], att_rows)], bits)
+    out_scatter = Scatter([outer_one([branch_own, branch_other], jnp.concatenate([att_first, att_last], 1))], bits)
     sent_one, kept_one, sent_two, kept_two = outer(
         [after(blocks[0], out_scatter.kept[0], *first_scatter.kept), *blocks[1:]],
         grad_blocks,
@@ -818,7 +867,6 @@
     second_scatter = Scatter([(sent_one, kept_one), (sent_two, kept_two)], bits)
     out_scatter.wait(kept_one)
     out_scatter.step()
-    split = qk_rows.shape[1] // 256
     mixed_first, bias_first, *carry = attend_back(
         parity,
         after(branch_own, kept_one, out_scatter.kept[0]),
@@ -844,20 +892,21 @@
         cosine,
         sine_part,
         split,
-        2 * split,
+        qk_rows.shape[1] // 128,
         carry,
     )
     bias_grad = jnp.concatenate([bias_first, bias_last], 1)[0]
     first_scatter.wait(mixed_last)
-    second_scatter.wait(mixed_last)
-    out_scatter.wait(mixed_last)
     grad_mixed = jnp.concatenate([mixed_first, mixed_last], 1)
+    qkv_scatter = Scatter([outer_one([normed_own, normed_other], grad_mixed)], bits)
+    passed = qkv_scatter.kept[0]
+    first_scatter.wait(passed)
+    second_scatter.wait(passed)
+    out_scatter.wait(passed)
     second_scatter.step()
-    layer_output = unstored((middle + summed(1, after(down_back, grad_mixed))).astype(bf16))
-    qkv_scatter = Scatter([outer_one([normed_own, normed_other], after(grad_mixed, second_scatter.kept[0]))], bits)
+    layer_output = unstored((middle + summed(1, after(down_back, passed))).astype(bf16))
     qkv_full = jnp.concatenate(qkv_pieces, 0)
-    grad_mixed = after(grad_mixed, qkv_scatter.kept[0])
-    out_scatter.wait(qkv_scatter.kept[0])
+    grad_mixed = after(grad_mixed, passed, *second_scatter.kept)
     out_scatter.step()
     partial = jnp.einsum("tc,dc->td", grad_mixed, qkv_full, preferred_element_type=f32)
     grad_normed_one = partial[:tok_local] + flip(
@@ -892,6 +941,9 @@
         small = small + flip(small, "col", bit)
     for bit in range(bits):
         small = small + flip(small, "row", bit)
+    qkv_scatter.step()
+    qkv_scatter.step()
+    qkv_scatter.wait(small)
     qkv_total = to_columns(qkv_scatter.total(), qkv_cols)
     out_total = to_columns(out_scatter.total(), out_cols)
     mlp_totals = []

time: 405 us -> 426 us (1.052)
  waiting for transfers between devices: 79.4 us -> 112 us
  local copies, waits for them, and re-layouts: 34.3 us -> 20.7 us
    ppermute x52 -> x51, waiting for transfers between devices: 79.3 us -> 109 us  [flip(): return lax.ppermute(block, axis, [(i, i ^ 1 << bit) for i in range(count)])]
    unnamed x168 -> x156, local copies, waits for them, and re-layouts: 18.4 us -> 8.61 us
    pallas_call x1, Pallas kernels: 19.9 us -> 12.4 us  [attend(): pl.pallas_call(functools.partial(attend_kernel, block=block, count=len(pi...]
    pallas_call x0 -> x1, Pallas kernels: none -> 7.07 us  [attend_rest(): pl.pallas_call(functools.partial(attend_kernel, block=block, count=0, fir...]
    convert_element_type x7 -> x8, other arithmetic: 6.98 us -> 10.6 us  [step(): (kept[half:] + got[half:].astype(f32)).astype(bf16)]
    ppermute x52 -> x51, starting transfers between devices: 53.5 us -> 51.1 us  [flip(): return lax.ppermute(block, axis, [(i, i ^ 1 << bit) for i in range(count)])]
  transfers between devices with their start and end apart: 58 -> 61, of which waited for: 15 -> 21; matrix products, arithmetic and copies ran while one was open for 19% -> 16% of each run, Pallas kernels for 40% -> 38%
where the time goes in v6:
time: 426 us; the launch traced here: 418 us
  Pallas kernels  161 us (38%)
  waiting for transfers between devices  112 us (26%)
  starting transfers between devices  64 us (15%)
  other arithmetic  41.7 us (10%)
  local copies, waits for them, and re-layouts  20.7 us (5%)
  matrix products  16.8 us (4%)
    ppermute x51, waiting for transfers between devices, flip(): return lax.ppermute(block, axis, [(i, i ^ 1 << bit) for i in range(count)])  109 us
    pallas_call x4, Pallas kernels, mlp(): pl.pallas_call(functools.partial(mlp_kernel, count=len(pieces), add=add),...  67.6 us
    ppermute x51, starting transfers between devices, flip(): return lax.ppermute(block, axis, [(i, i ^ 1 << bit) for i in range(count)])  51.1 us
    pallas_call x2, Pallas kernels, attend_back(): pl.pallas_call(functools.partial(attend_back_kernel, block=block, count=l...  32.7 us
    pallas_call x2, Pallas kernels, outer(): pl.pallas_call(functools.partial(outer_kernel, blocks=len(rows)), grid=(3...  32.3 us
    pallas_call x1, Pallas kernels, attend(): pl.pallas_call(functools.partial(attend_kernel, block=block, count=len(pi...  12.4 us
    convert_element_type x8, other arithmetic, step(): (kept[half:] + got[half:].astype(f32)).astype(bf16)  10.6 us
    unnamed x156, local copies, waits for them, and re-layouts  8.61 us
  transfers between devices with their start and end apart: 61, of which 21 were waited for; matrix products, arithmetic and copies ran while one was open for 16% of the time, Pallas kernels for 38%

profile of v6, /device:TPU:0, one launch (start us, length us, event | category | flops | bytes accessed | tf_op | source)
XLA Modules:
  0.0 418.1 jit_solution(2747511779888010686)
XLA Ops:
  1.7 4.1 collective-permute-start.1
  8.0 2.5 fusion.11
  11.0 2.8 bitcast_convert_fusion
  13.8 1.6 collective-permute-start.6
  16.3 2.0 fusion.61
  20.3 1.6 collective-permute-start.2
  22.4 5.7 %collective-permute-done.2 = bf16[224,288]{1,0:T(8,128)(2,1)S(1)} collective-permute-done((bf16[224,288]{1,0:T(8,128)(2,1)S(1)}, bf16[224,288]{1,0:T(8,128)(2,1)S(1)}, u32[]{:S(2)}, u32[]{:S(2)}) %collective-permute-start.2) | collective-permute-done | bytes 129056 | tf_op jit(solution)/shard_map/ppermute | solution.py:23
  28.1 1.6 collective-permute-start.5
  31.2 6.3 %collective-permute-done.5 = bf16[448,288]{1,0:T(8,128)(2,1)S(1)} collective-permute-done((bf16[448,288]{1,0:T(8,128)(2,1)S(1)}, bf16[448,288]{1,0:T(8,128)(2,1)S(1)}, u32[]{:S(2)}, u32[]{:S(2)}) %collective-permute-start.5) | collective-permute-done | bytes 258080 | tf_op jit(solution)/shard_map/ppermute | solution.py:23
  38.2 2.0 collective-permute-done.9.rest_1_
  41.1 4.8 %collective-permute-done.12 = bf16[112,224]{1,0:T(8,128)(2,1)S(1)} collective-permute-done((bf16[112,224]{1,0:T(8,128)(2,1)S(1)}, bf16[112,224]{1,0:T(8,128)(2,1)S(1)}, u32[]{:S(2)}, u32[]{:S(2)}) %collective-permute-start.12) | collective-permute-done | bytes 50208 | tf_op jit(solution)/shard_map/ppermute | solution.py:23
  45.9 1.5 collective-permute-start.10
  48.0 4.3 %collective-permute-done.13 = bf16[224,224]{1,0:T(8,128)(2,1)S(1)} collective-permute-done((bf16[224,224]{1,0:T(8,128)(2,1)S(1)}, bf16[224,224]{1,0:T(8,128)(2,1)S(1)}, u32[]{:S(2)}, u32[]{:S(2)}) %collective-permute-start.13) | collective-permute-done | bytes 100384 | tf_op jit(solution)/shard_map/ppermute | solution.py:23
  52.3 1.9 collective-permute-done.10.rest_3_
  56.4 2.7 collective-permute-start.14
  60.3 1.4 collective-permute-start.11
  62.8 4.3 %collective-permute-start.18 = (bf16[896,224]{1,0:T(8,128)(2,1)S(1)}, bf16[896,224]{1,0:T(8,128)(2,1)S(1)}, u32[]{:S(2)}, u32[]{:S(2)}) collective-permute-start(bf16[896,224]{1,0:T(8,128)(2,1)S(1)} %pad_maximum_fusion.8), channel_id=1, source_target_pairs={{0,2},{1,0},{2,3},{3,1},{4,6},{5,4},{6,7},{7,5},{8,10},{9,8},{10,1... | collective-permute-start | bytes 1204232 | tf_op jit(solution)/shard_map/ppermute | solution.py:685
  68.1 3.1 collective-permute-start.15
  71.2 12.4 %shard_map.186 = (bf16[1024,512]{1,0:T(8,128)(2,1)S(1)}, bf16[1024,64]{1,0:T(8,128)(2,1)S(1)}, bf16[1024,256]{1,0:T(8,128)(2,1)S(1)}, f32[8,1024]{1,0:T(8,128)S(1)}) custom-call(s32[1]{0:T(128)} %bitcast.1.parity_ref, bf16[512,896]{1,0:T(8,128)(2,1)S(1)} %fusion.13.rest_0_.refs_0_, bf16[512,896]{1,0:T(8,128)(2,1)} %collective-permute-done.rest_1_.refs_1_, ...), custom_call_target="tpu_custom_call" | custom-call | flops 8000000000 | bytes 6000000 | tf_op jit(solution)/shard_map/pallas_call | solution.py:167
  83.7 7.1 %shard_map.187 = (bf16[1024,256]{1,0:T(8,128)(2,1)S(1)}, f32[8,1024]{1,0:T(8,128)S(1)}) custom-call(s32[1]{0:T(128)} %bitcast.1.parity_ref, bf16[1024,512]{1,0:T(8,128)(2,1)S(1)} %get-tuple-element.94.rest_0_.qk_ref, bf16[1024,64]{1,0:T(8,128)(2,1)S(1)} %get-tuple-element.95.rest_1_.v_ref), custom_call_target="tpu_custom_call" | custom-call | flops 6000000000 | bytes 4000000 | tf_op jit(solution)/shard_map/pallas_call | solution.py:201
  91.7 2.6 collective-permute-done.15.rest_1_
  94.3 2.0 shard_map.188
  101.0 14.1 %collective-permute-done.21.rest_5_ = bf16[224,1536]{1,0:T(8,128)(2,1)S(1)} collective-permute-done((bf16[224,1536]{1,0:T(8,128)(2,1)S(1)}, bf16[224,1536]{1,0:T(8,128)(2,1)S(1)}, u32[]{:S(2)}, u32[]{:S(2)}) %collective-permute-start.21) | collective-permute-done | bytes 688160 | tf_op jit(solution)/shard_map/ppermute | solution.py:23
  117.8 2.6 collective-permute-start.26
  120.4 17.5 %collective-permute-done.20.x0_ref.refs_2_ = bf16[512,896]{1,0:T(8,128)(2,1)} collective-permute-done((bf16[512,896]{1,0:T(8,128)(2,1)S(1)}, bf16[512,896]{1,0:T(8,128)(2,1)}, u32[]{:S(2)}, u32[]{:S(2)}) %collective-permute-start.20) | collective-permute-done | bytes 917536 | tf_op jit(solution)/shard_map/ppermute | solution.py:23
  137.9 13.8 %shard_map.189 = (bf16[1024,1536]{1,0:T(8,128)(2,1)}, bf16[2,512,896]{2,1,0:T(8,128)(2,1)}, bf16[2,512,896]{2,1,0:T(8,128)(2,1)}) custom-call(bf16[512,896]{1,0:T(8,128)(2,1)} %copy-done.36, bf16[512,896]{1,0:T(8,128)(2,1)} %copy-done.68, bf16[512,896]{1,0:T(8,128)(2,1)} %get-tuple-element.105.g0_ref.refs_4_, ...), custom_call_target="tpu_custom_call" | custom-call | flops 5637144576 | bytes 31457280 | tf_op jit(solution)/shard_map/pallas_call | solution.py:478
  153.4 13.8 %shard_map.190 = (bf16[1024,1536]{1,0:T(8,128)(2,1)}, bf16[2,512,896]{2,1,0:T(8,128)(2,1)}, bf16[2,512,896]{2,1,0:T(8,128)(2,1)}) custom-call(bf16[512,896]{1,0:T(8,128)(2,1)} %collective-permute-done.20.x0_ref.refs_2_, bf16[512,896]{1,0:T(8,128)(2,1)} %collective-permute-done.23.x1_ref.refs_3_, bf16[512,896]{1,0:T(8,128)(2,1)} %collective-permute-done.6.g0_ref.refs_6_, ...), custom_call_target="tpu_custom_call" | custom-call | flops 5637144576 | bytes 31457280 | tf_op jit(solution)/shard_map/pallas_call | solution.py:478
  167.2 15.6 %shard_map.191 = (bf16[448,1024]{1,0:T(8,128)(2,1)}, f32[448,1024]{1,0:T(8,128)}, bf16[448,512]{1,0:T(8,128)(2,1)}, f32[448,512]{1,0:T(8,128)}) custom-call(bf16[512,896]{1,0:T(8,128)(2,1)} %copy-done.36, bf16[512,896]{1,0:T(8,128)(2,1)} %copy-done.68, bf16[512,896]{1,0:T(8,128)(2,1)} %collective-permute-done.20.x0_ref.refs_2_, ...), custom_call_target="tpu_custom_call" | custom-call | flops 5637144576 | bytes 20971520 | tf_op jit(solution)/shard_map/pallas_call | solution.py:542
  182.8 1.5 collective-permute-start.29
  184.2 2.9 collective-permute-start.30
  187.1 19.9 %shard_map.192 = (bf16[1024,2304]{1,0:T(8,128)(2,1)}, bf16[2,512,896]{2,1,0:T(8,128)(2,1)}, bf16[2,512,896]{2,1,0:T(8,128)(2,1)}) custom-call(bf16[512,896]{1,0:T(8,128)(2,1)} %collective-permute-done.20.x0_ref.refs_2_, bf16[512,896]{1,0:T(8,128)(2,1)} %collective-permute-done.23.x1_ref.refs_3_, bf16[512,896]{1,0:T(8,128)(2,1)} %collective-permute-done.6.g0_ref.refs_6_, ...), custom_call_target="tpu_custom_call" | custom-call | flops 8455716864 | bytes 31457280 | tf_op jit(solution)/shard_map/pallas_call | solution.py:478
  208.4 2.7 collective-permute-done.31
  215.8 20.1 %shard_map.193 = (bf16[1024,2304]{1,0:T(8,128)(2,1)}, bf16[2,512,896]{2,1,0:T(8,128)(2,1)}, bf16[2,512,896]{2,1,0:T(8,128)(2,1)}) custom-call(bf16[512,896]{1,0:T(8,128)(2,1)} %copy-done.36, bf16[512,896]{1,0:T(8,128)(2,1)} %copy-done.68, bf16[512,896]{1,0:T(8,128)(2,1)} %get-tuple-element.105.g0_ref.refs_4_, ...), custom_call_target="tpu_custom_call" | custom-call | flops 8455716864 | bytes 31457280 | tf_op jit(solution)/shard_map/pallas_call | solution.py:478
  235.9 3.1 slice_bitcast_fusion.3
  240.4 1.9 slice_add_fusion.13
  242.3 2.1 slice_add_fusion.5
  245.1 3.4 collective-permute-start.59
  249.9 2.3 multiply_reduce_fusion
  252.3 4.8 %fusion.71 = (bf16[512,896]{1,0:T(8,128)(2,1)S(1)}, f32[512,896]{1,0:T(8,128)}) fusion(f32[512,896]{1,0:T(8,128)} %copy-done.15, f32[512]{0:T(512)S(1)} %fusion.67, bf16[512,896]{1,0:T(8,128)(2,1)} %collective-permute-done.32, bf16[512,896]{1,0:T(8,128)(2,1)} %collective-permute-done.35, bf16[2,512,896]{2,1,0:T(8,128)(2,1)} %get-tuple-element.124, ...), kind=kLoop, calls=%fused_computation.194 | loop fusion | flops 5046272 | bytes 9182720 | tf_op jit(solution)/shard_map/convert_element_type | solution.py:859
  259.8 2.9 shard_map.194
  262.7 1.6 collective-permute-start.39
  264.3 16.7 %shard_map.195 = (bf16[448,1536]{1,0:T(8,128)(2,1)}, f32[448,1536]{1,0:T(8,128)}, bf16[448,768]{1,0:T(8,128)(2,1)}, f32[448,768]{1,0:T(8,128)}) custom-call(bf16[512,896]{1,0:T(8,128)(2,1)} %copy-done.36, bf16[512,896]{1,0:T(8,128)(2,1)} %copy-done.68, bf16[512,896]{1,0:T(8,128)(2,1)} %collective-permute-done.20.x0_ref.refs_2_, ...), custom_call_target="tpu_custom_call" | custom-call | flops 8455716864 | bytes 20971520 | tf_op jit(solution)/shard_map/pallas_call | solution.py:542
  282.7 17.6 %shard_map.196 = (bf16[1024,256]{1,0:T(8,128)(2,1)S(1)}, f32[1,256]{1,0:T(1,128)S(1)}, f32[1024,128]{1,0:T(8,128)S(1)}, f32[1024,128]{1,0:T(8,128)S(1)}) custom-call(s32[1]{0:T(128)} %bitcast.1.parity_ref, bf16[512,896]{1,0:T(8,128)(2,1)S(1)} %get-tuple-element.141.refs_0_.own_ref, bf16[512,896]{1,0:T(8,128)(2,1)} %collective-permute-done.38.refs_1_.other_ref, ...), custom_call_target="tpu_custom_call" | custom-call | flops 12000000000 | bytes 6000000 | tf_op jit(solution)/shard_map/pallas_call | solution.py:394
  300.4 15.1 %shard_map.197 = (bf16[1024,320]{1,0:T(8,128)(2,1)S(1)}, f32[1,320]{1,0:T(1,128)S(1)}) custom-call(s32[1]{0:T(128)} %bitcast.1.parity_ref, bf16[512,896]{1,0:T(8,128)(2,1)S(1)} %get-tuple-element.141.refs_0_.own_ref, bf16[512,896]{1,0:T(8,128)(2,1)} %collective-permute-done.38.refs_1_.other_ref, bf16[1024,512]{1,0:T(8,128)(2,1)} %copy-done.12, ...), custom_call_target="tpu_custom_call" | custom-call | flops 12000000000 | bytes 6000000 | tf_op jit(solution)/shard_map/pallas_call | solution.py:394
  316.9 3.5 shard_map.198
  320.4 1.6 collective-permute-start.50
  323.1 4.0 fusion.26
  328.0 2.4 add_convert_fusion.3
  330.4 3.8 collective-permute-done.56
  335.2 2.0 collective-permute-start.58
  337.3 1.7 add_convert_fusion.1
  339.0 1.7 fusion.28
  344.8 2.0 add_convert_fusion.4
  346.8 6.7 %collective-permute-done.44 = bf16[224,768]{1,0:T(8,128)(2,1)} collective-permute-done((bf16[224,768]{1,0:T(8,128)(2,1)S(1)}, bf16[224,768]{1,0:T(8,128)(2,1)}, u32[]{:S(2)}, u32[]{:S(2)}) %collective-permute-start.44) | collective-permute-done | bytes 344096 | tf_op jit(solution)/shard_map/ppermute | solution.py:23
  353.5 1.7 fusion.53
  355.3 2.6 fusion.19
  358.4 13.6 %collective-permute-done.43 = bf16[224,1536]{1,0:T(8,128)(2,1)S(1)} collective-permute-done((bf16[224,1536]{1,0:T(8,128)(2,1)}, bf16[224,1536]{1,0:T(8,128)(2,1)S(1)}, u32[]{:S(2)}, u32[]{:S(2)}) %collective-permute-start.43) | collective-permute-done | bytes 688160 | tf_op jit(solution)/shard_map/ppermute | solution.py:23
  375.7 1.5 collective-permute-done.46
  377.9 3.0 collective-permute-start.60
  381.7 9.6 %collective-permute-done.48 = f32[23,128]{1,0:T(8,128)S(1)} collective-permute-done((f32[23,128]{1,0:T(8,128)S(1)}, f32[23,128]{1,0:T(8,128)S(1)}, u32[]{:S(2)}, u32[]{:S(2)}) %collective-permute-start.48) | collective-permute-done | bytes 11808 | tf_op jit(solution)/shard_map/ppermute | solution.py:23
  392.7 4.4 %fusion.27 = bf16[512,896]{1,0:T(8,128)(2,1)} fusion(s32[896]{0:T(1024)S(1)} %copy-done.64, f32[896,512]{0,1:T(8,128)S(1)} %copy-done.21, f32[512,896]{1,0:T(8,128)S(1)} %copy-done.28, f32[512]{0:T(512)S(1)} %fusion.69, f32[896]{0:T(1024)S(1)} %copy-done.59, f32[512]{0:T(512)S(1)} %copy-done.56, f32[1024,896]{1,0:T(8,128)} %copy-done.25, ...), kind=kOutput, calls=%fused_computation.48 | convolution fusion | flops 827015168 | bytes 7351296 | tf_op jit(solution)/shard_map/dot_general | solution.py:753
  397.2 8.4 %collective-permute-done.49 = f32[23,128]{1,0:T(8,128)S(1)} collective-permute-done((f32[23,128]{1,0:T(8,128)S(1)}, f32[23,128]{1,0:T(8,128)S(1)}, u32[]{:S(2)}, u32[]{:S(2)}) %collective-permute-start.49) | collective-permute-done | bytes 11808 | tf_op jit(solution)/shard_map/ppermute | solution.py:23
  407.4 2.2 collective-permute-start.54
  410.8 2.8 collective-permute-done.54
  (351 shorter events, 61.9 us)
Async XLA Ops:
  1.7 18.5 %collective-permute-start.1 = (bf16[112,288]{1,0:T(8,128)(2,1)S(1)}, bf16[112,288]{1,0:T(8,128)(2,1)S(1)}, u32[]{:S(2)}, u32[]{:S(2)}) collective-permute-start(bf16[112,288]{1,0:T(8,128)(2,1)S(1)} %copy.24), channel_id=1, source_target_pairs={{0,16},{4,20},{8,24},{12,28},{16,0},{20,4},{24,8},{28,12},{1,17},{... | collective-permute-start | bytes 193544 | tf_op jit(solution)/shard_map/ppermute | solution.py:23
  6.7 90.2 %copy-start.62 = (s32[896]{0:T(1024)}, s32[896]{0:T(1024)S(1)}, u32[]{:S(2)}) copy-start(s32[896]{0:T(1024)S(1)} %fusion.62) | copy-start | bytes 10756
  10.9 57.2 %collective-permute-start = (bf16[512,896]{1,0:T(8,128)(2,1)S(1)}, bf16[512,896]{1,0:T(8,128)(2,1)}, u32[]{:S(2)}, u32[]{:S(2)}) collective-permute-start(bf16[512,896]{1,0:T(8,128)(2,1)S(1)} %fusion.13.rest_0_.refs_0_), channel_id=1, source_target_pairs={{0,1},{1,0},{2,3},{3,2},{4,5},{5,4},{6,7},{7,6},{8,9},{9,8},{10,11... | collective-permute-start | bytes 2752520 | tf_op jit(solution)/shard_map/ppermute | solution.py:23
  13.8 41.9 %collective-permute-start.6 = (bf16[512,896]{1,0:T(8,128)(2,1)}, bf16[512,896]{1,0:T(8,128)(2,1)}, u32[]{:S(2)}, u32[]{:S(2)}) collective-permute-start(bf16[512,896]{1,0:T(8,128)(2,1)} %get-tuple-element.105.g0_ref.refs_4_), channel_id=1, source_target_pairs={{0,2},{1,3},{2,0},{3,1},{4,6},{5,7},{6,4},{7,5},{8,10},{9,11},{10,... | collective-permute-start | bytes 2752520 | tf_op jit(solution)/shard_map/ppermute | solution.py:23
  20.3 7.8 %collective-permute-start.2 = (bf16[224,288]{1,0:T(8,128)(2,1)S(1)}, bf16[224,288]{1,0:T(8,128)(2,1)S(1)}, u32[]{:S(2)}, u32[]{:S(2)}) collective-permute-start(bf16[224,288]{1,0:T(8,128)(2,1)S(1)} %pad_maximum_fusion.13), channel_id=1, source_target_pairs={{0,8},{4,12},{8,0},{12,4},{16,24},{20,28},{24,16},{28,20},{1,9},{5... | collective-permute-start | bytes 387080 | tf_op jit(solution)/shard_map/ppermute | solution.py:23
  22.0 18.2 %collective-permute-start.9 = (bf16[112,1536]{1,0:T(8,128)(2,1)S(1)}, bf16[112,1536]{1,0:T(8,128)(2,1)S(1)}, u32[]{:S(2)}, u32[]{:S(2)}) collective-permute-start(bf16[112,1536]{1,0:T(8,128)(2,1)S(1)} %pad_maximum_fusion.10.rest_0_), channel_id=1, source_target_pairs={{0,16},{4,20},{8,24},{12,28},{16,0},{20,4},{24,8},{28,12},{1,17},{... | collective-permute-start | bytes 1032200 | tf_op jit(solution)/shard_map/ppermute | solution.py:23
  28.1 9.3 %collective-permute-start.5 = (bf16[448,288]{1,0:T(8,128)(2,1)S(1)}, bf16[448,288]{1,0:T(8,128)(2,1)S(1)}, u32[]{:S(2)}, u32[]{:S(2)}) collective-permute-start(bf16[448,288]{1,0:T(8,128)(2,1)S(1)} %pad_maximum_fusion.9), channel_id=1, source_target_pairs={{0,4},{4,0},{8,12},{12,8},{16,20},{20,16},{24,28},{28,24},{1,5},{5... | collective-permute-start | bytes 774152 | tf_op jit(solution)/shard_map/ppermute | solution.py:23
  30.6 40.6 %copy-start.5 = (f32[1024,128]{1,0:T(8,128)}, f32[1024,128]{1,0:T(8,128)S(1)}, u32[]{:S(2)}) copy-start(f32[1024,128]{1,0:T(8,128)S(1)} %get-tuple-element.251.rest_3_.cos_ref) | copy-start | bytes 1572868
  30.6 40.6 %copy-start.7 = (f32[1024,128]{1,0:T(8,128)}, f32[1024,128]{1,0:T(8,128)S(1)}, u32[]{:S(2)}) copy-start(f32[1024,128]{1,0:T(8,128)S(1)} %get-tuple-element.252.rest_4_.sin_ref) | copy-start | bytes 1572868
  30.7 16.8 %collective-permute-start.4 = (bf16[464,288]{1,0:T(8,128)(2,1)S(1)}, bf16[464,288]{1,0:T(8,128)(2,1)S(1)}, u32[]{:S(2)}, u32[]{:S(2)}) collective-permute-start(bf16[464,288]{1,0:T(8,128)(2,1)S(1)} %fusion.52), channel_id=1, source_target_pairs={{0,2},{1,0},{2,3},{3,1},{4,6},{5,4},{6,7},{7,5},{8,10},{9,8},{10,1... | collective-permute-start | bytes 801800 | tf_op jit(solution)/shard_map/ppermute | solution.py:685
  37.5 10.0 %collective-permute-start.3 = (bf16[464,288]{1,0:T(8,128)(2,1)S(1)}, bf16[464,288]{1,0:T(8,128)(2,1)S(1)}, u32[]{:S(2)}, u32[]{:S(2)}) collective-permute-start(bf16[464,288]{1,0:T(8,128)(2,1)S(1)} %fusion.52), channel_id=1, source_target_pairs={{0,0},{1,2},{2,1},{3,3},{4,4},{5,6},{6,5},{7,7},{8,8},{9,10},{10,9... | collective-permute-start | bytes 801800 | tf_op jit(solution)/shard_map/ppermute | solution.py:685
  40.2 5.7 %collective-permute-start.12 = (bf16[112,224]{1,0:T(8,128)(2,1)S(1)}, bf16[112,224]{1,0:T(8,128)(2,1)S(1)}, u32[]{:S(2)}, u32[]{:S(2)}) collective-permute-start(bf16[112,224]{1,0:T(8,128)(2,1)S(1)} %bitcast.132), channel_id=1, source_target_pairs={{0,16},{4,20},{8,24},{12,28},{16,0},{20,4},{24,8},{28,12},{1,17},{... | collective-permute-start | bytes 150536 | tf_op jit(solution)/shard_map/ppermute | solution.py:23
  45.9 8.3 %collective-permute-start.10 = (bf16[112,1536]{1,0:T(8,128)(2,1)S(1)}, bf16[112,1536]{1,0:T(8,128)(2,1)S(1)}, u32[]{:S(2)}, u32[]{:S(2)}) collective-permute-start(bf16[112,1536]{1,0:T(8,128)(2,1)S(1)} %pad_maximum_fusion.10.rest_0_), channel_id=1, source_target_pairs={{0,4},{4,0},{8,12},{12,8},{16,20},{20,16},{24,28},{28,24},{1,5},{5... | collective-permute-start | bytes 1032200 | tf_op jit(solution)/shard_map/ppermute | solution.py:23
  47.4 4.9 %collective-permute-start.13 = (bf16[224,224]{1,0:T(8,128)(2,1)S(1)}, bf16[224,224]{1,0:T(8,128)(2,1)S(1)}, u32[]{:S(2)}, u32[]{:S(2)}) collective-permute-start(bf16[224,224]{1,0:T(8,128)(2,1)S(1)} %pad_maximum_fusion.14), channel_id=1, source_target_pairs={{0,8},{4,12},{8,0},{12,4},{16,24},{20,28},{24,16},{28,20},{1,9},{5... | collective-permute-start | bytes 301064 | tf_op jit(solution)/shard_map/ppermute | solution.py:23
  54.3 6.0 %collective-permute-start.16 = (bf16[448,224]{1,0:T(8,128)(2,1)S(1)}, bf16[448,224]{1,0:T(8,128)(2,1)S(1)}, u32[]{:S(2)}, u32[]{:S(2)}) collective-permute-start(bf16[448,224]{1,0:T(8,128)(2,1)S(1)} %pad_maximum_fusion.12), channel_id=1, source_target_pairs={{0,4},{4,0},{8,12},{12,8},{16,20},{20,16},{24,28},{28,24},{1,5},{5... | collective-permute-start | bytes 602120 | tf_op jit(solution)/shard_map/ppermute | solution.py:23
  55.7 6.7 %collective-permute-start.8 = (bf16[448,288]{1,0:T(8,128)(2,1)S(1)}, bf16[448,288]{1,0:T(8,128)(2,1)S(1)}, u32[]{:S(2)}, u32[]{:S(2)}) collective-permute-start(bf16[448,288]{1,0:T(8,128)(2,1)S(1)} %collective-permute-done.5), channel_id=1, source_target_pairs={{0,2},{1,0},{2,3},{3,1},{4,6},{5,4},{6,7},{7,5},{8,10},{9,8},{10,1... | collective-permute-start | bytes 774152 | tf_op jit(solution)/shard_map/ppermute | solution.py:685
  55.7 6.7 %collective-permute-start.7 = (bf16[448,288]{1,0:T(8,128)(2,1)S(1)}, bf16[448,288]{1,0:T(8,128)(2,1)S(1)}, u32[]{:S(2)}, u32[]{:S(2)}) collective-permute-start(bf16[448,288]{1,0:T(8,128)(2,1)S(1)} %collective-permute-done.5), channel_id=1, source_target_pairs={{0,0},{1,2},{2,1},{3,3},{4,4},{5,6},{6,5},{7,7},{8,8},{9,10},{10,9... | collective-permute-start | bytes 774152 | tf_op jit(solution)/shard_map/ppermute | solution.py:685
  56.4 27.3 %collective-permute-start.14 = (bf16[224,1536]{1,0:T(8,128)(2,1)S(1)}, bf16[224,1536]{1,0:T(8,128)(2,1)S(1)}, u32[]{:S(2)}, u32[]{:S(2)}) collective-permute-start(bf16[224,1536]{1,0:T(8,128)(2,1)S(1)} %pad_maximum_fusion.1), channel_id=1, source_target_pairs={{0,8},{4,12},{8,0},{12,4},{16,24},{20,28},{24,16},{28,20},{1,9},{5... | collective-permute-start | bytes 2064392 | tf_op jit(solution)/shard_map/ppermute | solution.py:23
  60.3 23.4 %collective-permute-start.11 = (bf16[112,1536]{1,0:T(8,128)(2,1)S(1)}, bf16[112,1536]{1,0:T(8,128)(2,1)S(1)}, u32[]{:S(2)}, u32[]{:S(2)}) collective-permute-start(bf16[112,1536]{1,0:T(8,128)(2,1)S(1)} %collective-permute-done.9.rest_1_), channel_id=1, source_target_pairs={{0,4},{4,0},{8,12},{12,8},{16,20},{20,16},{24,28},{28,24},{1,5},{5... | collective-permute-start | bytes 1032200 | tf_op jit(solution)/shard_map/ppermute | solution.py:23
  62.8 28.0 %collective-permute-start.18 = (bf16[896,224]{1,0:T(8,128)(2,1)S(1)}, bf16[896,224]{1,0:T(8,128)(2,1)S(1)}, u32[]{:S(2)}, u32[]{:S(2)}) collective-permute-start(bf16[896,224]{1,0:T(8,128)(2,1)S(1)} %pad_maximum_fusion.8), channel_id=1, source_target_pairs={{0,2},{1,0},{2,3},{3,1},{4,6},{5,4},{6,7},{7,5},{8,10},{9,8},{10,1... | collective-permute-start | bytes 1204232 | tf_op jit(solution)/shard_map/ppermute | solution.py:685
  67.1 23.8 %collective-permute-start.17 = (bf16[896,224]{1,0:T(8,128)(2,1)S(1)}, bf16[896,224]{1,0:T(8,128)(2,1)S(1)}, u32[]{:S(2)}, u32[]{:S(2)}) collective-permute-start(bf16[896,224]{1,0:T(8,128)(2,1)S(1)} %pad_maximum_fusion.8), channel_id=1, source_target_pairs={{0,0},{1,2},{2,1},{3,3},{4,4},{5,6},{6,5},{7,7},{8,8},{9,10},{10,9... | collective-permute-start | bytes 1204232 | tf_op jit(solution)/shard_map/ppermute | solution.py:685
  68.1 26.2 %collective-permute-start.15 = (bf16[112,2304]{1,0:T(8,128)(2,1)S(1)}, bf16[112,2304]{1,0:T(8,128)(2,1)S(1)}, u32[]{:S(2)}, u32[]{:S(2)}) collective-permute-start(bf16[112,2304]{1,0:T(8,128)(2,1)S(1)} %copy-done.26), channel_id=1, source_target_pairs={{0,16},{4,20},{8,24},{12,28},{16,0},{20,4},{24,8},{28,12},{1,17},{... | collective-permute-start | bytes 1548296 | tf_op jit(solution)/shard_map/ppermute | solution.py:23
  96.4 2.6 collective-permute-start.19
  97.5 17.5 %collective-permute-start.21 = (bf16[224,1536]{1,0:T(8,128)(2,1)S(1)}, bf16[224,1536]{1,0:T(8,128)(2,1)S(1)}, u32[]{:S(2)}, u32[]{:S(2)}) collective-permute-start(bf16[224,1536]{1,0:T(8,128)(2,1)S(1)} %collective-permute-done.14.rest_2_), channel_id=1, source_target_pairs={{0,4},{4,0},{8,12},{12,8},{16,20},{20,16},{24,28},{28,24},{1,5},{5... | collective-permute-start | bytes 2064392 | tf_op jit(solution)/shard_map/ppermute | solution.py:23
  115.0 5.4 %collective-permute-start.22 = (bf16[512,896]{1,0:T(8,128)(2,1)S(1)}, bf16[512,896]{1,0:T(8,128)(2,1)S(1)}, u32[]{:S(2)}, u32[]{:S(2)}) collective-permute-start(bf16[512,896]{1,0:T(8,128)(2,1)S(1)} %multiply_convert_fusion.x0_ref.refs_0_), channel_id=1, source_target_pairs={{0,1},{1,0},{2,3},{3,2},{4,5},{5,4},{6,7},{7,6},{8,9},{9,8},{10,11... | collective-permute-start | bytes 2752520 | tf_op jit(solution)/shard_map/ppermute | solution.py:23
  115.0 22.9 %collective-permute-start.20 = (bf16[512,896]{1,0:T(8,128)(2,1)S(1)}, bf16[512,896]{1,0:T(8,128)(2,1)}, u32[]{:S(2)}, u32[]{:S(2)}) collective-permute-start(bf16[512,896]{1,0:T(8,128)(2,1)S(1)} %multiply_convert_fusion.x0_ref.refs_0_), channel_id=1, source_target_pairs={{0,2},{1,3},{2,0},{3,1},{4,6},{5,7},{6,4},{7,5},{8,10},{9,11},{10,... | collective-permute-start | bytes 2752520 | tf_op jit(solution)/shard_map/ppermute | solution.py:23
  115.0 22.9 %collective-permute-start.24 = (bf16[512,896]{1,0:T(8,128)(2,1)}, bf16[512,896]{1,0:T(8,128)(2,1)}, u32[]{:S(2)}, u32[]{:S(2)}) collective-permute-start(bf16[512,896]{1,0:T(8,128)(2,1)} %get-tuple-element.105.g0_ref.refs_4_), channel_id=1, source_target_pairs={{0,1},{1,0},{2,3},{3,2},{4,5},{5,4},{6,7},{7,6},{8,9},{9,8},{10,11... | collective-permute-start | bytes 2752520 | tf_op jit(solution)/shard_map/ppermute | solution.py:23
  117.2 34.6 %collective-permute-start.27 = (bf16[224,2304]{1,0:T(8,128)(2,1)}, bf16[224,2304]{1,0:T(8,128)(2,1)S(1)}, u32[]{:S(2)}, u32[]{:S(2)}) collective-permute-start(bf16[224,2304]{1,0:T(8,128)(2,1)} %constant_dynamic-update-slice_fusion), channel_id=1, source_target_pairs={{0,4},{4,0},{8,12},{12,8},{16,20},{20,16},{24,28},{28,24},{1,5},{5... | collective-permute-start | bytes 3096584 | tf_op jit(solution)/shard_map/ppermute | solution.py:23
  117.8 34.0 %collective-permute-start.26 = (bf16[224,2304]{1,0:T(8,128)(2,1)}, bf16[224,2304]{1,0:T(8,128)(2,1)}, u32[]{:S(2)}, u32[]{:S(2)}) collective-permute-start(bf16[224,2304]{1,0:T(8,128)(2,1)} %constant_dynamic-update-slice_fusion), channel_id=1, source_target_pairs={{0,8},{4,12},{8,0},{12,4},{16,24},{20,28},{24,16},{28,20},{1,9},{5... | collective-permute-start | bytes 3096584 | tf_op jit(solution)/shard_map/ppermute | solution.py:23
  120.4 32.1 %collective-permute-start.25 = (bf16[512,896]{1,0:T(8,128)(2,1)}, bf16[512,896]{1,0:T(8,128)(2,1)S(1)}, u32[]{:S(2)}, u32[]{:S(2)}) collective-permute-start(bf16[512,896]{1,0:T(8,128)(2,1)} %collective-permute-done.6.g0_ref.refs_6_), channel_id=1, source_target_pairs={{0,1},{1,0},{2,3},{3,2},{4,5},{5,4},{6,7},{7,6},{8,9},{9,8},{10,11... | collective-permute-start | bytes 2752520 | tf_op jit(solution)/shard_map/ppermute | solution.py:23
  137.9 14.6 %collective-permute-start.23 = (bf16[512,896]{1,0:T(8,128)(2,1)}, bf16[512,896]{1,0:T(8,128)(2,1)}, u32[]{:S(2)}, u32[]{:S(2)}) collective-permute-start(bf16[512,896]{1,0:T(8,128)(2,1)} %collective-permute-done.20.x0_ref.refs_2_), channel_id=1, source_target_pairs={{0,1},{1,0},{2,3},{3,2},{4,5},{5,4},{6,7},{7,6},{8,9},{9,8},{10,11... | collective-permute-start | bytes 2752520 | tf_op jit(solution)/shard_map/ppermute | solution.py:23
  151.8 35.3 %collective-permute-start.28 = (bf16[224,2304]{1,0:T(8,128)(2,1)}, bf16[224,2304]{1,0:T(8,128)(2,1)}, u32[]{:S(2)}, u32[]{:S(2)}) collective-permute-start(bf16[224,2304]{1,0:T(8,128)(2,1)} %collective-permute-done.26.rest_2_), channel_id=1, source_target_pairs={{0,4},{4,0},{8,12},{12,8},{16,20},{20,16},{24,28},{28,24},{1,5},{5... | collective-permute-start | bytes 3096584 | tf_op jit(solution)/shard_map/ppermute | solution.py:23
  182.8 24.3 %collective-permute-start.29 = (bf16[448,1024]{1,0:T(8,128)(2,1)}, bf16[448,1024]{1,0:T(8,128)(2,1)S(1)}, u32[]{:S(2)}, u32[]{:S(2)}) collective-permute-start(bf16[448,1024]{1,0:T(8,128)(2,1)} %get-tuple-element.118), channel_id=1, source_target_pairs={{0,4},{4,0},{8,12},{12,8},{16,20},{20,16},{24,28},{28,24},{1,5},{5... | collective-permute-start | bytes 2752520 | tf_op jit(solution)/shard_map/ppermute | solution.py:23
  184.2 22.8 %collective-permute-start.30 = (bf16[448,512]{1,0:T(8,128)(2,1)}, bf16[448,512]{1,0:T(8,128)(2,1)S(1)}, u32[]{:S(2)}, u32[]{:S(2)}) collective-permute-start(bf16[448,512]{1,0:T(8,128)(2,1)} %get-tuple-element.119), channel_id=1, source_target_pairs={{0,8},{4,12},{8,0},{12,4},{16,24},{20,28},{24,16},{28,20},{1,9},{5... | collective-permute-start | bytes 1376264 | tf_op jit(solution)/shard_map/ppermute | solution.py:23
  207.1 4.1 collective-permute-start.31
  208.1 27.8 %collective-permute-start.34 = (bf16[224,512]{1,0:T(8,128)(2,1)S(1)}, bf16[224,512]{1,0:T(8,128)(2,1)S(1)}, u32[]{:S(2)}, u32[]{:S(2)}) collective-permute-start(bf16[224,512]{1,0:T(8,128)(2,1)S(1)} %get-tuple-element.197), channel_id=1, source_target_pairs={{0,4},{4,0},{8,12},{12,8},{16,20},{20,16},{24,28},{28,24},{1,5},{5... | collective-permute-start | bytes 688136 | tf_op jit(solution)/shard_map/ppermute | solution.py:23
  212.8 23.1 %collective-permute-start.32 = (bf16[512,896]{1,0:T(8,128)(2,1)S(1)}, bf16[512,896]{1,0:T(8,128)(2,1)}, u32[]{:S(2)}, u32[]{:S(2)}) collective-permute-start(bf16[512,896]{1,0:T(8,128)(2,1)S(1)} %get-tuple-element.190), channel_id=1, source_target_pairs={{0,2},{1,3},{2,0},{3,1},{4,6},{5,7},{6,4},{7,5},{8,10},{9,11},{10,... | collective-permute-start | bytes 2752520 | tf_op jit(solution)/shard_map/ppermute | solution.py:23
  214.7 21.2 %collective-permute-start.33 = (bf16[224,1024]{1,0:T(8,128)(2,1)S(1)}, bf16[224,1024]{1,0:T(8,128)(2,1)S(1)}, u32[]{:S(2)}, u32[]{:S(2)}) collective-permute-start(bf16[224,1024]{1,0:T(8,128)(2,1)S(1)} %get-tuple-element.183), channel_id=1, source_target_pairs={{0,8},{4,12},{8,0},{12,4},{16,24},{20,28},{24,16},{28,20},{1,9},{5... | collective-permute-start | bytes 1376264 | tf_op jit(solution)/shard_map/ppermute | solution.py:23
  239.0 10.9 %collective-permute-start.35 = (bf16[512,896]{1,0:T(8,128)(2,1)}, bf16[512,896]{1,0:T(8,128)(2,1)}, u32[]{:S(2)}, u32[]{:S(2)}) collective-permute-start(bf16[512,896]{1,0:T(8,128)(2,1)} %get-tuple-element.189), channel_id=1, source_target_pairs={{0,1},{1,0},{2,3},{3,2},{4,5},{5,4},{6,7},{7,6},{8,9},{9,8},{10,11... | collective-permute-start | bytes 2752520 | tf_op jit(solution)/shard_map/ppermute | solution.py:23
  245.1 70.3 %collective-permute-start.59 = (bf16[112,1536]{1,0:T(8,128)(2,1)}, bf16[112,1536]{1,0:T(8,128)(2,1)}, u32[]{:S(2)}, u32[]{:S(2)}) collective-permute-start(bf16[112,1536]{1,0:T(8,128)(2,1)} %pad_maximum_fusion.11), channel_id=1, source_target_pairs={{0,16},{4,20},{8,24},{12,28},{16,0},{20,4},{24,8},{28,12},{1,17},{... | collective-permute-start | bytes 1032200 | tf_op jit(solution)/shard_map/ppermute | solution.py:23
  248.5 71.8 %collective-permute-start.37 = (bf16[512,896]{1,0:T(8,128)(2,1)}, bf16[512,896]{1,0:T(8,128)(2,1)}, u32[]{:S(2)}, u32[]{:S(2)}) collective-permute-start(bf16[512,896]{1,0:T(8,128)(2,1)} %get-tuple-element.129), channel_id=1, source_target_pairs={{0,2},{1,3},{2,0},{3,1},{4,6},{5,7},{6,4},{7,5},{8,10},{9,11},{10,... | collective-permute-start | bytes 2752520 | tf_op jit(solution)/shard_map/ppermute | solution.py:23
  257.2 2.6 collective-permute-start.38
  257.6 65.5 %collective-permute-start.36 = (bf16[512,896]{1,0:T(8,128)(2,1)}, bf16[512,896]{1,0:T(8,128)(2,1)}, u32[]{:S(2)}, u32[]{:S(2)}) collective-permute-start(bf16[512,896]{1,0:T(8,128)(2,1)} %get-tuple-element.128), channel_id=1, source_target_pairs={{0,1},{1,0},{2,3},{3,2},{4,5},{5,4},{6,7},{7,6},{8,9},{9,8},{10,11... | collective-permute-start | bytes 2752520 | tf_op jit(solution)/shard_map/ppermute | solution.py:23
  262.7 18.5 %collective-permute-start.39 = (bf16[448,512]{1,0:T(8,128)(2,1)S(1)}, bf16[448,512]{1,0:T(8,128)(2,1)S(1)}, u32[]{:S(2)}, u32[]{:S(2)}) collective-permute-start(bf16[448,512]{1,0:T(8,128)(2,1)S(1)} %get-tuple-element.135), channel_id=1, source_target_pairs={{0,4},{4,0},{8,12},{12,8},{16,20},{20,16},{24,28},{28,24},{1,5},{5... | collective-permute-start | bytes 1376264 | tf_op jit(solution)/shard_map/ppermute | solution.py:23
  281.1 46.0 %collective-permute-start.41 = (bf16[448,768]{1,0:T(8,128)(2,1)}, bf16[448,768]{1,0:T(8,128)(2,1)S(1)}, u32[]{:S(2)}, u32[]{:S(2)}) collective-permute-start(bf16[448,768]{1,0:T(8,128)(2,1)} %get-tuple-element.150), channel_id=1, source_target_pairs={{0,8},{4,12},{8,0},{12,4},{16,24},{20,28},{24,16},{28,20},{1,9},{5... | collective-permute-start | bytes 2064392 | tf_op jit(solution)/shard_map/ppermute | solution.py:23
  281.2 56.1 %collective-permute-start.40 = (bf16[448,1536]{1,0:T(8,128)(2,1)}, bf16[448,1536]{1,0:T(8,128)(2,1)S(1)}, u32[]{:S(2)}, u32[]{:S(2)}) collective-permute-start(bf16[448,1536]{1,0:T(8,128)(2,1)} %get-tuple-element.147), channel_id=1, source_target_pairs={{0,4},{4,0},{8,12},{12,8},{16,20},{20,16},{24,28},{28,24},{1,5},{5... | collective-permute-start | bytes 4128776 | tf_op jit(solution)/shard_map/ppermute | solution.py:23
  315.4 11.7 %collective-permute-start.55 = (bf16[224,512]{1,0:T(8,128)(2,1)S(1)}, bf16[224,512]{1,0:T(8,128)(2,1)S(1)}, u32[]{:S(2)}, u32[]{:S(2)}) collective-permute-start(bf16[224,512]{1,0:T(8,128)(2,1)S(1)} %get-tuple-element.198), channel_id=1, source_target_pairs={{0,8},{4,12},{8,0},{12,4},{16,24},{20,28},{24,16},{28,20},{1,9},{5... | collective-permute-start | bytes 688136 | tf_op jit(solution)/shard_map/ppermute | solution.py:23
  320.4 24.4 %collective-permute-start.50 = (bf16[448,576]{1,0:T(8,128)(2,1)S(1)}, bf16[448,576]{1,0:T(8,128)(2,1)}, u32[]{:S(2)}, u32[]{:S(2)}) collective-permute-start(bf16[448,576]{1,0:T(8,128)(2,1)S(1)} %get-tuple-element.156), channel_id=1, source_target_pairs={{0,4},{4,0},{8,12},{12,8},{16,20},{20,16},{24,28},{28,24},{1,5},{5... | collective-permute-start | bytes 1548296 | tf_op jit(solution)/shard_map/ppermute | solution.py:23
  327.2 7.0 %collective-permute-start.56 = (bf16[112,512]{1,0:T(8,128)(2,1)S(1)}, bf16[112,512]{1,0:T(8,128)(2,1)S(1)}, u32[]{:S(2)}, u32[]{:S(2)}) collective-permute-start(bf16[112,512]{1,0:T(8,128)(2,1)S(1)} %fusion.58), channel_id=1, source_target_pairs={{0,16},{4,20},{8,24},{12,28},{16,0},{20,4},{24,8},{28,12},{1,17},{... | collective-permute-start | bytes 344072 | tf_op jit(solution)/shard_map/ppermute | solution.py:23
  334.3 9.7 %collective-permute-start.57 = (bf16[112,224]{1,0:T(8,128)(2,1)S(1)}, bf16[112,224]{1,0:T(8,128)(2,1)S(1)}, u32[]{:S(2)}, u32[]{:S(2)}) collective-permute-start(bf16[112,224]{1,0:T(8,128)(2,1)S(1)} %get-tuple-element.212), channel_id=1, source_target_pairs={{0,0},{1,2},{2,1},{3,3},{4,4},{5,6},{6,5},{7,7},{8,8},{9,10},{10,9... | collective-permute-start | bytes 150536 | tf_op jit(solution)/shard_map/ppermute | solution.py:691
  335.2 8.8 %collective-permute-start.58 = (bf16[112,224]{1,0:T(8,128)(2,1)S(1)}, bf16[112,224]{1,0:T(8,128)(2,1)S(1)}, u32[]{:S(2)}, u32[]{:S(2)}) collective-permute-start(bf16[112,224]{1,0:T(8,128)(2,1)S(1)} %get-tuple-element.213), channel_id=1, source_target_pairs={{0,1},{1,3},{2,0},{3,2},{4,5},{5,7},{6,4},{7,6},{8,9},{9,11},{10,8... | collective-permute-start | bytes 150536 | tf_op jit(solution)/shard_map/ppermute | solution.py:691
  341.8 13.5 %collective-permute-start.42 = (bf16[512,896]{1,0:T(8,128)(2,1)}, bf16[512,896]{1,0:T(8,128)(2,1)}, u32[]{:S(2)}, u32[]{:S(2)}) collective-permute-start(bf16[512,896]{1,0:T(8,128)(2,1)} %slice.672), channel_id=1, source_target_pairs={{0,1},{1,0},{2,3},{3,2},{4,5},{5,4},{6,7},{7,6},{8,9},{9,8},{10,11... | collective-permute-start | bytes 2752520 | tf_op jit(solution)/shard_map/ppermute | solution.py:23
  343.3 10.2 %collective-permute-start.44 = (bf16[224,768]{1,0:T(8,128)(2,1)S(1)}, bf16[224,768]{1,0:T(8,128)(2,1)}, u32[]{:S(2)}, u32[]{:S(2)}) collective-permute-start(bf16[224,768]{1,0:T(8,128)(2,1)S(1)} %copy-done.48), channel_id=1, source_target_pairs={{0,4},{4,0},{8,12},{12,8},{16,20},{20,16},{24,28},{28,24},{1,5},{5... | collective-permute-start | bytes 1032200 | tf_op jit(solution)/shard_map/ppermute | solution.py:23
  346.8 25.3 %collective-permute-start.51 = (bf16[224,576]{1,0:T(8,128)(2,1)}, bf16[224,576]{1,0:T(8,128)(2,1)}, u32[]{:S(2)}, u32[]{:S(2)}) collective-permute-start(bf16[224,576]{1,0:T(8,128)(2,1)} %get-tuple-element.192), channel_id=1, source_target_pairs={{0,8},{4,12},{8,0},{12,4},{16,24},{20,28},{24,16},{28,20},{1,9},{5... | collective-permute-start | bytes 774152 | tf_op jit(solution)/shard_map/ppermute | solution.py:23
  355.2 16.8 %collective-permute-start.43 = (bf16[224,1536]{1,0:T(8,128)(2,1)}, bf16[224,1536]{1,0:T(8,128)(2,1)S(1)}, u32[]{:S(2)}, u32[]{:S(2)}) collective-permute-start(bf16[224,1536]{1,0:T(8,128)(2,1)} %get-tuple-element.180), channel_id=1, source_target_pairs={{0,8},{4,12},{8,0},{12,4},{16,24},{20,28},{24,16},{28,20},{1,9},{5... | collective-permute-start | bytes 2064392 | tf_op jit(solution)/shard_map/ppermute | solution.py:23
  372.0 1.3 collective-permute-start.45
  373.3 32.3 %collective-permute-start.52 = (bf16[112,576]{1,0:T(8,128)(2,1)S(1)}, bf16[112,576]{1,0:T(8,128)(2,1)S(1)}, u32[]{:S(2)}, u32[]{:S(2)}) collective-permute-start(bf16[112,576]{1,0:T(8,128)(2,1)S(1)} %fusion.54), channel_id=1, source_target_pairs={{0,16},{4,20},{8,24},{12,28},{16,0},{20,4},{24,8},{28,12},{1,17},{... | collective-permute-start | bytes 387080 | tf_op jit(solution)/shard_map/ppermute | solution.py:23
  373.4 3.8 collective-permute-start.46
  377.2 3.7 collective-permute-start.47
  377.9 36.5 %collective-permute-start.60 = (bf16[112,2304]{1,0:T(8,128)(2,1)S(1)}, bf16[112,2304]{1,0:T(8,128)(2,1)S(1)}, u32[]{:S(2)}, u32[]{:S(2)}) collective-permute-start(bf16[112,2304]{1,0:T(8,128)(2,1)S(1)} %pad_maximum_fusion.7), channel_id=1, source_target_pairs={{0,16},{4,20},{8,24},{12,28},{16,0},{20,4},{24,8},{28,12},{1,17},{... | collective-permute-start | bytes 1548296 | tf_op jit(solution)/shard_map/ppermute | solution.py:23
  380.9 10.4 %collective-permute-start.48 = (f32[23,128]{1,0:T(8,128)S(1)}, f32[23,128]{1,0:T(8,128)S(1)}, u32[]{:S(2)}, u32[]{:S(2)}) collective-permute-start(f32[23,128]{1,0:T(8,128)S(1)} %add.255), channel_id=1, source_target_pairs={{0,8},{4,12},{8,0},{12,4},{16,24},{20,28},{24,16},{28,20},{1,9},{5... | collective-permute-start | bytes 35336 | tf_op jit(solution)/shard_map/ppermute | solution.py:23
  391.3 14.3 %collective-permute-start.49 = (f32[23,128]{1,0:T(8,128)S(1)}, f32[23,128]{1,0:T(8,128)S(1)}, u32[]{:S(2)}, u32[]{:S(2)}) collective-permute-start(f32[23,128]{1,0:T(8,128)S(1)} %add.256), channel_id=1, source_target_pairs={{0,16},{4,20},{8,24},{12,28},{16,0},{20,4},{24,8},{28,12},{1,17},{... | collective-permute-start | bytes 35336 | tf_op jit(solution)/shard_map/ppermute | solution.py:23
  406.7 4.2 collective-permute-start.53
  407.4 6.3 %collective-permute-start.54 = (bf16[112,288]{1,0:T(8,128)(2,1)S(1)}, bf16[112,288]{1,0:T(8,128)(2,1)S(1)}, u32[]{:S(2)}, u32[]{:S(2)}) collective-permute-start(bf16[112,288]{1,0:T(8,128)(2,1)S(1)} %get-tuple-element.211), channel_id=1, source_target_pairs={{0,1},{1,3},{2,0},{3,2},{4,5},{5,7},{6,4},{7,6},{8,9},{9,11},{10,8... | collective-permute-start | bytes 193544 | tf_op jit(solution)/shard_map/ppermute | solution.py:691
  (73 other events, 636.1 us)

commit v7 on v6

--- a/solution.py
+++ b/solution.py
@@ -601,11 +601,6 @@
         self.left -= 1
         return self.pieces[-1]
 
-    def double_all(self):
-        while self.left > 0:
-            self.double()
-        return self.pieces[-1]
-
     def send(self, *earlier):
         piece = self.pieces[self.sent]
         self.sent += 1
@@ -669,14 +664,6 @@
             self.step()
         totals = [kept + got.astype(f32) for kept, got in zip(self.kept, self.got)]
         return jnp.concatenate(totals, 1)
-
-
-def in_order(first, second, parity, axis=0):
-    return jnp.where(
-        parity == 0,
-        jnp.concatenate([first, second], axis),
-        jnp.concatenate([second, first], axis),
-    )
 
 
 def turned_pairs(block):
@@ -724,13 +711,24 @@
     group_width = 2 * qkv_cols
     query_width = group_width - 2 * HD
 
-    qkv_gather = Gather(qkv_weight, bits)
-    out_gather = Gather(out_weight.T, bits)
-
-    def both(block):
-        first, second = turned_pairs(block)
-        return in_order(first, second, sequence, 1)
-
+    bias_rows = jnp.pad(qkv_bias[None, :], ((0, 15), (0, 0)))
+    first, second = turned_pairs(
+        jnp.concatenate(
+            [
+                jnp.concatenate([qkv_weight, bias_rows], 0),
+                jnp.pad(out_weight.T, ((0, 16), (0, 0))),
+            ],
+            1,
+        )
+    )
+    low = jnp.where(sequence == 0, first, second)
+    high = jnp.where(sequence == 0, second, first)
+    qkv_own = jnp.concatenate([low[:, :qkv_cols], high[:, :qkv_cols]], 1)
+    bias_full = qkv_own[deep : deep + 1].astype(f32)
+    out_own = jnp.concatenate([low[:deep, qkv_cols:], high[:deep, qkv_cols:]], 1)
+    out_own = jnp.pad(out_own, ((0, 0), (0, HD)))
+    qkv_gather = Gather(qkv_own[:deep], bits)
+    out_gather = Gather(out_own, bits)
     down_flipped = down_weight.T
     mlp_gathers = []
     for start, stop in cuts(ff_cols):
@@ -763,8 +761,7 @@
             blocks = jnp.where((row >> bit) % 2 == 1, turned, blocks)
         return blocks.reshape(model_width)
 
-    input_rows = stored(layer_input)
-    grad_out = stored(cotangent)
+    input_rows = stored(after(layer_input, first, second))
     gain_one = stored(gain_attn[None, :])
     gain_two = stored(gain_mlp[None, :])
 
@@ -772,39 +769,35 @@
     normed_own = (input_rows * scale_one[:, None] * gain_one).astype(bf16)
     normed_other = flip(normed_own, "col", 0)
     cosine, sine_part = rope_tables(length)
+
+    near, far = mlp_gathers
+    a_own = qkv_gather.send()
+    a_four = qkv_gather.double()
+    a_two = qkv_gather.double(a_own)
+    a_beside = qkv_gather.send(a_own)
+    o_four = out_gather.double(a_two)
+    a_last = qkv_gather.send(a_beside)
+    qkv_pieces = qkv_gather.all()
+    near.ready(a_two)
+    n_four = near.double()
+    n_own = near.send(a_last)
+    o_two = out_gather.double()
+    grad_out = stored(after(cotangent, a_four))
     grad_blocks = [grad_out.astype(bf16)]
-
-    near, far = mlp_gathers
-    a_four = qkv_gather.double()
-    n_four = near.double(a_four)
-    a_two = qkv_gather.double_all()
-    a_rows = jnp.concatenate(qkv_gather.pieces, 0)
-    a_beside = qkv_gather.catch_up()
-    bias_rows = jnp.pad(qkv_bias[None, :], ((0, 15), (0, 0)))
-    a_first = both(jnp.concatenate([a_rows, bias_rows], 0))
-    bias_full = a_first[-16:-15].astype(f32)
     across = flip(grad_blocks[0], "col", 1)
-    a_last = both(after(a_beside, across))
-    qkv_pieces = [a_first[:-16], a_last]
-    o_four = out_gather.double(a_beside)
-    n_own = near.send(a_beside)
-    o_two = out_gather.double_all()
-    o_beside = out_gather.catch_up(n_own)
-    o_rows = jnp.concatenate([*out_gather.pieces, o_beside], 0)
-    n_two = near.double(o_two)
-    n_beside = near.send(n_own)
-    far.ready(a_last, n_four, o_four)
-    f_four = far.double()
-    out_full = jnp.pad(both(after(o_rows, a_last)), ((0, 0), (0, HD)))
-    out_pieces = [out_full]
     split = -(-(query_width + HD) // 256)
     qk_rows, value_rows, att_first, log_first = attend(
         parity, normed_own, normed_other, qkv_pieces, bias_full, cosine, sine_part, split
     )
-    n_last = near.send(n_beside, att_first)
-    att_last, log_last = attend_rest(parity, after(qk_rows, n_beside, n_two), value_rows, split)
+    out_pieces = out_gather.finish(att_first, o_two)
+    n_two = near.double(att_first)
+    n_beside = near.send(n_own)
+    att_last, log_last = attend_rest(parity, after(qk_rows, n_four, n_own), value_rows, split)
     log_totals = log_first + log_last
-    att_own, att_other = project(att_first, after(att_last, f_four), out_pieces)
+    far.ready(n_two)
+    f_four = far.double()
+    n_last = near.send(n_beside)
+    att_own, att_other = project(att_first, after(att_last, n_beside, n_two, across), out_pieces)
     att_got = flip(att_other, "col", 0)
     grad_blocks.append(flip(after(grad_blocks[0], att_got), "col", 0))
     grad_blocks += [across, flip(after(across, att_got), "col", 0)]
@@ -816,10 +809,10 @@
     blocks += [across, flip(across, "col", 0)]
 
     f_beside = far.catch_up(n_last)
-    f_two = far.double(blocks[0])
+    f_two = far.double(blocks[2])
     f_last = far.send(f_beside)
     first_pieces, second_pieces = (gather.all() for gather in mlp_gathers)
-    act_own, *sums_own = mlp(blocks[:2], grad_blocks[:2], first_pieces)
+    act_own, *sums_own = mlp([after(blocks[0], blocks[2]), blocks[1]], grad_blocks[:2], first_pieces)
     act_far, *sums_far = mlp(blocks[2:], grad_blocks[2:], first_pieces)
     sent_one, kept_one, sent_two, kept_two = outer(blocks, grad_blocks, [act_own, act_far])
     first_scatter = Scatter([(sent_one, kept_one), (sent_two, kept_two)], bits)
@@ -838,9 +831,7 @@
         sums_own,
     )
     first_scatter.step()
-    far_own = after(far_own, normed_back, *first_scatter.got)
-    beside = [flip(far_own[0], "col", 0)]
-    beside.append(flip(after(far_own[1], beside[0]), "col", 0))
+    beside = flip(after(far_own, normed_back, *first_scatter.got), "col", 0)
     first_scatter.step()
     down_back = flip(after(across[1], normed_back), "col", 1)
 
@@ -881,9 +872,13 @@
         split,
     )
     out_scatter.wait(mixed_first)
+    out_scatter.step()
+    first_scatter.wait(mixed_first)
+    first_total = first_scatter.total()
+    layer_output = unstored((middle + summed(1, after(down_back, mixed_first))).astype(bf16))
     mixed_last, bias_last = attend_back(
         parity,
-        after(branch_own, mixed_first),
+        after(branch_own, out_scatter.kept[0], first_total, layer_output),
         branch_other,
         out_pieces,
         qk_rows,
@@ -896,18 +891,14 @@
         carry,
     )
     bias_grad = jnp.concatenate([bias_first, bias_last], 1)[0]
-    first_scatter.wait(mixed_last)
     grad_mixed = jnp.concatenate([mixed_first, mixed_last], 1)
     qkv_scatter = Scatter([outer_one([normed_own, normed_other], grad_mixed)], bits)
     passed = qkv_scatter.kept[0]
-    first_scatter.wait(passed)
     second_scatter.wait(passed)
     out_scatter.wait(passed)
     second_scatter.step()
-    layer_output = unstored((middle + summed(1, after(down_back, passed))).astype(bf16))
     qkv_full = jnp.concatenate(qkv_pieces, 0)
     grad_mixed = after(grad_mixed, passed, *second_scatter.kept)
-    out_scatter.step()
     partial = jnp.einsum("tc,dc->td", grad_mixed, qkv_full, preferred_element_type=f32)
     grad_normed_one = partial[:tok_local] + flip(
         partial[tok_local:].astype(bf16), "col", 0
@@ -935,7 +926,6 @@
     )
     small = jnp.concatenate([unstored_row(gain_one_grad), unstored_row(gain_two_grad), bias_row])
     small = jnp.pad(small, (0, -small.shape[0] % 128)).reshape(-1, 128)
-    small = after(small, *second_scatter.got)
     second_scatter.step()
     for bit in range(2):
         small = small + flip(small, "col", bit)
@@ -948,7 +938,7 @@
     out_total = to_columns(out_scatter.total(), out_cols)
     mlp_totals = []
     for scatter, (start, stop) in zip((first_scatter, second_scatter), cuts(ff_cols)):
-        total = scatter.total()
+        total = first_total if scatter is first_scatter else scatter.total()
         padded = total.shape[1] // 3
         mlp_totals.append(
             [total[:, k * padded : k * padded + stop - start] for k in range(3)]

time: 426 us -> 425 us (level)
  local copies, waits for them, and re-layouts: 20.7 us -> 32.3 us
  starting transfers between devices: 64 us -> 54.4 us
    ppermute x51 -> x52, starting transfers between devices: 51.1 us -> 44.1 us  [flip(): return lax.ppermute(block, axis, [(i, i ^ 1 << bit) for i in range(count)])]
    unnamed x156 -> x180, local copies, waits for them, and re-layouts: 8.61 us -> 14.9 us
    ppermute x51 -> x52, waiting for transfers between devices: 109 us -> 106 us  [flip(): return lax.ppermute(block, axis, [(i, i ^ 1 << bit) for i in range(count)])]
  transfers between devices with their start and end apart: 61 -> 58, of which waited for: 21 -> 18; matrix products, arithmetic and copies ran while one was open for 16% -> 18% of each run, Pallas kernels for 38% -> 38%
where the time goes in v7:
time: 425 us; the launch traced here: 418 us
  Pallas kernels  163 us (38%)
  waiting for transfers between devices  109 us (26%)
  starting transfers between devices  54.4 us (13%)
  other arithmetic  39.8 us (9%)
  local copies, waits for them, and re-layouts  32.3 us (8%)
  matrix products  17.1 us (4%)
    ppermute x52, waiting for transfers between devices, flip(): return lax.ppermute(block, axis, [(i, i ^ 1 << bit) for i in range(count)])  106 us
    pallas_call x4, Pallas kernels, mlp(): pl.pallas_call(functools.partial(mlp_kernel, count=len(pieces), add=add),...  67.8 us
    ppermute x52, starting transfers between devices, flip(): return lax.ppermute(block, axis, [(i, i ^ 1 << bit) for i in range(count)])  44.1 us
    pallas_call x2, Pallas kernels, attend_back(): pl.pallas_call(functools.partial(attend_back_kernel, block=block, count=l...  33.5 us
    pallas_call x2, Pallas kernels, outer(): pl.pallas_call(functools.partial(outer_kernel, blocks=len(rows)), grid=(3...  32.2 us
    unnamed x180, local copies, waits for them, and re-layouts  14.9 us
    pallas_call x1, Pallas kernels, attend(): pl.pallas_call(functools.partial(attend_kernel, block=block, count=len(pi...  13.9 us
  transfers between devices with their start and end apart: 58, of which 18 were waited for; matrix products, arithmetic and copies ran while one was open for 18% of the time, Pallas kernels for 38%

profile of v7, /device:TPU:0, one launch (start us, length us, event | category | flops | bytes accessed | tf_op | source)
XLA Modules:
  0.0 418.1 jit_solution(9900672069235101850)
XLA Ops:
  3.5 3.0 collective-permute-start.1
  9.6 2.0 fusion.46
  13.8 1.5 collective-permute-start.4
  15.3 2.6 collective-permute-start.3
  17.9 1.3 multiply_reduce_fusion.5
  20.4 5.4 %collective-permute-done.3.rest_6_ = bf16[112,576]{1,0:T(8,128)(2,1)S(1)} collective-permute-done((bf16[112,576]{1,0:T(8,128)(2,1)S(1)}, bf16[112,576]{1,0:T(8,128)(2,1)S(1)}, u32[]{:S(2)}, u32[]{:S(2)}) %collective-permute-start.3) | collective-permute-done | bytes 129056 | tf_op jit(solution)/shard_map/ppermute | solution.py:23
  30.9 4.8 %collective-permute-done.5.rest_7_ = bf16[224,576]{1,0:T(8,128)(2,1)} collective-permute-done((bf16[224,576]{1,0:T(8,128)(2,1)}, bf16[224,576]{1,0:T(8,128)(2,1)}, u32[]{:S(2)}, u32[]{:S(2)}) %collective-permute-start.5) | collective-permute-done | bytes 258080 | tf_op jit(solution)/shard_map/ppermute | solution.py:23
  35.7 2.4 collective-permute-start.13
  39.2 2.5 fusion.67
  41.7 10.2 %collective-permute-done.13.rest_1_ = bf16[112,512]{1,0:T(8,128)(2,1)S(1)} collective-permute-done((bf16[112,512]{1,0:T(8,128)(2,1)S(1)}, bf16[112,512]{1,0:T(8,128)(2,1)S(1)}, u32[]{:S(2)}, u32[]{:S(2)}) %collective-permute-start.13) | collective-permute-done | bytes 114720 | tf_op jit(solution)/shard_map/ppermute | solution.py:23
  52.7 5.7 %collective-permute-done.8.rest_1_ = bf16[112,1536]{1,0:T(8,128)(2,1)S(1)} collective-permute-done((bf16[112,1536]{1,0:T(8,128)(2,1)}, bf16[112,1536]{1,0:T(8,128)(2,1)S(1)}, u32[]{:S(2)}, u32[]{:S(2)}) %collective-permute-start.8) | collective-permute-done | bytes 344096 | tf_op jit(solution)/shard_map/ppermute | solution.py:23
  58.5 13.9 %shard_map.186 = (bf16[1024,512]{1,0:T(8,128)(2,1)S(1)}, bf16[1024,64]{1,0:T(8,128)(2,1)S(1)}, bf16[1024,256]{1,0:T(8,128)(2,1)S(1)}, f32[8,1024]{1,0:T(8,128)S(1)}) custom-call(s32[1]{0:T(128)} %bitcast.1.parity_ref, bf16[512,896]{1,0:T(8,128)(2,1)S(1)} %multiply_convert_fusion.1.rest_0_.refs_0_, bf16[512,896]{1,0:T(8,128)(2,1)} %collective-permute-done.2.rest_1_.refs_1_, ...), custom_call_target="tpu_custom_call" | custom-call | flops 8000000000 | bytes 6000000 | tf_op jit(solution)/shard_map/pallas_call | solution.py:167
  73.8 1.6 collective-permute-start.10
  75.4 7.0 %shard_map.187 = (bf16[1024,256]{1,0:T(8,128)(2,1)S(1)}, f32[8,1024]{1,0:T(8,128)S(1)}) custom-call(s32[1]{0:T(128)} %bitcast.1.parity_ref, bf16[1024,512]{1,0:T(8,128)(2,1)S(1)} %get-tuple-element.95.rest_0_.qk_ref, bf16[1024,64]{1,0:T(8,128)(2,1)S(1)} %get-tuple-element.96.rest_1_.v_ref), custom_call_target="tpu_custom_call" | custom-call | flops 6000000000 | bytes 4000000 | tf_op jit(solution)/shard_map/pallas_call | solution.py:201
  82.5 10.3 %collective-permute-done.10.rest_4_ = bf16[112,1536]{1,0:T(8,128)(2,1)S(1)} collective-permute-done((bf16[112,1536]{1,0:T(8,128)(2,1)S(1)}, bf16[112,1536]{1,0:T(8,128)(2,1)S(1)}, u32[]{:S(2)}, u32[]{:S(2)}) %collective-permute-start.10) | collective-permute-done | bytes 344096 | tf_op jit(solution)/shard_map/ppermute | solution.py:23
  93.6 2.6 shard_map.188
  100.8 3.3 collective-permute-start.23
  104.2 10.8 %collective-permute-done.18.rest_5_ = bf16[224,1536]{1,0:T(8,128)(2,1)} collective-permute-done((bf16[224,1536]{1,0:T(8,128)(2,1)S(1)}, bf16[224,1536]{1,0:T(8,128)(2,1)}, u32[]{:S(2)}, u32[]{:S(2)}) %collective-permute-start.18) | collective-permute-done | bytes 688160 | tf_op jit(solution)/shard_map/ppermute | solution.py:23
  115.5 11.5 %collective-permute-done.23.rest_1_ = bf16[112,2304]{1,0:T(8,128)(2,1)S(1)} collective-permute-done((bf16[112,2304]{1,0:T(8,128)(2,1)S(1)}, bf16[112,2304]{1,0:T(8,128)(2,1)S(1)}, u32[]{:S(2)}, u32[]{:S(2)}) %collective-permute-start.23) | collective-permute-done | bytes 516128 | tf_op jit(solution)/shard_map/ppermute | solution.py:23
  129.2 13.9 %shard_map.189 = (bf16[1024,1536]{1,0:T(8,128)(2,1)}, bf16[2,512,896]{2,1,0:T(8,128)(2,1)}, bf16[2,512,896]{2,1,0:T(8,128)(2,1)}) custom-call(bf16[512,896]{1,0:T(8,128)(2,1)} %copy-done.43, bf16[512,896]{1,0:T(8,128)(2,1)} %copy-done.80, bf16[512,896]{1,0:T(8,128)(2,1)} %copy-done.78, bf16[512,896]{1,0:T(8,128)(2,1)} %collective-permute-done.21.g1_ref.refs_5_, ...), custom_call_target="tpu_custom_call" | custom-call | flops 5637144576 | bytes 31457280 | tf_op jit(solution)/shard_map/pallas_call | solution.py:478
  143.1 8.9 %collective-permute-done.25.rest_3_ = bf16[224,2304]{1,0:T(8,128)(2,1)} collective-permute-done((bf16[224,2304]{1,0:T(8,128)(2,1)S(1)}, bf16[224,2304]{1,0:T(8,128)(2,1)}, u32[]{:S(2)}, u32[]{:S(2)}) %collective-permute-start.25) | collective-permute-done | bytes 1032224 | tf_op jit(solution)/shard_map/ppermute | solution.py:23
  152.2 1.5 collective-permute-start.26
  153.8 13.9 %shard_map.190 = (bf16[1024,1536]{1,0:T(8,128)(2,1)}, bf16[2,512,896]{2,1,0:T(8,128)(2,1)}, bf16[2,512,896]{2,1,0:T(8,128)(2,1)}) custom-call(bf16[512,896]{1,0:T(8,128)(2,1)} %copy-done.79, bf16[512,896]{1,0:T(8,128)(2,1)} %collective-permute-done.20.x1_ref.refs_3_, bf16[512,896]{1,0:T(8,128)(2,1)} %collective-permute-done.12.g0_ref.refs_6_, ...), custom_call_target="tpu_custom_call" | custom-call | flops 5637144576 | bytes 31457280 | tf_op jit(solution)/shard_map/pallas_call | solution.py:478
  167.6 15.6 %shard_map.191 = (bf16[448,1024]{1,0:T(8,128)(2,1)}, f32[448,1024]{1,0:T(8,128)}, bf16[448,512]{1,0:T(8,128)(2,1)}, f32[448,512]{1,0:T(8,128)}) custom-call(bf16[512,896]{1,0:T(8,128)(2,1)} %copy-done.43, bf16[512,896]{1,0:T(8,128)(2,1)} %copy-done.80, bf16[512,896]{1,0:T(8,128)(2,1)} %copy-done.79, bf16[512,896]{1,0:T(8,128)(2,1)} %collective-permute-done.20.x1_ref.refs_3_, ...), custom_call_target="tpu_custom_call" | custom-call | flops 5637144576 | bytes 20971520 | tf_op jit(solution)/shard_map/pallas_call | solution.py:542
  185.0 19.9 %shard_map.192 = (bf16[1024,2304]{1,0:T(8,128)(2,1)}, bf16[2,512,896]{2,1,0:T(8,128)(2,1)}, bf16[2,512,896]{2,1,0:T(8,128)(2,1)}) custom-call(bf16[512,896]{1,0:T(8,128)(2,1)} %copy-done.79, bf16[512,896]{1,0:T(8,128)(2,1)} %collective-permute-done.20.x1_ref.refs_3_, bf16[512,896]{1,0:T(8,128)(2,1)} %collective-permute-done.12.g0_ref.refs_6_, ...), custom_call_target="tpu_custom_call" | custom-call | flops 8455716864 | bytes 31457280 | tf_op jit(solution)/shard_map/pallas_call | solution.py:478
  206.1 1.5 collective-permute-start.32
  207.6 1.4 collective-permute-done.29
  210.6 1.7 collective-permute-start.30
  213.6 1.7 collective-permute-start.31
  215.3 20.1 %shard_map.193 = (bf16[1024,2304]{1,0:T(8,128)(2,1)}, bf16[2,512,896]{2,1,0:T(8,128)(2,1)}, bf16[2,512,896]{2,1,0:T(8,128)(2,1)}) custom-call(bf16[512,896]{1,0:T(8,128)(2,1)} %copy-done.43, bf16[512,896]{1,0:T(8,128)(2,1)} %copy-done.80, bf16[512,896]{1,0:T(8,128)(2,1)} %copy-done.78, bf16[512,896]{1,0:T(8,128)(2,1)} %collective-permute-done.21.g1_ref.refs_5_, ...), custom_call_target="tpu_custom_call" | custom-call | flops 8455716864 | bytes 31457280 | tf_op jit(solution)/shard_map/pallas_call | solution.py:478
  236.9 1.8 constant_dynamic-update-slice_fusion.7
  245.6 2.3 multiply_reduce_fusion
  249.2 4.7 %fusion.58 = (bf16[512,896]{1,0:T(8,128)(2,1)S(1)}, f32[512,896]{1,0:T(8,128)}) fusion(f32[512,896]{1,0:T(8,128)} %copy-done.23, f32[512]{0:T(512)} %fusion.55, f32[512,896]{1,0:T(8,128)} %get-tuple-element.256, bf16[512,896]{1,0:T(8,128)(2,1)} %collective-permute-done.30, bf16[2,512,896]{2,1,0:T(8,128)(2,1)} %collective-permute-done.33, ...), kind=kLoop, calls=%fused_computation.187 | loop fusion | flops 5046272 | bytes 9182720 | tf_op jit(solution)/shard_map/convert_element_type | solution.py:850
  255.2 1.4 concatenate.143
  256.5 1.4 reshape.250
  259.1 1.4 reshape.249
  261.8 1.4 reshape.248
  264.5 2.9 shard_map.194
  267.4 1.6 collective-permute-start.36
  269.0 16.6 %shard_map.195 = (bf16[448,1536]{1,0:T(8,128)(2,1)}, f32[448,1536]{1,0:T(8,128)}, bf16[448,768]{1,0:T(8,128)(2,1)}, f32[448,768]{1,0:T(8,128)}) custom-call(bf16[512,896]{1,0:T(8,128)(2,1)} %copy-done.43, bf16[512,896]{1,0:T(8,128)(2,1)} %copy-done.80, bf16[512,896]{1,0:T(8,128)(2,1)} %copy-done.79, bf16[512,896]{1,0:T(8,128)(2,1)} %collective-permute-done.20.x1_ref.refs_3_, ...), custom_call_target="tpu_custom_call" | custom-call | flops 8455716864 | bytes 20971520 | tf_op jit(solution)/shard_map/pallas_call | solution.py:542
  285.6 1.8 collective-permute-start.40
  288.5 18.5 %shard_map.196 = (bf16[1024,256]{1,0:T(8,128)(2,1)S(1)}, f32[1,256]{1,0:T(1,128)S(1)}, f32[1024,128]{1,0:T(8,128)S(1)}, f32[1024,128]{1,0:T(8,128)S(1)}) custom-call(s32[1]{0:T(128)} %bitcast.1.parity_ref, bf16[512,896]{1,0:T(8,128)(2,1)} %copy-done.2, bf16[512,896]{1,0:T(8,128)(2,1)} %collective-permute-done.35.refs_1_.other_ref, ...), custom_call_target="tpu_custom_call" | custom-call | flops 12000000000 | bytes 6000000 | tf_op jit(solution)/shard_map/pallas_call | solution.py:394
  308.1 3.9 fusion.14
  312.2 2.1 collective-permute-start.52
  314.3 15.0 %shard_map.197 = (bf16[1024,320]{1,0:T(8,128)(2,1)S(1)}, f32[1,320]{1,0:T(1,128)S(1)}) custom-call(s32[1]{0:T(128)} %bitcast.1.parity_ref, bf16[512,896]{1,0:T(8,128)(2,1)} %copy-done.2, bf16[512,896]{1,0:T(8,128)(2,1)} %collective-permute-done.35.refs_1_.other_ref, bf16[1024,512]{1,0:T(8,128)(2,1)} %copy-done.20, bf16[1024,64]{1,0:T(8,128)(2,1)S(1)} %copy-done.22, ...), custom_call_target="tpu_custom_call" | custom-call | flops 12000000000 | bytes 6000000 | tf_op jit(solution)/shard_map/pallas_call | solution.py:394
  329.5 3.4 shard_map.198
  333.8 1.5 collective-permute-start.56
  336.6 2.6 collective-permute-start.54
  339.3 3.1 add_convert_fusion.1
  342.4 3.6 fusion.68
  345.9 2.5 slice.696
  350.6 1.9 fusion.34
  352.5 3.0 collective-permute-done.47
  358.7 2.5 multiply_reduce_fusion.1
  361.8 6.1 %collective-permute-done.48 = bf16[224,576]{1,0:T(8,128)(2,1)S(1)} collective-permute-done((bf16[224,576]{1,0:T(8,128)(2,1)S(1)}, bf16[224,576]{1,0:T(8,128)(2,1)S(1)}, u32[]{:S(2)}, u32[]{:S(2)}) %collective-permute-start.48) | collective-permute-done | bytes 258080 | tf_op jit(solution)/shard_map/ppermute | solution.py:23
  369.5 12.0 %collective-permute-done.55 = bf16[224,1536]{1,0:T(8,128)(2,1)} collective-permute-done((bf16[224,1536]{1,0:T(8,128)(2,1)}, bf16[224,1536]{1,0:T(8,128)(2,1)}, u32[]{:S(2)}, u32[]{:S(2)}) %collective-permute-start.55) | collective-permute-done | bytes 688160 | tf_op jit(solution)/shard_map/ppermute | solution.py:23
  382.7 1.6 collective-permute-start.44
  384.4 2.1 collective-permute-done.44
  386.6 6.6 %collective-permute-done.45 = f32[23,128]{1,0:T(8,128)S(1)} collective-permute-done((f32[23,128]{1,0:T(8,128)S(1)}, f32[23,128]{1,0:T(8,128)S(1)}, u32[]{:S(2)}, u32[]{:S(2)}) %collective-permute-start.45) | collective-permute-done | bytes 11808 | tf_op jit(solution)/shard_map/ppermute | solution.py:23
  393.3 2.7 collective-permute-start.46
  396.0 4.5 %fusion.15 = bf16[512,896]{1,0:T(8,128)(2,1)} fusion(s32[896]{0:T(1024)S(1)} %copy-done.74, f32[512,896]{1,0:T(8,128)S(1)} %copy-done.29, f32[512,896]{1,0:T(8,128)S(1)} %copy-done.36, f32[512]{0:T(512)S(1)} %fusion.57, f32[896]{0:T(1024)S(1)} %copy-done.69, f32[512]{0:T(512)S(1)} %copy-done.66, f32[1024,896]{1,0:T(8,128)} %fusion.68, ...), kind=kOutput, calls=%fused_computation.35 | convolution fusion | flops 827015168 | bytes 7351296 | tf_op jit(solution)/shard_map/dot_general | solution.py:751
  400.4 6.1 %collective-permute-done.46 = f32[23,128]{1,0:T(8,128)S(1)} collective-permute-done((f32[23,128]{1,0:T(8,128)S(1)}, f32[23,128]{1,0:T(8,128)S(1)}, u32[]{:S(2)}, u32[]{:S(2)}) %collective-permute-start.46) | collective-permute-done | bytes 11808 | tf_op jit(solution)/shard_map/ppermute | solution.py:23
  407.4 2.6 collective-permute-start.51
  411.3 2.3 collective-permute-done.51
  (371 shorter events, 65.6 us)
Async XLA Ops:
  3.5 9.5 %collective-permute-start.1 = (bf16[128,512]{1,0:T(8,128)(2,1)S(1)}, bf16[128,512]{1,0:T(8,128)(2,1)S(1)}, u32[]{:S(2)}, u32[]{:S(2)}) collective-permute-start(bf16[128,512]{1,0:T(8,128)(2,1)S(1)} %fusion.47), channel_id=1, source_target_pairs={{0,2},{1,0},{2,3},{3,1},{4,6},{5,4},{6,7},{7,5},{8,10},{9,8},{10,1... | collective-permute-start | bytes 393224 | tf_op jit(solution)/shard_map/ppermute | solution.py:672
  6.5 6.5 %collective-permute-start = (bf16[128,512]{1,0:T(8,128)(2,1)S(1)}, bf16[128,512]{1,0:T(8,128)(2,1)S(1)}, u32[]{:S(2)}, u32[]{:S(2)}) collective-permute-start(bf16[128,512]{1,0:T(8,128)(2,1)S(1)} %fusion.47), channel_id=1, source_target_pairs={{0,0},{1,2},{2,1},{3,3},{4,4},{5,6},{6,5},{7,7},{8,8},{9,10},{10,9... | collective-permute-start | bytes 393224 | tf_op jit(solution)/shard_map/ppermute | solution.py:672
  8.0 88.3 %copy-start.72 = (s32[896]{0:T(1024)}, s32[896]{0:T(1024)S(1)}, u32[]{:S(2)}) copy-start(s32[896]{0:T(1024)S(1)} %fusion.50) | copy-start | bytes 10756
  13.8 12.7 %collective-permute-start.4 = (bf16[112,576]{1,0:T(8,128)(2,1)S(1)}, bf16[112,576]{1,0:T(8,128)(2,1)S(1)}, u32[]{:S(2)}, u32[]{:S(2)}) collective-permute-start(bf16[112,576]{1,0:T(8,128)(2,1)S(1)} %get-tuple-element.179.rest_5_), channel_id=1, source_target_pairs={{0,4},{4,0},{8,12},{12,8},{16,20},{20,16},{24,28},{28,24},{1,5},{5... | collective-permute-start | bytes 387080 | tf_op jit(solution)/shard_map/ppermute | solution.py:23
  15.3 10.5 %collective-permute-start.3 = (bf16[112,576]{1,0:T(8,128)(2,1)S(1)}, bf16[112,576]{1,0:T(8,128)(2,1)S(1)}, u32[]{:S(2)}, u32[]{:S(2)}) collective-permute-start(bf16[112,576]{1,0:T(8,128)(2,1)S(1)} %get-tuple-element.179.rest_5_), channel_id=1, source_target_pairs={{0,16},{4,20},{8,24},{12,28},{16,0},{20,4},{24,8},{28,12},{1,17},{... | collective-permute-start | bytes 387080 | tf_op jit(solution)/shard_map/ppermute | solution.py:23
  19.6 38.9 %collective-permute-start.2 = (bf16[512,896]{1,0:T(8,128)(2,1)S(1)}, bf16[512,896]{1,0:T(8,128)(2,1)}, u32[]{:S(2)}, u32[]{:S(2)}) collective-permute-start(bf16[512,896]{1,0:T(8,128)(2,1)S(1)} %multiply_convert_fusion.1.rest_0_.refs_0_), channel_id=1, source_target_pairs={{0,1},{1,0},{2,3},{3,2},{4,5},{5,4},{6,7},{7,6},{8,9},{9,8},{10,11... | collective-permute-start | bytes 2752520 | tf_op jit(solution)/shard_map/ppermute | solution.py:23
  26.6 9.2 %collective-permute-start.5 = (bf16[224,576]{1,0:T(8,128)(2,1)}, bf16[224,576]{1,0:T(8,128)(2,1)}, u32[]{:S(2)}, u32[]{:S(2)}) collective-permute-start(bf16[224,576]{1,0:T(8,128)(2,1)} %pad_maximum_fusion.11), channel_id=1, source_target_pairs={{0,8},{4,12},{8,0},{12,4},{16,24},{20,28},{24,16},{28,20},{1,9},{5... | collective-permute-start | bytes 774152 | tf_op jit(solution)/shard_map/ppermute | solution.py:23
  28.3 7.5 %collective-permute-start.6 = (bf16[112,576]{1,0:T(8,128)(2,1)S(1)}, bf16[112,576]{1,0:T(8,128)(2,1)S(1)}, u32[]{:S(2)}, u32[]{:S(2)}) collective-permute-start(bf16[112,576]{1,0:T(8,128)(2,1)S(1)} %collective-permute-done.3.rest_6_), channel_id=1, source_target_pairs={{0,4},{4,0},{8,12},{12,8},{16,20},{20,16},{24,28},{28,24},{1,5},{5... | collective-permute-start | bytes 387080 | tf_op jit(solution)/shard_map/ppermute | solution.py:23
  35.7 16.2 %collective-permute-start.13 = (bf16[112,512]{1,0:T(8,128)(2,1)S(1)}, bf16[112,512]{1,0:T(8,128)(2,1)S(1)}, u32[]{:S(2)}, u32[]{:S(2)}) collective-permute-start(bf16[112,512]{1,0:T(8,128)(2,1)S(1)} %fusion.49.rest_0_), channel_id=1, source_target_pairs={{0,16},{4,20},{8,24},{12,28},{16,0},{20,4},{24,8},{28,12},{1,17},{... | collective-permute-start | bytes 344072 | tf_op jit(solution)/shard_map/ppermute | solution.py:23
  38.2 13.9 %collective-permute-start.7 = (bf16[224,576]{1,0:T(8,128)(2,1)}, bf16[224,576]{1,0:T(8,128)(2,1)S(1)}, u32[]{:S(2)}, u32[]{:S(2)}) collective-permute-start(bf16[224,576]{1,0:T(8,128)(2,1)} %collective-permute-done.5.rest_7_), channel_id=1, source_target_pairs={{0,4},{4,0},{8,12},{12,8},{16,20},{20,16},{24,28},{28,24},{1,5},{5... | collective-permute-start | bytes 774152 | tf_op jit(solution)/shard_map/ppermute | solution.py:23
  38.7 19.7 %collective-permute-start.8 = (bf16[112,1536]{1,0:T(8,128)(2,1)}, bf16[112,1536]{1,0:T(8,128)(2,1)S(1)}, u32[]{:S(2)}, u32[]{:S(2)}) collective-permute-start(bf16[112,1536]{1,0:T(8,128)(2,1)} %pad_maximum_fusion.9.rest_0_), channel_id=1, source_target_pairs={{0,16},{4,20},{8,24},{12,28},{16,0},{20,4},{24,8},{28,12},{1,17},{... | collective-permute-start | bytes 1032200 | tf_op jit(solution)/shard_map/ppermute | solution.py:23
  41.7 73.2 %copy-start.78 = (bf16[512,896]{1,0:T(8,128)(2,1)}, bf16[512,896]{1,0:T(8,128)(2,1)S(1)}, u32[]{:S(2)}) copy-start(bf16[512,896]{1,0:T(8,128)(2,1)S(1)} %get-tuple-element.108.g0_ref.refs_4_) | copy-start | bytes 2752516
  41.7 40.8 %collective-permute-start.12 = (bf16[512,896]{1,0:T(8,128)(2,1)S(1)}, bf16[512,896]{1,0:T(8,128)(2,1)}, u32[]{:S(2)}, u32[]{:S(2)}) collective-permute-start(bf16[512,896]{1,0:T(8,128)(2,1)S(1)} %get-tuple-element.108.g0_ref.refs_4_), channel_id=1, source_target_pairs={{0,2},{1,3},{2,0},{3,1},{4,6},{5,7},{6,4},{7,5},{8,10},{9,11},{10,... | collective-permute-start | bytes 2752520 | tf_op jit(solution)/shard_map/ppermute | solution.py:23
  51.9 41.6 %copy-start.8 = (bf16[112,512]{1,0:T(8,128)(2,1)}, bf16[112,512]{1,0:T(8,128)(2,1)S(1)}, u32[]{:S(2)}) copy-start(bf16[112,512]{1,0:T(8,128)(2,1)S(1)} %collective-permute-done.13.rest_1_) | copy-start | bytes 344068
  51.9 21.2 %collective-permute-start.14 = (bf16[224,512]{1,0:T(8,128)(2,1)S(1)}, bf16[224,512]{1,0:T(8,128)(2,1)S(1)}, u32[]{:S(2)}, u32[]{:S(2)}) collective-permute-start(bf16[224,512]{1,0:T(8,128)(2,1)S(1)} %pad_maximum_fusion.12), channel_id=1, source_target_pairs={{0,8},{4,12},{8,0},{12,4},{16,24},{20,28},{24,16},{28,20},{1,9},{5... | collective-permute-start | bytes 688136 | tf_op jit(solution)/shard_map/ppermute | solution.py:23
  52.1 21.8 %collective-permute-start.9 = (bf16[112,1536]{1,0:T(8,128)(2,1)S(1)}, bf16[112,1536]{1,0:T(8,128)(2,1)S(1)}, u32[]{:S(2)}, u32[]{:S(2)}) collective-permute-start(bf16[112,1536]{1,0:T(8,128)(2,1)S(1)} %copy-done.42), channel_id=1, source_target_pairs={{0,4},{4,0},{8,12},{12,8},{16,20},{20,16},{24,28},{28,24},{1,5},{5... | collective-permute-start | bytes 1032200 | tf_op jit(solution)/shard_map/ppermute | solution.py:23
  72.4 20.4 %collective-permute-start.11 = (bf16[224,1536]{1,0:T(8,128)(2,1)S(1)}, bf16[224,1536]{1,0:T(8,128)(2,1)S(1)}, u32[]{:S(2)}, u32[]{:S(2)}) collective-permute-start(bf16[224,1536]{1,0:T(8,128)(2,1)S(1)} %pad_maximum_fusion.1), channel_id=1, source_target_pairs={{0,8},{4,12},{8,0},{12,4},{16,24},{20,28},{24,16},{28,20},{1,9},{5... | collective-permute-start | bytes 2064392 | tf_op jit(solution)/shard_map/ppermute | solution.py:23
  73.2 20.3 %collective-permute-start.15 = (bf16[448,512]{1,0:T(8,128)(2,1)S(1)}, bf16[448,512]{1,0:T(8,128)(2,1)S(1)}, u32[]{:S(2)}, u32[]{:S(2)}) collective-permute-start(bf16[448,512]{1,0:T(8,128)(2,1)S(1)} %pad_maximum_fusion.8), channel_id=1, source_target_pairs={{0,4},{4,0},{8,12},{12,8},{16,20},{20,16},{24,28},{28,24},{1,5},{5... | collective-permute-start | bytes 1376264 | tf_op jit(solution)/shard_map/ppermute | solution.py:23
  73.8 19.0 %collective-permute-start.10 = (bf16[112,1536]{1,0:T(8,128)(2,1)S(1)}, bf16[112,1536]{1,0:T(8,128)(2,1)S(1)}, u32[]{:S(2)}, u32[]{:S(2)}) collective-permute-start(bf16[112,1536]{1,0:T(8,128)(2,1)S(1)} %collective-permute-done.8.rest_1_), channel_id=1, source_target_pairs={{0,4},{4,0},{8,12},{12,8},{16,20},{20,16},{24,28},{28,24},{1,5},{5... | collective-permute-start | bytes 1032200 | tf_op jit(solution)/shard_map/ppermute | solution.py:23
  96.2 2.5 collective-permute-start.16
  97.0 148.6 %copy-start.63 = (f32[896]{0:T(1024)}, f32[896]{0:T(1024)S(1)}, u32[]{:S(2)}) copy-start(f32[896]{0:T(1024)S(1)} %fusion.17) | copy-start | bytes 10756
  97.0 18.0 %collective-permute-start.18 = (bf16[224,1536]{1,0:T(8,128)(2,1)S(1)}, bf16[224,1536]{1,0:T(8,128)(2,1)}, u32[]{:S(2)}, u32[]{:S(2)}) collective-permute-start(bf16[224,1536]{1,0:T(8,128)(2,1)S(1)} %collective-permute-done.11.rest_2_), channel_id=1, source_target_pairs={{0,4},{4,0},{8,12},{12,8},{16,20},{20,16},{24,28},{28,24},{1,5},{5... | collective-permute-start | bytes 2064392 | tf_op jit(solution)/shard_map/ppermute | solution.py:23
  99.1 146.4 %copy-start.64 = (f32[512]{0:T(512)}, f32[512]{0:T(512)S(1)}, u32[]{:S(2)}) copy-start(f32[512]{0:T(512)S(1)} %add_rsqrt_fusion) | copy-start | bytes 6148
  100.7 27.0 %collective-permute-start.17 = (bf16[512,896]{1,0:T(8,128)(2,1)S(1)}, bf16[512,896]{1,0:T(8,128)(2,1)S(1)}, u32[]{:S(2)}, u32[]{:S(2)}) collective-permute-start(bf16[512,896]{1,0:T(8,128)(2,1)S(1)} %multiply_convert_fusion.x0_ref.refs_0_), channel_id=1, source_target_pairs={{0,2},{1,3},{2,0},{3,1},{4,6},{5,7},{6,4},{7,5},{8,10},{9,11},{10,... | collective-permute-start | bytes 2752520 | tf_op jit(solution)/shard_map/ppermute | solution.py:23
  100.8 42.3 %copy-start.33 = (bf16[112,2304]{1,0:T(8,128)(2,1)}, bf16[112,2304]{1,0:T(8,128)(2,1)S(1)}, u32[]{:S(2)}) copy-start(bf16[112,2304]{1,0:T(8,128)(2,1)S(1)} %fusion.32.rest_0_) | copy-start | bytes 1548292
  100.8 26.2 %collective-permute-start.23 = (bf16[112,2304]{1,0:T(8,128)(2,1)S(1)}, bf16[112,2304]{1,0:T(8,128)(2,1)S(1)}, u32[]{:S(2)}, u32[]{:S(2)}) collective-permute-start(bf16[112,2304]{1,0:T(8,128)(2,1)S(1)} %fusion.32.rest_0_), channel_id=1, source_target_pairs={{0,16},{4,20},{8,24},{12,28},{16,0},{20,4},{24,8},{28,12},{1,17},{... | collective-permute-start | bytes 1548296 | tf_op jit(solution)/shard_map/ppermute | solution.py:23
  115.0 12.7 %collective-permute-start.19 = (bf16[512,896]{1,0:T(8,128)(2,1)S(1)}, bf16[512,896]{1,0:T(8,128)(2,1)S(1)}, u32[]{:S(2)}, u32[]{:S(2)}) collective-permute-start(bf16[512,896]{1,0:T(8,128)(2,1)S(1)} %multiply_convert_fusion.x0_ref.refs_0_), channel_id=1, source_target_pairs={{0,1},{1,0},{2,3},{3,2},{4,5},{5,4},{6,7},{7,6},{8,9},{9,8},{10,11... | collective-permute-start | bytes 2752520 | tf_op jit(solution)/shard_map/ppermute | solution.py:23
  115.0 14.2 %collective-permute-start.21 = (bf16[512,896]{1,0:T(8,128)(2,1)S(1)}, bf16[512,896]{1,0:T(8,128)(2,1)}, u32[]{:S(2)}, u32[]{:S(2)}) collective-permute-start(bf16[512,896]{1,0:T(8,128)(2,1)S(1)} %get-tuple-element.108.g0_ref.refs_4_), channel_id=1, source_target_pairs={{0,1},{1,0},{2,3},{3,2},{4,5},{5,4},{6,7},{7,6},{8,9},{9,8},{10,11... | collective-permute-start | bytes 2752520 | tf_op jit(solution)/shard_map/ppermute | solution.py:23
  127.1 24.9 %collective-permute-start.25 = (bf16[224,2304]{1,0:T(8,128)(2,1)S(1)}, bf16[224,2304]{1,0:T(8,128)(2,1)}, u32[]{:S(2)}, u32[]{:S(2)}) collective-permute-start(bf16[224,2304]{1,0:T(8,128)(2,1)S(1)} %constant_dynamic-update-slice_fusion), channel_id=1, source_target_pairs={{0,4},{4,0},{8,12},{12,8},{16,20},{20,16},{24,28},{28,24},{1,5},{5... | collective-permute-start | bytes 3096584 | tf_op jit(solution)/shard_map/ppermute | solution.py:23
  127.6 24.6 %collective-permute-start.24 = (bf16[224,2304]{1,0:T(8,128)(2,1)S(1)}, bf16[224,2304]{1,0:T(8,128)(2,1)}, u32[]{:S(2)}, u32[]{:S(2)}) collective-permute-start(bf16[224,2304]{1,0:T(8,128)(2,1)S(1)} %constant_dynamic-update-slice_fusion), channel_id=1, source_target_pairs={{0,8},{4,12},{8,0},{12,4},{16,24},{20,28},{24,16},{28,20},{1,9},{5... | collective-permute-start | bytes 3096584 | tf_op jit(solution)/shard_map/ppermute | solution.py:23
  127.6 26.1 %collective-permute-start.22 = (bf16[512,896]{1,0:T(8,128)(2,1)}, bf16[512,896]{1,0:T(8,128)(2,1)}, u32[]{:S(2)}, u32[]{:S(2)}) collective-permute-start(bf16[512,896]{1,0:T(8,128)(2,1)} %collective-permute-done.12.g0_ref.refs_6_), channel_id=1, source_target_pairs={{0,1},{1,0},{2,3},{3,2},{4,5},{5,4},{6,7},{7,6},{8,9},{9,8},{10,11... | collective-permute-start | bytes 2752520 | tf_op jit(solution)/shard_map/ppermute | solution.py:23
  128.8 25.0 %collective-permute-start.20 = (bf16[512,896]{1,0:T(8,128)(2,1)S(1)}, bf16[512,896]{1,0:T(8,128)(2,1)}, u32[]{:S(2)}, u32[]{:S(2)}) collective-permute-start(bf16[512,896]{1,0:T(8,128)(2,1)S(1)} %collective-permute-done.17.x0_ref.refs_2_), channel_id=1, source_target_pairs={{0,1},{1,0},{2,3},{3,2},{4,5},{5,4},{6,7},{7,6},{8,9},{9,8},{10,11... | collective-permute-start | bytes 2752520 | tf_op jit(solution)/shard_map/ppermute | solution.py:23
  152.2 31.8 %collective-permute-start.26 = (bf16[224,2304]{1,0:T(8,128)(2,1)}, bf16[224,2304]{1,0:T(8,128)(2,1)S(1)}, u32[]{:S(2)}, u32[]{:S(2)}) collective-permute-start(bf16[224,2304]{1,0:T(8,128)(2,1)} %collective-permute-done.24.rest_2_), channel_id=1, source_target_pairs={{0,4},{4,0},{8,12},{12,8},{16,20},{20,16},{24,28},{28,24},{1,5},{5... | collective-permute-start | bytes 3096584 | tf_op jit(solution)/shard_map/ppermute | solution.py:23
  183.2 21.8 %collective-permute-start.27 = (bf16[448,1024]{1,0:T(8,128)(2,1)}, bf16[448,1024]{1,0:T(8,128)(2,1)S(1)}, u32[]{:S(2)}, u32[]{:S(2)}) collective-permute-start(bf16[448,1024]{1,0:T(8,128)(2,1)} %get-tuple-element.123), channel_id=1, source_target_pairs={{0,4},{4,0},{8,12},{12,8},{16,20},{20,16},{24,28},{28,24},{1,5},{5... | collective-permute-start | bytes 2752520 | tf_op jit(solution)/shard_map/ppermute | solution.py:23
  183.8 21.2 %collective-permute-start.28 = (bf16[448,512]{1,0:T(8,128)(2,1)}, bf16[448,512]{1,0:T(8,128)(2,1)S(1)}, u32[]{:S(2)}, u32[]{:S(2)}) collective-permute-start(bf16[448,512]{1,0:T(8,128)(2,1)} %get-tuple-element.124), channel_id=1, source_target_pairs={{0,8},{4,12},{8,0},{12,4},{16,24},{20,28},{24,16},{28,20},{1,9},{5... | collective-permute-start | bytes 1376264 | tf_op jit(solution)/shard_map/ppermute | solution.py:23
  205.0 4.1 collective-permute-start.29
  206.1 29.4 %collective-permute-start.32 = (bf16[224,512]{1,0:T(8,128)(2,1)}, bf16[224,512]{1,0:T(8,128)(2,1)S(1)}, u32[]{:S(2)}, u32[]{:S(2)}) collective-permute-start(bf16[224,512]{1,0:T(8,128)(2,1)} %get-tuple-element.199), channel_id=1, source_target_pairs={{0,4},{4,0},{8,12},{12,8},{16,20},{20,16},{24,28},{28,24},{1,5},{5... | collective-permute-start | bytes 688136 | tf_op jit(solution)/shard_map/ppermute | solution.py:23
  210.6 24.9 %collective-permute-start.30 = (bf16[512,896]{1,0:T(8,128)(2,1)S(1)}, bf16[512,896]{1,0:T(8,128)(2,1)}, u32[]{:S(2)}, u32[]{:S(2)}) collective-permute-start(bf16[512,896]{1,0:T(8,128)(2,1)S(1)} %get-tuple-element.192), channel_id=1, source_target_pairs={{0,2},{1,3},{2,0},{3,1},{4,6},{5,7},{6,4},{7,5},{8,10},{9,11},{10,... | collective-permute-start | bytes 2752520 | tf_op jit(solution)/shard_map/ppermute | solution.py:23
  213.6 21.9 %collective-permute-start.31 = (bf16[224,1024]{1,0:T(8,128)(2,1)S(1)}, bf16[224,1024]{1,0:T(8,128)(2,1)S(1)}, u32[]{:S(2)}, u32[]{:S(2)}) collective-permute-start(bf16[224,1024]{1,0:T(8,128)(2,1)S(1)} %get-tuple-element.187), channel_id=1, source_target_pairs={{0,8},{4,12},{8,0},{12,4},{16,24},{20,28},{24,16},{28,20},{1,9},{5... | collective-permute-start | bytes 1376264 | tf_op jit(solution)/shard_map/ppermute | solution.py:23
  236.2 9.3 %collective-permute-start.33 = (bf16[2,512,896]{2,1,0:T(8,128)(2,1)}, bf16[2,512,896]{2,1,0:T(8,128)(2,1)}, u32[]{:S(2)}, u32[]{:S(2)}) collective-permute-start(bf16[2,512,896]{2,1,0:T(8,128)(2,1)} %get-tuple-element.132), channel_id=1, source_target_pairs={{0,1},{1,0},{2,3},{3,2},{4,5},{5,4},{6,7},{7,6},{8,9},{9,8},{10,11... | collective-permute-start | bytes 5505032 | tf_op jit(solution)/shard_map/ppermute | solution.py:23
  244.4 62.6 %collective-permute-start.38 = (bf16[112,1536]{1,0:T(8,128)(2,1)}, bf16[112,1536]{1,0:T(8,128)(2,1)}, u32[]{:S(2)}, u32[]{:S(2)}) collective-permute-start(bf16[112,1536]{1,0:T(8,128)(2,1)} %pad_maximum_fusion.10), channel_id=1, source_target_pairs={{0,16},{4,20},{8,24},{12,28},{16,0},{20,4},{24,8},{28,12},{1,17},{... | collective-permute-start | bytes 1032200 | tf_op jit(solution)/shard_map/ppermute | solution.py:23
  244.8 62.2 %collective-permute-start.34 = (bf16[512,896]{1,0:T(8,128)(2,1)}, bf16[512,896]{1,0:T(8,128)(2,1)}, u32[]{:S(2)}, u32[]{:S(2)}) collective-permute-start(bf16[512,896]{1,0:T(8,128)(2,1)} %get-tuple-element.133), channel_id=1, source_target_pairs={{0,2},{1,3},{2,0},{3,1},{4,6},{5,7},{6,4},{7,5},{8,10},{9,11},{10,... | collective-permute-start | bytes 2752520 | tf_op jit(solution)/shard_map/ppermute | solution.py:23
  253.9 10.5 %collective-permute-start.35 = (bf16[512,896]{1,0:T(8,128)(2,1)S(1)}, bf16[512,896]{1,0:T(8,128)(2,1)}, u32[]{:S(2)}, u32[]{:S(2)}) collective-permute-start(bf16[512,896]{1,0:T(8,128)(2,1)S(1)} %get-tuple-element.148.refs_0_.own_ref), channel_id=1, source_target_pairs={{0,1},{1,0},{2,3},{3,2},{4,5},{5,4},{6,7},{7,6},{8,9},{9,8},{10,11... | collective-permute-start | bytes 2752520 | tf_op jit(solution)/shard_map/ppermute | solution.py:23
  267.4 20.6 %collective-permute-start.36 = (bf16[448,512]{1,0:T(8,128)(2,1)S(1)}, bf16[448,512]{1,0:T(8,128)(2,1)S(1)}, u32[]{:S(2)}, u32[]{:S(2)}) collective-permute-start(bf16[448,512]{1,0:T(8,128)(2,1)S(1)} %get-tuple-element.139), channel_id=1, source_target_pairs={{0,4},{4,0},{8,12},{12,8},{16,20},{20,16},{24,28},{28,24},{1,5},{5... | collective-permute-start | bytes 1376264 | tf_op jit(solution)/shard_map/ppermute | solution.py:23
  285.6 47.3 %collective-permute-start.40 = (bf16[448,768]{1,0:T(8,128)(2,1)}, bf16[448,768]{1,0:T(8,128)(2,1)S(1)}, u32[]{:S(2)}, u32[]{:S(2)}) collective-permute-start(bf16[448,768]{1,0:T(8,128)(2,1)} %get-tuple-element.156), channel_id=1, source_target_pairs={{0,8},{4,12},{8,0},{12,4},{16,24},{20,28},{24,16},{28,20},{1,9},{5... | collective-permute-start | bytes 2064392 | tf_op jit(solution)/shard_map/ppermute | solution.py:23
  287.5 51.8 %collective-permute-start.39 = (bf16[448,1536]{1,0:T(8,128)(2,1)}, bf16[448,1536]{1,0:T(8,128)(2,1)}, u32[]{:S(2)}, u32[]{:S(2)}) collective-permute-start(bf16[448,1536]{1,0:T(8,128)(2,1)} %get-tuple-element.153), channel_id=1, source_target_pairs={{0,4},{4,0},{8,12},{12,8},{16,20},{20,16},{24,28},{28,24},{1,5},{5... | collective-permute-start | bytes 4128776 | tf_op jit(solution)/shard_map/ppermute | solution.py:23
  288.2 23.9 %collective-permute-start.37 = (bf16[224,512]{1,0:T(8,128)(2,1)S(1)}, bf16[224,512]{1,0:T(8,128)(2,1)S(1)}, u32[]{:S(2)}, u32[]{:S(2)}) collective-permute-start(bf16[224,512]{1,0:T(8,128)(2,1)S(1)} %get-tuple-element.200), channel_id=1, source_target_pairs={{0,8},{4,12},{8,0},{12,4},{16,24},{20,28},{24,16},{28,20},{1,9},{5... | collective-permute-start | bytes 688136 | tf_op jit(solution)/shard_map/ppermute | solution.py:23
  312.2 23.7 %collective-permute-start.52 = (bf16[112,512]{1,0:T(8,128)(2,1)S(1)}, bf16[112,512]{1,0:T(8,128)(2,1)S(1)}, u32[]{:S(2)}, u32[]{:S(2)}) collective-permute-start(bf16[112,512]{1,0:T(8,128)(2,1)S(1)} %get-tuple-element.210), channel_id=1, source_target_pairs={{0,16},{4,20},{8,24},{12,28},{16,0},{20,4},{24,8},{28,12},{1,17},{... | collective-permute-start | bytes 344072 | tf_op jit(solution)/shard_map/ppermute | solution.py:23
  333.8 16.8 %collective-permute-start.56 = (bf16[224,768]{1,0:T(8,128)(2,1)}, bf16[224,768]{1,0:T(8,128)(2,1)}, u32[]{:S(2)}, u32[]{:S(2)}) collective-permute-start(bf16[224,768]{1,0:T(8,128)(2,1)} %get-tuple-element.190), channel_id=1, source_target_pairs={{0,4},{4,0},{8,12},{12,8},{16,20},{20,16},{24,28},{28,24},{1,5},{5... | collective-permute-start | bytes 1032200 | tf_op jit(solution)/shard_map/ppermute | solution.py:23
  335.3 20.1 %collective-permute-start.47 = (bf16[448,576]{1,0:T(8,128)(2,1)S(1)}, bf16[448,576]{1,0:T(8,128)(2,1)}, u32[]{:S(2)}, u32[]{:S(2)}) collective-permute-start(bf16[448,576]{1,0:T(8,128)(2,1)S(1)} %get-tuple-element.161), channel_id=1, source_target_pairs={{0,4},{4,0},{8,12},{12,8},{16,20},{20,16},{24,28},{28,24},{1,5},{5... | collective-permute-start | bytes 1548296 | tf_op jit(solution)/shard_map/ppermute | solution.py:23
  336.0 13.9 %collective-permute-start.53 = (bf16[112,224]{1,0:T(8,128)(2,1)S(1)}, bf16[112,224]{1,0:T(8,128)(2,1)S(1)}, u32[]{:S(2)}, u32[]{:S(2)}) collective-permute-start(bf16[112,224]{1,0:T(8,128)(2,1)S(1)} %get-tuple-element.218), channel_id=1, source_target_pairs={{0,0},{1,2},{2,1},{3,3},{4,4},{5,6},{6,5},{7,7},{8,8},{9,10},{10,9... | collective-permute-start | bytes 150536 | tf_op jit(solution)/shard_map/ppermute | solution.py:678
  336.6 13.2 %collective-permute-start.54 = (bf16[112,224]{1,0:T(8,128)(2,1)S(1)}, bf16[112,224]{1,0:T(8,128)(2,1)S(1)}, u32[]{:S(2)}, u32[]{:S(2)}) collective-permute-start(bf16[112,224]{1,0:T(8,128)(2,1)S(1)} %get-tuple-element.219), channel_id=1, source_target_pairs={{0,1},{1,3},{2,0},{3,2},{4,5},{5,7},{6,4},{7,6},{8,9},{9,11},{10,8... | collective-permute-start | bytes 150536 | tf_op jit(solution)/shard_map/ppermute | solution.py:678
  348.4 10.3 %collective-permute-start.41 = (bf16[512,896]{1,0:T(8,128)(2,1)}, bf16[512,896]{1,0:T(8,128)(2,1)}, u32[]{:S(2)}, u32[]{:S(2)}) collective-permute-start(bf16[512,896]{1,0:T(8,128)(2,1)} %slice.696), channel_id=1, source_target_pairs={{0,1},{1,0},{2,3},{3,2},{4,5},{5,4},{6,7},{7,6},{8,9},{9,8},{10,11... | collective-permute-start | bytes 2752520 | tf_op jit(solution)/shard_map/ppermute | solution.py:23
  356.6 11.4 %collective-permute-start.48 = (bf16[224,576]{1,0:T(8,128)(2,1)S(1)}, bf16[224,576]{1,0:T(8,128)(2,1)S(1)}, u32[]{:S(2)}, u32[]{:S(2)}) collective-permute-start(bf16[224,576]{1,0:T(8,128)(2,1)S(1)} %get-tuple-element.194), channel_id=1, source_target_pairs={{0,8},{4,12},{8,0},{12,4},{16,24},{20,28},{24,16},{28,20},{1,9},{5... | collective-permute-start | bytes 774152 | tf_op jit(solution)/shard_map/ppermute | solution.py:23
  357.4 24.1 %collective-permute-start.55 = (bf16[224,1536]{1,0:T(8,128)(2,1)}, bf16[224,1536]{1,0:T(8,128)(2,1)}, u32[]{:S(2)}, u32[]{:S(2)}) collective-permute-start(bf16[224,1536]{1,0:T(8,128)(2,1)} %get-tuple-element.184), channel_id=1, source_target_pairs={{0,8},{4,12},{8,0},{12,4},{16,24},{20,28},{24,16},{28,20},{1,9},{5... | collective-permute-start | bytes 2064392 | tf_op jit(solution)/shard_map/ppermute | solution.py:23
  361.8 6.3 %collective-permute-start.42 = (f32[23,128]{1,0:T(8,128)S(1)}, f32[23,128]{1,0:T(8,128)S(1)}, u32[]{:S(2)}, u32[]{:S(2)}) collective-permute-start(f32[23,128]{1,0:T(8,128)S(1)} %maximum_bitcast_fusion.1), channel_id=1, source_target_pairs={{0,1},{1,0},{2,3},{3,2},{4,5},{5,4},{6,7},{7,6},{8,9},{9,8},{10,11... | collective-permute-start | bytes 35336 | tf_op jit(solution)/shard_map/ppermute | solution.py:23
  368.0 38.5 %collective-permute-start.49 = (bf16[112,576]{1,0:T(8,128)(2,1)S(1)}, bf16[112,576]{1,0:T(8,128)(2,1)S(1)}, u32[]{:S(2)}, u32[]{:S(2)}) collective-permute-start(bf16[112,576]{1,0:T(8,128)(2,1)S(1)} %fusion.35), channel_id=1, source_target_pairs={{0,16},{4,20},{8,24},{12,28},{16,0},{20,4},{24,8},{28,12},{1,17},{... | collective-permute-start | bytes 387080 | tf_op jit(solution)/shard_map/ppermute | solution.py:23
  368.2 14.5 %collective-permute-start.43 = (f32[23,128]{1,0:T(8,128)S(1)}, f32[23,128]{1,0:T(8,128)S(1)}, u32[]{:S(2)}, u32[]{:S(2)}) collective-permute-start(f32[23,128]{1,0:T(8,128)S(1)} %fusion.75), channel_id=1, source_target_pairs={{0,2},{1,3},{2,0},{3,1},{4,6},{5,7},{6,4},{7,5},{8,10},{9,11},{10,... | collective-permute-start | bytes 35336 | tf_op jit(solution)/shard_map/ppermute | solution.py:23
  382.7 3.8 collective-permute-start.44
  384.4 30.1 %collective-permute-start.57 = (bf16[112,2304]{1,0:T(8,128)(2,1)S(1)}, bf16[112,2304]{1,0:T(8,128)(2,1)S(1)}, u32[]{:S(2)}, u32[]{:S(2)}) collective-permute-start(bf16[112,2304]{1,0:T(8,128)(2,1)S(1)} %pad_maximum_fusion.7), channel_id=1, source_target_pairs={{0,16},{4,20},{8,24},{12,28},{16,0},{20,4},{24,8},{28,12},{1,17},{... | collective-permute-start | bytes 1548296 | tf_op jit(solution)/shard_map/ppermute | solution.py:23
  386.5 6.8 %collective-permute-start.45 = (f32[23,128]{1,0:T(8,128)S(1)}, f32[23,128]{1,0:T(8,128)S(1)}, u32[]{:S(2)}, u32[]{:S(2)}) collective-permute-start(f32[23,128]{1,0:T(8,128)S(1)} %add.268), channel_id=1, source_target_pairs={{0,8},{4,12},{8,0},{12,4},{16,24},{20,28},{24,16},{28,20},{1,9},{5... | collective-permute-start | bytes 35336 | tf_op jit(solution)/shard_map/ppermute | solution.py:23
  393.3 13.3 %collective-permute-start.46 = (f32[23,128]{1,0:T(8,128)S(1)}, f32[23,128]{1,0:T(8,128)S(1)}, u32[]{:S(2)}, u32[]{:S(2)}) collective-permute-start(f32[23,128]{1,0:T(8,128)S(1)} %add.269), channel_id=1, source_target_pairs={{0,16},{4,20},{8,24},{12,28},{16,0},{20,4},{24,8},{28,12},{1,17},{... | collective-permute-start | bytes 35336 | tf_op jit(solution)/shard_map/ppermute | solution.py:23
  406.7 4.6 %collective-permute-start.50 = (bf16[112,288]{1,0:T(8,128)(2,1)S(1)}, bf16[112,288]{1,0:T(8,128)(2,1)S(1)}, u32[]{:S(2)}, u32[]{:S(2)}) collective-permute-start(bf16[112,288]{1,0:T(8,128)(2,1)S(1)} %get-tuple-element.216), channel_id=1, source_target_pairs={{0,0},{1,2},{2,1},{3,3},{4,4},{5,6},{6,5},{7,7},{8,8},{9,10},{10,9... | collective-permute-start | bytes 193544 | tf_op jit(solution)/shard_map/ppermute | solution.py:678
  407.4 6.2 %collective-permute-start.51 = (bf16[112,288]{1,0:T(8,128)(2,1)S(1)}, bf16[112,288]{1,0:T(8,128)(2,1)S(1)}, u32[]{:S(2)}, u32[]{:S(2)}) collective-permute-start(bf16[112,288]{1,0:T(8,128)(2,1)S(1)} %get-tuple-element.217), channel_id=1, source_target_pairs={{0,1},{1,3},{2,0},{3,2},{4,5},{5,7},{6,4},{7,6},{8,9},{9,11},{10,8... | collective-permute-start | bytes 193544 | tf_op jit(solution)/shard_map/ppermute | solution.py:678
  (82 other events, 875.5 us)

commit v8 on v5

--- a/solution.py
+++ b/solution.py
@@ -514,6 +514,70 @@
     )(*flat, *acts)
 
 
+def outer_whole_kernel(row_ref, *refs, blocks, count, moved):
+    rows, grads, rights, out_ref = refs[:blocks], refs[blocks : 2 * blocks], refs[2 * blocks : -1], refs[-1]
+    step = pl.program_id(0)
+    t, d = rows[0].shape
+    deep = d // count
+    bits = count.bit_length() - 1
+
+    def product(lefts):
+        for part in range(2):
+            start = part * (d // 2)
+            total = 0.0
+            for i, left in enumerate(lefts):
+                right = rights[i * t // rights[0].shape[0]]
+                at = i * t % right.shape[0]
+                total = total + lax.dot_general(
+                    left[:, start : start + d // 2],
+                    right[at : at + t, :],
+                    TN,
+                    preferred_element_type=f32,
+                )
+            total = total.astype(bf16)
+            if not moved:
+                out_ref[start : start + d // 2, :] = total
+                continue
+            for p in range(part * count // 2, (part + 1) * count // 2):
+                to = (row_ref[0] ^ bit_reversed(p, bits)) * deep
+                here = p * deep - start
+                out_ref[pl.ds(pl.multiple_of(to, 16), deep), :] = total[here : here + deep]
+
+    @pl.when(step < 2)
+    def _():
+        product(rows)
+
+    @pl.when(step == 2)
+    def _():
+        product(grads)
+
+
+def outer_whole(row, rows, grads, acts, count):
+    t, d = rows[0].shape
+    tall, columns = acts[0].shape
+    n = columns // 3
+    flat = [*rows, *grads]
+    deep = d // count
+    bits = count.bit_length() - 1
+    moved = deep % 16 == 0
+    out = pl.pallas_call(
+        functools.partial(outer_whole_kernel, blocks=len(rows), count=count, moved=moved),
+        grid=(3,),
+        in_specs=[pl.BlockSpec(memory_space=pltpu.SMEM)]
+        + [whole(left) for left in flat]
+        + [pl.BlockSpec((tall, n), lambda k: (0, k)) for _ in acts],
+        out_specs=pl.BlockSpec((d, n), lambda k: (0, k)),
+        out_shape=jax.ShapeDtypeStruct((d, columns), bf16),
+        compiler_params=kernel_params(58),
+        cost_estimate=cost(2 * t * len(rows) * d * columns, 20 * MIB),
+    )(row, *flat, *acts)
+    if moved:
+        return out
+    places = jnp.array([bit_reversed(m, bits) for m in range(count)], jnp.int32)
+    order = places[jnp.arange(count, dtype=jnp.int32) ^ row[0]]
+    return out.reshape(count, deep, columns)[order].reshape(d, columns)
+
+
 def outer_one_kernel(*refs):
     fill(refs[-2], refs[-1], refs[:-3], refs[-3:-2], False)
 
@@ -798,7 +862,15 @@
     def summed(k, back):
         return near_own[k].astype(f32) + beside[k].astype(f32) + back.astype(f32)
 
-    grad_normed_two = summed(0, normed_back)
+    second_whole = outer_whole(
+        row.astype(jnp.int32).reshape(1),
+        [after(blocks[0], near_own, *first_scatter.kept), *blocks[1:]],
+        grad_blocks,
+        [act_own, act_far],
+        row_count,
+    )
+    second_total = lax.psum_scatter(second_whole, "row", scatter_dimension=0, tiled=True)
+    grad_normed_two = summed(0, after(normed_back, second_whole))
     scaled_two = gain_two * grad_normed_two
     inner_two = jnp.sum(scaled_two * middle, axis=1)
     grad_middle = (
@@ -810,18 +882,10 @@
     branch_own = grad_middle.astype(bf16)
     branch_other = flip(branch_own, "col", 0)
     out_scatter = Scatter([outer_one([branch_own, branch_other], att_rows)], bits)
-    sent_one, kept_one, sent_two, kept_two = outer(
-        [after(blocks[0], out_scatter.kept[0], *first_scatter.kept), *blocks[1:]],
-        grad_blocks,
-        [act_own, act_far],
-    )
-    second_scatter = Scatter([(sent_one, kept_one), (sent_two, kept_two)], bits)
-    out_scatter.wait(kept_one)
-    out_scatter.step()
     split = qk_rows.shape[1] // 256
     mixed_first, bias_first, *carry = attend_back(
         parity,
-        after(branch_own, kept_one, out_scatter.kept[0]),
+        after(branch_own, out_scatter.kept[0]),
         branch_other,
         out_pieces,
         qk_rows,
@@ -833,9 +897,10 @@
         split,
     )
     out_scatter.wait(mixed_first)
+    out_scatter.step()
     mixed_last, bias_last = attend_back(
         parity,
-        after(branch_own, mixed_first),
+        after(branch_own, out_scatter.kept[0]),
         branch_other,
         out_pieces,
         qk_rows,
@@ -848,16 +913,15 @@
         carry,
     )
     bias_grad = jnp.concatenate([bias_first, bias_last], 1)[0]
-    first_scatter.wait(mixed_last)
-    second_scatter.wait(mixed_last)
-    out_scatter.wait(mixed_last)
     grad_mixed = jnp.concatenate([mixed_first, mixed_last], 1)
-    second_scatter.step()
-    layer_output = unstored((middle + summed(1, after(down_back, grad_mixed))).astype(bf16))
-    qkv_scatter = Scatter([outer_one([normed_own, normed_other], after(grad_mixed, second_scatter.kept[0]))], bits)
+    qkv_scatter = Scatter([outer_one([normed_own, normed_other], grad_mixed)], bits)
+    passed = qkv_scatter.kept[0]
+    out_scatter.wait(passed)
+    first_scatter.wait(passed)
+    first_total = first_scatter.total()
+    layer_output = unstored((middle + summed(1, after(down_back, passed))).astype(bf16))
     qkv_full = jnp.concatenate(qkv_pieces, 0)
-    grad_mixed = after(grad_mixed, qkv_scatter.kept[0])
-    out_scatter.wait(qkv_scatter.kept[0])
+    grad_mixed = after(grad_mixed, passed)
     out_scatter.step()
     partial = jnp.einsum("tc,dc->td", grad_mixed, qkv_full, preferred_element_type=f32)
     grad_normed_one = partial[:tok_local] + flip(
@@ -886,17 +950,19 @@
     )
     small = jnp.concatenate([unstored_row(gain_one_grad), unstored_row(gain_two_grad), bias_row])
     small = jnp.pad(small, (0, -small.shape[0] % 128)).reshape(-1, 128)
-    small = after(small, *second_scatter.got)
-    second_scatter.step()
     for bit in range(2):
         small = small + flip(small, "col", bit)
     for bit in range(bits):
         small = small + flip(small, "row", bit)
+    qkv_scatter.step()
+    qkv_scatter.step()
+    qkv_scatter.wait(small)
     qkv_total = to_columns(qkv_scatter.total(), qkv_cols)
     out_total = to_columns(out_scatter.total(), out_cols)
     mlp_totals = []
-    for scatter, (start, stop) in zip((first_scatter, second_scatter), cuts(ff_cols)):
-        total = scatter.total()
+    for total, (start, stop) in zip(
+        (first_total, after(second_total, small).astype(f32)), cuts(ff_cols)
+    ):
         padded = total.shape[1] // 3
         mlp_totals.append(
             [total[:, k * padded : k * padded + stop - start] for k in range(3)]

time: 405 us -> 394 us (0.973)
  between operations: 2.23 us -> 15.9 us
  waiting for transfers between devices: 79.4 us -> 67.7 us
  starting transfers between devices: 63.3 us -> 59 us
    pallas_call x2 -> x1, Pallas kernels: 31.7 us -> 15.4 us  [outer(): pl.pallas_call(functools.partial(outer_kernel, blocks=len(rows)), grid=(3...]
    pallas_call x0 -> x1, Pallas kernels: none -> 15.5 us  [outer_whole(): pl.pallas_call(functools.partial(outer_whole_kernel, blocks=len(rows), co...]
    ppermute x52 -> x47, waiting for transfers between devices: 79.3 us -> 65.6 us  [flip(): return lax.ppermute(block, axis, [(i, i ^ 1 << bit) for i in range(count)])]
    convert_element_type x7 -> x4, other arithmetic: 6.98 us -> 1.33 us  [step(): (kept[half:] + got[half:].astype(f32)).astype(bf16)]
    ppermute x52 -> x47, starting transfers between devices: 53.5 us -> 50 us  [flip(): return lax.ppermute(block, axis, [(i, i ^ 1 << bit) for i in range(count)])]
    unnamed x168 -> x138, local copies, waits for them, and re-layouts: 18.4 us -> 17.2 us
  transfers between devices with their start and end apart: 58 -> 54, of which waited for: 15 -> 13; matrix products, arithmetic and copies ran while one was open for 19% -> 17% of each run, Pallas kernels for 40% -> 41%
where the time goes in v8:
time: 394 us; the launch traced here: 386 us
  Pallas kernels  160 us (41%)
  waiting for transfers between devices  67.7 us (17%)
  starting transfers between devices  59 us (15%)
  other arithmetic  37.1 us (9%)
  local copies, waits for them, and re-layouts  30.4 us (8%)
  matrix products  16.5 us (4%)
  between operations  15.9 us (4%)
    pallas_call x4, Pallas kernels, mlp(): pl.pallas_call(functools.partial(mlp_kernel, count=len(pieces), add=add),...  68.5 us
    ppermute x47, waiting for transfers between devices, flip(): return lax.ppermute(block, axis, [(i, i ^ 1 << bit) for i in range(count)])  65.6 us
    ppermute x47, starting transfers between devices, flip(): return lax.ppermute(block, axis, [(i, i ^ 1 << bit) for i in range(count)])  50 us
    pallas_call x2, Pallas kernels, attend_back(): pl.pallas_call(functools.partial(attend_back_kernel, block=block, count=l...  33.3 us
    pallas_call x1, Pallas kernels, attend(): pl.pallas_call(functools.partial(attend_kernel, block=block, count=len(pi...  19.9 us
    unnamed x138, local copies, waits for them, and re-layouts  17.2 us
    pallas_call x1, Pallas kernels, outer_whole(): pl.pallas_call(functools.partial(outer_whole_kernel, blocks=len(rows), co...  15.5 us
    pallas_call x1, Pallas kernels, outer(): pl.pallas_call(functools.partial(outer_kernel, blocks=len(rows)), grid=(3...  15.4 us
  transfers between devices with their start and end apart: 54, of which 13 were waited for; matrix products, arithmetic and copies ran while one was open for 17% of the time, Pallas kernels for 41%

profile of v8, /device:TPU:0, one launch (start us, length us, event | category | flops | bytes accessed | tf_op | source)
XLA Modules:
  0.0 386.5 jit_solution(5354079792241633008)
XLA Ops:
  10.1 3.0 collective-permute-start.1
  17.2 2.6 collective-permute-start.9
  19.8 1.5 collective-permute-start.7
  21.6 2.0 fusion.47
  23.6 2.8 bitcast_convert_fusion
  29.7 1.3 multiply_reduce_fusion.5
  31.8 10.7 %collective-permute-done.3.rest_1_ = bf16[112,576]{1,0:T(8,128)(2,1)S(1)} collective-permute-done((bf16[112,576]{1,0:T(8,128)(2,1)S(1)}, bf16[112,576]{1,0:T(8,128)(2,1)S(1)}, u32[]{:S(2)}, u32[]{:S(2)}) %collective-permute-start.3) | collective-permute-done | bytes 129056 | tf_op jit(solution)/shard_map/ppermute | solution.py:23
  43.8 4.3 %collective-permute-start.5 = (bf16[224,576]{1,0:T(8,128)(2,1)}, bf16[224,576]{1,0:T(8,128)(2,1)S(1)}, u32[]{:S(2)}, u32[]{:S(2)}) collective-permute-start(bf16[224,576]{1,0:T(8,128)(2,1)} %pad_maximum_fusion.9), channel_id=1, source_target_pairs={{0,8},{4,12},{8,0},{12,4},{16,24},{20,28},{24,16},{28,20},{1,9},{5... | collective-permute-start | bytes 774152 | tf_op jit(solution)/shard_map/ppermute | solution.py:23
  49.1 2.0 collective-permute-done.11.rest_1_
  51.1 1.5 collective-permute-start.6
  52.7 3.8 collective-permute-done.5.rest_2_
  57.1 1.5 collective-permute-start.8
  59.6 2.1 collective-permute-start.15
  61.7 4.8 %collective-permute-done.12.rest_2_ = bf16[224,512]{1,0:T(8,128)(2,1)S(1)} collective-permute-done((bf16[224,512]{1,0:T(8,128)(2,1)S(1)}, bf16[224,512]{1,0:T(8,128)(2,1)S(1)}, u32[]{:S(2)}, u32[]{:S(2)}) %collective-permute-start.12) | collective-permute-done | bytes 229408 | tf_op jit(solution)/shard_map/ppermute | solution.py:23
  66.5 1.9 collective-permute-start.10
  69.5 19.9 %shard_map.186 = (bf16[1024,512]{1,0:T(8,128)(2,1)S(1)}, bf16[1024,64]{1,0:T(8,128)(2,1)S(1)}, bf16[1024,512]{1,0:T(8,128)(2,1)S(1)}, f32[8,1024]{1,0:T(8,128)S(1)}) custom-call(s32[1]{0:T(128)} %bitcast.1.parity_ref, bf16[512,896]{1,0:T(8,128)(2,1)S(1)} %multiply_convert_fusion.1.own_ref.refs_0_, bf16[512,896]{1,0:T(8,128)(2,1)} %collective-permute-done.2.other_ref.refs_1_, ...), custom_call_target="tpu_custom_call" | custom-call | flops 12000000000 | bytes 8000000 | tf_op jit(solution)/shard_map/pallas_call | solution.py:159
  90.6 2.2 shard_map.187
  93.6 1.9 collective-permute-start.19
  96.1 1.8 collective-permute-start.18
  97.9 13.6 %collective-permute-done.19.rest_5_ = bf16[224,1536]{1,0:T(8,128)(2,1)S(1)} collective-permute-done((bf16[224,1536]{1,0:T(8,128)(2,1)S(1)}, bf16[224,1536]{1,0:T(8,128)(2,1)S(1)}, u32[]{:S(2)}, u32[]{:S(2)}) %collective-permute-start.19) | collective-permute-done | bytes 688160 | tf_op jit(solution)/shard_map/ppermute | solution.py:23
  112.2 1.8 collective-permute-start.25
  114.0 4.8 %collective-permute-done.18.x0_ref.refs_2_ = bf16[512,896]{1,0:T(8,128)(2,1)} collective-permute-done((bf16[512,896]{1,0:T(8,128)(2,1)S(1)}, bf16[512,896]{1,0:T(8,128)(2,1)}, u32[]{:S(2)}, u32[]{:S(2)}) %collective-permute-start.18) | collective-permute-done | bytes 917536 | tf_op jit(solution)/shard_map/ppermute | solution.py:23
  118.7 2.0 collective-permute-start.24
  122.2 14.0 %shard_map.188 = (bf16[1024,1536]{1,0:T(8,128)(2,1)}, bf16[2,512,896]{2,1,0:T(8,128)(2,1)}, bf16[2,512,896]{2,1,0:T(8,128)(2,1)}) custom-call(bf16[512,896]{1,0:T(8,128)(2,1)} %copy-done.33, bf16[512,896]{1,0:T(8,128)(2,1)} %copy-done.58, bf16[512,896]{1,0:T(8,128)(2,1)} %get-tuple-element.95.g0_ref.refs_4_, ...), custom_call_target="tpu_custom_call" | custom-call | flops 5637144576 | bytes 31457280 | tf_op jit(solution)/shard_map/pallas_call | solution.py:436
  137.0 6.2 %collective-permute-done.24.rest_2_ = bf16[224,2304]{1,0:T(8,128)(2,1)} collective-permute-done((bf16[224,2304]{1,0:T(8,128)(2,1)S(1)}, bf16[224,2304]{1,0:T(8,128)(2,1)}, u32[]{:S(2)}, u32[]{:S(2)}) %collective-permute-start.24) | collective-permute-done | bytes 1032224 | tf_op jit(solution)/shard_map/ppermute | solution.py:23
  143.2 1.6 collective-permute-start.26
  144.8 14.1 %shard_map.189 = (bf16[1024,1536]{1,0:T(8,128)(2,1)}, bf16[2,512,896]{2,1,0:T(8,128)(2,1)}, bf16[2,512,896]{2,1,0:T(8,128)(2,1)}) custom-call(bf16[512,896]{1,0:T(8,128)(2,1)} %collective-permute-done.18.x0_ref.refs_2_, bf16[512,896]{1,0:T(8,128)(2,1)} %collective-permute-done.21.x1_ref.refs_3_, bf16[512,896]{1,0:T(8,128)(2,1)} %collective-permute-done.14.g0_ref.refs_6_, ...), custom_call_target="tpu_custom_call" | custom-call | flops 5637144576 | bytes 31457280 | tf_op jit(solution)/shard_map/pallas_call | solution.py:436
  158.9 15.4 %shard_map.190 = (bf16[448,1024]{1,0:T(8,128)(2,1)}, f32[448,1024]{1,0:T(8,128)}, bf16[448,512]{1,0:T(8,128)(2,1)}, f32[448,512]{1,0:T(8,128)}) custom-call(bf16[512,896]{1,0:T(8,128)(2,1)} %copy-done.33, bf16[512,896]{1,0:T(8,128)(2,1)} %copy-done.58, bf16[512,896]{1,0:T(8,128)(2,1)} %collective-permute-done.18.x0_ref.refs_2_, ...), custom_call_target="tpu_custom_call" | custom-call | flops 5637144576 | bytes 20971520 | tf_op jit(solution)/shard_map/pallas_call | solution.py:500
  174.8 1.7 collective-permute-start.28
  177.5 20.3 %shard_map.191 = (bf16[1024,2304]{1,0:T(8,128)(2,1)}, bf16[2,512,896]{2,1,0:T(8,128)(2,1)}, bf16[2,512,896]{2,1,0:T(8,128)(2,1)}) custom-call(bf16[512,896]{1,0:T(8,128)(2,1)} %collective-permute-done.18.x0_ref.refs_2_, bf16[512,896]{1,0:T(8,128)(2,1)} %collective-permute-done.21.x1_ref.refs_3_, bf16[512,896]{1,0:T(8,128)(2,1)} %collective-permute-done.14.g0_ref.refs_6_, ...), custom_call_target="tpu_custom_call" | custom-call | flops 8455716864 | bytes 31457280 | tf_op jit(solution)/shard_map/pallas_call | solution.py:436
  199.3 1.9 convert_add_fusion.5
  201.2 1.6 collective-permute-start.32
  202.8 2.0 add_convert_fusion
  205.8 1.7 collective-permute-start.30
  207.6 2.2 convert_add_fusion.1
  210.1 20.2 %shard_map.192 = (bf16[1024,2304]{1,0:T(8,128)(2,1)}, bf16[2,512,896]{2,1,0:T(8,128)(2,1)}, bf16[2,512,896]{2,1,0:T(8,128)(2,1)}) custom-call(bf16[512,896]{1,0:T(8,128)(2,1)} %copy-done.33, bf16[512,896]{1,0:T(8,128)(2,1)} %copy-done.58, bf16[512,896]{1,0:T(8,128)(2,1)} %get-tuple-element.95.g0_ref.refs_4_, ...), custom_call_target="tpu_custom_call" | custom-call | flops 8455716864 | bytes 31457280 | tf_op jit(solution)/shard_map/pallas_call | solution.py:436
  232.7 1.7 slice_add_fusion.9
  236.0 1.7 collective-permute-start.52
  237.8 15.5 %shard_map.193 = bf16[896,2304]{1,0:T(8,128)(2,1)} custom-call(s32[1]{0:T(128)} %bitcast.8.row_ref, bf16[512,896]{1,0:T(8,128)(2,1)} %copy-done.33, bf16[512,896]{1,0:T(8,128)(2,1)} %copy-done.58, bf16[512,896]{1,0:T(8,128)(2,1)} %collective-permute-done.18.x0_ref.refs_2_, bf16[512,896]{1,0:T(8,128)(2,1)} %collective-permute-done.21.x1_ref.refs_3_, ...), custom_call_target="tpu_custom_call" | custom-call | flops 8455716864 | bytes 20971520 | tf_op jit(solution)/shard_map/pallas_call | solution.py:563
  254.8 2.5 multiply_reduce_fusion
  257.4 5.2 %fusion.59 = (bf16[512,896]{1,0:T(8,128)(2,1)S(1)}, f32[512,896]{1,0:T(8,128)}) fusion(f32[512,896]{1,0:T(8,128)} %copy-done.21, f32[512]{0:T(512)S(1)} %fusion.56, bf16[512,896]{1,0:T(8,128)(2,1)} %copy-done.26, bf16[2,512,896]{2,1,0:T(8,128)(2,1)} %collective-permute-done.33, bf16[2,512,896]{2,1,0:T(8,128)(2,1)} %get-tuple-element.115, ...), kind=kLoop, calls=%fused_computation.177 | loop fusion | flops 5046272 | bytes 9182720 | tf_op jit(solution)/shard_map/convert_element_type | solution.py:882
  267.2 1.2 copy-done.13
  268.4 1.2 copy-done.17
  269.7 1.7 shard_map.194
  274.5 17.9 %shard_map.195 = (bf16[1024,256]{1,0:T(8,128)(2,1)S(1)}, f32[1,256]{1,0:T(1,128)S(1)}, f32[1024,128]{1,0:T(8,128)S(1)}, f32[1024,128]{1,0:T(8,128)S(1)}) custom-call(s32[1]{0:T(128)} %bitcast.1.parity_ref, bf16[512,896]{1,0:T(8,128)(2,1)} %copy-done.2, bf16[512,896]{1,0:T(8,128)(2,1)} %copy-done.12, bf16[1024,512]{1,0:T(8,128)(2,1)} %copy-done.18, ...), custom_call_target="tpu_custom_call" | custom-call | flops 12000000000 | bytes 6000000 | tf_op jit(solution)/shard_map/pallas_call | solution.py:352
  293.8 15.4 %shard_map.196 = (bf16[1024,320]{1,0:T(8,128)(2,1)S(1)}, f32[1,320]{1,0:T(1,128)S(1)}) custom-call(s32[1]{0:T(128)} %bitcast.1.parity_ref, bf16[512,896]{1,0:T(8,128)(2,1)} %copy-done.2, bf16[512,896]{1,0:T(8,128)(2,1)} %copy-done.12, bf16[1024,512]{1,0:T(8,128)(2,1)} %copy-done.18, bf16[1024,64]{1,0:T(8,128)(2,1)S(1)} %copy-done.20, ...), custom_call_target="tpu_custom_call" | custom-call | flops 12000000000 | bytes 6000000 | tf_op jit(solution)/shard_map/pallas_call | solution.py:352
  309.4 3.4 shard_map.197
  312.9 1.6 collective-permute-start.43
  314.4 1.7 fusion.69
  317.2 2.2 convert_add_fusion.2
  319.5 3.9 %fusion.15 = bf16[512,896]{1,0:T(8,128)(2,1)} fusion(s32[896]{0:T(1024)S(1)} %copy-done.50, f32[512,896]{1,0:T(8,128)S(1)} %copy-done.23, bf16[512,896]{1,0:T(8,128)(2,1)} %collective-permute-done.34, bf16[2,512,896]{2,1,0:T(8,128)(2,1)} %collective-permute-done.33, bf16[2,512,896]{2,1,0:T(8,128)(2,1)S(1)} %copy-done.30), kind=kOutput, calls=%fused_computation.36 | convolution fusion | flops 826556416 | bytes 5509120 | tf_op jit(solution)/shard_map/dot_general | solution.py:773
  323.5 1.7 collective-permute-start.49
  326.3 11.7 %collective-permute-done.49 = bf16[112,512]{1,0:T(8,128)(2,1)} collective-permute-done((bf16[112,512]{1,0:T(8,128)(2,1)S(1)}, bf16[112,512]{1,0:T(8,128)(2,1)}, u32[]{:S(2)}, u32[]{:S(2)}) %collective-permute-start.49) | collective-permute-done | bytes 114720 | tf_op jit(solution)/shard_map/ppermute | solution.py:23
  339.7 1.4 collective-permute-start.51
  341.1 3.0 multiply_reduce_fusion.1
  346.0 2.2 collective-permute-start.39
  350.7 4.4 %collective-permute-done.44 = bf16[224,576]{1,0:T(8,128)(2,1)S(1)} collective-permute-done((bf16[224,576]{1,0:T(8,128)(2,1)S(1)}, bf16[224,576]{1,0:T(8,128)(2,1)S(1)}, u32[]{:S(2)}, u32[]{:S(2)}) %collective-permute-start.44) | collective-permute-done | bytes 258080 | tf_op jit(solution)/shard_map/ppermute | solution.py:23
  355.9 1.7 collective-permute-start.41
  357.6 1.9 collective-permute-done.41
  359.6 2.8 collective-permute-start.42
  362.4 5.4 %fusion.16 = bf16[512,896]{1,0:T(8,128)(2,1)} fusion(s32[896]{0:T(1024)S(1)} %copy-done.51, f32[512,896]{1,0:T(8,128)} %copy-done.24, f32[512,896]{1,0:T(8,128)} %get-tuple-element.163, f32[512]{0:T(512)S(1)} %fusion.58, f32[896]{0:T(1024)S(1)} %copy-done.46, f32[512]{0:T(512)S(1)} %copy-done.43, f32[1024,896]{1,0:T(8,128)} %copy-done.27, ...), kind=kOutput, calls=%fused_computation.37 | convolution fusion | flops 827015168 | bytes 7351296 | tf_op jit(solution)/shard_map/dot_general | solution.py:773
  368.7 2.6 collective-permute-start.47
  372.5 2.0 collective-permute-done.47
  375.3 1.2 fusion.62
  (311 shorter events, 55.1 us)
Async XLA Ops:
  7.2 368.1 %reduce-scatter.2.cloned.1.call-start = ((), (), s32[]{:S(2)}) async-start(), calls=%async_computation.1 | async-start | bytes 4644864 | tf_op jit(solution)/shard_map/reduce_scatter | solution.py:872
  10.1 17.8 %collective-permute-start.1 = (bf16[128,512]{1,0:T(8,128)(2,1)S(1)}, bf16[128,512]{1,0:T(8,128)(2,1)S(1)}, u32[]{:S(2)}, u32[]{:S(2)}) collective-permute-start(bf16[128,512]{1,0:T(8,128)(2,1)S(1)} %fusion.48), channel_id=1, source_target_pairs={{0,2},{1,0},{2,3},{3,1},{4,6},{5,4},{6,7},{7,5},{8,10},{9,8},{10,1... | collective-permute-start | bytes 393224 | tf_op jit(solution)/shard_map/ppermute | solution.py:694
  13.1 14.8 %collective-permute-start = (bf16[128,512]{1,0:T(8,128)(2,1)S(1)}, bf16[128,512]{1,0:T(8,128)(2,1)S(1)}, u32[]{:S(2)}, u32[]{:S(2)}) collective-permute-start(bf16[128,512]{1,0:T(8,128)(2,1)S(1)} %fusion.48), channel_id=1, source_target_pairs={{0,0},{1,2},{2,1},{3,3},{4,4},{5,6},{6,5},{7,7},{8,8},{9,10},{10,9... | collective-permute-start | bytes 393224 | tf_op jit(solution)/shard_map/ppermute | solution.py:694
  17.2 41.3 %collective-permute-start.9 = (bf16[112,1536]{1,0:T(8,128)(2,1)}, bf16[112,1536]{1,0:T(8,128)(2,1)}, u32[]{:S(2)}, u32[]{:S(2)}) collective-permute-start(bf16[112,1536]{1,0:T(8,128)(2,1)} %pad_maximum_fusion.7.rest_0_), channel_id=1, source_target_pairs={{0,16},{4,20},{8,24},{12,28},{16,0},{20,4},{24,8},{28,12},{1,17},{... | collective-permute-start | bytes 1032200 | tf_op jit(solution)/shard_map/ppermute | solution.py:23
  19.8 36.7 %collective-permute-start.7 = (bf16[112,1536]{1,0:T(8,128)(2,1)}, bf16[112,1536]{1,0:T(8,128)(2,1)}, u32[]{:S(2)}, u32[]{:S(2)}) collective-permute-start(bf16[112,1536]{1,0:T(8,128)(2,1)} %pad_maximum_fusion.7.rest_0_), channel_id=1, source_target_pairs={{0,4},{4,0},{8,12},{12,8},{16,20},{20,16},{24,28},{28,24},{1,5},{5... | collective-permute-start | bytes 1032200 | tf_op jit(solution)/shard_map/ppermute | solution.py:23
  21.5 71.4 %copy-start.49 = (s32[896]{0:T(1024)}, s32[896]{0:T(1024)S(1)}, u32[]{:S(2)}) copy-start(s32[896]{0:T(1024)S(1)} %fusion.51) | copy-start | bytes 10756
  28.9 14.3 %collective-permute-start.4 = (bf16[112,576]{1,0:T(8,128)(2,1)S(1)}, bf16[112,576]{1,0:T(8,128)(2,1)S(1)}, u32[]{:S(2)}, u32[]{:S(2)}) collective-permute-start(bf16[112,576]{1,0:T(8,128)(2,1)S(1)} %get-tuple-element.161.rest_0_), channel_id=1, source_target_pairs={{0,4},{4,0},{8,12},{12,8},{16,20},{20,16},{24,28},{28,24},{1,5},{5... | collective-permute-start | bytes 387080 | tf_op jit(solution)/shard_map/ppermute | solution.py:23
  29.4 13.1 %collective-permute-start.3 = (bf16[112,576]{1,0:T(8,128)(2,1)S(1)}, bf16[112,576]{1,0:T(8,128)(2,1)S(1)}, u32[]{:S(2)}, u32[]{:S(2)}) collective-permute-start(bf16[112,576]{1,0:T(8,128)(2,1)S(1)} %get-tuple-element.161.rest_0_), channel_id=1, source_target_pairs={{0,16},{4,20},{8,24},{12,28},{16,0},{20,4},{24,8},{28,12},{1,17},{... | collective-permute-start | bytes 387080 | tf_op jit(solution)/shard_map/ppermute | solution.py:23
  31.4 37.0 %collective-permute-start.2 = (bf16[512,896]{1,0:T(8,128)(2,1)S(1)}, bf16[512,896]{1,0:T(8,128)(2,1)}, u32[]{:S(2)}, u32[]{:S(2)}) collective-permute-start(bf16[512,896]{1,0:T(8,128)(2,1)S(1)} %multiply_convert_fusion.1.own_ref.refs_0_), channel_id=1, source_target_pairs={{0,1},{1,0},{2,3},{3,2},{4,5},{5,4},{6,7},{7,6},{8,9},{9,8},{10,11... | collective-permute-start | bytes 2752520 | tf_op jit(solution)/shard_map/ppermute | solution.py:23
  42.4 8.7 %collective-permute-start.11 = (bf16[112,512]{1,0:T(8,128)(2,1)S(1)}, bf16[112,512]{1,0:T(8,128)(2,1)S(1)}, u32[]{:S(2)}, u32[]{:S(2)}) collective-permute-start(bf16[112,512]{1,0:T(8,128)(2,1)S(1)} %fusion.50.rest_0_), channel_id=1, source_target_pairs={{0,16},{4,20},{8,24},{12,28},{16,0},{20,4},{24,8},{28,12},{1,17},{... | collective-permute-start | bytes 344072 | tf_op jit(solution)/shard_map/ppermute | solution.py:23
  43.8 12.6 %collective-permute-start.5 = (bf16[224,576]{1,0:T(8,128)(2,1)}, bf16[224,576]{1,0:T(8,128)(2,1)S(1)}, u32[]{:S(2)}, u32[]{:S(2)}) collective-permute-start(bf16[224,576]{1,0:T(8,128)(2,1)} %pad_maximum_fusion.9), channel_id=1, source_target_pairs={{0,8},{4,12},{8,0},{12,4},{16,24},{20,28},{24,16},{28,20},{1,9},{5... | collective-permute-start | bytes 774152 | tf_op jit(solution)/shard_map/ppermute | solution.py:23
  49.1 40.3 %copy-start.3 = (f32[1024,128]{1,0:T(8,128)}, f32[1024,128]{1,0:T(8,128)S(1)}, u32[]{:S(2)}) copy-start(f32[1024,128]{1,0:T(8,128)S(1)} %get-tuple-element.230.sin_ref) | copy-start | bytes 1572868
  51.1 5.4 %collective-permute-start.6 = (bf16[112,576]{1,0:T(8,128)(2,1)S(1)}, bf16[112,576]{1,0:T(8,128)(2,1)S(1)}, u32[]{:S(2)}, u32[]{:S(2)}) collective-permute-start(bf16[112,576]{1,0:T(8,128)(2,1)S(1)} %collective-permute-done.3.rest_1_), channel_id=1, source_target_pairs={{0,4},{4,0},{8,12},{12,8},{16,20},{20,16},{24,28},{28,24},{1,5},{5... | collective-permute-start | bytes 387080 | tf_op jit(solution)/shard_map/ppermute | solution.py:23
  56.5 34.0 %collective-permute-start.14 = (bf16[512,896]{1,0:T(8,128)(2,1)}, bf16[512,896]{1,0:T(8,128)(2,1)}, u32[]{:S(2)}, u32[]{:S(2)}) collective-permute-start(bf16[512,896]{1,0:T(8,128)(2,1)} %get-tuple-element.95.g0_ref.refs_4_), channel_id=1, source_target_pairs={{0,2},{1,3},{2,0},{3,1},{4,6},{5,7},{6,4},{7,5},{8,10},{9,11},{10,... | collective-permute-start | bytes 2752520 | tf_op jit(solution)/shard_map/ppermute | solution.py:23
  56.5 32.9 %copy-start.10 = (bf16[112,576]{1,0:T(8,128)(2,1)}, bf16[112,576]{1,0:T(8,128)(2,1)S(1)}, u32[]{:S(2)}) copy-start(bf16[112,576]{1,0:T(8,128)(2,1)S(1)} %collective-permute-done.6.rest_4_) | copy-start | bytes 387076
  56.5 9.9 %collective-permute-start.12 = (bf16[224,512]{1,0:T(8,128)(2,1)S(1)}, bf16[224,512]{1,0:T(8,128)(2,1)S(1)}, u32[]{:S(2)}, u32[]{:S(2)}) collective-permute-start(bf16[224,512]{1,0:T(8,128)(2,1)S(1)} %pad_maximum_fusion.10), channel_id=1, source_target_pairs={{0,8},{4,12},{8,0},{12,4},{16,24},{20,28},{24,16},{28,20},{1,9},{5... | collective-permute-start | bytes 688136 | tf_op jit(solution)/shard_map/ppermute | solution.py:23
  57.1 9.4 %collective-permute-start.8 = (bf16[224,576]{1,0:T(8,128)(2,1)S(1)}, bf16[224,576]{1,0:T(8,128)(2,1)S(1)}, u32[]{:S(2)}, u32[]{:S(2)}) collective-permute-start(bf16[224,576]{1,0:T(8,128)(2,1)S(1)} %collective-permute-done.5.rest_2_), channel_id=1, source_target_pairs={{0,4},{4,0},{8,12},{12,8},{16,20},{20,16},{24,28},{28,24},{1,5},{5... | collective-permute-start | bytes 774152 | tf_op jit(solution)/shard_map/ppermute | solution.py:23
  59.6 30.9 %collective-permute-start.15 = (bf16[112,2304]{1,0:T(8,128)(2,1)}, bf16[112,2304]{1,0:T(8,128)(2,1)S(1)}, u32[]{:S(2)}, u32[]{:S(2)}) collective-permute-start(bf16[112,2304]{1,0:T(8,128)(2,1)} %fusion.32.rest_0_), channel_id=1, source_target_pairs={{0,16},{4,20},{8,24},{12,28},{16,0},{20,4},{24,8},{28,12},{1,17},{... | collective-permute-start | bytes 1548296 | tf_op jit(solution)/shard_map/ppermute | solution.py:23
  66.4 24.1 %copy-start.5 = (bf16[224,512]{1,0:T(8,128)(2,1)}, bf16[224,512]{1,0:T(8,128)(2,1)S(1)}, u32[]{:S(2)}) copy-start(bf16[224,512]{1,0:T(8,128)(2,1)S(1)} %collective-permute-done.12.rest_2_) | copy-start | bytes 688132
  66.4 24.1 %collective-permute-start.13 = (bf16[224,1536]{1,0:T(8,128)(2,1)S(1)}, bf16[224,1536]{1,0:T(8,128)(2,1)S(1)}, u32[]{:S(2)}, u32[]{:S(2)}) collective-permute-start(bf16[224,1536]{1,0:T(8,128)(2,1)S(1)} %pad_maximum_fusion), channel_id=1, source_target_pairs={{0,8},{4,12},{8,0},{12,4},{16,24},{20,28},{24,16},{28,20},{1,9},{5... | collective-permute-start | bytes 2064392 | tf_op jit(solution)/shard_map/ppermute | solution.py:23
  66.5 24.0 %collective-permute-start.10 = (bf16[112,1536]{1,0:T(8,128)(2,1)}, bf16[112,1536]{1,0:T(8,128)(2,1)S(1)}, u32[]{:S(2)}, u32[]{:S(2)}) collective-permute-start(bf16[112,1536]{1,0:T(8,128)(2,1)} %collective-permute-done.9.rest_1_), channel_id=1, source_target_pairs={{0,4},{4,0},{8,12},{12,8},{16,20},{20,16},{24,28},{28,24},{1,5},{5... | collective-permute-start | bytes 1032200 | tf_op jit(solution)/shard_map/ppermute | solution.py:23
  68.4 22.2 %collective-permute-start.16 = (bf16[448,512]{1,0:T(8,128)(2,1)S(1)}, bf16[448,512]{1,0:T(8,128)(2,1)S(1)}, u32[]{:S(2)}, u32[]{:S(2)}) collective-permute-start(bf16[448,512]{1,0:T(8,128)(2,1)S(1)} %pad_maximum_fusion.6), channel_id=1, source_target_pairs={{0,4},{4,0},{8,12},{12,8},{16,20},{20,16},{24,28},{28,24},{1,5},{5... | collective-permute-start | bytes 1376264 | tf_op jit(solution)/shard_map/ppermute | solution.py:23
  90.5 21.6 %copy-start.37 = (bf16[112,2304]{1,0:T(8,128)(2,1)}, bf16[112,2304]{1,0:T(8,128)(2,1)S(1)}, u32[]{:S(2)}) copy-start(bf16[112,2304]{1,0:T(8,128)(2,1)S(1)} %collective-permute-done.15.rest_1_) | copy-start | bytes 1548292
  92.8 2.7 collective-permute-start.17
  93.6 18.0 %collective-permute-start.19 = (bf16[224,1536]{1,0:T(8,128)(2,1)S(1)}, bf16[224,1536]{1,0:T(8,128)(2,1)S(1)}, u32[]{:S(2)}, u32[]{:S(2)}) collective-permute-start(bf16[224,1536]{1,0:T(8,128)(2,1)S(1)} %collective-permute-done.13.rest_2_), channel_id=1, source_target_pairs={{0,4},{4,0},{8,12},{12,8},{16,20},{20,16},{24,28},{28,24},{1,5},{5... | collective-permute-start | bytes 2064392 | tf_op jit(solution)/shard_map/ppermute | solution.py:23
  96.1 26.1 %copy-start.33 = (bf16[512,896]{1,0:T(8,128)(2,1)}, bf16[512,896]{1,0:T(8,128)(2,1)S(1)}, u32[]{:S(2)}) copy-start(bf16[512,896]{1,0:T(8,128)(2,1)S(1)} %multiply_convert_fusion.x0_ref.refs_0_) | copy-start | bytes 2752516
  96.1 22.6 %collective-permute-start.18 = (bf16[512,896]{1,0:T(8,128)(2,1)S(1)}, bf16[512,896]{1,0:T(8,128)(2,1)}, u32[]{:S(2)}, u32[]{:S(2)}) collective-permute-start(bf16[512,896]{1,0:T(8,128)(2,1)S(1)} %multiply_convert_fusion.x0_ref.refs_0_), channel_id=1, source_target_pairs={{0,2},{1,3},{2,0},{3,1},{4,6},{5,7},{6,4},{7,5},{8,10},{9,11},{10,... | collective-permute-start | bytes 2752520 | tf_op jit(solution)/shard_map/ppermute | solution.py:23
  111.5 9.2 %collective-permute-start.20 = (bf16[512,896]{1,0:T(8,128)(2,1)S(1)}, bf16[512,896]{1,0:T(8,128)(2,1)S(1)}, u32[]{:S(2)}, u32[]{:S(2)}) collective-permute-start(bf16[512,896]{1,0:T(8,128)(2,1)S(1)} %multiply_convert_fusion.x0_ref.refs_0_), channel_id=1, source_target_pairs={{0,1},{1,0},{2,3},{3,2},{4,5},{5,4},{6,7},{7,6},{8,9},{9,8},{10,11... | collective-permute-start | bytes 2752520 | tf_op jit(solution)/shard_map/ppermute | solution.py:23
  111.5 10.7 %collective-permute-start.22 = (bf16[512,896]{1,0:T(8,128)(2,1)S(1)}, bf16[512,896]{1,0:T(8,128)(2,1)}, u32[]{:S(2)}, u32[]{:S(2)}) collective-permute-start(bf16[512,896]{1,0:T(8,128)(2,1)S(1)} %copy-done.57), channel_id=1, source_target_pairs={{0,1},{1,0},{2,3},{3,2},{4,5},{5,4},{6,7},{7,6},{8,9},{9,8},{10,11... | collective-permute-start | bytes 2752520 | tf_op jit(solution)/shard_map/ppermute | solution.py:23
  112.2 24.8 %collective-permute-start.25 = (bf16[224,2304]{1,0:T(8,128)(2,1)S(1)}, bf16[224,2304]{1,0:T(8,128)(2,1)S(1)}, u32[]{:S(2)}, u32[]{:S(2)}) collective-permute-start(bf16[224,2304]{1,0:T(8,128)(2,1)S(1)} %constant_dynamic-update-slice_fusion), channel_id=1, source_target_pairs={{0,4},{4,0},{8,12},{12,8},{16,20},{20,16},{24,28},{28,24},{1,5},{5... | collective-permute-start | bytes 3096584 | tf_op jit(solution)/shard_map/ppermute | solution.py:23
  118.7 24.5 %collective-permute-start.24 = (bf16[224,2304]{1,0:T(8,128)(2,1)S(1)}, bf16[224,2304]{1,0:T(8,128)(2,1)}, u32[]{:S(2)}, u32[]{:S(2)}) collective-permute-start(bf16[224,2304]{1,0:T(8,128)(2,1)S(1)} %constant_dynamic-update-slice_fusion), channel_id=1, source_target_pairs={{0,8},{4,12},{8,0},{12,4},{16,24},{20,28},{24,16},{28,20},{1,9},{5... | collective-permute-start | bytes 3096584 | tf_op jit(solution)/shard_map/ppermute | solution.py:23
  120.8 24.0 %collective-permute-start.23 = (bf16[512,896]{1,0:T(8,128)(2,1)}, bf16[512,896]{1,0:T(8,128)(2,1)}, u32[]{:S(2)}, u32[]{:S(2)}) collective-permute-start(bf16[512,896]{1,0:T(8,128)(2,1)} %collective-permute-done.14.g0_ref.refs_6_), channel_id=1, source_target_pairs={{0,1},{1,0},{2,3},{3,2},{4,5},{5,4},{6,7},{7,6},{8,9},{9,8},{10,11... | collective-permute-start | bytes 2752520 | tf_op jit(solution)/shard_map/ppermute | solution.py:23
  121.7 23.1 %collective-permute-start.21 = (bf16[512,896]{1,0:T(8,128)(2,1)}, bf16[512,896]{1,0:T(8,128)(2,1)}, u32[]{:S(2)}, u32[]{:S(2)}) collective-permute-start(bf16[512,896]{1,0:T(8,128)(2,1)} %collective-permute-done.18.x0_ref.refs_2_), channel_id=1, source_target_pairs={{0,1},{1,0},{2,3},{3,2},{4,5},{5,4},{6,7},{7,6},{8,9},{9,8},{10,11... | collective-permute-start | bytes 2752520 | tf_op jit(solution)/shard_map/ppermute | solution.py:23
  137.0 21.8 %copy-start.54 = (bf16[224,2304]{1,0:T(8,128)(2,1)}, bf16[224,2304]{1,0:T(8,128)(2,1)S(1)}, u32[]{:S(2)}) copy-start(bf16[224,2304]{1,0:T(8,128)(2,1)S(1)} %collective-permute-done.25.rest_3_) | copy-start | bytes 3096580
  143.2 33.3 %collective-permute-start.26 = (bf16[224,2304]{1,0:T(8,128)(2,1)}, bf16[224,2304]{1,0:T(8,128)(2,1)S(1)}, u32[]{:S(2)}, u32[]{:S(2)}) collective-permute-start(bf16[224,2304]{1,0:T(8,128)(2,1)} %collective-permute-done.24.rest_2_), channel_id=1, source_target_pairs={{0,4},{4,0},{8,12},{12,8},{16,20},{20,16},{24,28},{28,24},{1,5},{5... | collective-permute-start | bytes 3096584 | tf_op jit(solution)/shard_map/ppermute | solution.py:23
  174.2 23.5 %collective-permute-start.27 = (bf16[448,1024]{1,0:T(8,128)(2,1)}, bf16[448,1024]{1,0:T(8,128)(2,1)}, u32[]{:S(2)}, u32[]{:S(2)}) collective-permute-start(bf16[448,1024]{1,0:T(8,128)(2,1)} %get-tuple-element.109), channel_id=1, source_target_pairs={{0,4},{4,0},{8,12},{12,8},{16,20},{20,16},{24,28},{28,24},{1,5},{5... | collective-permute-start | bytes 2752520 | tf_op jit(solution)/shard_map/ppermute | solution.py:23
  174.8 23.0 %collective-permute-start.28 = (bf16[448,512]{1,0:T(8,128)(2,1)}, bf16[448,512]{1,0:T(8,128)(2,1)}, u32[]{:S(2)}, u32[]{:S(2)}) collective-permute-start(bf16[448,512]{1,0:T(8,128)(2,1)} %get-tuple-element.110), channel_id=1, source_target_pairs={{0,8},{4,12},{8,0},{12,4},{16,24},{20,28},{24,16},{28,20},{1,9},{5... | collective-permute-start | bytes 1376264 | tf_op jit(solution)/shard_map/ppermute | solution.py:23
  177.5 21.8 %copy-start.34 = (f32[448,512]{1,0:T(8,128)S(1)}, f32[448,512]{1,0:T(8,128)}, u32[]{:S(2)}) copy-start(f32[448,512]{1,0:T(8,128)} %get-tuple-element.117) | copy-start | bytes 2752516
  197.8 5.0 %collective-permute-start.29 = (bf16[2,512,896]{2,1,0:T(8,128)(2,1)}, bf16[2,512,896]{2,1,0:T(8,128)(2,1)}, u32[]{:S(2)}, u32[]{:S(2)}) collective-permute-start(bf16[2,512,896]{2,1,0:T(8,128)(2,1)} %get-tuple-element.111), channel_id=1, source_target_pairs={{0,1},{1,0},{2,3},{3,2},{4,5},{5,4},{6,7},{7,6},{8,9},{9,8},{10,11... | collective-permute-start | bytes 5505032 | tf_op jit(solution)/shard_map/ppermute | solution.py:23
  201.2 29.1 %collective-permute-start.32 = (bf16[224,512]{1,0:T(8,128)(2,1)}, bf16[224,512]{1,0:T(8,128)(2,1)S(1)}, u32[]{:S(2)}, u32[]{:S(2)}) collective-permute-start(bf16[224,512]{1,0:T(8,128)(2,1)} %get-tuple-element.175), channel_id=1, source_target_pairs={{0,4},{4,0},{8,12},{12,8},{16,20},{20,16},{24,28},{28,24},{1,5},{5... | collective-permute-start | bytes 688136 | tf_op jit(solution)/shard_map/ppermute | solution.py:23
  205.8 24.5 %collective-permute-start.30 = (bf16[512,896]{1,0:T(8,128)(2,1)S(1)}, bf16[512,896]{1,0:T(8,128)(2,1)S(1)}, u32[]{:S(2)}, u32[]{:S(2)}) collective-permute-start(bf16[512,896]{1,0:T(8,128)(2,1)S(1)} %get-tuple-element.168), channel_id=1, source_target_pairs={{0,2},{1,3},{2,0},{3,1},{4,6},{5,7},{6,4},{7,5},{8,10},{9,11},{10,... | collective-permute-start | bytes 2752520 | tf_op jit(solution)/shard_map/ppermute | solution.py:23
  209.8 20.5 %collective-permute-start.31 = (bf16[224,1024]{1,0:T(8,128)(2,1)}, bf16[224,1024]{1,0:T(8,128)(2,1)S(1)}, u32[]{:S(2)}, u32[]{:S(2)}) collective-permute-start(bf16[224,1024]{1,0:T(8,128)(2,1)} %get-tuple-element.167), channel_id=1, source_target_pairs={{0,8},{4,12},{8,0},{12,4},{16,24},{20,28},{24,16},{28,20},{1,9},{5... | collective-permute-start | bytes 1376264 | tf_op jit(solution)/shard_map/ppermute | solution.py:23
  210.1 20.3 %copy-start.9 = (bf16[112,576]{1,0:T(8,128)(2,1)S(1)}, bf16[112,576]{1,0:T(8,128)(2,1)}, u32[]{:S(2)}) copy-start(bf16[112,576]{1,0:T(8,128)(2,1)} %copy-done.7) | copy-start | bytes 387076
  210.1 21.1 %copy-start.11 = (bf16[112,576]{1,0:T(8,128)(2,1)S(1)}, bf16[112,576]{1,0:T(8,128)(2,1)}, u32[]{:S(2)}) copy-start(bf16[112,576]{1,0:T(8,128)(2,1)} %copy-done.10) | copy-start | bytes 387076
  230.4 23.7 %collective-permute-start.33 = (bf16[2,512,896]{2,1,0:T(8,128)(2,1)}, bf16[2,512,896]{2,1,0:T(8,128)(2,1)}, u32[]{:S(2)}, u32[]{:S(2)}) collective-permute-start(bf16[2,512,896]{2,1,0:T(8,128)(2,1)} %get-tuple-element.118), channel_id=1, source_target_pairs={{0,1},{1,0},{2,3},{3,2},{4,5},{5,4},{6,7},{7,6},{8,9},{9,8},{10,11... | collective-permute-start | bytes 5505032 | tf_op jit(solution)/shard_map/ppermute | solution.py:23
  236.0 76.8 %collective-permute-start.52 = (bf16[112,1536]{1,0:T(8,128)(2,1)}, bf16[112,1536]{1,0:T(8,128)(2,1)}, u32[]{:S(2)}, u32[]{:S(2)}) collective-permute-start(bf16[112,1536]{1,0:T(8,128)(2,1)} %pad_maximum_fusion.8), channel_id=1, source_target_pairs={{0,16},{4,20},{8,24},{12,28},{16,0},{20,4},{24,8},{28,12},{1,17},{... | collective-permute-start | bytes 1032200 | tf_op jit(solution)/shard_map/ppermute | solution.py:23
  253.3 59.6 %collective-permute-start.34 = (bf16[512,896]{1,0:T(8,128)(2,1)}, bf16[512,896]{1,0:T(8,128)(2,1)}, u32[]{:S(2)}, u32[]{:S(2)}) collective-permute-start(bf16[512,896]{1,0:T(8,128)(2,1)} %get-tuple-element.119), channel_id=1, source_target_pairs={{0,2},{1,3},{2,0},{3,1},{4,6},{5,7},{6,4},{7,5},{8,10},{9,11},{10,... | collective-permute-start | bytes 2752520 | tf_op jit(solution)/shard_map/ppermute | solution.py:23
  262.6 3.6 collective-permute-start.35
  271.4 21.1 %collective-permute-start.36 = (bf16[448,512]{1,0:T(8,128)(2,1)S(1)}, bf16[448,512]{1,0:T(8,128)(2,1)S(1)}, u32[]{:S(2)}, u32[]{:S(2)}) collective-permute-start(bf16[448,512]{1,0:T(8,128)(2,1)S(1)} %get-tuple-element.130), channel_id=1, source_target_pairs={{0,4},{4,0},{8,12},{12,8},{16,20},{20,16},{24,28},{28,24},{1,5},{5... | collective-permute-start | bytes 1376264 | tf_op jit(solution)/shard_map/ppermute | solution.py:23
  292.6 30.8 %collective-permute-start.48 = (bf16[224,512]{1,0:T(8,128)(2,1)S(1)}, bf16[224,512]{1,0:T(8,128)(2,1)S(1)}, u32[]{:S(2)}, u32[]{:S(2)}) collective-permute-start(bf16[224,512]{1,0:T(8,128)(2,1)S(1)} %get-tuple-element.176), channel_id=1, source_target_pairs={{0,8},{4,12},{8,0},{12,4},{16,24},{20,28},{24,16},{28,20},{1,9},{5... | collective-permute-start | bytes 688136 | tf_op jit(solution)/shard_map/ppermute | solution.py:23
  312.9 31.9 %collective-permute-start.43 = (bf16[448,576]{1,0:T(8,128)(2,1)S(1)}, bf16[448,576]{1,0:T(8,128)(2,1)}, u32[]{:S(2)}, u32[]{:S(2)}) collective-permute-start(bf16[448,576]{1,0:T(8,128)(2,1)S(1)} %get-tuple-element.141), channel_id=1, source_target_pairs={{0,4},{4,0},{8,12},{12,8},{16,20},{20,16},{24,28},{28,24},{1,5},{5... | collective-permute-start | bytes 1548296 | tf_op jit(solution)/shard_map/ppermute | solution.py:23
  317.2 23.8 %collective-permute-start.37 = (bf16[512,896]{1,0:T(8,128)(2,1)}, bf16[512,896]{1,0:T(8,128)(2,1)}, u32[]{:S(2)}, u32[]{:S(2)}) collective-permute-start(bf16[512,896]{1,0:T(8,128)(2,1)} %slice.608), channel_id=1, source_target_pairs={{0,1},{1,0},{2,3},{3,2},{4,5},{5,4},{6,7},{7,6},{8,9},{9,8},{10,11... | collective-permute-start | bytes 2752520 | tf_op jit(solution)/shard_map/ppermute | solution.py:23
  323.5 14.4 %collective-permute-start.49 = (bf16[112,512]{1,0:T(8,128)(2,1)S(1)}, bf16[112,512]{1,0:T(8,128)(2,1)}, u32[]{:S(2)}, u32[]{:S(2)}) collective-permute-start(bf16[112,512]{1,0:T(8,128)(2,1)S(1)} %fusion.42), channel_id=1, source_target_pairs={{0,16},{4,20},{8,24},{12,28},{16,0},{20,4},{24,8},{28,12},{1,17},{... | collective-permute-start | bytes 344072 | tf_op jit(solution)/shard_map/ppermute | solution.py:23
  339.0 9.1 %collective-permute-start.50 = (bf16[112,224]{1,0:T(8,128)(2,1)S(1)}, bf16[112,224]{1,0:T(8,128)(2,1)S(1)}, u32[]{:S(2)}, u32[]{:S(2)}) collective-permute-start(bf16[112,224]{1,0:T(8,128)(2,1)S(1)} %get-tuple-element.190), channel_id=1, source_target_pairs={{0,0},{1,2},{2,1},{3,3},{4,4},{5,6},{6,5},{7,7},{8,8},{9,10},{10,9... | collective-permute-start | bytes 150536 | tf_op jit(solution)/shard_map/ppermute | solution.py:700
  339.7 8.4 %collective-permute-start.51 = (bf16[112,224]{1,0:T(8,128)(2,1)S(1)}, bf16[112,224]{1,0:T(8,128)(2,1)S(1)}, u32[]{:S(2)}, u32[]{:S(2)}) collective-permute-start(bf16[112,224]{1,0:T(8,128)(2,1)S(1)} %get-tuple-element.191), channel_id=1, source_target_pairs={{0,1},{1,3},{2,0},{3,2},{4,5},{5,7},{6,4},{7,6},{8,9},{9,11},{10,8... | collective-permute-start | bytes 150536 | tf_op jit(solution)/shard_map/ppermute | solution.py:700
  344.6 1.3 collective-permute-start.38
  345.9 9.3 %collective-permute-start.44 = (bf16[224,576]{1,0:T(8,128)(2,1)S(1)}, bf16[224,576]{1,0:T(8,128)(2,1)S(1)}, u32[]{:S(2)}, u32[]{:S(2)}) collective-permute-start(bf16[224,576]{1,0:T(8,128)(2,1)S(1)} %get-tuple-element.170), channel_id=1, source_target_pairs={{0,8},{4,12},{8,0},{12,4},{16,24},{20,28},{24,16},{28,20},{1,9},{5... | collective-permute-start | bytes 774152 | tf_op jit(solution)/shard_map/ppermute | solution.py:23
  346.0 3.8 collective-permute-start.39
  349.8 6.0 %collective-permute-start.40 = (f32[23,128]{1,0:T(8,128)S(1)}, f32[23,128]{1,0:T(8,128)S(1)}, u32[]{:S(2)}, u32[]{:S(2)}) collective-permute-start(f32[23,128]{1,0:T(8,128)S(1)} %fusion.77), channel_id=1, source_target_pairs={{0,4},{4,0},{8,12},{12,8},{16,20},{20,16},{24,28},{28,24},{1,5},{5... | collective-permute-start | bytes 35336 | tf_op jit(solution)/shard_map/ppermute | solution.py:23
  355.2 12.6 %collective-permute-start.45 = (bf16[112,576]{1,0:T(8,128)(2,1)S(1)}, bf16[112,576]{1,0:T(8,128)(2,1)S(1)}, u32[]{:S(2)}, u32[]{:S(2)}) collective-permute-start(bf16[112,576]{1,0:T(8,128)(2,1)S(1)} %fusion.34), channel_id=1, source_target_pairs={{0,16},{4,20},{8,24},{12,28},{16,0},{20,4},{24,8},{28,12},{1,17},{... | collective-permute-start | bytes 387080 | tf_op jit(solution)/shard_map/ppermute | solution.py:23
  355.9 3.7 collective-permute-start.41
  359.6 8.2 %collective-permute-start.42 = (f32[23,128]{1,0:T(8,128)S(1)}, f32[23,128]{1,0:T(8,128)S(1)}, u32[]{:S(2)}, u32[]{:S(2)}) collective-permute-start(f32[23,128]{1,0:T(8,128)S(1)} %add.233), channel_id=1, source_target_pairs={{0,16},{4,20},{8,24},{12,28},{16,0},{20,4},{24,8},{28,12},{1,17},{... | collective-permute-start | bytes 35336 | tf_op jit(solution)/shard_map/ppermute | solution.py:23
  368.0 4.6 %collective-permute-start.46 = (bf16[112,288]{1,0:T(8,128)(2,1)S(1)}, bf16[112,288]{1,0:T(8,128)(2,1)S(1)}, u32[]{:S(2)}, u32[]{:S(2)}) collective-permute-start(bf16[112,288]{1,0:T(8,128)(2,1)S(1)} %get-tuple-element.188), channel_id=1, source_target_pairs={{0,0},{1,2},{2,1},{3,3},{4,4},{5,6},{6,5},{7,7},{8,8},{9,10},{10,9... | collective-permute-start | bytes 193544 | tf_op jit(solution)/shard_map/ppermute | solution.py:700
  368.7 5.9 %collective-permute-start.47 = (bf16[112,288]{1,0:T(8,128)(2,1)S(1)}, bf16[112,288]{1,0:T(8,128)(2,1)S(1)}, u32[]{:S(2)}, u32[]{:S(2)}) collective-permute-start(bf16[112,288]{1,0:T(8,128)(2,1)S(1)} %get-tuple-element.189), channel_id=1, source_target_pairs={{0,1},{1,3},{2,0},{3,2},{4,5},{5,7},{6,4},{7,6},{8,9},{9,11},{10,8... | collective-permute-start | bytes 193544 | tf_op jit(solution)/shard_map/ppermute | solution.py:700
  (55 other events, 363.1 us)
Sparse Core Ops, SparseCore 0:
  253.4 95.4 reduce-scatter.1

commit v9 on v8

--- a/solution.py
+++ b/solution.py
@@ -382,13 +382,12 @@
     )(parity, *ins, *pieces, *earlier)
 
 
-def mlp_kernel(x0_ref, x1_ref, g0_ref, g1_ref, *rest, count, add):
-    pieces = rest[:count]
-    rest = rest[count:]
-    if add:
-        near_in, far_in, act_ref, near_ref, far_ref, held, sems = rest
-    else:
-        act_ref, near_ref, far_ref, held, sems = rest
+def mlp_kernel(*refs, blocks, count, add):
+    rows, grads, rest = refs[:blocks], refs[blocks : 2 * blocks], refs[2 * blocks :]
+    pieces, rest = rest[:count], rest[count:]
+    earlier, rest = rest[: blocks * add], rest[blocks * add :]
+    act_ref, outs = rest[0], rest[1 : 1 + blocks]
+    held, sems = rest[1 + blocks :]
     n = held.shape[1] // 3
     step = pl.program_id(0)
 
@@ -396,9 +395,15 @@
     def _():
         assemble(pieces, held, sems)
 
+    def chosen(parts):
+        block = parts[0][...]
+        for k in range(1, blocks):
+            block = jnp.where(step == k, parts[k][...], block)
+        return block
+
     wg, wu, wd = (held[:, k * n : (k + 1) * n] for k in range(3))
-    x = jnp.where(step == 0, x0_ref[...], x1_ref[...])
-    g = jnp.where(step == 0, g0_ref[...], g1_ref[...])
+    x = chosen(rows)
+    g = chosen(grads)
     gate = jnp.dot(x, wg, preferred_element_type=f32)
     up = jnp.dot(x, wu, preferred_element_type=f32)
     gh = jnp.dot(g, wd, preferred_element_type=f32)
@@ -414,41 +419,36 @@
     ngrad = lax.dot_general(gg, wg, NT, preferred_element_type=f32)
     ngrad = ngrad + lax.dot_general(gu, wu, NT, preferred_element_type=f32)
     down = lax.dot_general(hid, wd, NT, preferred_element_type=f32)
-
-    @pl.when(step == 0)
-    def _():
-        near_ref[0] = (ngrad + near_in[0].astype(f32) if add else ngrad).astype(bf16)
-        near_ref[1] = (down + near_in[1].astype(f32) if add else down).astype(bf16)
-
-    @pl.when(step == 1)
-    def _():
-        far_ref[0] = (ngrad + far_in[0].astype(f32) if add else ngrad).astype(bf16)
-        far_ref[1] = (down + far_in[1].astype(f32) if add else down).astype(bf16)
+    for k in range(blocks):
+
+        @pl.when(step == k)
+        def _():
+            for part, value in enumerate((ngrad, down)):
+                if add:
+                    value = value + earlier[k][part].astype(f32)
+                outs[k][part] = value.astype(bf16)
 
 
 def mlp(rows, grads, pieces, sums=None):
     t, d = rows[0].shape
+    blocks = len(rows)
     columns = pieces[0].shape[1]
-    add = sums is not None
     ins = (*rows, *grads)
     sums = tuple(sums or ())
     both = pl.BlockSpec((2, t, d), lambda i: (0, 0, 0))
     return pl.pallas_call(
-        functools.partial(mlp_kernel, count=len(pieces), add=add),
-        grid=(2,),
+        functools.partial(mlp_kernel, blocks=blocks, count=len(pieces), add=bool(sums)),
+        grid=(blocks,),
         in_specs=[whole(a) for a in ins] + [in_place(p) for p in pieces] + [both] * len(sums),
-        out_specs=[pl.BlockSpec((t, columns), lambda i: (i, 0)), both, both],
-        out_shape=[
-            jax.ShapeDtypeStruct((2 * t, columns), bf16),
-            jax.ShapeDtypeStruct((2, t, d), bf16),
-            jax.ShapeDtypeStruct((2, t, d), bf16),
-        ],
+        out_specs=[pl.BlockSpec((t, columns), lambda i: (i, 0))] + [both] * blocks,
+        out_shape=[jax.ShapeDtypeStruct((blocks * t, columns), bf16)]
+        + [jax.ShapeDtypeStruct((2, t, d), bf16)] * blocks,
         scratch_shapes=[
             pltpu.VMEM((d, columns), bf16),
             pltpu.SemaphoreType.DMA((len(pieces),)),
         ],
         compiler_params=kernel_params(58),
-        cost_estimate=cost(8 * t * d * columns, 30 * MIB, 2 * t * columns),
+        cost_estimate=cost(6 * blocks * t * d * columns, 15 * blocks * MIB, blocks * t * columns),
     )(*ins, *pieces, *sums)
 
 
@@ -834,11 +834,12 @@
 
     f_beside = far.catch_up(n_last)
     f_two = far.double(blocks[2])
-    f_last = far.send(f_beside)
-    first_pieces, second_pieces = (gather.all() for gather in mlp_gathers)
-    act_own, *sums_own = mlp([after(blocks[0], blocks[2]), blocks[1]], grad_blocks[:2], first_pieces)
-    act_far, *sums_far = mlp(blocks[2:], grad_blocks[2:], first_pieces)
-    sent_one, kept_one, sent_two, kept_two = outer(blocks, grad_blocks, [act_own, act_far])
+    first_pieces = near.all()
+    act_all, *sums = mlp(blocks, grad_blocks, first_pieces)
+    sums_own, sums_far = sums[:2], sums[2:]
+    f_last = far.send(f_beside, act_all)
+    second_pieces = far.all()
+    sent_one, kept_one, sent_two, kept_two = outer(blocks, grad_blocks, [act_all])
     first_scatter = Scatter([(sent_one, kept_one), (sent_two, kept_two)], bits)
     start_far = after(blocks[2], kept_one)
     act_far, near_far, far_far = mlp(
@@ -923,10 +924,12 @@
     qkv_full = jnp.concatenate(qkv_pieces, 0)
     grad_mixed = after(grad_mixed, passed)
     out_scatter.step()
-    partial = jnp.einsum("tc,dc->td", grad_mixed, qkv_full, preferred_element_type=f32)
-    grad_normed_one = partial[:tok_local] + flip(
-        partial[tok_local:].astype(bf16), "col", 0
-    ).astype(f32)
+
+    def back_to_normed(rows):
+        return jnp.einsum("tc,dc->td", rows, qkv_full, preferred_element_type=f32)
+
+    other = flip(back_to_normed(grad_mixed[tok_local:]).astype(bf16), "col", 0)
+    grad_normed_one = back_to_normed(grad_mixed[:tok_local]) + other.astype(f32)
     scaled_one = gain_one * grad_normed_one
     inner_one = jnp.sum(scaled_one * input_rows, axis=1)
     input_grad = unstored(

time: 394 us -> 393 us (level)
  matrix products: 16.5 us -> 20.5 us
    dot_general x1 -> x2, matrix products: 1.73 us -> 6.68 us  [back_to_normed(): return jnp.einsum('tc,dc->td', rows, qkv_full, preferred_element_type=f32)]
    pallas_call x4 -> x3, Pallas kernels: 68.5 us -> 65.4 us  [mlp(): pl.pallas_call(functools.partial(mlp_kernel, blocks=blocks, count=len(pie...]
    unnamed x138 -> x156, local copies, waits for them, and re-layouts: 17.2 us -> 17.3 us
  transfers between devices with their start and end apart: 54 -> 54, of which waited for: 13 -> 16; matrix products, arithmetic and copies ran while one was open for 17% -> 17% of each run, Pallas kernels for 41% -> 40%
where the time goes in v9:
time: 393 us; the launch traced here: 386 us
  Pallas kernels  157 us (40%)
  waiting for transfers between devices  70.1 us (18%)
  starting transfers between devices  59 us (15%)
  other arithmetic  35.8 us (9%)
  local copies, waits for them, and re-layouts  28.1 us (7%)
  matrix products  20.5 us (5%)
  between operations  15.7 us (4%)
    ppermute x47, waiting for transfers between devices, flip(): return lax.ppermute(block, axis, [(i, i ^ 1 << bit) for i in range(count)])  68.1 us
    pallas_call x3, Pallas kernels, mlp(): pl.pallas_call(functools.partial(mlp_kernel, blocks=blocks, count=len(pie...  65.4 us
    ppermute x47, starting transfers between devices, flip(): return lax.ppermute(block, axis, [(i, i ^ 1 << bit) for i in range(count)])  49.2 us
    pallas_call x2, Pallas kernels, attend_back(): pl.pallas_call(functools.partial(attend_back_kernel, block=block, count=l...  32.6 us
    pallas_call x1, Pallas kernels, attend(): pl.pallas_call(functools.partial(attend_kernel, block=block, count=len(pi...  20 us
    unnamed x156, local copies, waits for them, and re-layouts  17.3 us
    pallas_call x1, Pallas kernels, outer_whole(): pl.pallas_call(functools.partial(outer_whole_kernel, blocks=len(rows), co...  15.5 us
    pallas_call x1, Pallas kernels, outer(): pl.pallas_call(functools.partial(outer_kernel, blocks=len(rows)), grid=(3...  15.5 us
  transfers between devices with their start and end apart: 54, of which 16 were waited for; matrix products, arithmetic and copies ran while one was open for 17% of the time, Pallas kernels for 40%

profile of v9, /device:TPU:0, one launch (start us, length us, event | category | flops | bytes accessed | tf_op | source)
XLA Modules:
  0.0 386.0 jit_solution(11425816060871249905)
XLA Ops:
  10.1 3.0 collective-permute-start.1
  17.3 2.6 collective-permute-start.9
  19.9 1.5 collective-permute-start.7
  21.7 2.0 fusion.49
  23.7 2.8 bitcast_convert_fusion
  29.9 1.3 multiply_reduce_fusion.5
  31.9 10.6 %collective-permute-done.3.rest_1_ = bf16[112,576]{1,0:T(8,128)(2,1)S(1)} collective-permute-done((bf16[112,576]{1,0:T(8,128)(2,1)S(1)}, bf16[112,576]{1,0:T(8,128)(2,1)S(1)}, u32[]{:S(2)}, u32[]{:S(2)}) %collective-permute-start.3) | collective-permute-done | bytes 129056 | tf_op jit(solution)/shard_map/ppermute | solution.py:23
  43.3 4.3 %collective-permute-start.5 = (bf16[224,576]{1,0:T(8,128)(2,1)}, bf16[224,576]{1,0:T(8,128)(2,1)S(1)}, u32[]{:S(2)}, u32[]{:S(2)}) collective-permute-start(bf16[224,576]{1,0:T(8,128)(2,1)} %pad_maximum_fusion.9), channel_id=1, source_target_pairs={{0,8},{4,12},{8,0},{12,4},{16,24},{20,28},{24,16},{28,20},{1,9},{5... | collective-permute-start | bytes 774152 | tf_op jit(solution)/shard_map/ppermute | solution.py:23
  48.6 2.6 collective-permute-done.11.rest_1_
  51.2 1.5 collective-permute-start.6
  53.5 2.4 collective-permute-done.5.rest_2_
  56.5 1.5 collective-permute-start.8
  59.2 2.7 collective-permute-start.15
  61.9 2.9 collective-permute-done.12.rest_2_
  64.9 3.7 collective-permute-start.10
  68.7 20.0 %shard_map.186 = (bf16[1024,512]{1,0:T(8,128)(2,1)S(1)}, bf16[1024,64]{1,0:T(8,128)(2,1)S(1)}, bf16[1024,512]{1,0:T(8,128)(2,1)S(1)}, f32[8,1024]{1,0:T(8,128)S(1)}) custom-call(s32[1]{0:T(128)} %bitcast.1.parity_ref, bf16[512,896]{1,0:T(8,128)(2,1)S(1)} %multiply_convert_fusion.1.own_ref.refs_0_, bf16[512,896]{1,0:T(8,128)(2,1)} %collective-permute-done.2.other_ref.refs_1_, ...), custom_call_target="tpu_custom_call" | custom-call | flops 12000000000 | bytes 8000000 | tf_op jit(solution)/shard_map/pallas_call | solution.py:159
  88.8 2.2 shard_map.187
  91.8 1.8 collective-permute-done.17
  94.0 1.2 copy-done.20
  95.5 1.8 collective-permute-start.18
  97.3 1.9 collective-permute-start.19
  99.2 15.6 %collective-permute-done.19.refs_13_ = bf16[224,1536]{1,0:T(8,128)(2,1)} collective-permute-done((bf16[224,1536]{1,0:T(8,128)(2,1)S(1)}, bf16[224,1536]{1,0:T(8,128)(2,1)}, u32[]{:S(2)}, u32[]{:S(2)}) %collective-permute-start.19) | collective-permute-done | bytes 688160 | tf_op jit(solution)/shard_map/ppermute | solution.py:23
  115.4 2.6 collective-permute-done.18.refs_2_.refs_0_
  118.0 2.0 collective-permute-start.25
  120.0 2.0 collective-permute-start.24
  124.0 24.7 %shard_map.188 = (bf16[2048,1536]{1,0:T(8,128)(2,1)}, bf16[2,512,896]{2,1,0:T(8,128)(2,1)}, bf16[2,512,896]{2,1,0:T(8,128)(2,1)}, bf16[2,512,896]{2,1,0:T(8,128)(2,1)}, bf16[2,512,896]{2,1,0:T(8,128)(2,1)}) custom-call(bf16[512,896]{1,0:T(8,128)(2,1)} %copy-done.37, bf16[512,896]{1,0:T(8,128)(2,1)} %copy-done.66, bf16[512,896]{1,0:T(8,128)(2,1)} %copy-done.65, ...), custom_call_target="tpu_custom_call" | custom-call | flops 16911433728 | bytes 62914560 | tf_op jit(solution)/shard_map/pallas_call | solution.py:439
  148.9 15.5 %shard_map.189 = (bf16[448,1024]{1,0:T(8,128)(2,1)}, f32[448,1024]{1,0:T(8,128)}, bf16[448,512]{1,0:T(8,128)(2,1)}, f32[448,512]{1,0:T(8,128)}) custom-call(bf16[512,896]{1,0:T(8,128)(2,1)} %copy-done.37, bf16[512,896]{1,0:T(8,128)(2,1)} %copy-done.66, bf16[512,896]{1,0:T(8,128)(2,1)} %copy-done.65, ...), custom_call_target="tpu_custom_call" | custom-call | flops 5637144576 | bytes 20971520 | tf_op jit(solution)/shard_map/pallas_call | solution.py:500
  165.3 1.2 collective-permute-start.27
  166.5 8.1 %collective-permute-done.26.refs_8_ = bf16[224,2304]{1,0:T(8,128)(2,1)S(1)} collective-permute-done((bf16[224,2304]{1,0:T(8,128)(2,1)}, bf16[224,2304]{1,0:T(8,128)(2,1)S(1)}, u32[]{:S(2)}, u32[]{:S(2)}) %collective-permute-start.26) | collective-permute-done | bytes 1032224 | tf_op jit(solution)/shard_map/ppermute | solution.py:23
  175.6 20.2 %shard_map.190 = (bf16[1024,2304]{1,0:T(8,128)(2,1)}, bf16[2,512,896]{2,1,0:T(8,128)(2,1)}, bf16[2,512,896]{2,1,0:T(8,128)(2,1)}) custom-call(bf16[512,896]{1,0:T(8,128)(2,1)} %copy-done.65, bf16[512,896]{1,0:T(8,128)(2,1)} %collective-permute-done.21.refs_3_.refs_1_, bf16[512,896]{1,0:T(8,128)(2,1)} %copy-done.64, bf16[512,896]{1,0:T(8,128)(2,1)} %copy-done.68, ...), custom_call_target="tpu_custom_call" | custom-call | flops 12683575296 | bytes 31457280 | tf_op jit(solution)/shard_map/pallas_call | solution.py:439
  197.5 1.2 convert_add_fusion.6
  198.8 2.3 convert_add_fusion.2
  202.1 2.0 add_convert_fusion
  205.2 1.2 collective-permute-start.30
  206.4 20.5 %shard_map.191 = (bf16[1024,2304]{1,0:T(8,128)(2,1)}, bf16[2,512,896]{2,1,0:T(8,128)(2,1)}, bf16[2,512,896]{2,1,0:T(8,128)(2,1)}) custom-call(bf16[512,896]{1,0:T(8,128)(2,1)} %copy-done.37, bf16[512,896]{1,0:T(8,128)(2,1)} %copy-done.66, bf16[512,896]{1,0:T(8,128)(2,1)} %get-tuple-element.93.refs_4_.refs_2_, bf16[512,896]{1,0:T(8,128)(2,1)} %copy-done.67, ...), custom_call_target="tpu_custom_call" | custom-call | flops 12683575296 | bytes 31457280 | tf_op jit(solution)/shard_map/pallas_call | solution.py:439
  230.2 1.9 slice_add_fusion.1
  232.9 2.9 collective-permute-start.52
  235.9 15.5 %shard_map.192 = bf16[896,2304]{1,0:T(8,128)(2,1)} custom-call(s32[1]{0:T(128)} %bitcast.8.row_ref, bf16[512,896]{1,0:T(8,128)(2,1)} %copy-done.37, bf16[512,896]{1,0:T(8,128)(2,1)} %copy-done.66, bf16[512,896]{1,0:T(8,128)(2,1)} %copy-done.65, bf16[512,896]{1,0:T(8,128)(2,1)} %collective-permute-done.21.refs_3_.refs_1_, ...), custom_call_target="tpu_custom_call" | custom-call | flops 8455716864 | bytes 20971520 | tf_op jit(solution)/shard_map/pallas_call | solution.py:563
  251.4 1.2 collective-permute-start.34
  252.9 2.5 multiply_reduce_fusion
  255.5 5.1 %fusion.61 = (bf16[512,896]{1,0:T(8,128)(2,1)S(1)}, f32[512,896]{1,0:T(8,128)}) fusion(f32[512,896]{1,0:T(8,128)} %copy-done.20, f32[512]{0:T(512)S(1)} %fusion.58, bf16[512,896]{1,0:T(8,128)(2,1)} %copy-done.26, bf16[2,512,896]{2,1,0:T(8,128)(2,1)} %collective-permute-done.33, bf16[2,512,896]{2,1,0:T(8,128)(2,1)} %get-tuple-element.111, ...), kind=kLoop, calls=%fused_computation.179 | loop fusion | flops 5046272 | bytes 9182720 | tf_op jit(solution)/shard_map/convert_element_type | solution.py:883
  261.2 1.9 collective-permute-done.35.refs_1_.other_ref
  264.1 1.2 copy-done.12
  265.3 1.2 copy-done.16
  266.5 1.7 shard_map.193
  272.4 17.6 %shard_map.194 = (bf16[1024,256]{1,0:T(8,128)(2,1)S(1)}, f32[1,256]{1,0:T(1,128)S(1)}, f32[1024,128]{1,0:T(8,128)S(1)}, f32[1024,128]{1,0:T(8,128)S(1)}) custom-call(s32[1]{0:T(128)} %bitcast.1.parity_ref, bf16[512,896]{1,0:T(8,128)(2,1)} %copy-done.2, bf16[512,896]{1,0:T(8,128)(2,1)} %copy-done.11, bf16[1024,512]{1,0:T(8,128)(2,1)} %copy-done.17, ...), custom_call_target="tpu_custom_call" | custom-call | flops 12000000000 | bytes 6000000 | tf_op jit(solution)/shard_map/pallas_call | solution.py:352
  290.2 2.1 collective-permute-start.48
  292.3 15.0 %shard_map.195 = (bf16[1024,320]{1,0:T(8,128)(2,1)S(1)}, f32[1,320]{1,0:T(1,128)S(1)}) custom-call(s32[1]{0:T(128)} %bitcast.1.parity_ref, bf16[512,896]{1,0:T(8,128)(2,1)} %copy-done.2, bf16[512,896]{1,0:T(8,128)(2,1)} %copy-done.11, bf16[1024,512]{1,0:T(8,128)(2,1)} %copy-done.17, bf16[1024,64]{1,0:T(8,128)(2,1)S(1)} %copy-done.19, ...), custom_call_target="tpu_custom_call" | custom-call | flops 12000000000 | bytes 6000000 | tf_op jit(solution)/shard_map/pallas_call | solution.py:352
  307.5 3.7 shard_map.196
  312.1 1.9 convolution_convert_fusion
  315.1 4.0 %fusion.15 = bf16[512,896]{1,0:T(8,128)(2,1)} fusion(s32[896]{0:T(1024)S(1)} %fusion.53, f32[512,896]{1,0:T(8,128)S(1)} %copy-done.22, bf16[512,896]{1,0:T(8,128)(2,1)} %collective-permute-done.34, bf16[2,512,896]{2,1,0:T(8,128)(2,1)} %collective-permute-done.33, bf16[2,512,896]{2,1,0:T(8,128)(2,1)S(1)} %copy-done.30), kind=kOutput, calls=%fused_computation.35 | convolution fusion | flops 826556416 | bytes 5509120 | tf_op jit(solution)/shard_map/dot_general | solution.py:773
  320.6 13.8 %collective-permute-done.49 = bf16[112,512]{1,0:T(8,128)(2,1)} collective-permute-done((bf16[112,512]{1,0:T(8,128)(2,1)S(1)}, bf16[112,512]{1,0:T(8,128)(2,1)}, u32[]{:S(2)}, u32[]{:S(2)}) %collective-permute-start.49) | collective-permute-done | bytes 114720 | tf_op jit(solution)/shard_map/ppermute | solution.py:23
  336.3 2.1 collective-permute-start.50
  338.5 4.8 %multiply_reduce_fusion.1 = (f32[896]{0:T(1024)S(1)}, f32[512]{0:T(512)}, f32[512,896]{1,0:T(8,128)}) fusion(f32[512,896]{1,0:T(8,128)} %copy-done.23, f32[512]{0:T(512)S(1)} %add_rsqrt_fusion.1, f32[896]{0:T(1024)S(1)} %fusion.17, bf16[512,896]{1,0:T(8,128)(2,1)S(1)} %collective-permute-done.37, bf16[896,576]{1,0:T(8,128)(2,1)} %constant_dynamic-update-slice_fusion.4, ...), kind=kOutput, calls=%fused_computation.17 | convolution fusion | flops 532150912 | bytes 6286848 | tf_op jit(solution)/shard_map/tc,dc->td/dot_general | solution.py:929
  344.0 2.0 add_convert_fusion.2
  346.0 2.0 collective-permute-start.39
  350.5 2.2 collective-permute-start.40
  352.7 2.6 collective-permute-done.44
  357.1 2.1 collective-permute-done.41
  359.2 3.1 collective-permute-start.42
  362.4 4.5 %fusion.16 = bf16[512,896]{1,0:T(8,128)(2,1)} fusion(s32[896]{0:T(1024)} %copy-done.57, f32[512,896]{1,0:T(8,128)S(1)} %copy-done.25, f32[512,896]{1,0:T(8,128)} %get-tuple-element.159, f32[512,896]{1,0:T(8,128)} %get-tuple-element.225, f32[512]{0:T(512)S(1)} %fusion.60, f32[896]{0:T(1024)} %copy-done.55, f32[512]{0:T(512)} %copy-done.54), kind=kOutput, calls=%fused_computation.36 | convolution fusion | flops 826097664 | bytes 6433792 | tf_op jit(solution)/shard_map/dot_general | solution.py:773
  367.8 3.3 collective-permute-start.47
  372.3 2.0 collective-permute-done.47
  375.1 1.3 fusion.64
  (327 shorter events, 51.4 us)
Async XLA Ops:
  7.2 367.8 %reduce-scatter.2.cloned.1.call-start = ((), (), s32[]{:S(2)}) async-start(), calls=%async_computation.1 | async-start | bytes 4644864 | tf_op jit(solution)/shard_map/reduce_scatter | solution.py:873
  10.1 17.9 %collective-permute-start.1 = (bf16[128,512]{1,0:T(8,128)(2,1)S(1)}, bf16[128,512]{1,0:T(8,128)(2,1)S(1)}, u32[]{:S(2)}, u32[]{:S(2)}) collective-permute-start(bf16[128,512]{1,0:T(8,128)(2,1)S(1)} %fusion.50), channel_id=1, source_target_pairs={{0,2},{1,0},{2,3},{3,1},{4,6},{5,4},{6,7},{7,5},{8,10},{9,8},{10,1... | collective-permute-start | bytes 393224 | tf_op jit(solution)/shard_map/ppermute | solution.py:694
  13.1 14.9 %collective-permute-start = (bf16[128,512]{1,0:T(8,128)(2,1)S(1)}, bf16[128,512]{1,0:T(8,128)(2,1)S(1)}, u32[]{:S(2)}, u32[]{:S(2)}) collective-permute-start(bf16[128,512]{1,0:T(8,128)(2,1)S(1)} %fusion.50), channel_id=1, source_target_pairs={{0,0},{1,2},{2,1},{3,3},{4,4},{5,6},{6,5},{7,7},{8,8},{9,10},{10,9... | collective-permute-start | bytes 393224 | tf_op jit(solution)/shard_map/ppermute | solution.py:694
  17.3 40.7 %collective-permute-start.9 = (bf16[112,1536]{1,0:T(8,128)(2,1)}, bf16[112,1536]{1,0:T(8,128)(2,1)}, u32[]{:S(2)}, u32[]{:S(2)}) collective-permute-start(bf16[112,1536]{1,0:T(8,128)(2,1)} %pad_maximum_fusion.7.refs_8_), channel_id=1, source_target_pairs={{0,16},{4,20},{8,24},{12,28},{16,0},{20,4},{24,8},{28,12},{1,17},{... | collective-permute-start | bytes 1032200 | tf_op jit(solution)/shard_map/ppermute | solution.py:23
  19.9 36.0 %collective-permute-start.7 = (bf16[112,1536]{1,0:T(8,128)(2,1)}, bf16[112,1536]{1,0:T(8,128)(2,1)}, u32[]{:S(2)}, u32[]{:S(2)}) collective-permute-start(bf16[112,1536]{1,0:T(8,128)(2,1)} %pad_maximum_fusion.7.refs_8_), channel_id=1, source_target_pairs={{0,4},{4,0},{8,12},{12,8},{16,20},{20,16},{24,28},{28,24},{1,5},{5... | collective-permute-start | bytes 1032200 | tf_op jit(solution)/shard_map/ppermute | solution.py:23
  21.7 293.4 %copy-start.57 = (s32[896]{0:T(1024)}, s32[896]{0:T(1024)S(1)}, u32[]{:S(2)}) copy-start(s32[896]{0:T(1024)S(1)} %fusion.53) | copy-start | bytes 10756
  27.9 310.5 %copy-start.55 = (f32[896]{0:T(1024)}, f32[896]{0:T(1024)S(1)}, u32[]{:S(2)}) copy-start(f32[896]{0:T(1024)S(1)} %fusion.17) | copy-start | bytes 10756
  29.0 14.3 %collective-permute-start.4 = (bf16[112,576]{1,0:T(8,128)(2,1)S(1)}, bf16[112,576]{1,0:T(8,128)(2,1)S(1)}, u32[]{:S(2)}, u32[]{:S(2)}) collective-permute-start(bf16[112,576]{1,0:T(8,128)(2,1)S(1)} %get-tuple-element.157.rest_0_), channel_id=1, source_target_pairs={{0,4},{4,0},{8,12},{12,8},{16,20},{20,16},{24,28},{28,24},{1,5},{5... | collective-permute-start | bytes 387080 | tf_op jit(solution)/shard_map/ppermute | solution.py:23
  29.5 13.0 %collective-permute-start.3 = (bf16[112,576]{1,0:T(8,128)(2,1)S(1)}, bf16[112,576]{1,0:T(8,128)(2,1)S(1)}, u32[]{:S(2)}, u32[]{:S(2)}) collective-permute-start(bf16[112,576]{1,0:T(8,128)(2,1)S(1)} %get-tuple-element.157.rest_0_), channel_id=1, source_target_pairs={{0,16},{4,20},{8,24},{12,28},{16,0},{20,4},{24,8},{28,12},{1,17},{... | collective-permute-start | bytes 387080 | tf_op jit(solution)/shard_map/ppermute | solution.py:23
  31.3 307.2 %copy-start.54 = (f32[512]{0:T(512)}, f32[512]{0:T(512)S(1)}, u32[]{:S(2)}) copy-start(f32[512]{0:T(512)S(1)} %add_rsqrt_fusion.1) | copy-start | bytes 6148
  31.5 37.1 %collective-permute-start.2 = (bf16[512,896]{1,0:T(8,128)(2,1)S(1)}, bf16[512,896]{1,0:T(8,128)(2,1)}, u32[]{:S(2)}, u32[]{:S(2)}) collective-permute-start(bf16[512,896]{1,0:T(8,128)(2,1)S(1)} %multiply_convert_fusion.1.own_ref.refs_0_), channel_id=1, source_target_pairs={{0,1},{1,0},{2,3},{3,2},{4,5},{5,4},{6,7},{7,6},{8,9},{9,8},{10,11... | collective-permute-start | bytes 2752520 | tf_op jit(solution)/shard_map/ppermute | solution.py:23
  42.6 8.7 %collective-permute-start.11 = (bf16[112,512]{1,0:T(8,128)(2,1)S(1)}, bf16[112,512]{1,0:T(8,128)(2,1)S(1)}, u32[]{:S(2)}, u32[]{:S(2)}) collective-permute-start(bf16[112,512]{1,0:T(8,128)(2,1)S(1)} %fusion.52.rest_0_), channel_id=1, source_target_pairs={{0,16},{4,20},{8,24},{12,28},{16,0},{20,4},{24,8},{28,12},{1,17},{... | collective-permute-start | bytes 344072 | tf_op jit(solution)/shard_map/ppermute | solution.py:23
  43.3 12.6 %collective-permute-start.5 = (bf16[224,576]{1,0:T(8,128)(2,1)}, bf16[224,576]{1,0:T(8,128)(2,1)S(1)}, u32[]{:S(2)}, u32[]{:S(2)}) collective-permute-start(bf16[224,576]{1,0:T(8,128)(2,1)} %pad_maximum_fusion.9), channel_id=1, source_target_pairs={{0,8},{4,12},{8,0},{12,4},{16,24},{20,28},{24,16},{28,20},{1,9},{5... | collective-permute-start | bytes 774152 | tf_op jit(solution)/shard_map/ppermute | solution.py:23
  48.5 40.1 %copy-start.3 = (f32[1024,128]{1,0:T(8,128)}, f32[1024,128]{1,0:T(8,128)S(1)}, u32[]{:S(2)}) copy-start(f32[1024,128]{1,0:T(8,128)S(1)} %get-tuple-element.226.cos_ref) | copy-start | bytes 1572868
  48.6 40.1 %copy-start.5 = (f32[1024,128]{1,0:T(8,128)}, f32[1024,128]{1,0:T(8,128)S(1)}, u32[]{:S(2)}) copy-start(f32[1024,128]{1,0:T(8,128)S(1)} %get-tuple-element.227.sin_ref) | copy-start | bytes 1572868
  51.2 5.1 %collective-permute-start.6 = (bf16[112,576]{1,0:T(8,128)(2,1)S(1)}, bf16[112,576]{1,0:T(8,128)(2,1)S(1)}, u32[]{:S(2)}, u32[]{:S(2)}) collective-permute-start(bf16[112,576]{1,0:T(8,128)(2,1)S(1)} %collective-permute-done.3.rest_1_), channel_id=1, source_target_pairs={{0,4},{4,0},{8,12},{12,8},{16,20},{20,16},{24,28},{28,24},{1,5},{5... | collective-permute-start | bytes 387080 | tf_op jit(solution)/shard_map/ppermute | solution.py:23
  56.0 32.8 %collective-permute-start.14 = (bf16[512,896]{1,0:T(8,128)(2,1)}, bf16[512,896]{1,0:T(8,128)(2,1)S(1)}, u32[]{:S(2)}, u32[]{:S(2)}) collective-permute-start(bf16[512,896]{1,0:T(8,128)(2,1)} %get-tuple-element.93.refs_4_.refs_2_), channel_id=1, source_target_pairs={{0,2},{1,3},{2,0},{3,1},{4,6},{5,7},{6,4},{7,5},{8,10},{9,11},{10,... | collective-permute-start | bytes 2752520 | tf_op jit(solution)/shard_map/ppermute | solution.py:23
  56.3 32.3 %copy-start.9 = (bf16[112,576]{1,0:T(8,128)(2,1)}, bf16[112,576]{1,0:T(8,128)(2,1)S(1)}, u32[]{:S(2)}) copy-start(bf16[112,576]{1,0:T(8,128)(2,1)S(1)} %collective-permute-done.6.rest_4_) | copy-start | bytes 387076
  56.3 8.5 %collective-permute-start.12 = (bf16[224,512]{1,0:T(8,128)(2,1)S(1)}, bf16[224,512]{1,0:T(8,128)(2,1)S(1)}, u32[]{:S(2)}, u32[]{:S(2)}) collective-permute-start(bf16[224,512]{1,0:T(8,128)(2,1)S(1)} %pad_maximum_fusion.10), channel_id=1, source_target_pairs={{0,8},{4,12},{8,0},{12,4},{16,24},{20,28},{24,16},{28,20},{1,9},{5... | collective-permute-start | bytes 688136 | tf_op jit(solution)/shard_map/ppermute | solution.py:23
  56.5 8.4 %collective-permute-start.8 = (bf16[224,576]{1,0:T(8,128)(2,1)S(1)}, bf16[224,576]{1,0:T(8,128)(2,1)S(1)}, u32[]{:S(2)}, u32[]{:S(2)}) collective-permute-start(bf16[224,576]{1,0:T(8,128)(2,1)S(1)} %collective-permute-done.5.rest_2_), channel_id=1, source_target_pairs={{0,4},{4,0},{8,12},{12,8},{16,20},{20,16},{24,28},{28,24},{1,5},{5... | collective-permute-start | bytes 774152 | tf_op jit(solution)/shard_map/ppermute | solution.py:23
  59.2 29.5 %collective-permute-start.15 = (bf16[112,2304]{1,0:T(8,128)(2,1)}, bf16[112,2304]{1,0:T(8,128)(2,1)S(1)}, u32[]{:S(2)}, u32[]{:S(2)}) collective-permute-start(bf16[112,2304]{1,0:T(8,128)(2,1)} %fusion.34.refs_4_), channel_id=1, source_target_pairs={{0,16},{4,20},{8,24},{12,28},{16,0},{20,4},{24,8},{28,12},{1,17},{... | collective-permute-start | bytes 1548296 | tf_op jit(solution)/shard_map/ppermute | solution.py:23
  64.9 204.4 %copy-start.7 = (bf16[224,512]{1,0:T(8,128)(2,1)}, bf16[224,512]{1,0:T(8,128)(2,1)S(1)}, u32[]{:S(2)}) copy-start(bf16[224,512]{1,0:T(8,128)(2,1)S(1)} %collective-permute-done.12.rest_2_) | copy-start | bytes 688132
  64.9 23.9 %collective-permute-start.13 = (bf16[224,1536]{1,0:T(8,128)(2,1)S(1)}, bf16[224,1536]{1,0:T(8,128)(2,1)S(1)}, u32[]{:S(2)}, u32[]{:S(2)}) collective-permute-start(bf16[224,1536]{1,0:T(8,128)(2,1)S(1)} %pad_maximum_fusion), channel_id=1, source_target_pairs={{0,8},{4,12},{8,0},{12,4},{16,24},{20,28},{24,16},{28,20},{1,9},{5... | collective-permute-start | bytes 2064392 | tf_op jit(solution)/shard_map/ppermute | solution.py:23
  64.9 23.8 %collective-permute-start.10 = (bf16[112,1536]{1,0:T(8,128)(2,1)}, bf16[112,1536]{1,0:T(8,128)(2,1)S(1)}, u32[]{:S(2)}, u32[]{:S(2)}) collective-permute-start(bf16[112,1536]{1,0:T(8,128)(2,1)} %collective-permute-done.9.refs_9_), channel_id=1, source_target_pairs={{0,4},{4,0},{8,12},{12,8},{16,20},{20,16},{24,28},{28,24},{1,5},{5... | collective-permute-start | bytes 1032200 | tf_op jit(solution)/shard_map/ppermute | solution.py:23
  68.6 20.2 %collective-permute-start.16 = (bf16[448,512]{1,0:T(8,128)(2,1)S(1)}, bf16[448,512]{1,0:T(8,128)(2,1)S(1)}, u32[]{:S(2)}, u32[]{:S(2)}) collective-permute-start(bf16[448,512]{1,0:T(8,128)(2,1)S(1)} %pad_maximum_fusion.6), channel_id=1, source_target_pairs={{0,4},{4,0},{8,12},{12,8},{16,20},{20,16},{24,28},{28,24},{1,5},{5... | collective-permute-start | bytes 1376264 | tf_op jit(solution)/shard_map/ppermute | solution.py:23
  88.7 29.3 %copy-start.45 = (bf16[112,2304]{1,0:T(8,128)(2,1)}, bf16[112,2304]{1,0:T(8,128)(2,1)S(1)}, u32[]{:S(2)}) copy-start(bf16[112,2304]{1,0:T(8,128)(2,1)S(1)} %collective-permute-done.15.refs_5_) | copy-start | bytes 1548292
  91.0 2.5 collective-permute-start.17
  95.5 22.5 %collective-permute-start.18 = (bf16[512,896]{1,0:T(8,128)(2,1)S(1)}, bf16[512,896]{1,0:T(8,128)(2,1)S(1)}, u32[]{:S(2)}, u32[]{:S(2)}) collective-permute-start(bf16[512,896]{1,0:T(8,128)(2,1)S(1)} %multiply_convert_fusion.refs_0_), channel_id=1, source_target_pairs={{0,2},{1,3},{2,0},{3,1},{4,6},{5,7},{6,4},{7,5},{8,10},{9,11},{10,... | collective-permute-start | bytes 2752520 | tf_op jit(solution)/shard_map/ppermute | solution.py:23
  97.3 17.5 %collective-permute-start.19 = (bf16[224,1536]{1,0:T(8,128)(2,1)S(1)}, bf16[224,1536]{1,0:T(8,128)(2,1)}, u32[]{:S(2)}, u32[]{:S(2)}) collective-permute-start(bf16[224,1536]{1,0:T(8,128)(2,1)S(1)} %collective-permute-done.13.refs_10_), channel_id=1, source_target_pairs={{0,4},{4,0},{8,12},{12,8},{16,20},{20,16},{24,28},{28,24},{1,5},{5... | collective-permute-start | bytes 2064392 | tf_op jit(solution)/shard_map/ppermute | solution.py:23
  114.8 5.3 %collective-permute-start.20 = (bf16[512,896]{1,0:T(8,128)(2,1)S(1)}, bf16[512,896]{1,0:T(8,128)(2,1)S(1)}, u32[]{:S(2)}, u32[]{:S(2)}) collective-permute-start(bf16[512,896]{1,0:T(8,128)(2,1)S(1)} %multiply_convert_fusion.refs_0_), channel_id=1, source_target_pairs={{0,1},{1,0},{2,3},{3,2},{4,5},{5,4},{6,7},{7,6},{8,9},{9,8},{10,11... | collective-permute-start | bytes 2752520 | tf_op jit(solution)/shard_map/ppermute | solution.py:23
  114.8 7.3 %collective-permute-start.22 = (bf16[512,896]{1,0:T(8,128)(2,1)S(1)}, bf16[512,896]{1,0:T(8,128)(2,1)S(1)}, u32[]{:S(2)}, u32[]{:S(2)}) collective-permute-start(bf16[512,896]{1,0:T(8,128)(2,1)S(1)} %copy-done.63), channel_id=1, source_target_pairs={{0,1},{1,0},{2,3},{3,2},{4,5},{5,4},{6,7},{7,6},{8,9},{9,8},{10,11... | collective-permute-start | bytes 2752520 | tf_op jit(solution)/shard_map/ppermute | solution.py:23
  115.3 6.8 %collective-permute-start.23 = (bf16[512,896]{1,0:T(8,128)(2,1)S(1)}, bf16[512,896]{1,0:T(8,128)(2,1)S(1)}, u32[]{:S(2)}, u32[]{:S(2)}) collective-permute-start(bf16[512,896]{1,0:T(8,128)(2,1)S(1)} %collective-permute-done.14.refs_6_.refs_2_), channel_id=1, source_target_pairs={{0,1},{1,0},{2,3},{3,2},{4,5},{5,4},{6,7},{7,6},{8,9},{9,8},{10,11... | collective-permute-start | bytes 2752520 | tf_op jit(solution)/shard_map/ppermute | solution.py:23
  117.9 6.0 %collective-permute-start.21 = (bf16[512,896]{1,0:T(8,128)(2,1)S(1)}, bf16[512,896]{1,0:T(8,128)(2,1)}, u32[]{:S(2)}, u32[]{:S(2)}) collective-permute-start(bf16[512,896]{1,0:T(8,128)(2,1)S(1)} %collective-permute-done.18.refs_2_.refs_0_), channel_id=1, source_target_pairs={{0,1},{1,0},{2,3},{3,2},{4,5},{5,4},{6,7},{7,6},{8,9},{9,8},{10,11... | collective-permute-start | bytes 2752520 | tf_op jit(solution)/shard_map/ppermute | solution.py:23
  118.0 30.6 %collective-permute-start.25 = (bf16[224,2304]{1,0:T(8,128)(2,1)S(1)}, bf16[224,2304]{1,0:T(8,128)(2,1)S(1)}, u32[]{:S(2)}, u32[]{:S(2)}) collective-permute-start(bf16[224,2304]{1,0:T(8,128)(2,1)S(1)} %constant_dynamic-update-slice_fusion), channel_id=1, source_target_pairs={{0,4},{4,0},{8,12},{12,8},{16,20},{20,16},{24,28},{28,24},{1,5},{5... | collective-permute-start | bytes 3096584 | tf_op jit(solution)/shard_map/ppermute | solution.py:23
  120.0 28.6 %collective-permute-start.24 = (bf16[224,2304]{1,0:T(8,128)(2,1)S(1)}, bf16[224,2304]{1,0:T(8,128)(2,1)}, u32[]{:S(2)}, u32[]{:S(2)}) collective-permute-start(bf16[224,2304]{1,0:T(8,128)(2,1)S(1)} %constant_dynamic-update-slice_fusion), channel_id=1, source_target_pairs={{0,8},{4,12},{8,0},{12,4},{16,24},{20,28},{24,16},{28,20},{1,9},{5... | collective-permute-start | bytes 3096584 | tf_op jit(solution)/shard_map/ppermute | solution.py:23
  148.7 26.0 %collective-permute-start.26 = (bf16[224,2304]{1,0:T(8,128)(2,1)}, bf16[224,2304]{1,0:T(8,128)(2,1)S(1)}, u32[]{:S(2)}, u32[]{:S(2)}) collective-permute-start(bf16[224,2304]{1,0:T(8,128)(2,1)} %collective-permute-done.24.refs_6_), channel_id=1, source_target_pairs={{0,4},{4,0},{8,12},{12,8},{16,20},{20,16},{24,28},{28,24},{1,5},{5... | collective-permute-start | bytes 3096584 | tf_op jit(solution)/shard_map/ppermute | solution.py:23
  164.4 31.5 %collective-permute-start.28 = (bf16[448,512]{1,0:T(8,128)(2,1)}, bf16[448,512]{1,0:T(8,128)(2,1)}, u32[]{:S(2)}, u32[]{:S(2)}) collective-permute-start(bf16[448,512]{1,0:T(8,128)(2,1)} %get-tuple-element.106), channel_id=1, source_target_pairs={{0,8},{4,12},{8,0},{12,4},{16,24},{20,28},{24,16},{28,20},{1,9},{5... | collective-permute-start | bytes 1376264 | tf_op jit(solution)/shard_map/ppermute | solution.py:23
  165.3 30.6 %collective-permute-start.27 = (bf16[448,1024]{1,0:T(8,128)(2,1)}, bf16[448,1024]{1,0:T(8,128)(2,1)}, u32[]{:S(2)}, u32[]{:S(2)}) collective-permute-start(bf16[448,1024]{1,0:T(8,128)(2,1)} %get-tuple-element.105), channel_id=1, source_target_pairs={{0,4},{4,0},{8,12},{12,8},{16,20},{20,16},{24,28},{28,24},{1,5},{5... | collective-permute-start | bytes 2752520 | tf_op jit(solution)/shard_map/ppermute | solution.py:23
  195.9 6.2 %collective-permute-start.29 = (bf16[2,512,896]{2,1,0:T(8,128)(2,1)}, bf16[2,512,896]{2,1,0:T(8,128)(2,1)}, u32[]{:S(2)}, u32[]{:S(2)}) collective-permute-start(bf16[2,512,896]{2,1,0:T(8,128)(2,1)} %get-tuple-element.107), channel_id=1, source_target_pairs={{0,1},{1,0},{2,3},{3,2},{4,5},{5,4},{6,7},{7,6},{8,9},{9,8},{10,11... | collective-permute-start | bytes 5505032 | tf_op jit(solution)/shard_map/ppermute | solution.py:23
  198.7 28.2 %collective-permute-start.32 = (bf16[224,512]{1,0:T(8,128)(2,1)S(1)}, bf16[224,512]{1,0:T(8,128)(2,1)S(1)}, u32[]{:S(2)}, u32[]{:S(2)}) collective-permute-start(bf16[224,512]{1,0:T(8,128)(2,1)S(1)} %get-tuple-element.171), channel_id=1, source_target_pairs={{0,4},{4,0},{8,12},{12,8},{16,20},{20,16},{24,28},{28,24},{1,5},{5... | collective-permute-start | bytes 688136 | tf_op jit(solution)/shard_map/ppermute | solution.py:23
  201.2 25.7 %collective-permute-start.31 = (bf16[224,1024]{1,0:T(8,128)(2,1)}, bf16[224,1024]{1,0:T(8,128)(2,1)}, u32[]{:S(2)}, u32[]{:S(2)}) collective-permute-start(bf16[224,1024]{1,0:T(8,128)(2,1)} %get-tuple-element.163), channel_id=1, source_target_pairs={{0,8},{4,12},{8,0},{12,4},{16,24},{20,28},{24,16},{28,20},{1,9},{5... | collective-permute-start | bytes 1376264 | tf_op jit(solution)/shard_map/ppermute | solution.py:23
  205.2 22.1 %collective-permute-start.30 = (bf16[512,896]{1,0:T(8,128)(2,1)S(1)}, bf16[512,896]{1,0:T(8,128)(2,1)S(1)}, u32[]{:S(2)}, u32[]{:S(2)}) collective-permute-start(bf16[512,896]{1,0:T(8,128)(2,1)S(1)} %get-tuple-element.164), channel_id=1, source_target_pairs={{0,2},{1,3},{2,0},{3,1},{4,6},{5,7},{6,4},{7,5},{8,10},{9,11},{10,... | collective-permute-start | bytes 2752520 | tf_op jit(solution)/shard_map/ppermute | solution.py:23
  227.3 25.3 %collective-permute-start.33 = (bf16[2,512,896]{2,1,0:T(8,128)(2,1)}, bf16[2,512,896]{2,1,0:T(8,128)(2,1)}, u32[]{:S(2)}, u32[]{:S(2)}) collective-permute-start(bf16[2,512,896]{2,1,0:T(8,128)(2,1)} %get-tuple-element.114), channel_id=1, source_target_pairs={{0,1},{1,0},{2,3},{3,2},{4,5},{5,4},{6,7},{7,6},{8,9},{9,8},{10,11... | collective-permute-start | bytes 5505032 | tf_op jit(solution)/shard_map/ppermute | solution.py:23
  232.9 78.3 %collective-permute-start.52 = (bf16[112,1536]{1,0:T(8,128)(2,1)}, bf16[112,1536]{1,0:T(8,128)(2,1)}, u32[]{:S(2)}, u32[]{:S(2)}) collective-permute-start(bf16[112,1536]{1,0:T(8,128)(2,1)} %pad_maximum_fusion.8), channel_id=1, source_target_pairs={{0,16},{4,20},{8,24},{12,28},{16,0},{20,4},{24,8},{28,12},{1,17},{... | collective-permute-start | bytes 1032200 | tf_op jit(solution)/shard_map/ppermute | solution.py:23
  251.4 59.8 %collective-permute-start.34 = (bf16[512,896]{1,0:T(8,128)(2,1)}, bf16[512,896]{1,0:T(8,128)(2,1)}, u32[]{:S(2)}, u32[]{:S(2)}) collective-permute-start(bf16[512,896]{1,0:T(8,128)(2,1)} %get-tuple-element.115), channel_id=1, source_target_pairs={{0,2},{1,3},{2,0},{3,1},{4,6},{5,7},{6,4},{7,5},{8,10},{9,11},{10,... | collective-permute-start | bytes 2752520 | tf_op jit(solution)/shard_map/ppermute | solution.py:23
  260.7 2.5 collective-permute-start.35
  261.2 82.6 %copy-start.50 = (f32[896]{0:T(1024)}, f32[896]{0:T(1024)S(1)}, u32[]{:S(2)}) copy-start(f32[896]{0:T(1024)S(1)} %select_select_fusion) | copy-start | bytes 10756
  268.2 21.8 %collective-permute-start.36 = (bf16[448,512]{1,0:T(8,128)(2,1)S(1)}, bf16[448,512]{1,0:T(8,128)(2,1)S(1)}, u32[]{:S(2)}, u32[]{:S(2)}) collective-permute-start(bf16[448,512]{1,0:T(8,128)(2,1)S(1)} %get-tuple-element.126), channel_id=1, source_target_pairs={{0,4},{4,0},{8,12},{12,8},{16,20},{20,16},{24,28},{28,24},{1,5},{5... | collective-permute-start | bytes 1376264 | tf_op jit(solution)/shard_map/ppermute | solution.py:23
  290.2 28.9 %copy-start.29 = (f32[224,512]{1,0:T(8,128)}, f32[224,512]{1,0:T(8,128)S(1)}, u32[]{:S(2)}) copy-start(f32[224,512]{1,0:T(8,128)S(1)} %get-tuple-element.173) | copy-start | bytes 1376260
  290.2 28.8 %collective-permute-start.48 = (bf16[224,512]{1,0:T(8,128)(2,1)S(1)}, bf16[224,512]{1,0:T(8,128)(2,1)S(1)}, u32[]{:S(2)}, u32[]{:S(2)}) collective-permute-start(bf16[224,512]{1,0:T(8,128)(2,1)S(1)} %get-tuple-element.172), channel_id=1, source_target_pairs={{0,8},{4,12},{8,0},{12,4},{16,24},{20,28},{24,16},{28,20},{1,9},{5... | collective-permute-start | bytes 688136 | tf_op jit(solution)/shard_map/ppermute | solution.py:23
  311.3 32.7 %collective-permute-start.43 = (bf16[448,576]{1,0:T(8,128)(2,1)}, bf16[448,576]{1,0:T(8,128)(2,1)}, u32[]{:S(2)}, u32[]{:S(2)}) collective-permute-start(bf16[448,576]{1,0:T(8,128)(2,1)} %get-tuple-element.137), channel_id=1, source_target_pairs={{0,4},{4,0},{8,12},{12,8},{16,20},{20,16},{24,28},{28,24},{1,5},{5... | collective-permute-start | bytes 1548296 | tf_op jit(solution)/shard_map/ppermute | solution.py:23
  314.0 24.5 %collective-permute-start.37 = (bf16[512,896]{1,0:T(8,128)(2,1)}, bf16[512,896]{1,0:T(8,128)(2,1)S(1)}, u32[]{:S(2)}, u32[]{:S(2)}) collective-permute-start(bf16[512,896]{1,0:T(8,128)(2,1)} %convolution_convert_fusion), channel_id=1, source_target_pairs={{0,1},{1,0},{2,3},{3,2},{4,5},{5,4},{6,7},{7,6},{8,9},{9,8},{10,11... | collective-permute-start | bytes 2752520 | tf_op jit(solution)/shard_map/ppermute | solution.py:23
  319.1 15.4 %collective-permute-start.49 = (bf16[112,512]{1,0:T(8,128)(2,1)S(1)}, bf16[112,512]{1,0:T(8,128)(2,1)}, u32[]{:S(2)}, u32[]{:S(2)}) collective-permute-start(bf16[112,512]{1,0:T(8,128)(2,1)S(1)} %fusion.44), channel_id=1, source_target_pairs={{0,16},{4,20},{8,24},{12,28},{16,0},{20,4},{24,8},{28,12},{1,17},{... | collective-permute-start | bytes 344072 | tf_op jit(solution)/shard_map/ppermute | solution.py:23
  336.3 11.7 %collective-permute-start.50 = (bf16[112,224]{1,0:T(8,128)(2,1)}, bf16[112,224]{1,0:T(8,128)(2,1)}, u32[]{:S(2)}, u32[]{:S(2)}) collective-permute-start(bf16[112,224]{1,0:T(8,128)(2,1)} %get-tuple-element.186), channel_id=1, source_target_pairs={{0,0},{1,2},{2,1},{3,3},{4,4},{5,6},{6,5},{7,7},{8,8},{9,10},{10,9... | collective-permute-start | bytes 150536 | tf_op jit(solution)/shard_map/ppermute | solution.py:700
  338.4 9.7 %collective-permute-start.51 = (bf16[112,224]{1,0:T(8,128)(2,1)}, bf16[112,224]{1,0:T(8,128)(2,1)}, u32[]{:S(2)}, u32[]{:S(2)}) collective-permute-start(bf16[112,224]{1,0:T(8,128)(2,1)} %get-tuple-element.187), channel_id=1, source_target_pairs={{0,1},{1,3},{2,0},{3,2},{4,5},{5,7},{6,4},{7,6},{8,9},{9,11},{10,8... | collective-permute-start | bytes 150536 | tf_op jit(solution)/shard_map/ppermute | solution.py:700
  343.9 2.1 collective-permute-start.38
  346.0 9.4 %collective-permute-start.44 = (bf16[224,576]{1,0:T(8,128)(2,1)}, bf16[224,576]{1,0:T(8,128)(2,1)S(1)}, u32[]{:S(2)}, u32[]{:S(2)}) collective-permute-start(bf16[224,576]{1,0:T(8,128)(2,1)} %get-tuple-element.166), channel_id=1, source_target_pairs={{0,8},{4,12},{8,0},{12,4},{16,24},{20,28},{24,16},{28,20},{1,9},{5... | collective-permute-start | bytes 774152 | tf_op jit(solution)/shard_map/ppermute | solution.py:23
  346.0 3.8 collective-permute-start.39
  350.5 4.9 %collective-permute-start.40 = (f32[23,128]{1,0:T(8,128)S(1)}, f32[23,128]{1,0:T(8,128)S(1)}, u32[]{:S(2)}, u32[]{:S(2)}) collective-permute-start(f32[23,128]{1,0:T(8,128)S(1)} %fusion.78), channel_id=1, source_target_pairs={{0,4},{4,0},{8,12},{12,8},{16,20},{20,16},{24,28},{28,24},{1,5},{5... | collective-permute-start | bytes 35336 | tf_op jit(solution)/shard_map/ppermute | solution.py:23
  355.4 11.6 %collective-permute-start.45 = (bf16[112,576]{1,0:T(8,128)(2,1)S(1)}, bf16[112,576]{1,0:T(8,128)(2,1)S(1)}, u32[]{:S(2)}, u32[]{:S(2)}) collective-permute-start(bf16[112,576]{1,0:T(8,128)(2,1)S(1)} %fusion.36), channel_id=1, source_target_pairs={{0,16},{4,20},{8,24},{12,28},{16,0},{20,4},{24,8},{28,12},{1,17},{... | collective-permute-start | bytes 387080 | tf_op jit(solution)/shard_map/ppermute | solution.py:23
  355.5 3.8 collective-permute-start.41
  359.2 7.6 %collective-permute-start.42 = (f32[23,128]{1,0:T(8,128)S(1)}, f32[23,128]{1,0:T(8,128)S(1)}, u32[]{:S(2)}, u32[]{:S(2)}) collective-permute-start(f32[23,128]{1,0:T(8,128)S(1)} %add.233), channel_id=1, source_target_pairs={{0,16},{4,20},{8,24},{12,28},{16,0},{20,4},{24,8},{28,12},{1,17},{... | collective-permute-start | bytes 35336 | tf_op jit(solution)/shard_map/ppermute | solution.py:23
  367.1 5.2 %collective-permute-start.46 = (bf16[112,288]{1,0:T(8,128)(2,1)S(1)}, bf16[112,288]{1,0:T(8,128)(2,1)S(1)}, u32[]{:S(2)}, u32[]{:S(2)}) collective-permute-start(bf16[112,288]{1,0:T(8,128)(2,1)S(1)} %get-tuple-element.184), channel_id=1, source_target_pairs={{0,0},{1,2},{2,1},{3,3},{4,4},{5,6},{6,5},{7,7},{8,8},{9,10},{10,9... | collective-permute-start | bytes 193544 | tf_op jit(solution)/shard_map/ppermute | solution.py:700
  367.8 6.5 %collective-permute-start.47 = (bf16[112,288]{1,0:T(8,128)(2,1)S(1)}, bf16[112,288]{1,0:T(8,128)(2,1)S(1)}, u32[]{:S(2)}, u32[]{:S(2)}) collective-permute-start(bf16[112,288]{1,0:T(8,128)(2,1)S(1)} %get-tuple-element.185), channel_id=1, source_target_pairs={{0,1},{1,3},{2,0},{3,2},{4,5},{5,7},{6,4},{7,6},{8,9},{9,11},{10,8... | collective-permute-start | bytes 193544 | tf_op jit(solution)/shard_map/ppermute | solution.py:700
  (64 other events, 429.8 us)
Sparse Core Ops, SparseCore 0:
  251.6 94.2 reduce-scatter.1

commit v10 on v9

--- a/solution.py
+++ b/solution.py
@@ -923,7 +923,6 @@
     layer_output = unstored((middle + summed(1, after(down_back, passed))).astype(bf16))
     qkv_full = jnp.concatenate(qkv_pieces, 0)
     grad_mixed = after(grad_mixed, passed)
-    out_scatter.step()
 
     def back_to_normed(rows):
         return jnp.einsum("tc,dc->td", rows, qkv_full, preferred_element_type=f32)
@@ -941,13 +940,6 @@
     )
     gain_one_grad = jnp.sum(grad_normed_one * input_rows * scale_one[:, None], axis=0)
 
-    def to_columns(total, width):
-        low, high = total[:, :width].astype(bf16), total[:, width : 2 * width].astype(bf16)
-        first, second = from_pairs(
-            jnp.where(sequence == 0, low, high), jnp.where(sequence == 0, high, low)
-        )
-        return first.astype(f32) + second.astype(f32)
-
     bias_row = lax.dynamic_update_slice_in_dim(
         jnp.zeros((group_width * 2,), f32), bias_grad, core * group_width, 0
     )
@@ -958,10 +950,20 @@
     for bit in range(bits):
         small = small + flip(small, "row", bit)
     qkv_scatter.step()
+    qkv_scatter.kept = [jnp.concatenate([qkv_scatter.kept[0], out_scatter.kept[0]], 1)]
+    qkv_scatter.got = [jnp.concatenate([qkv_scatter.got[0], out_scatter.got[0]], 1)]
     qkv_scatter.step()
     qkv_scatter.wait(small)
-    qkv_total = to_columns(qkv_scatter.total(), qkv_cols)
-    out_total = to_columns(out_scatter.total(), out_cols)
+    total = qkv_scatter.total().astype(bf16)
+    ends = (0, qkv_cols, group_width, group_width + out_cols, group_width + 2 * out_cols)
+    parts = [total[:, start:stop] for start, stop in zip(ends, ends[1:])]
+    low = jnp.concatenate([parts[0], parts[2]], 1)
+    high = jnp.concatenate([parts[1], parts[3]], 1)
+    first, second = from_pairs(
+        jnp.where(sequence == 0, low, high), jnp.where(sequence == 0, high, low)
+    )
+    both_totals = first.astype(f32) + second.astype(f32)
+    qkv_total, out_total = both_totals[:, :qkv_cols], both_totals[:, qkv_cols:]
     mlp_totals = []
     for total, (start, stop) in zip(
         (first_total, after(second_total, small).astype(f32)), cuts(ff_cols)

time: 393 us -> 392 us (level)
  waiting for transfers between devices: 70.1 us -> 78.1 us
    ppermute x47 -> x46, waiting for transfers between devices: 68.1 us -> 74.7 us  [flip(): return lax.ppermute(block, axis, [(i, i ^ 1 << bit) for i in range(count)])]
    ppermute x47 -> x46, starting transfers between devices: 49.2 us -> 48.8 us  [flip(): return lax.ppermute(block, axis, [(i, i ^ 1 << bit) for i in range(count)])]
    unnamed x156 -> x132, local copies, waits for them, and re-layouts: 17.3 us -> 17.2 us
  transfers between devices with their start and end apart: 54 -> 51, of which waited for: 16 -> 17; matrix products, arithmetic and copies ran while one was open for 17% -> 16% of each run, Pallas kernels for 40% -> 40%
where the time goes in v10:
time: 392 us; the launch traced here: 385 us
  Pallas kernels  157 us (40%)
  waiting for transfers between devices  78.1 us (20%)
  starting transfers between devices  56 us (14%)
  other arithmetic  32.2 us (8%)
  local copies, waits for them, and re-layouts  27.5 us (7%)
  matrix products  18.3 us (5%)
  between operations  15.8 us (4%)
    ppermute x46, waiting for transfers between devices, flip(): return lax.ppermute(block, axis, [(i, i ^ 1 << bit) for i in range(count)])  74.7 us
    pallas_call x3, Pallas kernels, mlp(): pl.pallas_call(functools.partial(mlp_kernel, blocks=blocks, count=len(pie...  65.1 us
    ppermute x46, starting transfers between devices, flip(): return lax.ppermute(block, axis, [(i, i ^ 1 << bit) for i in range(count)])  48.8 us
    pallas_call x2, Pallas kernels, attend_back(): pl.pallas_call(functools.partial(attend_back_kernel, block=block, count=l...  32.9 us
    pallas_call x1, Pallas kernels, attend(): pl.pallas_call(functools.partial(attend_kernel, block=block, count=len(pi...  19.9 us
    unnamed x132, local copies, waits for them, and re-layouts  17.2 us
    pallas_call x1, Pallas kernels, outer(): pl.pallas_call(functools.partial(outer_kernel, blocks=len(rows)), grid=(3...  15.6 us
    pallas_call x1, Pallas kernels, outer_whole(): pl.pallas_call(functools.partial(outer_whole_kernel, blocks=len(rows), co...  15.5 us
  transfers between devices with their start and end apart: 51, of which 17 were waited for; matrix products, arithmetic and copies ran while one was open for 16% of the time, Pallas kernels for 40%

profile of v10, /device:TPU:0, one launch (start us, length us, event | category | flops | bytes accessed | tf_op | source)
XLA Modules:
  0.0 384.6 jit_solution(11246881784216133652)
XLA Ops:
  10.1 3.0 collective-permute-start.1
  17.3 2.6 collective-permute-start.9
  19.9 1.5 collective-permute-start.7
  21.7 2.0 fusion.50
  23.7 2.8 bitcast_convert_fusion
  29.9 1.3 multiply_reduce_fusion.5
  31.9 10.7 %collective-permute-done.3.rest_1_ = bf16[112,576]{1,0:T(8,128)(2,1)S(1)} collective-permute-done((bf16[112,576]{1,0:T(8,128)(2,1)S(1)}, bf16[112,576]{1,0:T(8,128)(2,1)S(1)}, u32[]{:S(2)}, u32[]{:S(2)}) %collective-permute-start.3) | collective-permute-done | bytes 129056 | tf_op jit(solution)/shard_map/ppermute | solution.py:23
  43.3 4.3 %collective-permute-start.5 = (bf16[224,576]{1,0:T(8,128)(2,1)}, bf16[224,576]{1,0:T(8,128)(2,1)S(1)}, u32[]{:S(2)}, u32[]{:S(2)}) collective-permute-start(bf16[224,576]{1,0:T(8,128)(2,1)} %pad_maximum_fusion.10), channel_id=1, source_target_pairs={{0,8},{4,12},{8,0},{12,4},{16,24},{20,28},{24,16},{28,20},{1,9},{5... | collective-permute-start | bytes 774152 | tf_op jit(solution)/shard_map/ppermute | solution.py:23
  48.6 2.7 collective-permute-done.11.rest_1_
  51.2 1.5 collective-permute-start.6
  53.5 2.4 collective-permute-done.5.rest_2_
  56.5 1.5 collective-permute-start.8
  59.2 2.7 collective-permute-start.15
  61.9 2.9 collective-permute-done.12.rest_2_
  64.9 3.7 collective-permute-start.10
  68.7 19.9 %shard_map.186 = (bf16[1024,512]{1,0:T(8,128)(2,1)S(1)}, bf16[1024,64]{1,0:T(8,128)(2,1)S(1)}, bf16[1024,512]{1,0:T(8,128)(2,1)S(1)}, f32[8,1024]{1,0:T(8,128)S(1)}) custom-call(s32[1]{0:T(128)} %bitcast.1.parity_ref, bf16[512,896]{1,0:T(8,128)(2,1)S(1)} %multiply_convert_fusion.1.own_ref.refs_0_, bf16[512,896]{1,0:T(8,128)(2,1)} %collective-permute-done.2.other_ref.refs_1_, ...), custom_call_target="tpu_custom_call" | custom-call | flops 12000000000 | bytes 8000000 | tf_op jit(solution)/shard_map/pallas_call | solution.py:159
  88.8 2.2 shard_map.187
  91.7 1.8 collective-permute-done.17
  94.0 1.2 copy-done.20
  95.4 1.8 collective-permute-start.18
  97.2 1.9 collective-permute-start.19
  99.2 15.6 %collective-permute-done.19.refs_13_ = bf16[224,1536]{1,0:T(8,128)(2,1)} collective-permute-done((bf16[224,1536]{1,0:T(8,128)(2,1)S(1)}, bf16[224,1536]{1,0:T(8,128)(2,1)}, u32[]{:S(2)}, u32[]{:S(2)}) %collective-permute-start.19) | collective-permute-done | bytes 688160 | tf_op jit(solution)/shard_map/ppermute | solution.py:23
  115.3 2.6 collective-permute-done.18.refs_2_.refs_0_
  118.0 2.0 collective-permute-start.25
  120.0 2.0 collective-permute-start.24
  123.9 24.4 %shard_map.188 = (bf16[2048,1536]{1,0:T(8,128)(2,1)}, bf16[2,512,896]{2,1,0:T(8,128)(2,1)}, bf16[2,512,896]{2,1,0:T(8,128)(2,1)}, bf16[2,512,896]{2,1,0:T(8,128)(2,1)}, bf16[2,512,896]{2,1,0:T(8,128)(2,1)}) custom-call(bf16[512,896]{1,0:T(8,128)(2,1)} %copy-done.39, bf16[512,896]{1,0:T(8,128)(2,1)} %copy-done.54, bf16[512,896]{1,0:T(8,128)(2,1)} %copy-done.53, ...), custom_call_target="tpu_custom_call" | custom-call | flops 16911433728 | bytes 62914560 | tf_op jit(solution)/shard_map/pallas_call | solution.py:439
  148.6 15.6 %shard_map.189 = (bf16[448,1024]{1,0:T(8,128)(2,1)}, f32[448,1024]{1,0:T(8,128)}, bf16[448,512]{1,0:T(8,128)(2,1)}, f32[448,512]{1,0:T(8,128)}) custom-call(bf16[512,896]{1,0:T(8,128)(2,1)} %copy-done.39, bf16[512,896]{1,0:T(8,128)(2,1)} %copy-done.54, bf16[512,896]{1,0:T(8,128)(2,1)} %copy-done.53, ...), custom_call_target="tpu_custom_call" | custom-call | flops 5637144576 | bytes 20971520 | tf_op jit(solution)/shard_map/pallas_call | solution.py:500
  165.1 1.2 collective-permute-start.27
  166.3 8.1 %collective-permute-done.26.refs_8_ = bf16[224,2304]{1,0:T(8,128)(2,1)S(1)} collective-permute-done((bf16[224,2304]{1,0:T(8,128)(2,1)}, bf16[224,2304]{1,0:T(8,128)(2,1)S(1)}, u32[]{:S(2)}, u32[]{:S(2)}) %collective-permute-start.26) | collective-permute-done | bytes 1032224 | tf_op jit(solution)/shard_map/ppermute | solution.py:23
  175.4 20.4 %shard_map.190 = (bf16[1024,2304]{1,0:T(8,128)(2,1)}, bf16[2,512,896]{2,1,0:T(8,128)(2,1)}, bf16[2,512,896]{2,1,0:T(8,128)(2,1)}) custom-call(bf16[512,896]{1,0:T(8,128)(2,1)} %copy-done.53, bf16[512,896]{1,0:T(8,128)(2,1)} %collective-permute-done.21.refs_3_.refs_1_, bf16[512,896]{1,0:T(8,128)(2,1)} %copy-done.52, bf16[512,896]{1,0:T(8,128)(2,1)} %copy-done.56, ...), custom_call_target="tpu_custom_call" | custom-call | flops 12683575296 | bytes 31457280 | tf_op jit(solution)/shard_map/pallas_call | solution.py:439
  197.3 1.2 convert_add_fusion.6
  198.7 2.4 convert_add_fusion.2
  202.0 2.0 add_convert_fusion
  205.0 1.3 collective-permute-start.30
  206.3 20.3 %shard_map.191 = (bf16[1024,2304]{1,0:T(8,128)(2,1)}, bf16[2,512,896]{2,1,0:T(8,128)(2,1)}, bf16[2,512,896]{2,1,0:T(8,128)(2,1)}) custom-call(bf16[512,896]{1,0:T(8,128)(2,1)} %copy-done.39, bf16[512,896]{1,0:T(8,128)(2,1)} %copy-done.54, bf16[512,896]{1,0:T(8,128)(2,1)} %get-tuple-element.93.refs_4_.refs_2_, bf16[512,896]{1,0:T(8,128)(2,1)} %copy-done.55, ...), custom_call_target="tpu_custom_call" | custom-call | flops 12683575296 | bytes 31457280 | tf_op jit(solution)/shard_map/pallas_call | solution.py:439
  230.1 1.9 slice_add_fusion.1
  232.8 3.0 collective-permute-start.49
  235.8 15.5 %shard_map.192 = bf16[896,2304]{1,0:T(8,128)(2,1)} custom-call(s32[1]{0:T(128)} %bitcast.8.row_ref, bf16[512,896]{1,0:T(8,128)(2,1)} %copy-done.39, bf16[512,896]{1,0:T(8,128)(2,1)} %copy-done.54, bf16[512,896]{1,0:T(8,128)(2,1)} %copy-done.53, bf16[512,896]{1,0:T(8,128)(2,1)} %collective-permute-done.21.refs_3_.refs_1_, ...), custom_call_target="tpu_custom_call" | custom-call | flops 8455716864 | bytes 20971520 | tf_op jit(solution)/shard_map/pallas_call | solution.py:563
  251.3 1.2 collective-permute-start.34
  252.7 2.5 multiply_reduce_fusion
  255.4 5.1 %fusion.62 = (bf16[512,896]{1,0:T(8,128)(2,1)S(1)}, f32[512,896]{1,0:T(8,128)}) fusion(f32[512,896]{1,0:T(8,128)} %copy-done.20, f32[512]{0:T(512)S(1)} %fusion.59, bf16[512,896]{1,0:T(8,128)(2,1)} %copy-done.27, bf16[2,512,896]{2,1,0:T(8,128)(2,1)} %collective-permute-done.33, bf16[2,512,896]{2,1,0:T(8,128)(2,1)} %get-tuple-element.111, ...), kind=kLoop, calls=%fused_computation.182 | loop fusion | flops 5046272 | bytes 9182720 | tf_op jit(solution)/shard_map/convert_element_type | solution.py:883
  261.0 1.9 collective-permute-done.35.refs_1_.other_ref
  265.1 1.2 copy-done.16
  266.3 1.7 shard_map.193
  272.2 17.8 %shard_map.194 = (bf16[1024,256]{1,0:T(8,128)(2,1)S(1)}, f32[1,256]{1,0:T(1,128)S(1)}, f32[1024,128]{1,0:T(8,128)S(1)}, f32[1024,128]{1,0:T(8,128)S(1)}) custom-call(s32[1]{0:T(128)} %bitcast.1.parity_ref, bf16[512,896]{1,0:T(8,128)(2,1)} %copy-done.2, bf16[512,896]{1,0:T(8,128)(2,1)} %copy-done.11, bf16[1024,512]{1,0:T(8,128)(2,1)} %copy-done.17, ...), custom_call_target="tpu_custom_call" | custom-call | flops 12000000000 | bytes 6000000 | tf_op jit(solution)/shard_map/pallas_call | solution.py:352
  291.1 15.1 %shard_map.195 = (bf16[1024,320]{1,0:T(8,128)(2,1)S(1)}, f32[1,320]{1,0:T(1,128)S(1)}) custom-call(s32[1]{0:T(128)} %bitcast.1.parity_ref, bf16[512,896]{1,0:T(8,128)(2,1)} %copy-done.2, bf16[512,896]{1,0:T(8,128)(2,1)} %copy-done.11, bf16[1024,512]{1,0:T(8,128)(2,1)} %copy-done.17, bf16[1024,64]{1,0:T(8,128)(2,1)S(1)} %copy-done.19, ...), custom_call_target="tpu_custom_call" | custom-call | flops 12000000000 | bytes 6000000 | tf_op jit(solution)/shard_map/pallas_call | solution.py:352
  306.4 3.7 shard_map.196
  310.1 1.9 convolution_convert_fusion
  312.0 2.2 collective-permute-start.45
  315.5 4.9 %fusion.15 = bf16[512,896]{1,0:T(8,128)(2,1)} fusion(s32[896]{0:T(1024)S(1)} %fusion.54, f32[512,896]{1,0:T(8,128)} %copy-done.20, bf16[512,896]{1,0:T(8,128)(2,1)} %collective-permute-done.34, bf16[2,512,896]{2,1,0:T(8,128)(2,1)} %collective-permute-done.33, bf16[2,512,896]{2,1,0:T(8,128)(2,1)} %get-tuple-element.111), kind=kOutput, calls=%fused_computation.35 | convolution fusion | flops 826556416 | bytes 5508608 | tf_op jit(solution)/shard_map/dot_general | solution.py:773
  321.5 3.6 multiply_reduce_fusion.1
  325.8 9.3 %collective-permute-done.43 = bf16[448,576]{1,0:T(8,128)(2,1)} collective-permute-done((bf16[448,576]{1,0:T(8,128)(2,1)}, bf16[448,576]{1,0:T(8,128)(2,1)}, u32[]{:S(2)}, u32[]{:S(2)}) %collective-permute-start.43) | collective-permute-done | bytes 516128 | tf_op jit(solution)/shard_map/ppermute | solution.py:23
  335.1 1.3 add_convert_fusion.2
  336.9 1.3 collective-permute-start.39
  338.3 2.3 collective-permute-done.39
  341.3 6.8 %collective-permute-done.44 = bf16[224,576]{1,0:T(8,128)(2,1)S(1)} collective-permute-done((bf16[224,576]{1,0:T(8,128)(2,1)S(1)}, bf16[224,576]{1,0:T(8,128)(2,1)S(1)}, u32[]{:S(2)}, u32[]{:S(2)}) %collective-permute-start.44) | collective-permute-done | bytes 258080 | tf_op jit(solution)/shard_map/ppermute | solution.py:23
  348.3 1.5 collective-permute-start.46
  351.0 4.0 %collective-permute-done.41 = f32[23,128]{1,0:T(8,128)S(1)} collective-permute-done((f32[23,128]{1,0:T(8,128)S(1)}, f32[23,128]{1,0:T(8,128)S(1)}, u32[]{:S(2)}, u32[]{:S(2)}) %collective-permute-start.41) | collective-permute-done | bytes 11808 | tf_op jit(solution)/shard_map/ppermute | solution.py:23
  355.0 2.9 collective-permute-start.42
  357.9 2.5 fusion.16
  360.4 2.7 collective-permute-done.42
  364.9 2.9 collective-permute-start.48
  368.4 3.4 collective-permute-done.48
  373.5 1.2 fusion.65
  (297 shorter events, 49.8 us)
Async XLA Ops:
  7.2 366.2 %reduce-scatter.2.cloned.1.call-start = ((), (), s32[]{:S(2)}) async-start(), calls=%async_computation.1 | async-start | bytes 4644864 | tf_op jit(solution)/shard_map/reduce_scatter | solution.py:873
  10.1 17.9 %collective-permute-start.1 = (bf16[128,512]{1,0:T(8,128)(2,1)S(1)}, bf16[128,512]{1,0:T(8,128)(2,1)S(1)}, u32[]{:S(2)}, u32[]{:S(2)}) collective-permute-start(bf16[128,512]{1,0:T(8,128)(2,1)S(1)} %fusion.51), channel_id=1, source_target_pairs={{0,2},{1,0},{2,3},{3,1},{4,6},{5,4},{6,7},{7,5},{8,10},{9,8},{10,1... | collective-permute-start | bytes 393224 | tf_op jit(solution)/shard_map/ppermute | solution.py:694
  13.1 14.9 %collective-permute-start = (bf16[128,512]{1,0:T(8,128)(2,1)S(1)}, bf16[128,512]{1,0:T(8,128)(2,1)S(1)}, u32[]{:S(2)}, u32[]{:S(2)}) collective-permute-start(bf16[128,512]{1,0:T(8,128)(2,1)S(1)} %fusion.51), channel_id=1, source_target_pairs={{0,0},{1,2},{2,1},{3,3},{4,4},{5,6},{6,5},{7,7},{8,8},{9,10},{10,9... | collective-permute-start | bytes 393224 | tf_op jit(solution)/shard_map/ppermute | solution.py:694
  17.3 40.7 %collective-permute-start.9 = (bf16[112,1536]{1,0:T(8,128)(2,1)}, bf16[112,1536]{1,0:T(8,128)(2,1)}, u32[]{:S(2)}, u32[]{:S(2)}) collective-permute-start(bf16[112,1536]{1,0:T(8,128)(2,1)} %pad_maximum_fusion.8.refs_8_), channel_id=1, source_target_pairs={{0,16},{4,20},{8,24},{12,28},{16,0},{20,4},{24,8},{28,12},{1,17},{... | collective-permute-start | bytes 1032200 | tf_op jit(solution)/shard_map/ppermute | solution.py:23
  19.9 36.0 %collective-permute-start.7 = (bf16[112,1536]{1,0:T(8,128)(2,1)}, bf16[112,1536]{1,0:T(8,128)(2,1)}, u32[]{:S(2)}, u32[]{:S(2)}) collective-permute-start(bf16[112,1536]{1,0:T(8,128)(2,1)} %pad_maximum_fusion.8.refs_8_), channel_id=1, source_target_pairs={{0,4},{4,0},{8,12},{12,8},{16,20},{20,16},{24,28},{28,24},{1,5},{5... | collective-permute-start | bytes 1032200 | tf_op jit(solution)/shard_map/ppermute | solution.py:23
  29.0 14.3 %collective-permute-start.4 = (bf16[112,576]{1,0:T(8,128)(2,1)S(1)}, bf16[112,576]{1,0:T(8,128)(2,1)S(1)}, u32[]{:S(2)}, u32[]{:S(2)}) collective-permute-start(bf16[112,576]{1,0:T(8,128)(2,1)S(1)} %get-tuple-element.157.rest_0_), channel_id=1, source_target_pairs={{0,4},{4,0},{8,12},{12,8},{16,20},{20,16},{24,28},{28,24},{1,5},{5... | collective-permute-start | bytes 387080 | tf_op jit(solution)/shard_map/ppermute | solution.py:23
  29.5 13.1 %collective-permute-start.3 = (bf16[112,576]{1,0:T(8,128)(2,1)S(1)}, bf16[112,576]{1,0:T(8,128)(2,1)S(1)}, u32[]{:S(2)}, u32[]{:S(2)}) collective-permute-start(bf16[112,576]{1,0:T(8,128)(2,1)S(1)} %get-tuple-element.157.rest_0_), channel_id=1, source_target_pairs={{0,16},{4,20},{8,24},{12,28},{16,0},{20,4},{24,8},{28,12},{1,17},{... | collective-permute-start | bytes 387080 | tf_op jit(solution)/shard_map/ppermute | solution.py:23
  31.5 37.1 %collective-permute-start.2 = (bf16[512,896]{1,0:T(8,128)(2,1)S(1)}, bf16[512,896]{1,0:T(8,128)(2,1)}, u32[]{:S(2)}, u32[]{:S(2)}) collective-permute-start(bf16[512,896]{1,0:T(8,128)(2,1)S(1)} %multiply_convert_fusion.1.own_ref.refs_0_), channel_id=1, source_target_pairs={{0,1},{1,0},{2,3},{3,2},{4,5},{5,4},{6,7},{7,6},{8,9},{9,8},{10,11... | collective-permute-start | bytes 2752520 | tf_op jit(solution)/shard_map/ppermute | solution.py:23
  42.6 8.7 %collective-permute-start.11 = (bf16[112,512]{1,0:T(8,128)(2,1)S(1)}, bf16[112,512]{1,0:T(8,128)(2,1)S(1)}, u32[]{:S(2)}, u32[]{:S(2)}) collective-permute-start(bf16[112,512]{1,0:T(8,128)(2,1)S(1)} %fusion.53.rest_0_), channel_id=1, source_target_pairs={{0,16},{4,20},{8,24},{12,28},{16,0},{20,4},{24,8},{28,12},{1,17},{... | collective-permute-start | bytes 344072 | tf_op jit(solution)/shard_map/ppermute | solution.py:23
  43.3 12.6 %collective-permute-start.5 = (bf16[224,576]{1,0:T(8,128)(2,1)}, bf16[224,576]{1,0:T(8,128)(2,1)S(1)}, u32[]{:S(2)}, u32[]{:S(2)}) collective-permute-start(bf16[224,576]{1,0:T(8,128)(2,1)} %pad_maximum_fusion.10), channel_id=1, source_target_pairs={{0,8},{4,12},{8,0},{12,4},{16,24},{20,28},{24,16},{28,20},{1,9},{5... | collective-permute-start | bytes 774152 | tf_op jit(solution)/shard_map/ppermute | solution.py:23
  48.5 40.1 %copy-start.3 = (f32[1024,128]{1,0:T(8,128)}, f32[1024,128]{1,0:T(8,128)S(1)}, u32[]{:S(2)}) copy-start(f32[1024,128]{1,0:T(8,128)S(1)} %get-tuple-element.228.cos_ref) | copy-start | bytes 1572868
  48.6 40.1 %copy-start.5 = (f32[1024,128]{1,0:T(8,128)}, f32[1024,128]{1,0:T(8,128)S(1)}, u32[]{:S(2)}) copy-start(f32[1024,128]{1,0:T(8,128)S(1)} %get-tuple-element.229.sin_ref) | copy-start | bytes 1572868
  51.2 5.1 %collective-permute-start.6 = (bf16[112,576]{1,0:T(8,128)(2,1)S(1)}, bf16[112,576]{1,0:T(8,128)(2,1)S(1)}, u32[]{:S(2)}, u32[]{:S(2)}) collective-permute-start(bf16[112,576]{1,0:T(8,128)(2,1)S(1)} %collective-permute-done.3.rest_1_), channel_id=1, source_target_pairs={{0,4},{4,0},{8,12},{12,8},{16,20},{20,16},{24,28},{28,24},{1,5},{5... | collective-permute-start | bytes 387080 | tf_op jit(solution)/shard_map/ppermute | solution.py:23
  56.0 32.8 %collective-permute-start.14 = (bf16[512,896]{1,0:T(8,128)(2,1)}, bf16[512,896]{1,0:T(8,128)(2,1)S(1)}, u32[]{:S(2)}, u32[]{:S(2)}) collective-permute-start(bf16[512,896]{1,0:T(8,128)(2,1)} %get-tuple-element.93.refs_4_.refs_2_), channel_id=1, source_target_pairs={{0,2},{1,3},{2,0},{3,1},{4,6},{5,7},{6,4},{7,5},{8,10},{9,11},{10,... | collective-permute-start | bytes 2752520 | tf_op jit(solution)/shard_map/ppermute | solution.py:23
  56.3 32.3 %copy-start.9 = (bf16[112,576]{1,0:T(8,128)(2,1)}, bf16[112,576]{1,0:T(8,128)(2,1)S(1)}, u32[]{:S(2)}) copy-start(bf16[112,576]{1,0:T(8,128)(2,1)S(1)} %collective-permute-done.6.rest_4_) | copy-start | bytes 387076
  56.3 8.5 %collective-permute-start.12 = (bf16[224,512]{1,0:T(8,128)(2,1)S(1)}, bf16[224,512]{1,0:T(8,128)(2,1)S(1)}, u32[]{:S(2)}, u32[]{:S(2)}) collective-permute-start(bf16[224,512]{1,0:T(8,128)(2,1)S(1)} %pad_maximum_fusion.12), channel_id=1, source_target_pairs={{0,8},{4,12},{8,0},{12,4},{16,24},{20,28},{24,16},{28,20},{1,9},{5... | collective-permute-start | bytes 688136 | tf_op jit(solution)/shard_map/ppermute | solution.py:23
  56.5 8.4 %collective-permute-start.8 = (bf16[224,576]{1,0:T(8,128)(2,1)S(1)}, bf16[224,576]{1,0:T(8,128)(2,1)S(1)}, u32[]{:S(2)}, u32[]{:S(2)}) collective-permute-start(bf16[224,576]{1,0:T(8,128)(2,1)S(1)} %collective-permute-done.5.rest_2_), channel_id=1, source_target_pairs={{0,4},{4,0},{8,12},{12,8},{16,20},{20,16},{24,28},{28,24},{1,5},{5... | collective-permute-start | bytes 774152 | tf_op jit(solution)/shard_map/ppermute | solution.py:23
  59.2 29.5 %collective-permute-start.15 = (bf16[112,2304]{1,0:T(8,128)(2,1)}, bf16[112,2304]{1,0:T(8,128)(2,1)S(1)}, u32[]{:S(2)}, u32[]{:S(2)}) collective-permute-start(bf16[112,2304]{1,0:T(8,128)(2,1)} %fusion.34.refs_4_), channel_id=1, source_target_pairs={{0,16},{4,20},{8,24},{12,28},{16,0},{20,4},{24,8},{28,12},{1,17},{... | collective-permute-start | bytes 1548296 | tf_op jit(solution)/shard_map/ppermute | solution.py:23
  64.9 204.3 %copy-start.7 = (bf16[224,512]{1,0:T(8,128)(2,1)}, bf16[224,512]{1,0:T(8,128)(2,1)S(1)}, u32[]{:S(2)}) copy-start(bf16[224,512]{1,0:T(8,128)(2,1)S(1)} %collective-permute-done.12.rest_2_) | copy-start | bytes 688132
  64.9 23.8 %collective-permute-start.13 = (bf16[224,1536]{1,0:T(8,128)(2,1)S(1)}, bf16[224,1536]{1,0:T(8,128)(2,1)S(1)}, u32[]{:S(2)}, u32[]{:S(2)}) collective-permute-start(bf16[224,1536]{1,0:T(8,128)(2,1)S(1)} %pad_maximum_fusion), channel_id=1, source_target_pairs={{0,8},{4,12},{8,0},{12,4},{16,24},{20,28},{24,16},{28,20},{1,9},{5... | collective-permute-start | bytes 2064392 | tf_op jit(solution)/shard_map/ppermute | solution.py:23
  64.9 23.8 %collective-permute-start.10 = (bf16[112,1536]{1,0:T(8,128)(2,1)}, bf16[112,1536]{1,0:T(8,128)(2,1)S(1)}, u32[]{:S(2)}, u32[]{:S(2)}) collective-permute-start(bf16[112,1536]{1,0:T(8,128)(2,1)} %collective-permute-done.9.refs_9_), channel_id=1, source_target_pairs={{0,4},{4,0},{8,12},{12,8},{16,20},{20,16},{24,28},{28,24},{1,5},{5... | collective-permute-start | bytes 1032200 | tf_op jit(solution)/shard_map/ppermute | solution.py:23
  68.6 20.2 %collective-permute-start.16 = (bf16[448,512]{1,0:T(8,128)(2,1)S(1)}, bf16[448,512]{1,0:T(8,128)(2,1)S(1)}, u32[]{:S(2)}, u32[]{:S(2)}) collective-permute-start(bf16[448,512]{1,0:T(8,128)(2,1)S(1)} %pad_maximum_fusion.7), channel_id=1, source_target_pairs={{0,4},{4,0},{8,12},{12,8},{16,20},{20,16},{24,28},{28,24},{1,5},{5... | collective-permute-start | bytes 1376264 | tf_op jit(solution)/shard_map/ppermute | solution.py:23
  88.7 29.3 %copy-start.44 = (bf16[112,2304]{1,0:T(8,128)(2,1)}, bf16[112,2304]{1,0:T(8,128)(2,1)S(1)}, u32[]{:S(2)}) copy-start(bf16[112,2304]{1,0:T(8,128)(2,1)S(1)} %collective-permute-done.15.refs_5_) | copy-start | bytes 1548292
  88.7 26.5 %copy-start.52 = (bf16[512,896]{1,0:T(8,128)(2,1)}, bf16[512,896]{1,0:T(8,128)(2,1)S(1)}, u32[]{:S(2)}) copy-start(bf16[512,896]{1,0:T(8,128)(2,1)S(1)} %collective-permute-done.14.refs_6_.refs_2_) | copy-start | bytes 2752516
  91.0 2.5 collective-permute-start.17
  94.0 23.9 %copy-start.28 = (bf16[112,2304]{1,0:T(8,128)(2,1)S(1)}, bf16[112,2304]{1,0:T(8,128)(2,1)}, u32[]{:S(2)}) copy-start(bf16[112,2304]{1,0:T(8,128)(2,1)} %fusion.34.refs_4_) | copy-start | bytes 1548292
  95.4 28.5 %copy-start.39 = (bf16[512,896]{1,0:T(8,128)(2,1)}, bf16[512,896]{1,0:T(8,128)(2,1)S(1)}, u32[]{:S(2)}) copy-start(bf16[512,896]{1,0:T(8,128)(2,1)S(1)} %multiply_convert_fusion.refs_0_) | copy-start | bytes 2752516
  95.4 22.5 %collective-permute-start.18 = (bf16[512,896]{1,0:T(8,128)(2,1)S(1)}, bf16[512,896]{1,0:T(8,128)(2,1)S(1)}, u32[]{:S(2)}, u32[]{:S(2)}) collective-permute-start(bf16[512,896]{1,0:T(8,128)(2,1)S(1)} %multiply_convert_fusion.refs_0_), channel_id=1, source_target_pairs={{0,2},{1,3},{2,0},{3,1},{4,6},{5,7},{6,4},{7,5},{8,10},{9,11},{10,... | collective-permute-start | bytes 2752520 | tf_op jit(solution)/shard_map/ppermute | solution.py:23
  97.2 17.5 %collective-permute-start.19 = (bf16[224,1536]{1,0:T(8,128)(2,1)S(1)}, bf16[224,1536]{1,0:T(8,128)(2,1)}, u32[]{:S(2)}, u32[]{:S(2)}) collective-permute-start(bf16[224,1536]{1,0:T(8,128)(2,1)S(1)} %collective-permute-done.13.refs_10_), channel_id=1, source_target_pairs={{0,4},{4,0},{8,12},{12,8},{16,20},{20,16},{24,28},{28,24},{1,5},{5... | collective-permute-start | bytes 2064392 | tf_op jit(solution)/shard_map/ppermute | solution.py:23
  114.7 5.3 %collective-permute-start.20 = (bf16[512,896]{1,0:T(8,128)(2,1)S(1)}, bf16[512,896]{1,0:T(8,128)(2,1)S(1)}, u32[]{:S(2)}, u32[]{:S(2)}) collective-permute-start(bf16[512,896]{1,0:T(8,128)(2,1)S(1)} %multiply_convert_fusion.refs_0_), channel_id=1, source_target_pairs={{0,1},{1,0},{2,3},{3,2},{4,5},{5,4},{6,7},{7,6},{8,9},{9,8},{10,11... | collective-permute-start | bytes 2752520 | tf_op jit(solution)/shard_map/ppermute | solution.py:23
  114.7 7.3 %collective-permute-start.22 = (bf16[512,896]{1,0:T(8,128)(2,1)S(1)}, bf16[512,896]{1,0:T(8,128)(2,1)S(1)}, u32[]{:S(2)}, u32[]{:S(2)}) collective-permute-start(bf16[512,896]{1,0:T(8,128)(2,1)S(1)} %copy-done.51), channel_id=1, source_target_pairs={{0,1},{1,0},{2,3},{3,2},{4,5},{5,4},{6,7},{7,6},{8,9},{9,8},{10,11... | collective-permute-start | bytes 2752520 | tf_op jit(solution)/shard_map/ppermute | solution.py:23
  115.3 6.8 %collective-permute-start.23 = (bf16[512,896]{1,0:T(8,128)(2,1)S(1)}, bf16[512,896]{1,0:T(8,128)(2,1)S(1)}, u32[]{:S(2)}, u32[]{:S(2)}) collective-permute-start(bf16[512,896]{1,0:T(8,128)(2,1)S(1)} %collective-permute-done.14.refs_6_.refs_2_), channel_id=1, source_target_pairs={{0,1},{1,0},{2,3},{3,2},{4,5},{5,4},{6,7},{7,6},{8,9},{9,8},{10,11... | collective-permute-start | bytes 2752520 | tf_op jit(solution)/shard_map/ppermute | solution.py:23
  117.9 6.0 %collective-permute-start.21 = (bf16[512,896]{1,0:T(8,128)(2,1)S(1)}, bf16[512,896]{1,0:T(8,128)(2,1)}, u32[]{:S(2)}, u32[]{:S(2)}) collective-permute-start(bf16[512,896]{1,0:T(8,128)(2,1)S(1)} %collective-permute-done.18.refs_2_.refs_0_), channel_id=1, source_target_pairs={{0,1},{1,0},{2,3},{3,2},{4,5},{5,4},{6,7},{7,6},{8,9},{9,8},{10,11... | collective-permute-start | bytes 2752520 | tf_op jit(solution)/shard_map/ppermute | solution.py:23
  118.0 30.4 %collective-permute-start.25 = (bf16[224,2304]{1,0:T(8,128)(2,1)S(1)}, bf16[224,2304]{1,0:T(8,128)(2,1)S(1)}, u32[]{:S(2)}, u32[]{:S(2)}) collective-permute-start(bf16[224,2304]{1,0:T(8,128)(2,1)S(1)} %constant_dynamic-update-slice_fusion), channel_id=1, source_target_pairs={{0,4},{4,0},{8,12},{12,8},{16,20},{20,16},{24,28},{28,24},{1,5},{5... | collective-permute-start | bytes 3096584 | tf_op jit(solution)/shard_map/ppermute | solution.py:23
  120.0 28.4 %collective-permute-start.24 = (bf16[224,2304]{1,0:T(8,128)(2,1)S(1)}, bf16[224,2304]{1,0:T(8,128)(2,1)}, u32[]{:S(2)}, u32[]{:S(2)}) collective-permute-start(bf16[224,2304]{1,0:T(8,128)(2,1)S(1)} %constant_dynamic-update-slice_fusion), channel_id=1, source_target_pairs={{0,8},{4,12},{8,0},{12,4},{16,24},{20,28},{24,16},{28,20},{1,9},{5... | collective-permute-start | bytes 3096584 | tf_op jit(solution)/shard_map/ppermute | solution.py:23
  148.4 26.0 %collective-permute-start.26 = (bf16[224,2304]{1,0:T(8,128)(2,1)}, bf16[224,2304]{1,0:T(8,128)(2,1)S(1)}, u32[]{:S(2)}, u32[]{:S(2)}) collective-permute-start(bf16[224,2304]{1,0:T(8,128)(2,1)} %collective-permute-done.24.refs_6_), channel_id=1, source_target_pairs={{0,4},{4,0},{8,12},{12,8},{16,20},{20,16},{24,28},{28,24},{1,5},{5... | collective-permute-start | bytes 3096584 | tf_op jit(solution)/shard_map/ppermute | solution.py:23
  164.2 31.6 %collective-permute-start.28 = (bf16[448,512]{1,0:T(8,128)(2,1)}, bf16[448,512]{1,0:T(8,128)(2,1)}, u32[]{:S(2)}, u32[]{:S(2)}) collective-permute-start(bf16[448,512]{1,0:T(8,128)(2,1)} %get-tuple-element.106), channel_id=1, source_target_pairs={{0,8},{4,12},{8,0},{12,4},{16,24},{20,28},{24,16},{28,20},{1,9},{5... | collective-permute-start | bytes 1376264 | tf_op jit(solution)/shard_map/ppermute | solution.py:23
  165.1 30.7 %collective-permute-start.27 = (bf16[448,1024]{1,0:T(8,128)(2,1)}, bf16[448,1024]{1,0:T(8,128)(2,1)}, u32[]{:S(2)}, u32[]{:S(2)}) collective-permute-start(bf16[448,1024]{1,0:T(8,128)(2,1)} %get-tuple-element.105), channel_id=1, source_target_pairs={{0,4},{4,0},{8,12},{12,8},{16,20},{20,16},{24,28},{28,24},{1,5},{5... | collective-permute-start | bytes 2752520 | tf_op jit(solution)/shard_map/ppermute | solution.py:23
  175.4 22.0 %copy-start.40 = (f32[448,512]{1,0:T(8,128)S(1)}, f32[448,512]{1,0:T(8,128)}, u32[]{:S(2)}) copy-start(f32[448,512]{1,0:T(8,128)} %get-tuple-element.113) | copy-start | bytes 2752516
  195.8 6.2 %collective-permute-start.29 = (bf16[2,512,896]{2,1,0:T(8,128)(2,1)}, bf16[2,512,896]{2,1,0:T(8,128)(2,1)}, u32[]{:S(2)}, u32[]{:S(2)}) collective-permute-start(bf16[2,512,896]{2,1,0:T(8,128)(2,1)} %get-tuple-element.107), channel_id=1, source_target_pairs={{0,1},{1,0},{2,3},{3,2},{4,5},{5,4},{6,7},{7,6},{8,9},{9,8},{10,11... | collective-permute-start | bytes 5505032 | tf_op jit(solution)/shard_map/ppermute | solution.py:23
  198.5 28.1 %collective-permute-start.32 = (bf16[224,512]{1,0:T(8,128)(2,1)S(1)}, bf16[224,512]{1,0:T(8,128)(2,1)S(1)}, u32[]{:S(2)}, u32[]{:S(2)}) collective-permute-start(bf16[224,512]{1,0:T(8,128)(2,1)S(1)} %get-tuple-element.171), channel_id=1, source_target_pairs={{0,4},{4,0},{8,12},{12,8},{16,20},{20,16},{24,28},{28,24},{1,5},{5... | collective-permute-start | bytes 688136 | tf_op jit(solution)/shard_map/ppermute | solution.py:23
  201.0 25.6 %collective-permute-start.31 = (bf16[224,1024]{1,0:T(8,128)(2,1)}, bf16[224,1024]{1,0:T(8,128)(2,1)}, u32[]{:S(2)}, u32[]{:S(2)}) collective-permute-start(bf16[224,1024]{1,0:T(8,128)(2,1)} %get-tuple-element.163), channel_id=1, source_target_pairs={{0,8},{4,12},{8,0},{12,4},{16,24},{20,28},{24,16},{28,20},{1,9},{5... | collective-permute-start | bytes 1376264 | tf_op jit(solution)/shard_map/ppermute | solution.py:23
  205.0 22.1 %collective-permute-start.30 = (bf16[512,896]{1,0:T(8,128)(2,1)S(1)}, bf16[512,896]{1,0:T(8,128)(2,1)S(1)}, u32[]{:S(2)}, u32[]{:S(2)}) collective-permute-start(bf16[512,896]{1,0:T(8,128)(2,1)S(1)} %get-tuple-element.164), channel_id=1, source_target_pairs={{0,2},{1,3},{2,0},{3,1},{4,6},{5,7},{6,4},{7,5},{8,10},{9,11},{10,... | collective-permute-start | bytes 2752520 | tf_op jit(solution)/shard_map/ppermute | solution.py:23
  206.3 21.6 %copy-start.10 = (bf16[112,576]{1,0:T(8,128)(2,1)S(1)}, bf16[112,576]{1,0:T(8,128)(2,1)}, u32[]{:S(2)}) copy-start(bf16[112,576]{1,0:T(8,128)(2,1)} %copy-done.9) | copy-start | bytes 387076
  227.2 25.3 %collective-permute-start.33 = (bf16[2,512,896]{2,1,0:T(8,128)(2,1)}, bf16[2,512,896]{2,1,0:T(8,128)(2,1)}, u32[]{:S(2)}, u32[]{:S(2)}) collective-permute-start(bf16[2,512,896]{2,1,0:T(8,128)(2,1)} %get-tuple-element.114), channel_id=1, source_target_pairs={{0,1},{1,0},{2,3},{3,2},{4,5},{5,4},{6,7},{7,6},{8,9},{9,8},{10,11... | collective-permute-start | bytes 5505032 | tf_op jit(solution)/shard_map/ppermute | solution.py:23
  232.8 81.5 %collective-permute-start.49 = (bf16[112,1536]{1,0:T(8,128)(2,1)}, bf16[112,1536]{1,0:T(8,128)(2,1)}, u32[]{:S(2)}, u32[]{:S(2)}) collective-permute-start(bf16[112,1536]{1,0:T(8,128)(2,1)} %pad_maximum_fusion.9), channel_id=1, source_target_pairs={{0,16},{4,20},{8,24},{12,28},{16,0},{20,4},{24,8},{28,12},{1,17},{... | collective-permute-start | bytes 1032200 | tf_op jit(solution)/shard_map/ppermute | solution.py:23
  251.3 63.0 %collective-permute-start.34 = (bf16[512,896]{1,0:T(8,128)(2,1)}, bf16[512,896]{1,0:T(8,128)(2,1)}, u32[]{:S(2)}, u32[]{:S(2)}) collective-permute-start(bf16[512,896]{1,0:T(8,128)(2,1)} %get-tuple-element.115), channel_id=1, source_target_pairs={{0,2},{1,3},{2,0},{3,1},{4,6},{5,7},{6,4},{7,5},{8,10},{9,11},{10,... | collective-permute-start | bytes 2752520 | tf_op jit(solution)/shard_map/ppermute | solution.py:23
  260.5 2.5 collective-permute-start.35
  268.1 22.0 %collective-permute-start.36 = (bf16[448,512]{1,0:T(8,128)(2,1)S(1)}, bf16[448,512]{1,0:T(8,128)(2,1)S(1)}, u32[]{:S(2)}, u32[]{:S(2)}) collective-permute-start(bf16[448,512]{1,0:T(8,128)(2,1)S(1)} %get-tuple-element.126), channel_id=1, source_target_pairs={{0,4},{4,0},{8,12},{12,8},{16,20},{20,16},{24,28},{28,24},{1,5},{5... | collective-permute-start | bytes 1376264 | tf_op jit(solution)/shard_map/ppermute | solution.py:23
  312.0 9.5 %collective-permute-start.37 = (bf16[512,896]{1,0:T(8,128)(2,1)}, bf16[512,896]{1,0:T(8,128)(2,1)}, u32[]{:S(2)}, u32[]{:S(2)}) collective-permute-start(bf16[512,896]{1,0:T(8,128)(2,1)} %convolution_convert_fusion), channel_id=1, source_target_pairs={{0,1},{1,0},{2,3},{3,2},{4,5},{5,4},{6,7},{7,6},{8,9},{9,8},{10,11... | collective-permute-start | bytes 2752520 | tf_op jit(solution)/shard_map/ppermute | solution.py:23
  312.0 26.2 %collective-permute-start.45 = (bf16[224,512]{1,0:T(8,128)(2,1)}, bf16[224,512]{1,0:T(8,128)(2,1)S(1)}, u32[]{:S(2)}, u32[]{:S(2)}) collective-permute-start(bf16[224,512]{1,0:T(8,128)(2,1)} %get-tuple-element.172), channel_id=1, source_target_pairs={{0,8},{4,12},{8,0},{12,4},{16,24},{20,28},{24,16},{28,20},{1,9},{5... | collective-permute-start | bytes 688136 | tf_op jit(solution)/shard_map/ppermute | solution.py:23
  314.2 20.9 %collective-permute-start.43 = (bf16[448,576]{1,0:T(8,128)(2,1)}, bf16[448,576]{1,0:T(8,128)(2,1)}, u32[]{:S(2)}, u32[]{:S(2)}) collective-permute-start(bf16[448,576]{1,0:T(8,128)(2,1)} %get-tuple-element.137), channel_id=1, source_target_pairs={{0,4},{4,0},{8,12},{12,8},{16,20},{20,16},{24,28},{28,24},{1,5},{5... | collective-permute-start | bytes 1548296 | tf_op jit(solution)/shard_map/ppermute | solution.py:23
  325.7 32.2 %copy-start.31 = (f32[512,896]{1,0:T(8,128)S(1)}, f32[512,896]{1,0:T(8,128)}, u32[]{:S(2)}) copy-start(f32[512,896]{1,0:T(8,128)} %get-tuple-element.159) | copy-start | bytes 5505028
  325.7 22.4 %copy-start.26 = (f32[224,512]{1,0:T(8,128)S(1)}, f32[224,512]{1,0:T(8,128)}, u32[]{:S(2)}) copy-start(f32[224,512]{1,0:T(8,128)} %get-tuple-element.173) | copy-start | bytes 1376260
  325.7 11.1 %collective-permute-start.38 = (f32[23,128]{1,0:T(8,128)S(1)}, f32[23,128]{1,0:T(8,128)S(1)}, u32[]{:S(2)}, u32[]{:S(2)}) collective-permute-start(f32[23,128]{1,0:T(8,128)S(1)} %maximum_bitcast_fusion.1), channel_id=1, source_target_pairs={{0,1},{1,0},{2,3},{3,2},{4,5},{5,4},{6,7},{7,6},{8,9},{9,8},{10,11... | collective-permute-start | bytes 35336 | tf_op jit(solution)/shard_map/ppermute | solution.py:23
  335.1 22.8 %copy-start.29 = (f32[512,896]{1,0:T(8,128)S(1)}, f32[512,896]{1,0:T(8,128)}, u32[]{:S(2)}) copy-start(f32[512,896]{1,0:T(8,128)} %get-tuple-element.227) | copy-start | bytes 5505028
  336.4 11.8 %collective-permute-start.44 = (bf16[224,576]{1,0:T(8,128)(2,1)S(1)}, bf16[224,576]{1,0:T(8,128)(2,1)S(1)}, u32[]{:S(2)}, u32[]{:S(2)}) collective-permute-start(bf16[224,576]{1,0:T(8,128)(2,1)S(1)} %get-tuple-element.166), channel_id=1, source_target_pairs={{0,8},{4,12},{8,0},{12,4},{16,24},{20,28},{24,16},{28,20},{1,9},{5... | collective-permute-start | bytes 774152 | tf_op jit(solution)/shard_map/ppermute | solution.py:23
  336.9 3.8 collective-permute-start.39
  340.6 9.2 %collective-permute-start.40 = (f32[23,128]{1,0:T(8,128)S(1)}, f32[23,128]{1,0:T(8,128)S(1)}, u32[]{:S(2)}, u32[]{:S(2)}) collective-permute-start(f32[23,128]{1,0:T(8,128)S(1)} %fusion.81), channel_id=1, source_target_pairs={{0,4},{4,0},{8,12},{12,8},{16,20},{20,16},{24,28},{28,24},{1,5},{5... | collective-permute-start | bytes 35336 | tf_op jit(solution)/shard_map/ppermute | solution.py:23
  348.3 15.4 %collective-permute-start.46 = (bf16[112,1088]{1,0:T(8,128)(2,1)S(1)}, bf16[112,1088]{1,0:T(8,128)(2,1)S(1)}, u32[]{:S(2)}, u32[]{:S(2)}) collective-permute-start(bf16[112,1088]{1,0:T(8,128)(2,1)S(1)} %fusion.40), channel_id=1, source_target_pairs={{0,16},{4,20},{8,24},{12,28},{16,0},{20,4},{24,8},{28,12},{1,17},{... | collective-permute-start | bytes 731144 | tf_op jit(solution)/shard_map/ppermute | solution.py:23
  349.8 5.1 %collective-permute-start.41 = (f32[23,128]{1,0:T(8,128)S(1)}, f32[23,128]{1,0:T(8,128)S(1)}, u32[]{:S(2)}, u32[]{:S(2)}) collective-permute-start(f32[23,128]{1,0:T(8,128)S(1)} %add.220), channel_id=1, source_target_pairs={{0,8},{4,12},{8,0},{12,4},{16,24},{20,28},{24,16},{28,20},{1,9},{5... | collective-permute-start | bytes 35336 | tf_op jit(solution)/shard_map/ppermute | solution.py:23
  355.0 8.1 %collective-permute-start.42 = (f32[23,128]{1,0:T(8,128)S(1)}, f32[23,128]{1,0:T(8,128)S(1)}, u32[]{:S(2)}, u32[]{:S(2)}) collective-permute-start(f32[23,128]{1,0:T(8,128)S(1)} %add.221), channel_id=1, source_target_pairs={{0,16},{4,20},{8,24},{12,28},{16,0},{20,4},{24,8},{28,12},{1,17},{... | collective-permute-start | bytes 35336 | tf_op jit(solution)/shard_map/ppermute | solution.py:23
  364.2 4.1 %collective-permute-start.47 = (bf16[112,512]{1,0:T(8,128)(2,1)S(1)}, bf16[112,512]{1,0:T(8,128)(2,1)S(1)}, u32[]{:S(2)}, u32[]{:S(2)}) collective-permute-start(bf16[112,512]{1,0:T(8,128)(2,1)S(1)} %get-tuple-element.182), channel_id=1, source_target_pairs={{0,0},{1,2},{2,1},{3,3},{4,4},{5,6},{6,5},{7,7},{8,8},{9,10},{10,9... | collective-permute-start | bytes 344072 | tf_op jit(solution)/shard_map/ppermute | solution.py:700
  364.9 6.9 %collective-permute-start.48 = (bf16[112,512]{1,0:T(8,128)(2,1)S(1)}, bf16[112,512]{1,0:T(8,128)(2,1)S(1)}, u32[]{:S(2)}, u32[]{:S(2)}) collective-permute-start(bf16[112,512]{1,0:T(8,128)(2,1)S(1)} %get-tuple-element.183), channel_id=1, source_target_pairs={{0,1},{1,3},{2,0},{3,2},{4,5},{5,7},{6,4},{7,6},{8,9},{9,11},{10,8... | collective-permute-start | bytes 344072 | tf_op jit(solution)/shard_map/ppermute | solution.py:700
  (49 other events, 249.7 us)
Sparse Core Ops, SparseCore 0:
  251.4 93.5 reduce-scatter.1
